TPU v7x, 512 devices: a whole 4x8x8 slice. The times are simulated.
512 devices in a mesh: delay: 64 (over y, z_hi, core), dom: 8 (over x, z_lo).
Axes of the slice: x: 4, y: 8, z: 8 (z_hi: 4, z_lo: 2; z = z_hi * 2 + z_lo), core: 2. Of those that a mesh axis runs over, the one named last changes fastest.
Arguments:
- excitation: float32 [2, 4096, 128], P(None, 'dom', 'delay'), may hold values from -6 to 6
- retarded: bfloat16 [128, 4096, 512], P('delay', 'dom'), may hold values from -0.0234375 to 0.0234375
- history: bfloat16 [128, 4096, 128], P('delay', 'dom'), may hold values from -16 to 16
- inverse: bfloat16 [4096, 512], P('dom'), may hold values from -0.25 to 0.25
- transfer: bfloat16 [4096, 256], P('dom'), may hold values from -0.375 to 0.375
- faces: int32 [8, 256], P('dom'), may hold values from 0 to 511
- counts: int32 [8], P('dom'), may hold values from 64 to 128, as said below
Outputs:
- currents: float32 [2, 4096, 128], P(None, 'dom', 'delay')
- new_history: bfloat16 [128, 4096, 128], P('delay', 'dom')
Inputs may be any that keep to these rules, and one draw needn't show every extreme that they name: `faces`: each entry names an unknown of the domain's own cluster. `counts`: at least one domain couples through all 128 delays.
All inputs are finite; a program needn't handle non-finite values.
Results may differ from a plain program's by a relative error of at most 0.006.
Values may be sent and summed in bfloat16 or wider, within the bound.
No kernel may reach another device: no remote copies, remote signals or barrier semaphores. Data moves between devices by JAX's collectives and lax.ppermute only.
A program may use at most 64 MiB of HBM per device.

v0:
```python
import jax
import jax.numpy as jnp
from jax import lax
from jax.sharding import PartitionSpec as P


def with_halo(value, sides, width):
    for axis, dim in sides:
        devices, length = (lax.axis_size(axis), value.shape[dim])
        up = [(i, (i + 1) % devices) for i in range(devices)]
        down = [(j, i) for i, j in up]
        last = lax.slice_in_dim(value, length - width, length, axis=dim)
        initial = lax.slice_in_dim(value, 0, width, axis=dim)
        before = lax.ppermute(last, axis, up)
        after = lax.ppermute(initial, axis, down)
        value = jnp.concatenate([before, value, after], axis=dim)
    return value


def from_behind(value, axis, steps):
    count = lax.axis_size(axis)
    initial, last = (max(0, -steps), min(count, count - steps))
    return lax.ppermute(value, axis, [(source, source + steps) for source in range(initial, last)])


def cut_along(value, dim, devices):
    before, after = (value.shape[:dim], value.shape[dim + 1 :])
    return jnp.moveaxis(value.reshape(*before, devices, -1, *after), dim, 0)


def sent_and_summed(value, axis, dim):
    devices = lax.axis_size(axis)
    tiles = lax.all_to_all(cut_along(value, dim, devices), axis, 0, 0, tiled=True)
    return jnp.sum(tiles, axis=0)


def joined_along(tiles, dim):
    tiles = jnp.moveaxis(tiles, 0, dim)
    shape = tiles.shape
    return tiles.reshape(*shape[:dim], shape[dim] * shape[dim + 1], *shape[dim + 2 :])


def sent_to_all(value, axis):
    copies = jnp.broadcast_to(value, (lax.axis_size(axis), *value.shape))
    return lax.all_to_all(copies, axis, split_axis=0, concat_axis=0, tiled=True)


def gathered_copies(value, axis, dim):
    return joined_along(sent_to_all(value, axis), dim)


def body(excitation, retarded, history, inverse, transfer, faces, counts):
    position = lax.axis_index("delay")
    local_delays = retarded.shape[0]
    step_count = excitation.shape[0]
    face_rows = faces.shape[1] // 2
    delay_ids = position * local_delays + jnp.arange(local_delays, dtype=jnp.int32)
    live_mask = (delay_ids < counts[0]).astype(jnp.bfloat16)
    masked = retarded * live_mask[:, None, None]
    leading = position == 0
    incoming = from_behind(history, "delay", 1)

    def assemble(fresh_list, step_index):
        pieces = []
        for slot_index in range(local_delays):
            if slot_index >= step_index:
                pieces.append(history[slot_index - step_index])
            else:
                pieces.append(
                    jnp.where(
                        leading,
                        fresh_list[step_index - 1 - slot_index],
                        incoming[step_count - step_index + slot_index],
                    )
                )
        return jnp.stack(pieces)

    history_slots = history
    fresh_list = []
    outputs = []
    for step_index in range(step_count):
        history_slots = assemble(fresh_list, step_index)
        partial_value = jnp.einsum(
            "iab,ibn->an", masked, history_slots, preferred_element_type=jnp.float32
        )
        share_sum = sent_and_summed(partial_value, "delay", 1)
        first_pass = jnp.dot(
            inverse,
            (excitation[step_index] - share_sum).astype(jnp.bfloat16),
            preferred_element_type=jnp.float32,
        )
        trace_rows = jnp.take(first_pass, faces[0], axis=0).astype(jnp.bfloat16)
        extended = with_halo(trace_rows, (("dom", 0),), face_rows)
        neighbour = jnp.concatenate([extended[:face_rows], extended[3 * face_rows :]], axis=0)
        coupling = jnp.dot(transfer, neighbour, preferred_element_type=jnp.float32).astype(
            jnp.bfloat16
        )
        current = first_pass - jnp.dot(inverse, coupling, preferred_element_type=jnp.float32)
        outputs.append(current)
        newest = gathered_copies(current.astype(jnp.bfloat16), "delay", 1)
        fresh_list.append(newest)
    history_slots = assemble(fresh_list, step_count)
    return (jnp.stack(outputs), history_slots)


def solution(mesh):
    placed = (
        P(None, "dom", "delay"),
        P("delay", "dom", None),
        P("delay", "dom", None),
        P("dom", None),
        P("dom", None),
        P("dom", None),
        P("dom"),
    )
    return jax.shard_map(
        body,
        mesh=mesh,
        in_specs=placed,
        out_specs=(P(None, "dom", "delay"), P("delay", "dom", None)),
        check_vma=False,
    )
```

profile of v0, /device:TPU:1, one launch (start us, length us, event | category | flops | bytes accessed | tf_op | source)
XLA Modules:
  0.0 123.3 jit_solution(956541894638793999)
XLA Ops:
  1.4 1.8 %convolution_bitcast_fusion.1 = f32[512,128]{0,1:T(8,128)S(1)} fusion(bf16[2,512,128]{2,1,0:T(8,128)(2,1)} %param.11, bf16[2,512,512]{2,1,0:T(8,128)(2,1)} %param.10, bf16[2]{0:T(256)(128)(2,1)S(1)} %compare_convert_fusion), kind=kOutput, calls=%fused_computation.3 | convolution fusion | flops 134742016 | bytes 1572868 | tf_op jit(solution)/shard_map/iab,ibn->an/dot_general | solution.py:83
  3.2 0.8 reshape.29
  4.0 17.6 %all-to-all-start = ((f32[64,512,2]{1,2,0:T(2,128)}), f32[64,512,2]{1,2,0:T(2,128)S(1)}, u32[]{:S(2)}, u32[]{:S(2)}) async-start(f32[64,512,2]{1,2,0:T(2,128)} %bitcast.3), calls=%async_computation | async-start | bytes 524288 | tf_op jit(solution)/shard_map/all_to_all | solution.py:33
  21.7 0.7 copy-done.5
  22.4 14.8 %all-to-all-done = f32[64,512,2]{1,2,0:T(2,128)S(1)} async-done(((f32[64,512,2]{1,2,0:T(2,128)}), f32[64,512,2]{1,2,0:T(2,128)S(1)}, u32[]{:S(2)}, u32[]{:S(2)}) %all-to-all-start) | async-done | bytes 262176 | tf_op jit(solution)/shard_map/all_to_all | solution.py:33
  37.2 0.1 reduce_sum.18
  37.4 0.2 convolution_bitcast_fusion.5
  37.6 0.2 copy.16
  37.8 0.9 gather_fusion
  38.8 3.1 %collective-permute-start = (bf16[128,2]{1,0:T(8,128)(2,1)S(1)}, bf16[128,2]{1,0:T(8,128)(2,1)S(1)}, u32[]{:S(2)}, u32[]{:S(2)}) collective-permute-start(bf16[128,2]{1,0:T(8,128)(2,1)S(1)} %get-tuple-element.9), channel_id=1, source_target_pairs={{0,1},{1,2},{2,3},{3,4},{4,5},{5,6},{6,7},{7,0},{8,9},{9,10},{10,1... | collective-permute-start | bytes 1544 | tf_op jit(solution)/shard_map/ppermute | solution.py:14
  41.9 4.4 %collective-permute-start.1 = (bf16[128,2]{1,0:T(8,128)(2,1)S(1)}, bf16[128,2]{1,0:T(8,128)(2,1)S(1)}, u32[]{:S(2)}, u32[]{:S(2)}) collective-permute-start(bf16[128,2]{1,0:T(8,128)(2,1)S(1)} %get-tuple-element.10), channel_id=1, source_target_pairs={{1,0},{2,1},{3,2},{4,3},{5,4},{6,5},{7,6},{0,7},{9,8},{10,9},{11,1... | collective-permute-start | bytes 1544 | tf_op jit(solution)/shard_map/ppermute | solution.py:15
  46.3 0.1 copy.19
  46.5 3.8 %collective-permute-start.2 = (bf16[2,512,128]{1,2,0:T(8,128)(2,1)S(1)}, bf16[2,512,128]{1,2,0:T(8,128)(2,1)S(1)}, u32[]{:S(2)}, u32[]{:S(2)}) collective-permute-start(bf16[2,512,128]{1,2,0:T(8,128)(2,1)S(1)} %copy.19), channel_id=1, source_target_pairs={{0,8},{8,16},{16,24},{24,32},{32,40},{40,48},{48,56},{56,64},{64,7... | collective-permute-start | bytes 786440 | tf_op jit(solution)/shard_map/ppermute | solution.py:23
  50.5 0.3 fusion.32
  50.8 0.8 broadcast_in_dim.16
  51.6 6.7 %all-to-all-start.1 = ((bf16[64,512,2]{1,2,0:T(2,128)(2,1)}), bf16[64,512,2]{1,2,0:T(2,128)(2,1)S(1)}, u32[]{:S(2)}, u32[]{:S(2)}) async-start(bf16[64,512,2]{1,2,0:T(2,128)(2,1)} %broadcast_in_dim.16), calls=%async_computation.1 | async-start | bytes 262144 | tf_op jit(solution)/shard_map/all_to_all | solution.py:45
  58.3 13.5 %all-to-all-done.1 = bf16[64,512,2]{1,2,0:T(2,128)(2,1)S(1)} async-done(((bf16[64,512,2]{1,2,0:T(2,128)(2,1)}), bf16[64,512,2]{1,2,0:T(2,128)(2,1)S(1)}, u32[]{:S(2)}, u32[]{:S(2)}) %all-to-all-start.1) | async-done | bytes 131104 | tf_op jit(solution)/shard_map/all_to_all | solution.py:45
  71.9 0.5 convolution_bitcast_fusion
  72.5 0.1 reshape.31
  72.6 19.3 %all_to_all.20 = f32[64,512,2]{1,2,0:T(2,128)S(1)} all-to-all(f32[64,512,2]{1,2,0:T(2,128)S(1)} %bitcast.50), channel_id=1, replica_groups=mesh['delay'=64,'dom'=8] {'delay'}, dimensions={0} | all-to-all | bytes 524288 | tf_op jit(solution)/shard_map/all_to_all | solution.py:33
  92.0 0.2 convolution_bitcast_fusion.3
  92.3 0.2 copy.21
  92.5 0.9 gather_fusion.1
  93.5 1.9 %collective-permute-start.3 = (bf16[128,2]{1,0:T(8,128)(2,1)S(1)}, bf16[128,2]{1,0:T(8,128)(2,1)S(1)}, u32[]{:S(2)}, u32[]{:S(2)}) collective-permute-start(bf16[128,2]{1,0:T(8,128)(2,1)S(1)} %get-tuple-element.7), channel_id=1, source_target_pairs={{0,1},{1,2},{2,3},{3,4},{4,5},{5,6},{6,7},{7,0},{8,9},{9,10},{10,1... | collective-permute-start | bytes 1544 | tf_op jit(solution)/shard_map/ppermute | solution.py:14
  95.4 5.5 %collective-permute-start.4 = (bf16[128,2]{1,0:T(8,128)(2,1)S(1)}, bf16[128,2]{1,0:T(8,128)(2,1)S(1)}, u32[]{:S(2)}, u32[]{:S(2)}) collective-permute-start(bf16[128,2]{1,0:T(8,128)(2,1)S(1)} %get-tuple-element.8), channel_id=1, source_target_pairs={{1,0},{2,1},{3,2},{4,3},{5,4},{6,5},{7,6},{0,7},{9,8},{10,9},{11,1... | collective-permute-start | bytes 1544 | tf_op jit(solution)/shard_map/ppermute | solution.py:15
  101.0 0.9 collective-permute-done.4
  101.9 0.4 fusion.35
  102.3 0.8 broadcast_in_dim.17
  103.1 5.5 %all-to-all-start.3 = ((bf16[64,512,2]{1,2,0:T(2,128)(2,1)}), bf16[64,512,2]{1,2,0:T(2,128)(2,1)S(1)}, u32[]{:S(2)}, u32[]{:S(2)}) async-start(bf16[64,512,2]{1,2,0:T(2,128)(2,1)} %broadcast_in_dim.17), calls=%async_computation.3 | async-start | bytes 262144 | tf_op jit(solution)/shard_map/all_to_all | solution.py:45
  108.5 0.6 pad_maximum_fusion.1
  109.1 13.1 %all-to-all-done.3 = bf16[64,512,2]{1,2,0:T(2,128)(2,1)S(1)} async-done(((bf16[64,512,2]{1,2,0:T(2,128)(2,1)}), bf16[64,512,2]{1,2,0:T(2,128)(2,1)S(1)}, u32[]{:S(2)}, u32[]{:S(2)}) %all-to-all-start.3) | async-done | bytes 131104 | tf_op jit(solution)/shard_map/all_to_all | solution.py:45
  122.4 0.8 copy.24
  (34 shorter events, 0.9 us)
Async XLA Ops:
  0.6 36.7 %copy-start = (bf16[512,512]{1,0:T(8,128)(2,1)S(1)}, bf16[512,512]{1,0:T(8,128)(2,1)}, u32[]{:S(2)}) copy-start(bf16[512,512]{1,0:T(8,128)(2,1)} %param.12) | copy-start | bytes 1572868
  4.0 33.2 %all-to-all-start = ((f32[64,512,2]{1,2,0:T(2,128)}), f32[64,512,2]{1,2,0:T(2,128)S(1)}, u32[]{:S(2)}, u32[]{:S(2)}) async-start(f32[64,512,2]{1,2,0:T(2,128)} %bitcast.3), calls=%async_computation | async-start | bytes 524288 | tf_op jit(solution)/shard_map/all_to_all | solution.py:33
  21.7 0.7 copy-start.5
  22.4 15.0 %copy-start.4 = (f32[2,512,2]{1,2,0:T(2,128)S(1)}, f32[2,512,2]{1,2,0:T(2,128)}, u32[]{:S(2)}) copy-start(f32[2,512,2]{1,2,0:T(2,128)} %param.9) | copy-start | bytes 24580
  38.7 7.7 %copy-start.3 = (bf16[2,512,128]{2,1,0:T(8,128)(2,1)S(1)}, bf16[2,512,128]{2,1,0:T(8,128)(2,1)}, u32[]{:S(2)}) copy-start(bf16[2,512,128]{2,1,0:T(8,128)(2,1)} %param.11) | copy-start | bytes 786436
  38.8 11.5 %collective-permute-start = (bf16[128,2]{1,0:T(8,128)(2,1)S(1)}, bf16[128,2]{1,0:T(8,128)(2,1)S(1)}, u32[]{:S(2)}, u32[]{:S(2)}) collective-permute-start(bf16[128,2]{1,0:T(8,128)(2,1)S(1)} %get-tuple-element.9), channel_id=1, source_target_pairs={{0,1},{1,2},{2,3},{3,4},{4,5},{5,6},{6,7},{7,0},{8,9},{9,10},{10,1... | collective-permute-start | bytes 1544 | tf_op jit(solution)/shard_map/ppermute | solution.py:14
  41.9 8.6 %copy-start.2 = (bf16[512,256]{1,0:T(8,128)(2,1)S(1)}, bf16[512,256]{1,0:T(8,128)(2,1)}, u32[]{:S(2)}) copy-start(bf16[512,256]{1,0:T(8,128)(2,1)} %param.13) | copy-start | bytes 786436
  41.9 8.5 %collective-permute-start.1 = (bf16[128,2]{1,0:T(8,128)(2,1)S(1)}, bf16[128,2]{1,0:T(8,128)(2,1)S(1)}, u32[]{:S(2)}, u32[]{:S(2)}) collective-permute-start(bf16[128,2]{1,0:T(8,128)(2,1)S(1)} %get-tuple-element.10), channel_id=1, source_target_pairs={{1,0},{2,1},{3,2},{4,3},{5,4},{6,5},{7,6},{0,7},{9,8},{10,9},{11,1... | collective-permute-start | bytes 1544 | tf_op jit(solution)/shard_map/ppermute | solution.py:15
  46.5 25.4 %collective-permute-start.2 = (bf16[2,512,128]{1,2,0:T(8,128)(2,1)S(1)}, bf16[2,512,128]{1,2,0:T(8,128)(2,1)S(1)}, u32[]{:S(2)}, u32[]{:S(2)}) collective-permute-start(bf16[2,512,128]{1,2,0:T(8,128)(2,1)S(1)} %copy.19), channel_id=1, source_target_pairs={{0,8},{8,16},{16,24},{24,32},{32,40},{40,48},{48,56},{56,64},{64,7... | collective-permute-start | bytes 786440 | tf_op jit(solution)/shard_map/ppermute | solution.py:23
  50.5 21.4 %copy-start.1 = (bf16[2,512,512]{2,1,0:T(8,128)(2,1)S(1)}, bf16[2,512,512]{2,1,0:T(8,128)(2,1)}, u32[]{:S(2)}) copy-start(bf16[2,512,512]{2,1,0:T(8,128)(2,1)} %param.10) | copy-start | bytes 3145732
  51.6 20.2 %all-to-all-start.1 = ((bf16[64,512,2]{1,2,0:T(2,128)(2,1)}), bf16[64,512,2]{1,2,0:T(2,128)(2,1)S(1)}, u32[]{:S(2)}, u32[]{:S(2)}) async-start(bf16[64,512,2]{1,2,0:T(2,128)(2,1)} %broadcast_in_dim.16), calls=%async_computation.1 | async-start | bytes 262144 | tf_op jit(solution)/shard_map/all_to_all | solution.py:45
  93.5 7.4 %collective-permute-start.3 = (bf16[128,2]{1,0:T(8,128)(2,1)S(1)}, bf16[128,2]{1,0:T(8,128)(2,1)S(1)}, u32[]{:S(2)}, u32[]{:S(2)}) collective-permute-start(bf16[128,2]{1,0:T(8,128)(2,1)S(1)} %get-tuple-element.7), channel_id=1, source_target_pairs={{0,1},{1,2},{2,3},{3,4},{4,5},{5,6},{6,7},{7,0},{8,9},{9,10},{10,1... | collective-permute-start | bytes 1544 | tf_op jit(solution)/shard_map/ppermute | solution.py:14
  95.4 6.5 %collective-permute-start.4 = (bf16[128,2]{1,0:T(8,128)(2,1)S(1)}, bf16[128,2]{1,0:T(8,128)(2,1)S(1)}, u32[]{:S(2)}, u32[]{:S(2)}) collective-permute-start(bf16[128,2]{1,0:T(8,128)(2,1)S(1)} %get-tuple-element.8), channel_id=1, source_target_pairs={{1,0},{2,1},{3,2},{4,3},{5,4},{6,5},{7,6},{0,7},{9,8},{10,9},{11,1... | collective-permute-start | bytes 1544 | tf_op jit(solution)/shard_map/ppermute | solution.py:15
  103.1 19.2 %all-to-all-start.3 = ((bf16[64,512,2]{1,2,0:T(2,128)(2,1)}), bf16[64,512,2]{1,2,0:T(2,128)(2,1)S(1)}, u32[]{:S(2)}, u32[]{:S(2)}) async-start(bf16[64,512,2]{1,2,0:T(2,128)(2,1)} %broadcast_in_dim.17), calls=%async_computation.3 | async-start | bytes 262144 | tf_op jit(solution)/shard_map/all_to_all | solution.py:45
where the time goes:
time: 124 us; the launch traced here: 123 us
  starting transfers between devices  48.5 us (39%)
  waiting for transfers between devices  42.4 us (34%)
  blocking collectives  19.3 us (16%)
  local copies, waits for them, and re-layouts  6.78 us (5%)
  matrix products  3.52 us (3%)
  between operations  1.64 us (1%)
    all_to_all x2, waiting for transfers between devices, sent_to_all(): return lax.all_to_all(copies, axis, split_axis=0, concat_axis=0, tiled=True)  26.6 us
    all_to_all x1, blocking collectives, sent_and_summed(): lax.all_to_all(cut_along(value, dim, devices), axis, 0, 0, tiled=True)  19.3 us
    all_to_all x1, starting transfers between devices, sent_and_summed(): lax.all_to_all(cut_along(value, dim, devices), axis, 0, 0, tiled=True)  17.6 us
    all_to_all x1, waiting for transfers between devices, sent_and_summed(): lax.all_to_all(cut_along(value, dim, devices), axis, 0, 0, tiled=True)  14.8 us
    all_to_all x2, starting transfers between devices, sent_to_all(): return lax.all_to_all(copies, axis, split_axis=0, concat_axis=0, tiled=True)  12.2 us
    ppermute x2, starting transfers between devices, with_halo(): after = lax.ppermute(initial, axis, down)  9.9 us
    ppermute x2, starting transfers between devices, with_halo(): before = lax.ppermute(last, axis, up)  5.02 us
    ppermute x1, starting transfers between devices, from_behind(): lax.ppermute(value, axis, [(source, source + steps) for source in range(i...  3.79 us
  transfers between devices with their start and end apart: 8, of which 4 were waited for; matrix products, arithmetic and copies ran while one was open for 2% of the time, Pallas kernels for 0%

commit v1 on v0

v1 whole, which is shorter than its diff:
```python
import functools

import jax
import jax.numpy as jnp
from jax import lax
from jax.experimental import pallas as pl
from jax.experimental.pallas import tpu as pltpu
from jax.sharding import Mesh, PartitionSpec as P

Y, ZH, CORE, DOM = 8, 4, 2, 8
OWNERS = Y * CORE
DELAY = ("y", "zh", "c")
F32, BF16 = jnp.float32, jnp.bfloat16
VMEM = pl.BlockSpec(memory_space=pltpu.VMEM)
SMEM = pl.BlockSpec(memory_space=pltpu.SMEM)


def call(kernel, out_shape, in_specs, flops, nbytes, **more):
    out_specs = jax.tree.map(lambda _: VMEM, out_shape)
    return pl.pallas_call(
        kernel,
        out_shape=out_shape,
        in_specs=in_specs,
        out_specs=out_specs,
        compiler_params=pltpu.CompilerParams(vmem_limit_bytes=32 * 1024 * 1024),
        cost_estimate=pl.CostEstimate(flops=flops, bytes_accessed=nbytes, transcendentals=0),
        **more,
    )


def shape(dims, dtype):
    return jax.ShapeDtypeStruct(dims, dtype)


def dot(a, b):
    return jnp.dot(a, b, preferred_element_type=F32)


def dot_t(a, b):
    return lax.dot_general(a, b, (((1,), (1,)), ((), ())), preferred_element_type=F32)


def one_hot_rows(faces, rows):
    ids = lax.broadcasted_iota(jnp.int32, (rows, faces.shape[1]), 0)
    return (ids == faces).astype(F32).astype(BF16)


def position():
    return (lax.axis_index("y") * ZH + lax.axis_index("zh")) * CORE + lax.axis_index("c")


def live(counts, slot):
    return (position() * 2 + slot < counts[0]).astype(F32)


def own_partials(counts, exc, ret, hist, inv, faces, d0_ref, d1_ref, up_ref, down_ref, last_ref):
    last_ref[...] = hist[hist.shape[0] - 1]
    half = faces.shape[1] // 2
    rows = lax.broadcasted_iota(jnp.int32, (hist.shape[2], 1), 0)
    first_col = position() * 2
    m0, m1 = live(counts, 0), live(counts, 1)

    def placed(step):
        e = exc[step]
        return jnp.where(rows == first_col, e[0:1], jnp.where(rows == first_col + 1, e[1:2], 0.0))

    p0 = dot(ret[0], hist[0]) * m0 + dot(ret[1], hist[1]) * m1
    d0 = (placed(0) - p0.T).astype(BF16)
    d0_ref[...] = d0
    first = dot_t(d0, inv[...]).astype(BF16)
    trace = dot(first, one_hot_rows(faces[...], inv.shape[0])).astype(BF16)
    down_ref[...] = trace[:, :half]
    up_ref[...] = trace[:, half:]
    d1_ref[...] = placed(1) - (dot(ret[1], hist[0]) * m1).T


def pack_partials(counts, d0, d1, up, down, ret0, before, out):
    n = d0.shape[1]
    half = up.shape[1]
    out[:, :n] = d0[...]
    out[:, n : n + half] = up[...]
    out[:, n + half : n + 2 * half] = down[...]
    p1 = dot(ret0[...], before[...]) * live(counts, 0)
    out[:, n + 2 * half :] = (d1[...] - p1.T).astype(BF16)


def sum_and_copy(x, out):
    total = x[0].astype(F32)
    for i in range(1, x.shape[0]):
        total += x[i].astype(F32)
    total = total.astype(BF16)
    for i in range(out.shape[0]):
        out[i] = total


def two_firsts(counts, x, inv, tra, faces, r0_even, r0_odd, cur_ref, first_ref, up_ref, down_ref, r0, sem):
    odd = lax.axis_index("c") == 1

    @pl.when(odd)
    def _():
        copied(r0_odd, r0, sem)

    @pl.when(jnp.logical_not(odd))
    def _():
        copied(r0_even, r0, sem)

    n = inv.shape[0]
    faces_count = faces.shape[1]
    half = faces_count // 2
    total = x[0].astype(F32)
    for i in range(1, x.shape[0]):
        total += x[i].astype(F32)
    rhs = total[:, :n].astype(BF16)
    neighbour = total[:, n : n + faces_count].astype(BF16)
    d1 = total[:, n + faces_count :]
    coupling = dot_t(neighbour, tra[...]).astype(BF16)
    cur = dot_t(rhs, inv[...]) - dot_t(coupling, inv[...])
    cur_ref[...] = cur
    alive = (counts[0] > 0).astype(F32)
    newest = dot_t(cur.astype(BF16), r0[...]) * alive
    first = dot_t((d1 - newest).astype(BF16), inv[...])
    first_ref[...] = first
    trace = dot(first.astype(BF16), one_hot_rows(faces[...], n)).astype(BF16)
    down_ref[...] = trace[:, :half]
    up_ref[...] = trace[:, half:]


def second_current(cur0, first, up, down, inv, tra, gather_ref, share_ref):
    half = up.shape[1]
    coupling = dot_t(up[...], tra[:, :half]) + dot_t(down[...], tra[:, half:])
    cur1 = first[...] - dot_t(coupling.astype(BF16), inv[...])
    c0 = cur0[...]
    both = jnp.concatenate([cur1.astype(BF16), c0.astype(BF16)], axis=0)
    for i in range(gather_ref.shape[0]):
        gather_ref[i] = both
    for i in range(share_ref.shape[0]):
        q = 2 * (i % 4)
        share_ref[i, 0] = c0[q : q + 2]
        share_ref[i, 1] = cur1[q : q + 2]


def finish(gathered, shared, incoming, cur_ref, hist_ref, sem):
    source = lax.axis_index("zh") // 2
    cur_ref[...] = jnp.where(source == 0, shared[0], shared[1])
    leading = position() == 0

    @pl.when(leading)
    def _():
        owners, cols = gathered.shape[0], gathered.shape[1] // 2
        for slot in range(2):
            both = gathered[:, slot * cols : (slot + 1) * cols, :].reshape(owners * cols, -1)
            hist_ref[slot] = both.astype(F32).T.astype(BF16)

    @pl.when(jnp.logical_not(leading))
    def _():
        hist_ref[...] = incoming[...]


def copied(source, target, sem):
    copy = pltpu.make_async_copy(source, target, sem)
    copy.start()
    copy.wait()


def relay(held_at, first_at, held, first, second, after, out, sem):
    y = lax.axis_index("y")
    holds, from_first = one_of(y, held_at), one_of(y, first_at)

    @pl.when(holds)
    def _():
        copied(held, out, sem)

    @pl.when(jnp.logical_and(jnp.logical_not(holds), from_first))
    def _():
        copied(first, out, sem)

    @pl.when(jnp.logical_not(jnp.logical_or(holds, from_first)))
    def _():
        copied(second, out, sem)


def one_of(value, members):
    found = value == members[0]
    for member in members[1:]:
        found = jnp.logical_or(found, value == member)
    return found


def permute(value, axes, pairs):
    return lax.ppermute(value, axes, pairs)


def body(excitation, retarded, history, inverse, transfer, faces, counts):
    slots, n, width = history.shape
    steps = excitation.shape[0]
    half = faces.shape[1] // 2
    devices = Y * ZH * CORE
    cols = width // OWNERS
    exc = jnp.transpose(excitation, (0, 2, 1))
    any_spec = pl.BlockSpec(memory_space=pl.ANY)

    def at(yy, z, c):
        return (yy * ZH + z) * CORE + c

    def spread(value, *hops):
        return permute(value, DELAY, [(at(i, 0, 0), at(j, 0, 0)) for i, j in hops])

    def relayed(held_at, first_at, *operands):
        return call(
            functools.partial(relay, held_at, first_at),
            shape((n, n), BF16),
            [any_spec] * 4,
            0,
            1024 * 1024,
            scratch_shapes=[pltpu.SemaphoreType.DMA],
        )(*operands)

    ring = [(i, (i + 1) % DOM) for i in range(DOM)]
    back = [(j, i) for i, j in ring]
    chain = [(i, i + 1) for i in range(devices - 1)]

    r0 = retarded[0]
    s1a, s1b = spread(r0, (0, 3)), spread(r0, (0, 5))
    macs = n * n * width
    d0, d1, up, down, last = call(
        own_partials,
        (
            shape((width, n), BF16),
            shape((width, n), F32),
            shape((width, half), BF16),
            shape((width, half), BF16),
            shape((n, width), BF16),
        ),
        [SMEM] + [VMEM] * 5,
        2 * macs * 4,
        2 * 1024 * 1024,
    )(counts, exc, retarded, history, inverse, faces)
    up = permute(up, "dom", ring)
    down = permute(down, "dom", back)
    before = permute(last, DELAY, chain)
    lanes = 2 * n + 2 * half
    packed = call(pack_partials, shape((width, lanes), BF16), [SMEM] + [VMEM] * 6, 2 * macs, 1024 * 1024)(
        counts, d0, d1, up, down, r0, before
    )
    x = lax.all_to_all(packed.reshape(OWNERS, cols, lanes), ("y", "c"), 0, 0, tiled=True)
    r0 = relayed((0,), (3,), r0, s1a, s1b, packed)
    s2a, s2b = spread(r0, (0, 1), (3, 2), (5, 6)), spread(r0, (0, 7), (3, 4))
    x = call(sum_and_copy, shape((ZH, cols, lanes), BF16), [VMEM], 0, 512 * 1024)(x)
    r0 = relayed((0, 3, 5), (1, 2, 6), r0, s2a, s2b, x)
    x = lax.all_to_all(x, "zh", 0, 0, tiled=True)
    s3 = permute(r0, DELAY, [(at(i, 0, 0), at(i, 0, 1)) for i in range(Y)])

    cur0, first, up, down = call(
        two_firsts,
        (shape((cols, n), F32), shape((cols, n), F32), shape((cols, half), BF16), shape((cols, half), BF16)),
        [SMEM] + [VMEM] * 4 + [any_spec] * 2,
        2 * 8 * n * n * 6,
        2 * 1024 * 1024,
        scratch_shapes=[pltpu.VMEM((n, n), BF16), pltpu.SemaphoreType.DMA],
    )(counts, x, inverse, transfer, faces, r0, s3)
    up = permute(up, "dom", ring)
    down = permute(down, "dom", back)
    gather, share = call(
        second_current,
        (shape((OWNERS, 2 * cols, n), BF16), shape((ZH * CORE, steps, 2, n), F32)),
        [VMEM] * 6,
        2 * 8 * n * n * 2,
        1024 * 1024,
    )(cur0, first, up, down, inverse, transfer)
    incoming = permute(history, DELAY, chain)
    share = lax.all_to_all(share, ("zh", "c"), 0, 0, tiled=True)
    gather = lax.all_to_all(gather, ("y", "c"), 0, 0, tiled=True)
    share = lax.slice_in_dim(share, 0, 2, axis=0)
    currents, new_history = call(
        finish,
        (shape((steps, 2, n), F32), shape(history.shape, BF16)),
        [VMEM] * 3,
        0,
        1024 * 1024,
        scratch_shapes=[pltpu.SemaphoreType.DMA],
    )(gather, share, incoming)
    return jnp.transpose(currents, (0, 2, 1)), new_history


def solution(mesh):
    split = Mesh(mesh.devices.reshape(Y, ZH, CORE, DOM), ("y", "zh", "c", "dom"))
    placed = (
        P(None, "dom", DELAY),
        P(DELAY, "dom", None),
        P(DELAY, "dom", None),
        P("dom", None),
        P("dom", None),
        P("dom", None),
        P("dom"),
    )
    return jax.shard_map(
        body,
        mesh=split,
        in_specs=placed,
        out_specs=(P(None, "dom", DELAY), P(DELAY, "dom", None)),
        check_vma=False,
    )
```

time: 124 us -> 103 us (0.83)
  the two profiles are of different devices: /device:TPU:1 before, /device:TPU:38 now
where the time goes in v1:
time: 103 us; the launch traced here: 102 us
  starting transfers between devices  36.9 us (36%)
  waiting for transfers between devices  33.9 us (33%)
  blocking collectives  21.3 us (21%)
  Pallas kernels  5.24 us (5%)
  local copies, waits for them, and re-layouts  3.03 us (3%)
  between operations  1.51 us (1%)
    ppermute x11, waiting for transfers between devices, permute(): return lax.ppermute(value, axes, pairs)  27.2 us
    ppermute x11, starting transfers between devices, permute(): return lax.ppermute(value, axes, pairs)  22.3 us
    all_to_all x1, blocking collectives, body(): x = lax.all_to_all(x, 'zh', 0, 0, tiled=True)  10.7 us
    all_to_all x1, blocking collectives, body(): share = lax.all_to_all(share, ('zh', 'c'), 0, 0, tiled=True)  10.6 us
    all_to_all x1, starting transfers between devices, body(): lax.all_to_all(packed.reshape(OWNERS, cols, lanes), ('y', 'c'), 0, 0, til...  7.4 us
    all_to_all x1, starting transfers between devices, body(): gather = lax.all_to_all(gather, ('y', 'c'), 0, 0, tiled=True)  7.23 us
    all_to_all x1, waiting for transfers between devices, body(): lax.all_to_all(packed.reshape(OWNERS, cols, lanes), ('y', 'c'), 0, 0, til...  6.68 us
  transfers between devices with their start and end apart: 13, of which 6 were waited for; matrix products, arithmetic and copies ran while one was open for 0% of the time, Pallas kernels for 2%

profile of v1, /device:TPU:38, one launch (start us, length us, event | category | flops | bytes accessed | tf_op | source)
XLA Modules:
  0.0 101.9 jit_solution(17675681294830371036)
XLA Ops:
  0.7 1.1 %slice_bitcast_fusion.ret0.held = bf16[512,512]{1,0:T(8,128)(2,1)S(1)} fusion(bf16[2,512,512]{2,1,0:T(8,128)(2,1)} %ret.1), kind=kLoop, calls=%fused_computation | loop fusion | bytes 1048576 | tf_op jit(solution)/shard_map/squeeze | solution.py:222
  1.8 0.7 collective-permute-start.3
  2.5 0.7 collective-permute-start.4
  3.9 0.0 copy-start.5
  3.9 0.6 copy-done.5
  4.5 1.2 %copy-done.1 = bf16[2,512,512]{2,1,0:T(8,128)(2,1)S(1)} copy-done((bf16[2,512,512]{2,1,0:T(8,128)(2,1)S(1)}, bf16[2,512,512]{2,1,0:T(8,128)(2,1)}, u32[]{:S(2)}) %copy-start.1) | copy-done | bytes 1048600
  5.8 1.2 %shard_map.86 = (bf16[128,512]{1,0:T(8,128)(2,1)S(1)}, f32[128,512]{1,0:T(8,128)S(1)}, bf16[128,128]{1,0:T(8,128)(2,1)S(1)}, bf16[128,128]{1,0:T(8,128)(2,1)S(1)}, bf16[512,128]{1,0:T(8,128)(2,1)S(1)}) custom-call(s32[1]{0:T(128)S(6)} %copy.9.counts, f32[2,2,512]{2,1,0:T(2,128)S(1)} %bitcast.5, bf16[2,512,512]{2,1,0:T(8,128)(2,1)S(1)} %copy-done.1, ...), custom_call_target="tpu_custom_call" | custom-call | flops 268435456 | bytes 2097152 | tf_op jit(solution)/shard_map/pallas_call | solution.py:225
  6.9 1.9 %collective-permute-start.2 = (bf16[512,128]{1,0:T(8,128)(2,1)S(1)}, bf16[512,128]{1,0:T(8,128)(2,1)S(1)}, u32[]{:S(2)}, u32[]{:S(2)}) collective-permute-start(bf16[512,128]{1,0:T(8,128)(2,1)S(1)} %get-tuple-element.19), channel_id=1, source_target_pairs={{0,8},{8,16},{16,24},{24,32},{32,40},{40,48},{48,56},{56,64},{64,7... | collective-permute-start | bytes 393224 | tf_op jit(solution)/shard_map/ppermute | solution.py:190
  8.9 4.3 %collective-permute-start = (bf16[128,128]{1,0:T(8,128)(2,1)S(1)}, bf16[128,128]{1,0:T(8,128)(2,1)S(1)}, u32[]{:S(2)}, u32[]{:S(2)}) collective-permute-start(bf16[128,128]{1,0:T(8,128)(2,1)S(1)} %get-tuple-element.17), channel_id=1, source_target_pairs={{0,1},{1,2},{2,3},{3,4},{4,5},{5,6},{6,7},{7,0},{8,9},{9,10},{10,1... | collective-permute-start | bytes 98312 | tf_op jit(solution)/shard_map/ppermute | solution.py:190
  13.2 2.5 %collective-permute-start.1 = (bf16[128,128]{1,0:T(8,128)(2,1)S(1)}, bf16[128,128]{1,0:T(8,128)(2,1)S(1)}, u32[]{:S(2)}, u32[]{:S(2)}) collective-permute-start(bf16[128,128]{1,0:T(8,128)(2,1)S(1)} %get-tuple-element.18), channel_id=1, source_target_pairs={{1,0},{2,1},{3,2},{4,3},{5,4},{6,5},{7,6},{0,7},{9,8},{10,9},{11,1... | collective-permute-start | bytes 98312 | tf_op jit(solution)/shard_map/ppermute | solution.py:190
  15.6 0.0 collective-permute-done.up
  15.6 3.3 %collective-permute-done.1.down = bf16[128,128]{1,0:T(8,128)(2,1)S(1)} collective-permute-done((bf16[128,128]{1,0:T(8,128)(2,1)S(1)}, bf16[128,128]{1,0:T(8,128)(2,1)S(1)}, u32[]{:S(2)}, u32[]{:S(2)}) %collective-permute-start.1) | collective-permute-done | bytes 32800 | tf_op jit(solution)/shard_map/ppermute | solution.py:190
  19.0 2.3 %collective-permute-done.2.before = bf16[512,128]{1,0:T(8,128)(2,1)S(1)} collective-permute-done((bf16[512,128]{1,0:T(8,128)(2,1)S(1)}, bf16[512,128]{1,0:T(8,128)(2,1)S(1)}, u32[]{:S(2)}, u32[]{:S(2)}) %collective-permute-start.2) | collective-permute-done | bytes 131104 | tf_op jit(solution)/shard_map/ppermute | solution.py:190
  21.3 1.1 %shard_map.87.after = bf16[128,1280]{1,0:T(8,128)(2,1)} custom-call(s32[1]{0:T(128)S(6)} %copy.9.counts, bf16[128,512]{1,0:T(8,128)(2,1)S(1)} %get-tuple-element.15.d0, f32[128,512]{1,0:T(8,128)S(1)} %get-tuple-element.16.d1, bf16[128,128]{1,0:T(8,128)(2,1)S(1)} %collective-permute-done.up, bf16[128,128]{1,0:T(8,128)(2,1)S(1)} %collective-permute-done.1.down, ...), custom_call_target="tpu_custom_call" | custom-call | flops 67108864 | bytes 1048576 | tf_op jit(solution)/shard_map/pallas_call | solution.py:242
  22.4 7.4 %all-to-all-start = ((bf16[16,8,1280]{2,1,0:T(8,128)(2,1)}), bf16[16,8,1280]{2,1,0:T(8,128)(2,1)S(1)}, u32[]{:S(2)}, u32[]{:S(2)}) async-start(bf16[16,8,1280]{2,1,0:T(8,128)(2,1)} %bitcast.2), calls=%async_computation | async-start | bytes 655360 | tf_op jit(solution)/shard_map/all_to_all | solution.py:245
  29.8 0.1 shard_map.89.held
  29.8 0.7 collective-permute-start.5
  30.6 1.3 %collective-permute-start.6 = (bf16[512,512]{1,0:T(8,128)(2,1)S(1)}, bf16[512,512]{1,0:T(8,128)(2,1)S(1)}, u32[]{:S(2)}, u32[]{:S(2)}) collective-permute-start(bf16[512,512]{1,0:T(8,128)(2,1)S(1)} %shard_map.89.held), channel_id=1, source_target_pairs={{0,448},{192,256},{1,449},{193,257},{2,450},{194,258},{3,451},{195... | collective-permute-start | bytes 1572872 | tf_op jit(solution)/shard_map/ppermute | solution.py:190
  31.9 6.7 %all-to-all-done.x = bf16[16,8,1280]{2,1,0:T(8,128)(2,1)S(1)} async-done(((bf16[16,8,1280]{2,1,0:T(8,128)(2,1)}), bf16[16,8,1280]{2,1,0:T(8,128)(2,1)S(1)}, u32[]{:S(2)}, u32[]{:S(2)}) %all-to-all-start) | async-done | bytes 327712 | tf_op jit(solution)/shard_map/all_to_all | solution.py:245
  38.6 5.6 %collective-permute-done.6.second = bf16[512,512]{1,0:T(8,128)(2,1)S(1)} collective-permute-done((bf16[512,512]{1,0:T(8,128)(2,1)S(1)}, bf16[512,512]{1,0:T(8,128)(2,1)S(1)}, u32[]{:S(2)}, u32[]{:S(2)}) %collective-permute-start.6) | collective-permute-done | bytes 524320 | tf_op jit(solution)/shard_map/ppermute | solution.py:190
  44.2 1.5 %collective-permute-start.7 = (bf16[512,512]{1,0:T(8,128)(2,1)S(1)}, bf16[512,512]{1,0:T(8,128)(2,1)S(1)}, u32[]{:S(2)}, u32[]{:S(2)}) collective-permute-start(bf16[512,512]{1,0:T(8,128)(2,1)S(1)} %shard_map.90.r0_even), channel_id=1, source_target_pairs={{0,8},{64,72},{128,136},{192,200},{256,264},{320,328},{384,392},{4... | collective-permute-start | bytes 1572872 | tf_op jit(solution)/shard_map/ppermute | solution.py:190
  45.7 10.7 %all_to_all.20.x = bf16[4,8,1280]{2,1,0:T(8,128)(2,1)S(1)} all-to-all(bf16[4,8,1280]{2,1,0:T(8,128)(2,1)S(1)} %shard_map.88.after), channel_id=1, replica_groups=mesh['y'=8,'zh'=4,'c'=2,'dom'=8] {'zh'}, dimensions={0} | all-to-all | bytes 163840 | tf_op jit(solution)/shard_map/all_to_all | solution.py:250
  56.4 1.0 shard_map.91
  57.4 4.3 %collective-permute-start.8 = (bf16[8,128]{1,0:T(8,128)(2,1)S(1)}, bf16[8,128]{1,0:T(8,128)(2,1)S(1)}, u32[]{:S(2)}, u32[]{:S(2)}) collective-permute-start(bf16[8,128]{1,0:T(8,128)(2,1)S(1)} %get-tuple-element.22), channel_id=1, source_target_pairs={{0,1},{1,2},{2,3},{3,4},{4,5},{5,6},{6,7},{7,0},{8,9},{9,10},{10,1... | collective-permute-start | bytes 6152 | tf_op jit(solution)/shard_map/ppermute | solution.py:190
  61.7 2.4 %collective-permute-start.9 = (bf16[8,128]{1,0:T(8,128)(2,1)S(1)}, bf16[8,128]{1,0:T(8,128)(2,1)S(1)}, u32[]{:S(2)}, u32[]{:S(2)}) collective-permute-start(bf16[8,128]{1,0:T(8,128)(2,1)S(1)} %get-tuple-element.23), channel_id=1, source_target_pairs={{1,0},{2,1},{3,2},{4,3},{5,4},{6,5},{7,6},{0,7},{9,8},{10,9},{11,1... | collective-permute-start | bytes 6152 | tf_op jit(solution)/shard_map/ppermute | solution.py:190
  64.1 3.0 %collective-permute-done.9.down = bf16[8,128]{1,0:T(8,128)(2,1)S(1)} collective-permute-done((bf16[8,128]{1,0:T(8,128)(2,1)S(1)}, bf16[8,128]{1,0:T(8,128)(2,1)S(1)}, u32[]{:S(2)}, u32[]{:S(2)}) %collective-permute-start.9) | collective-permute-done | bytes 2080 | tf_op jit(solution)/shard_map/ppermute | solution.py:190
  67.2 1.1 %shard_map.92 = (bf16[16,16,512]{2,1,0:T(8,128)(2,1)}, f32[8,2,2,512]{3,2,1,0:T(2,128)S(1)}) custom-call(f32[8,512]{1,0:T(8,128)S(1)} %get-tuple-element.20.cur0, f32[8,512]{1,0:T(8,128)S(1)} %get-tuple-element.21.first, bf16[8,128]{1,0:T(8,128)(2,1)S(1)} %collective-permute-done.8.up, bf16[8,128]{1,0:T(8,128)(2,1)S(1)} %collective-permute-done.9.down, ...), custom_call_target="tpu_custom_call" | custom-call | flops 8388608 | bytes 1048576 | tf_op jit(solution)/shard_map/pallas_call | solution.py:263
  68.3 10.6 %all_to_all.21 = f32[8,2,2,512]{3,2,1,0:T(2,128)S(1)} all-to-all(f32[8,2,2,512]{3,2,1,0:T(2,128)S(1)} %get-tuple-element.25), channel_id=1, replica_groups=mesh['y'=8,'zh'=4,'c'=2,'dom'=8] {'zh','c'}, dimensions={0} | all-to-all | bytes 131072 | tf_op jit(solution)/shard_map/all_to_all | solution.py:271
  78.8 7.2 %all-to-all-start.2 = ((bf16[16,16,512]{2,1,0:T(8,128)(2,1)}), bf16[16,16,512]{2,1,0:T(8,128)(2,1)S(1)}, u32[]{:S(2)}, u32[]{:S(2)}) async-start(bf16[16,16,512]{2,1,0:T(8,128)(2,1)} %get-tuple-element.24), calls=%async_computation.2 | async-start | bytes 524288 | tf_op jit(solution)/shard_map/all_to_all | solution.py:272
  86.1 2.0 %collective-permute-start.10 = (bf16[2,512,128]{2,1,0:T(8,128)(2,1)S(1)}, bf16[2,512,128]{2,1,0:T(8,128)(2,1)S(1)}, u32[]{:S(2)}, u32[]{:S(2)}) collective-permute-start(bf16[2,512,128]{2,1,0:T(8,128)(2,1)S(1)} %copy-done.3), channel_id=1, source_target_pairs={{0,8},{8,16},{16,24},{24,32},{32,40},{40,48},{48,56},{56,64},{64,7... | collective-permute-start | bytes 786440 | tf_op jit(solution)/shard_map/ppermute | solution.py:190
  88.1 13.0 %collective-permute-done.10.incoming = bf16[2,512,128]{2,1,0:T(8,128)(2,1)S(1)} collective-permute-done((bf16[2,512,128]{2,1,0:T(8,128)(2,1)S(1)}, bf16[2,512,128]{2,1,0:T(8,128)(2,1)S(1)}, u32[]{:S(2)}, u32[]{:S(2)}) %collective-permute-start.10) | collective-permute-done | bytes 262176 | tf_op jit(solution)/shard_map/ppermute | solution.py:190
  101.2 0.7 shard_map.93
  (18 shorter events, 0.1 us)
Async XLA Ops:
  0.6 3.2 %copy-start = (bf16[512,512]{1,0:T(8,128)(2,1)S(1)}, bf16[512,512]{1,0:T(8,128)(2,1)}, u32[]{:S(2)}) copy-start(bf16[512,512]{1,0:T(8,128)(2,1)} %inv.5) | copy-start | bytes 1572868
  0.6 3.2 %copy-start.3 = (bf16[2,512,128]{2,1,0:T(8,128)(2,1)S(1)}, bf16[2,512,128]{2,1,0:T(8,128)(2,1)}, u32[]{:S(2)}) copy-start(bf16[2,512,128]{2,1,0:T(8,128)(2,1)} %hist.1) | copy-start | bytes 786436
  0.6 3.2 %copy-start.4 = (f32[2,512,2]{1,2,0:T(2,128)S(1)}, f32[2,512,2]{1,2,0:T(2,128)}, u32[]{:S(2)}) copy-start(f32[2,512,2]{1,2,0:T(2,128)} %param.7) | copy-start | bytes 24580
  1.8 27.9 %collective-permute-start.3 = (bf16[512,512]{1,0:T(8,128)(2,1)S(1)}, bf16[512,512]{1,0:T(8,128)(2,1)S(1)}, u32[]{:S(2)}, u32[]{:S(2)}) collective-permute-start(bf16[512,512]{1,0:T(8,128)(2,1)S(1)} %slice_bitcast_fusion.ret0.held), channel_id=1, source_target_pairs={{0,192},{1,193},{2,194},{3,195},{4,196},{5,197},{6,198},{7,199}} | collective-permute-start | bytes 1572872 | tf_op jit(solution)/shard_map/ppermute | solution.py:190
  2.5 27.2 %collective-permute-start.4 = (bf16[512,512]{1,0:T(8,128)(2,1)S(1)}, bf16[512,512]{1,0:T(8,128)(2,1)S(1)}, u32[]{:S(2)}, u32[]{:S(2)}) collective-permute-start(bf16[512,512]{1,0:T(8,128)(2,1)S(1)} %slice_bitcast_fusion.ret0.held), channel_id=1, source_target_pairs={{0,320},{1,321},{2,322},{3,323},{4,324},{5,325},{6,326},{7,327}} | collective-permute-start | bytes 1572872 | tf_op jit(solution)/shard_map/ppermute | solution.py:190
  3.9 0.7 copy-start.5
  4.5 1.2 %copy-start.1 = (bf16[2,512,512]{2,1,0:T(8,128)(2,1)S(1)}, bf16[2,512,512]{2,1,0:T(8,128)(2,1)}, u32[]{:S(2)}) copy-start(bf16[2,512,512]{2,1,0:T(8,128)(2,1)} %ret.1) | copy-start | bytes 3145732
  6.9 14.3 %collective-permute-start.2 = (bf16[512,128]{1,0:T(8,128)(2,1)S(1)}, bf16[512,128]{1,0:T(8,128)(2,1)S(1)}, u32[]{:S(2)}, u32[]{:S(2)}) collective-permute-start(bf16[512,128]{1,0:T(8,128)(2,1)S(1)} %get-tuple-element.19), channel_id=1, source_target_pairs={{0,8},{8,16},{16,24},{24,32},{32,40},{40,48},{48,56},{56,64},{64,7... | collective-permute-start | bytes 393224 | tf_op jit(solution)/shard_map/ppermute | solution.py:190
  8.9 6.8 %collective-permute-start = (bf16[128,128]{1,0:T(8,128)(2,1)S(1)}, bf16[128,128]{1,0:T(8,128)(2,1)S(1)}, u32[]{:S(2)}, u32[]{:S(2)}) collective-permute-start(bf16[128,128]{1,0:T(8,128)(2,1)S(1)} %get-tuple-element.17), channel_id=1, source_target_pairs={{0,1},{1,2},{2,3},{3,4},{4,5},{5,6},{6,7},{7,0},{8,9},{9,10},{10,1... | collective-permute-start | bytes 98312 | tf_op jit(solution)/shard_map/ppermute | solution.py:190
  13.2 5.8 %collective-permute-start.1 = (bf16[128,128]{1,0:T(8,128)(2,1)S(1)}, bf16[128,128]{1,0:T(8,128)(2,1)S(1)}, u32[]{:S(2)}, u32[]{:S(2)}) collective-permute-start(bf16[128,128]{1,0:T(8,128)(2,1)S(1)} %get-tuple-element.18), channel_id=1, source_target_pairs={{1,0},{2,1},{3,2},{4,3},{5,4},{6,5},{7,6},{0,7},{9,8},{10,9},{11,1... | collective-permute-start | bytes 98312 | tf_op jit(solution)/shard_map/ppermute | solution.py:190
  22.4 16.2 %all-to-all-start = ((bf16[16,8,1280]{2,1,0:T(8,128)(2,1)}), bf16[16,8,1280]{2,1,0:T(8,128)(2,1)S(1)}, u32[]{:S(2)}, u32[]{:S(2)}) async-start(bf16[16,8,1280]{2,1,0:T(8,128)(2,1)} %bitcast.2), calls=%async_computation | async-start | bytes 655360 | tf_op jit(solution)/shard_map/all_to_all | solution.py:245
  29.8 8.7 %collective-permute-start.5 = (bf16[512,512]{1,0:T(8,128)(2,1)S(1)}, bf16[512,512]{1,0:T(8,128)(2,1)S(1)}, u32[]{:S(2)}, u32[]{:S(2)}) collective-permute-start(bf16[512,512]{1,0:T(8,128)(2,1)S(1)} %shard_map.89.held), channel_id=1, source_target_pairs={{0,64},{192,128},{320,384},{1,65},{193,129},{321,385},{2,66},{194,... | collective-permute-start | bytes 1572872 | tf_op jit(solution)/shard_map/ppermute | solution.py:190
  30.6 13.6 %collective-permute-start.6 = (bf16[512,512]{1,0:T(8,128)(2,1)S(1)}, bf16[512,512]{1,0:T(8,128)(2,1)S(1)}, u32[]{:S(2)}, u32[]{:S(2)}) collective-permute-start(bf16[512,512]{1,0:T(8,128)(2,1)S(1)} %shard_map.89.held), channel_id=1, source_target_pairs={{0,448},{192,256},{1,449},{193,257},{2,450},{194,258},{3,451},{195... | collective-permute-start | bytes 1572872 | tf_op jit(solution)/shard_map/ppermute | solution.py:190
  44.2 12.2 %copy-start.2 = (bf16[512,256]{1,0:T(8,128)(2,1)S(1)}, bf16[512,256]{1,0:T(8,128)(2,1)}, u32[]{:S(2)}) copy-start(bf16[512,256]{1,0:T(8,128)(2,1)} %tra.3) | copy-start | bytes 786436
  44.2 12.2 %collective-permute-start.7 = (bf16[512,512]{1,0:T(8,128)(2,1)S(1)}, bf16[512,512]{1,0:T(8,128)(2,1)S(1)}, u32[]{:S(2)}, u32[]{:S(2)}) collective-permute-start(bf16[512,512]{1,0:T(8,128)(2,1)S(1)} %shard_map.90.r0_even), channel_id=1, source_target_pairs={{0,8},{64,72},{128,136},{192,200},{256,264},{320,328},{384,392},{4... | collective-permute-start | bytes 1572872 | tf_op jit(solution)/shard_map/ppermute | solution.py:190
  57.4 6.8 %collective-permute-start.8 = (bf16[8,128]{1,0:T(8,128)(2,1)S(1)}, bf16[8,128]{1,0:T(8,128)(2,1)S(1)}, u32[]{:S(2)}, u32[]{:S(2)}) collective-permute-start(bf16[8,128]{1,0:T(8,128)(2,1)S(1)} %get-tuple-element.22), channel_id=1, source_target_pairs={{0,1},{1,2},{2,3},{3,4},{4,5},{5,6},{6,7},{7,0},{8,9},{9,10},{10,1... | collective-permute-start | bytes 6152 | tf_op jit(solution)/shard_map/ppermute | solution.py:190
  61.7 5.5 %collective-permute-start.9 = (bf16[8,128]{1,0:T(8,128)(2,1)S(1)}, bf16[8,128]{1,0:T(8,128)(2,1)S(1)}, u32[]{:S(2)}, u32[]{:S(2)}) collective-permute-start(bf16[8,128]{1,0:T(8,128)(2,1)S(1)} %get-tuple-element.23), channel_id=1, source_target_pairs={{1,0},{2,1},{3,2},{4,3},{5,4},{6,5},{7,6},{0,7},{9,8},{10,9},{11,1... | collective-permute-start | bytes 6152 | tf_op jit(solution)/shard_map/ppermute | solution.py:190
  78.8 22.3 %all-to-all-start.2 = ((bf16[16,16,512]{2,1,0:T(8,128)(2,1)}), bf16[16,16,512]{2,1,0:T(8,128)(2,1)S(1)}, u32[]{:S(2)}, u32[]{:S(2)}) async-start(bf16[16,16,512]{2,1,0:T(8,128)(2,1)} %get-tuple-element.24), calls=%async_computation.2 | async-start | bytes 524288 | tf_op jit(solution)/shard_map/all_to_all | solution.py:272
  86.1 15.1 %collective-permute-start.10 = (bf16[2,512,128]{2,1,0:T(8,128)(2,1)S(1)}, bf16[2,512,128]{2,1,0:T(8,128)(2,1)S(1)}, u32[]{:S(2)}, u32[]{:S(2)}) collective-permute-start(bf16[2,512,128]{2,1,0:T(8,128)(2,1)S(1)} %copy-done.3), channel_id=1, source_target_pairs={{0,8},{8,16},{16,24},{24,32},{32,40},{40,48},{48,56},{56,64},{64,7... | collective-permute-start | bytes 786440 | tf_op jit(solution)/shard_map/ppermute | solution.py:190

commit v2 on v1

--- a/solution.py
+++ b/solution.py
@@ -13,16 +13,18 @@
 F32, BF16 = jnp.float32, jnp.bfloat16
 VMEM = pl.BlockSpec(memory_space=pltpu.VMEM)
 SMEM = pl.BlockSpec(memory_space=pltpu.SMEM)
-
-
-def call(kernel, out_shape, in_specs, flops, nbytes, **more):
-    out_specs = jax.tree.map(lambda _: VMEM, out_shape)
+HBM = pl.BlockSpec(memory_space=pltpu.HBM)
+
+
+def call(kernel, out_shape, in_specs, flops, nbytes, mib=32, out_specs=None, **more):
+    if out_specs is None:
+        out_specs = jax.tree.map(lambda _: VMEM, out_shape)
     return pl.pallas_call(
         kernel,
         out_shape=out_shape,
         in_specs=in_specs,
         out_specs=out_specs,
-        compiler_params=pltpu.CompilerParams(vmem_limit_bytes=32 * 1024 * 1024),
+        compiler_params=pltpu.CompilerParams(vmem_limit_bytes=mib * 1024 * 1024),
         cost_estimate=pl.CostEstimate(flops=flops, bytes_accessed=nbytes, transcendentals=0),
         **more,
     )
@@ -53,38 +55,100 @@
     return (position() * 2 + slot < counts[0]).astype(F32)
 
 
-def own_partials(counts, exc, ret, hist, inv, faces, d0_ref, d1_ref, up_ref, down_ref, last_ref):
-    last_ref[...] = hist[hist.shape[0] - 1]
+def copied(source, target, sem):
+    copy = pltpu.make_async_copy(source, target, sem)
+    copy.start()
+    copy.wait()
+
+
+def column_of(row):
+    c, zh = (row // 8) % 2, (row // 2) % 4
+    return (row // 16) * 16 + zh * 4 + c * 2 + row % 2
+
+
+def permutation(width):
+    cols = lax.broadcasted_iota(jnp.int32, (width, width), 0)
+    rows = lax.broadcasted_iota(jnp.int32, (width, width), 1)
+    return (cols == column_of(rows)).astype(F32).astype(BF16)
+
+
+def permuted(block, order):
+    return dot(block, order).astype(BF16)
+
+
+def own_partials(
+    counts, exc, faces, ret, hist, inv,
+    d0_ref, d1_ref, up_ref, down_ref, r0_ref, h0_ref, h1_ref,
+    r1, inv_v, exc_v, faces_v, sems,
+):
+    moves = [(hist.at[0], h0_ref), (ret.at[0], r0_ref), (hist.at[1], h1_ref), (ret.at[1], r1), (exc, exc_v)]
+    moves += [(inv, inv_v), (faces, faces_v)]
+    copies = [pltpu.make_async_copy(a, b, sems.at[k]) for k, (a, b) in enumerate(moves)]
+    for copy in copies:
+        copy.start()
+    width = hist.shape[2]
     half = faces.shape[1] // 2
-    rows = lax.broadcasted_iota(jnp.int32, (hist.shape[2], 1), 0)
+    col = column_of(lax.broadcasted_iota(jnp.int32, (width, 1), 0))
     first_col = position() * 2
     m0, m1 = live(counts, 0), live(counts, 1)
+    order = permutation(width)
 
     def placed(step):
-        e = exc[step]
-        return jnp.where(rows == first_col, e[0:1], jnp.where(rows == first_col + 1, e[1:2], 0.0))
-
-    p0 = dot(ret[0], hist[0]) * m0 + dot(ret[1], hist[1]) * m1
+        e = exc_v[step]
+        return jnp.where(col == first_col, e[0:1], jnp.where(col == first_col + 1, e[1:2], 0.0))
+
+    copies[0].wait()
+    h0 = permuted(h0_ref[...], order)
+    copies[1].wait()
+    p0 = dot(r0_ref[...], h0) * m0
+    copies[2].wait()
+    h1 = permuted(h1_ref[...], order)
+    copies[3].wait()
+    p0 += dot(r1[...], h1) * m1
+    copies[4].wait()
     d0 = (placed(0) - p0.T).astype(BF16)
     d0_ref[...] = d0
-    first = dot_t(d0, inv[...]).astype(BF16)
-    trace = dot(first, one_hot_rows(faces[...], inv.shape[0])).astype(BF16)
+    copies[5].wait()
+    first = dot_t(d0, inv_v[...]).astype(BF16)
+    copies[6].wait()
+    trace = dot(first, one_hot_rows(faces_v[...], inv.shape[0])).astype(BF16)
     down_ref[...] = trace[:, :half]
     up_ref[...] = trace[:, half:]
-    d1_ref[...] = placed(1) - (dot(ret[1], hist[0]) * m1).T
-
-
-def pack_partials(counts, d0, d1, up, down, ret0, before, out):
+    d1_ref[...] = placed(1) - (dot(r1[...], h0) * m1).T
+
+
+def pack_partials(
+    counts, d0, d1, up, down, r0, before, h0,
+    out, h0_out, done_ref,
+    d1_v, r0_v, before_v, p1_v, sems,
+):
     n = d0.shape[1]
     half = up.shape[1]
-    out[:, :n] = d0[...]
-    out[:, n : n + half] = up[...]
-    out[:, n + half : n + 2 * half] = down[...]
-    p1 = dot(ret0[...], before[...]) * live(counts, 0)
-    out[:, n + 2 * half :] = (d1[...] - p1.T).astype(BF16)
-
-
-def sum_and_copy(x, out):
+
+    def place(start, length):
+        return out.at[:, pl.ds(start, length)]
+
+    moves = [(before, before_v), (r0, r0_v), (d1, d1_v)]
+    moves += [(d0, place(0, n)), (up, place(n, half)), (down, place(n + half, half))]
+    copies = [pltpu.make_async_copy(a, b, sems.at[k]) for k, (a, b) in enumerate(moves)]
+    for copy in copies:
+        copy.start()
+    done_ref[...] = jnp.zeros_like(done_ref)
+    order = permutation(before.shape[1])
+    copies[0].wait()
+    packed = permuted(before_v[...], order)
+    copies[1].wait()
+    p1 = dot(r0_v[...], packed) * live(counts, 0)
+    copies[2].wait()
+    p1_v[...] = (d1_v[...] - p1.T).astype(BF16)
+    last = pltpu.make_async_copy(p1_v, place(n + 2 * half, n), sems.at[6])
+    last.start()
+    for copy in copies[3:]:
+        copy.wait()
+    last.wait()
+
+
+def sum_and_copy(x, after, out):
     total = x[0].astype(F32)
     for i in range(1, x.shape[0]):
         total += x[i].astype(F32)
@@ -125,7 +189,7 @@
     up_ref[...] = trace[:, half:]
 
 
-def second_current(cur0, first, up, down, inv, tra, gather_ref, share_ref):
+def second_current(cur0, first, up, down, inv, tra, gather_ref, *share_refs):
     half = up.shape[1]
     coupling = dot_t(up[...], tra[:, :half]) + dot_t(down[...], tra[:, half:])
     cur1 = first[...] - dot_t(coupling.astype(BF16), inv[...])
@@ -133,33 +197,28 @@
     both = jnp.concatenate([cur1.astype(BF16), c0.astype(BF16)], axis=0)
     for i in range(gather_ref.shape[0]):
         gather_ref[i] = both
-    for i in range(share_ref.shape[0]):
-        q = 2 * (i % 4)
-        share_ref[i, 0] = c0[q : q + 2]
-        share_ref[i, 1] = cur1[q : q + 2]
-
-
-def finish(gathered, shared, incoming, cur_ref, hist_ref, sem):
-    source = lax.axis_index("zh") // 2
-    cur_ref[...] = jnp.where(source == 0, shared[0], shared[1])
+    for i, share in enumerate(share_refs):
+        share[0] = c0[2 * i : 2 * i + 2]
+        share[1] = cur1[2 * i : 2 * i + 2]
+
+
+def finish(gathered, s0, s1, s2, s3, before0, before1, cur_ref, hist_ref):
+    zh = lax.axis_index("zh")
+    cur_ref[...] = jnp.where(zh < 2, jnp.where(zh == 0, s0[...], s1[...]), jnp.where(zh == 2, s2[...], s3[...]))
     leading = position() == 0
 
     @pl.when(leading)
     def _():
         owners, cols = gathered.shape[0], gathered.shape[1] // 2
+        order = permutation(owners * cols)
         for slot in range(2):
             both = gathered[:, slot * cols : (slot + 1) * cols, :].reshape(owners * cols, -1)
-            hist_ref[slot] = both.astype(F32).T.astype(BF16)
+            hist_ref[slot] = dot_t(both.astype(F32).T.astype(BF16), order).astype(BF16)
 
     @pl.when(jnp.logical_not(leading))
     def _():
-        hist_ref[...] = incoming[...]
-
-
-def copied(source, target, sem):
-    copy = pltpu.make_async_copy(source, target, sem)
-    copy.start()
-    copy.wait()
+        hist_ref[0] = before0[...]
+        hist_ref[1] = before1[...]
 
 
 def relay(held_at, first_at, held, first, second, after, out, sem):
@@ -219,33 +278,57 @@
     back = [(j, i) for i, j in ring]
     chain = [(i, i + 1) for i in range(devices - 1)]
 
-    r0 = retarded[0]
-    s1a, s1b = spread(r0, (0, 3)), spread(r0, (0, 5))
     macs = n * n * width
-    d0, d1, up, down, last = call(
+    d0, d1, up, down, r0, h0, h1 = call(
         own_partials,
         (
             shape((width, n), BF16),
             shape((width, n), F32),
             shape((width, half), BF16),
             shape((width, half), BF16),
+            shape((n, n), BF16),
+            shape((n, width), BF16),
             shape((n, width), BF16),
         ),
-        [SMEM] + [VMEM] * 5,
+        [SMEM] + [HBM] * 5,
         2 * macs * 4,
         2 * 1024 * 1024,
-    )(counts, exc, retarded, history, inverse, faces)
+        mib=60,
+        scratch_shapes=[
+            pltpu.VMEM((n, n), BF16),
+            pltpu.VMEM((n, n), BF16),
+            pltpu.VMEM((steps, 2, n), F32),
+            pltpu.VMEM(faces.shape, jnp.int32),
+            pltpu.SemaphoreType.DMA((7,)),
+        ],
+    )(counts, exc, faces, retarded, history, inverse)
     up = permute(up, "dom", ring)
     down = permute(down, "dom", back)
-    before = permute(last, DELAY, chain)
+    before = permute(h1, DELAY, chain)
+    s1a, s1b = spread(r0, (0, 3)), spread(r0, (0, 5))
     lanes = 2 * n + 2 * half
-    packed = call(pack_partials, shape((width, lanes), BF16), [SMEM] + [VMEM] * 6, 2 * macs, 1024 * 1024)(
-        counts, d0, d1, up, down, r0, before
-    )
+    packed, h0, done = call(
+        pack_partials,
+        (shape((width, lanes), BF16), shape((n, width), BF16), shape((8, 128), F32)),
+        [SMEM] + [any_spec] * 7,
+        2 * macs,
+        1024 * 1024,
+        mib=60,
+        out_specs=(any_spec, any_spec, VMEM),
+        input_output_aliases={7: 1},
+        scratch_shapes=[
+            pltpu.VMEM((width, n), F32),
+            pltpu.VMEM((n, n), BF16),
+            pltpu.VMEM((n, width), BF16),
+            pltpu.VMEM((width, n), BF16),
+            pltpu.SemaphoreType.DMA((7,)),
+        ],
+    )(counts, d0, d1, up, down, r0, before, h0)
     x = lax.all_to_all(packed.reshape(OWNERS, cols, lanes), ("y", "c"), 0, 0, tiled=True)
-    r0 = relayed((0,), (3,), r0, s1a, s1b, packed)
+    before0 = permute(h0, DELAY, chain)
+    r0 = relayed((0,), (3,), r0, s1a, s1b, done)
     s2a, s2b = spread(r0, (0, 1), (3, 2), (5, 6)), spread(r0, (0, 7), (3, 4))
-    x = call(sum_and_copy, shape((ZH, cols, lanes), BF16), [VMEM], 0, 512 * 1024)(x)
+    x = call(sum_and_copy, shape((ZH, cols, lanes), BF16), [VMEM, any_spec], 0, 512 * 1024)(x, before0)
     r0 = relayed((0, 3, 5), (1, 2, 6), r0, s2a, s2b, x)
     x = lax.all_to_all(x, "zh", 0, 0, tiled=True)
     s3 = permute(r0, DELAY, [(at(i, 0, 0), at(i, 0, 1)) for i in range(Y)])
@@ -260,25 +343,23 @@
     )(counts, x, inverse, transfer, faces, r0, s3)
     up = permute(up, "dom", ring)
     down = permute(down, "dom", back)
-    gather, share = call(
+    gather, *share = call(
         second_current,
-        (shape((OWNERS, 2 * cols, n), BF16), shape((ZH * CORE, steps, 2, n), F32)),
+        [shape((OWNERS, 2 * cols, n), BF16)] + [shape((steps, 2, n), F32)] * ZH,
         [VMEM] * 6,
         2 * 8 * n * n * 2,
         1024 * 1024,
     )(cur0, first, up, down, inverse, transfer)
-    incoming = permute(history, DELAY, chain)
-    share = lax.all_to_all(share, ("zh", "c"), 0, 0, tiled=True)
     gather = lax.all_to_all(gather, ("y", "c"), 0, 0, tiled=True)
-    share = lax.slice_in_dim(share, 0, 2, axis=0)
+    for z in range(1, ZH):
+        share[z] = permute(share[z], DELAY, [(at(i, 0, c), at(i, z, c)) for i in range(Y) for c in range(CORE)])
     currents, new_history = call(
         finish,
         (shape((steps, 2, n), F32), shape(history.shape, BF16)),
-        [VMEM] * 3,
+        [VMEM] * 7,
         0,
         1024 * 1024,
-        scratch_shapes=[pltpu.SemaphoreType.DMA],
-    )(gather, share, incoming)
+    )(gather, *share, before0, before)
     return jnp.transpose(currents, (0, 2, 1)), new_history
 
 

time: 103 us -> 100 us (0.971)
  the two profiles are of different devices: /device:TPU:38 before, /device:TPU:1 now
where the time goes in v2:
time: 100 us; the launch traced here: 99.3 us
  starting transfers between devices  53.4 us (53%)
  Pallas kernels  14.6 us (15%)
  blocking collectives  14.6 us (15%)
  waiting for transfers between devices  14.5 us (14%)
  between operations  1.59 us (2%)
    ppermute x14, starting transfers between devices, permute(): return lax.ppermute(value, axes, pairs)  37.6 us
    all_to_all x1, blocking collectives, body(): x = lax.all_to_all(x, 'zh', 0, 0, tiled=True)  14.6 us
    all_to_all x1, starting transfers between devices, body(): gather = lax.all_to_all(gather, ('y', 'c'), 0, 0, tiled=True)  8.34 us
    pallas_call x1, Pallas kernels, body(): call(pack_partials, (shape((width, lanes), BF16), shape((n, width), BF16)...  7.72 us
    all_to_all x1, starting transfers between devices, body(): lax.all_to_all(packed.reshape(OWNERS, cols, lanes), ('y', 'c'), 0, 0, til...  7.37 us
    all_to_all x1, waiting for transfers between devices, body(): gather = lax.all_to_all(gather, ('y', 'c'), 0, 0, tiled=True)  6.46 us
    ppermute x14, waiting for transfers between devices, permute(): return lax.ppermute(value, axes, pairs)  4.71 us
    pallas_call x1, Pallas kernels, body(): call(own_partials, (shape((width, n), BF16), shape((width, n), F32), shap...  3.84 us
  transfers between devices with their start and end apart: 16, of which 6 were waited for; matrix products, arithmetic and copies ran while one was open for 0% of the time, Pallas kernels for 8%

profile of v2, /device:TPU:1, one launch (start us, length us, event | category | flops | bytes accessed | tf_op | source)
XLA Modules:
  0.0 99.3 jit_solution(17126998867245519935)
XLA Ops:
  1.3 3.8 %shard_map.86 = (bf16[128,512]{1,0:T(8,128)(2,1)}, f32[128,512]{1,0:T(8,128)}, bf16[128,128]{1,0:T(8,128)(2,1)}, bf16[128,128]{1,0:T(8,128)(2,1)}, bf16[512,512]...) custom-call(s32[1]{0:T(128)S(6)} %copy.11.counts, f32[2,2,512]{2,1,0:T(2,128)} %bitcast.4, ...), custom_call_target="tpu_custom_call" | custom-call | flops 268435456 | bytes 2097152 | tf_op jit(solution)/shard_map/pallas_call | solution.py:282
  5.1 0.7 collective-permute-start.5
  5.8 0.7 collective-permute-start.4
  6.5 7.2 %collective-permute-start.2 = (bf16[512,128]{1,0:T(8,128)(2,1)}, bf16[512,128]{1,0:T(8,128)(2,1)S(1)}, u32[]{:S(2)}, u32[]{:S(2)}) collective-permute-start(bf16[512,128]{1,0:T(8,128)(2,1)} %get-tuple-element.28), channel_id=1, source_target_pairs={{0,8},{8,16},{16,24},{24,32},{32,40},{40,48},{48,56},{56,64},{64,7... | collective-permute-start | bytes 393224 | tf_op jit(solution)/shard_map/ppermute | solution.py:249
  13.7 4.0 %collective-permute-start = (bf16[128,128]{1,0:T(8,128)(2,1)}, bf16[128,128]{1,0:T(8,128)(2,1)S(1)}, u32[]{:S(2)}, u32[]{:S(2)}) collective-permute-start(bf16[128,128]{1,0:T(8,128)(2,1)} %get-tuple-element.25), channel_id=1, source_target_pairs={{0,1},{1,2},{2,3},{3,4},{4,5},{5,6},{6,7},{7,0},{8,9},{9,10},{10,1... | collective-permute-start | bytes 98312 | tf_op jit(solution)/shard_map/ppermute | solution.py:249
  17.7 4.1 %collective-permute-start.1 = (bf16[128,128]{1,0:T(8,128)(2,1)}, bf16[128,128]{1,0:T(8,128)(2,1)S(1)}, u32[]{:S(2)}, u32[]{:S(2)}) collective-permute-start(bf16[128,128]{1,0:T(8,128)(2,1)} %get-tuple-element.26), channel_id=1, source_target_pairs={{1,0},{2,1},{3,2},{4,3},{5,4},{6,5},{7,6},{0,7},{9,8},{10,9},{11,1... | collective-permute-start | bytes 98312 | tf_op jit(solution)/shard_map/ppermute | solution.py:249
  21.9 1.3 %collective-permute-done.1.down = bf16[128,128]{1,0:T(8,128)(2,1)S(1)} collective-permute-done((bf16[128,128]{1,0:T(8,128)(2,1)}, bf16[128,128]{1,0:T(8,128)(2,1)S(1)}, u32[]{:S(2)}, u32[]{:S(2)}) %collective-permute-start.1) | collective-permute-done | bytes 32800 | tf_op jit(solution)/shard_map/ppermute | solution.py:249
  23.2 0.6 copy-done.9
  23.8 0.1 copy-done.3
  23.9 7.7 %shard_map.87 = (bf16[128,1280]{1,0:T(8,128)(2,1)}, bf16[512,128]{1,0:T(8,128)(2,1)}, f32[8,128]{1,0:T(8,128)}) custom-call(s32[1]{0:T(128)S(6)} %copy.11.counts, bf16[128,512]{1,0:T(8,128)(2,1)} %get-tuple-element.23.d0, f32[128,512]{1,0:T(8,128)} %get-tuple-element.24.d1, bf16[128,128]{1,0:T(8,128)(2,1)} %copy-done.8, ...), custom_call_target="tpu_custom_call", output_to_operand_aliasing={{1}: (7, {})} | custom-call | flops 67108864 | bytes 1048576 | tf_op jit(solution)/shard_map/pallas_call | solution.py:310
  31.6 7.4 %all-to-all-start = ((bf16[16,8,1280]{2,1,0:T(8,128)(2,1)}), bf16[16,8,1280]{2,1,0:T(8,128)(2,1)S(1)}, u32[]{:S(2)}, u32[]{:S(2)}) async-start(bf16[16,8,1280]{2,1,0:T(8,128)(2,1)} %bitcast.3), calls=%async_computation | async-start | bytes 655360 | tf_op jit(solution)/shard_map/all_to_all | solution.py:327
  39.0 0.1 shard_map.89.held
  39.1 0.7 collective-permute-start.7
  39.8 0.7 collective-permute-start.6
  40.5 6.3 %collective-permute-start.3 = (bf16[512,128]{1,0:T(8,128)(2,1)S(1)}, bf16[512,128]{1,0:T(8,128)(2,1)S(1)}, u32[]{:S(2)}, u32[]{:S(2)}) collective-permute-start(bf16[512,128]{1,0:T(8,128)(2,1)S(1)} %copy-done.7), channel_id=1, source_target_pairs={{0,8},{8,16},{16,24},{24,32},{32,40},{40,48},{48,56},{56,64},{64,7... | collective-permute-start | bytes 393224 | tf_op jit(solution)/shard_map/ppermute | solution.py:249
  46.8 1.9 %collective-permute-done.3.after.before0 = bf16[512,128]{1,0:T(8,128)(2,1)S(1)} collective-permute-done((bf16[512,128]{1,0:T(8,128)(2,1)S(1)}, bf16[512,128]{1,0:T(8,128)(2,1)S(1)}, u32[]{:S(2)}, u32[]{:S(2)}) %collective-permute-start.3) | collective-permute-done | bytes 131104 | tf_op jit(solution)/shard_map/ppermute | solution.py:249
  48.7 3.3 %all-to-all-done.x = bf16[16,8,1280]{2,1,0:T(8,128)(2,1)S(1)} async-done(((bf16[16,8,1280]{2,1,0:T(8,128)(2,1)}), bf16[16,8,1280]{2,1,0:T(8,128)(2,1)S(1)}, u32[]{:S(2)}, u32[]{:S(2)}) %all-to-all-start) | async-done | bytes 327712 | tf_op jit(solution)/shard_map/all_to_all | solution.py:327
  52.1 0.1 shard_map.90.r0_even
  52.2 1.4 %collective-permute-start.8 = (bf16[512,512]{1,0:T(8,128)(2,1)S(1)}, bf16[512,512]{1,0:T(8,128)(2,1)S(1)}, u32[]{:S(2)}, u32[]{:S(2)}) collective-permute-start(bf16[512,512]{1,0:T(8,128)(2,1)S(1)} %shard_map.90.r0_even), channel_id=1, source_target_pairs={{0,8},{64,72},{128,136},{192,200},{256,264},{320,328},{384,392},{4... | collective-permute-start | bytes 1572872 | tf_op jit(solution)/shard_map/ppermute | solution.py:249
  53.7 14.6 %all_to_all.15.x = bf16[4,8,1280]{2,1,0:T(8,128)(2,1)S(1)} all-to-all(bf16[4,8,1280]{2,1,0:T(8,128)(2,1)S(1)} %shard_map.88.after), channel_id=1, replica_groups=mesh['y'=8,'zh'=4,'c'=2,'dom'=8] {'zh'}, dimensions={0} | all-to-all | bytes 163840 | tf_op jit(solution)/shard_map/all_to_all | solution.py:333
  68.3 1.0 %shard_map.91 = (f32[8,512]{1,0:T(8,128)S(1)}, f32[8,512]{1,0:T(8,128)S(1)}, bf16[8,128]{1,0:T(8,128)(2,1)S(1)}, bf16[8,128]{1,0:T(8,128)(2,1)S(1)}) custom-call(s32[1]{0:T(128)S(6)} %copy.11.counts, bf16[4,8,1280]{2,1,0:T(8,128)(2,1)S(1)} %all_to_all.15.x, bf16[512,512]{1,0:T(8,128)(2,1)S(1)} %copy-done, bf16[512,256]{1,0:T(8,128)(2,1)S(1)} %copy-done.2, ...), custom_call_target="tpu_custom_call" | custom-call | flops 25165824 | bytes 2097152 | tf_op jit(solution)/shard_map/pallas_call | solution.py:336
  69.3 2.8 %collective-permute-start.9 = (bf16[8,128]{1,0:T(8,128)(2,1)S(1)}, bf16[8,128]{1,0:T(8,128)(2,1)S(1)}, u32[]{:S(2)}, u32[]{:S(2)}) collective-permute-start(bf16[8,128]{1,0:T(8,128)(2,1)S(1)} %get-tuple-element.35), channel_id=1, source_target_pairs={{0,1},{1,2},{2,3},{3,4},{4,5},{5,6},{6,7},{7,0},{8,9},{9,10},{10,1... | collective-permute-start | bytes 6152 | tf_op jit(solution)/shard_map/ppermute | solution.py:249
  72.2 4.5 %collective-permute-start.10 = (bf16[8,128]{1,0:T(8,128)(2,1)S(1)}, bf16[8,128]{1,0:T(8,128)(2,1)S(1)}, u32[]{:S(2)}, u32[]{:S(2)}) collective-permute-start(bf16[8,128]{1,0:T(8,128)(2,1)S(1)} %get-tuple-element.36), channel_id=1, source_target_pairs={{1,0},{2,1},{3,2},{4,3},{5,4},{6,5},{7,6},{0,7},{9,8},{10,9},{11,1... | collective-permute-start | bytes 6152 | tf_op jit(solution)/shard_map/ppermute | solution.py:249
  76.7 0.7 collective-permute-done.10.down
  77.4 1.1 %shard_map.92 = (bf16[16,16,512]{2,1,0:T(8,128)(2,1)}, f32[2,2,512]{2,1,0:T(2,128)S(1)}, f32[2,2,512]{2,1,0:T(2,128)S(1)}, f32[2,2,512]{2,1,0:T(2,128)S(1)}, f32[2,2,512]{2,1,0:T(2,128)S(1)}) custom-call(f32[8,512]{1,0:T(8,128)S(1)} %get-tuple-element.33.cur0, f32[8,512]{1,0:T(8,128)S(1)} %get-tuple-element.34.first, ...), custom_call_target="tpu_custom_call" | custom-call | flops 8388608 | bytes 1048576 | tf_op jit(solution)/shard_map/pallas_call | solution.py:346
  78.5 8.3 %all-to-all-start.2 = ((bf16[16,16,512]{2,1,0:T(8,128)(2,1)}), bf16[16,16,512]{2,1,0:T(8,128)(2,1)S(1)}, u32[]{:S(2)}, u32[]{:S(2)}) async-start(bf16[16,16,512]{2,1,0:T(8,128)(2,1)} %get-tuple-element.37), calls=%async_computation.2 | async-start | bytes 524288 | tf_op jit(solution)/shard_map/all_to_all | solution.py:353
  86.9 1.9 %collective-permute-start.11 = (f32[2,2,512]{2,1,0:T(2,128)S(1)}, f32[2,2,512]{2,1,0:T(2,128)S(1)}, u32[]{:S(2)}, u32[]{:S(2)}) collective-permute-start(f32[2,2,512]{2,1,0:T(2,128)S(1)} %get-tuple-element.39), channel_id=1, source_target_pairs={{0,16},{8,24},{64,80},{72,88},{128,144},{136,152},{192,208},{200,2... | collective-permute-start | bytes 24584 | tf_op jit(solution)/shard_map/ppermute | solution.py:249
  88.7 1.3 %collective-permute-start.12 = (f32[2,2,512]{2,1,0:T(2,128)S(1)}, f32[2,2,512]{2,1,0:T(2,128)S(1)}, u32[]{:S(2)}, u32[]{:S(2)}) collective-permute-start(f32[2,2,512]{2,1,0:T(2,128)S(1)} %get-tuple-element.40), channel_id=1, source_target_pairs={{0,32},{8,40},{64,96},{72,104},{128,160},{136,168},{192,224},{200,... | collective-permute-start | bytes 24584 | tf_op jit(solution)/shard_map/ppermute | solution.py:249
  90.0 1.3 %collective-permute-start.13 = (f32[2,2,512]{2,1,0:T(2,128)S(1)}, f32[2,2,512]{2,1,0:T(2,128)S(1)}, u32[]{:S(2)}, u32[]{:S(2)}) collective-permute-start(f32[2,2,512]{2,1,0:T(2,128)S(1)} %get-tuple-element.41), channel_id=1, source_target_pairs={{0,48},{8,56},{64,112},{72,120},{128,176},{136,184},{192,240},{200... | collective-permute-start | bytes 24584 | tf_op jit(solution)/shard_map/ppermute | solution.py:249
  91.4 0.8 collective-permute-done.13.s3
  92.1 6.5 %all-to-all-done.2.gathered = bf16[16,16,512]{2,1,0:T(8,128)(2,1)S(1)} async-done(((bf16[16,16,512]{2,1,0:T(8,128)(2,1)}), bf16[16,16,512]{2,1,0:T(8,128)(2,1)S(1)}, u32[]{:S(2)}, u32[]{:S(2)}) %all-to-all-start.2) | async-done | bytes 262176 | tf_op jit(solution)/shard_map/all_to_all | solution.py:353
  98.6 0.7 shard_map.93
  (29 shorter events, 0.1 us)
Async XLA Ops:
  5.1 33.8 %collective-permute-start.5 = (bf16[512,512]{1,0:T(8,128)(2,1)}, bf16[512,512]{1,0:T(8,128)(2,1)S(1)}, u32[]{:S(2)}, u32[]{:S(2)}) collective-permute-start(bf16[512,512]{1,0:T(8,128)(2,1)} %get-tuple-element.27.r0.held), channel_id=1, source_target_pairs={{0,320},{1,321},{2,322},{3,323},{4,324},{5,325},{6,326},{7,327}} | collective-permute-start | bytes 1572872 | tf_op jit(solution)/shard_map/ppermute | solution.py:249
  5.8 33.1 %collective-permute-start.4 = (bf16[512,512]{1,0:T(8,128)(2,1)}, bf16[512,512]{1,0:T(8,128)(2,1)S(1)}, u32[]{:S(2)}, u32[]{:S(2)}) collective-permute-start(bf16[512,512]{1,0:T(8,128)(2,1)} %get-tuple-element.27.r0.held), channel_id=1, source_target_pairs={{0,192},{1,193},{2,194},{3,195},{4,196},{5,197},{6,198},{7,199}} | collective-permute-start | bytes 1572872 | tf_op jit(solution)/shard_map/ppermute | solution.py:249
  6.5 16.7 %collective-permute-start.2 = (bf16[512,128]{1,0:T(8,128)(2,1)}, bf16[512,128]{1,0:T(8,128)(2,1)S(1)}, u32[]{:S(2)}, u32[]{:S(2)}) collective-permute-start(bf16[512,128]{1,0:T(8,128)(2,1)} %get-tuple-element.28), channel_id=1, source_target_pairs={{0,8},{8,16},{16,24},{24,32},{32,40},{40,48},{48,56},{56,64},{64,7... | collective-permute-start | bytes 393224 | tf_op jit(solution)/shard_map/ppermute | solution.py:249
  13.7 8.1 %collective-permute-start = (bf16[128,128]{1,0:T(8,128)(2,1)}, bf16[128,128]{1,0:T(8,128)(2,1)S(1)}, u32[]{:S(2)}, u32[]{:S(2)}) collective-permute-start(bf16[128,128]{1,0:T(8,128)(2,1)} %get-tuple-element.25), channel_id=1, source_target_pairs={{0,1},{1,2},{2,3},{3,4},{4,5},{5,6},{6,7},{7,0},{8,9},{9,10},{10,1... | collective-permute-start | bytes 98312 | tf_op jit(solution)/shard_map/ppermute | solution.py:249
  17.7 5.4 %collective-permute-start.1 = (bf16[128,128]{1,0:T(8,128)(2,1)}, bf16[128,128]{1,0:T(8,128)(2,1)S(1)}, u32[]{:S(2)}, u32[]{:S(2)}) collective-permute-start(bf16[128,128]{1,0:T(8,128)(2,1)} %get-tuple-element.26), channel_id=1, source_target_pairs={{1,0},{2,1},{3,2},{4,3},{5,4},{6,5},{7,6},{0,7},{9,8},{10,9},{11,1... | collective-permute-start | bytes 98312 | tf_op jit(solution)/shard_map/ppermute | solution.py:249
  21.9 1.3 %copy-start.8 = (bf16[128,128]{1,0:T(8,128)(2,1)}, bf16[128,128]{1,0:T(8,128)(2,1)S(1)}, u32[]{:S(2)}) copy-start(bf16[128,128]{1,0:T(8,128)(2,1)S(1)} %collective-permute-done.up) | copy-start | bytes 98308
  23.2 0.6 copy-start.9
  23.2 0.7 copy-start.3
  31.6 7.4 %copy-start.1 = (bf16[512,512]{1,0:T(8,128)(2,1)S(1)}, bf16[512,512]{1,0:T(8,128)(2,1)}, u32[]{:S(2)}) copy-start(bf16[512,512]{1,0:T(8,128)(2,1)} %get-tuple-element.27.r0.held) | copy-start | bytes 1572868
  31.6 7.4 %copy-start.5 = (f32[8,128]{1,0:T(8,128)S(1)}, f32[8,128]{1,0:T(8,128)}, u32[]{:S(2)}) copy-start(f32[8,128]{1,0:T(8,128)} %get-tuple-element.32.after) | copy-start | bytes 12292
  31.6 20.4 %all-to-all-start = ((bf16[16,8,1280]{2,1,0:T(8,128)(2,1)}), bf16[16,8,1280]{2,1,0:T(8,128)(2,1)S(1)}, u32[]{:S(2)}, u32[]{:S(2)}) async-start(bf16[16,8,1280]{2,1,0:T(8,128)(2,1)} %bitcast.3), calls=%async_computation | async-start | bytes 655360 | tf_op jit(solution)/shard_map/all_to_all | solution.py:327
  39.0 1.5 %copy-start.7 = (bf16[512,128]{1,0:T(8,128)(2,1)S(1)}, bf16[512,128]{1,0:T(8,128)(2,1)}, u32[]{:S(2)}) copy-start(bf16[512,128]{1,0:T(8,128)(2,1)} %get-tuple-element.31) | copy-start | bytes 393220
  39.1 13.0 %collective-permute-start.7 = (bf16[512,512]{1,0:T(8,128)(2,1)S(1)}, bf16[512,512]{1,0:T(8,128)(2,1)S(1)}, u32[]{:S(2)}, u32[]{:S(2)}) collective-permute-start(bf16[512,512]{1,0:T(8,128)(2,1)S(1)} %shard_map.89.held), channel_id=1, source_target_pairs={{0,448},{192,256},{1,449},{193,257},{2,450},{194,258},{3,451},{195... | collective-permute-start | bytes 1572872 | tf_op jit(solution)/shard_map/ppermute | solution.py:249
  39.8 12.3 %collective-permute-start.6 = (bf16[512,512]{1,0:T(8,128)(2,1)S(1)}, bf16[512,512]{1,0:T(8,128)(2,1)S(1)}, u32[]{:S(2)}, u32[]{:S(2)}) collective-permute-start(bf16[512,512]{1,0:T(8,128)(2,1)S(1)} %shard_map.89.held), channel_id=1, source_target_pairs={{0,64},{192,128},{320,384},{1,65},{193,129},{321,385},{2,66},{194,... | collective-permute-start | bytes 1572872 | tf_op jit(solution)/shard_map/ppermute | solution.py:249
  40.5 8.2 %collective-permute-start.3 = (bf16[512,128]{1,0:T(8,128)(2,1)S(1)}, bf16[512,128]{1,0:T(8,128)(2,1)S(1)}, u32[]{:S(2)}, u32[]{:S(2)}) collective-permute-start(bf16[512,128]{1,0:T(8,128)(2,1)S(1)} %copy-done.7), channel_id=1, source_target_pairs={{0,8},{8,16},{16,24},{24,32},{32,40},{40,48},{48,56},{56,64},{64,7... | collective-permute-start | bytes 393224 | tf_op jit(solution)/shard_map/ppermute | solution.py:249
  52.1 16.2 %copy-start = (bf16[512,512]{1,0:T(8,128)(2,1)S(1)}, bf16[512,512]{1,0:T(8,128)(2,1)}, u32[]{:S(2)}) copy-start(bf16[512,512]{1,0:T(8,128)(2,1)} %inv.5) | copy-start | bytes 1572868
  52.1 16.2 %copy-start.2 = (bf16[512,256]{1,0:T(8,128)(2,1)S(1)}, bf16[512,256]{1,0:T(8,128)(2,1)}, u32[]{:S(2)}) copy-start(bf16[512,256]{1,0:T(8,128)(2,1)} %tra.3) | copy-start | bytes 786436
  52.2 16.1 %copy-start.6 = (s32[1,256]{1,0:T(1,128)S(1)}, s32[1,256]{1,0:T(1,128)}, u32[]{:S(2)}) copy-start(s32[1,256]{1,0:T(1,128)} %faces.3) | copy-start | bytes 3076
  52.2 16.1 %collective-permute-start.8 = (bf16[512,512]{1,0:T(8,128)(2,1)S(1)}, bf16[512,512]{1,0:T(8,128)(2,1)S(1)}, u32[]{:S(2)}, u32[]{:S(2)}) collective-permute-start(bf16[512,512]{1,0:T(8,128)(2,1)S(1)} %shard_map.90.r0_even), channel_id=1, source_target_pairs={{0,8},{64,72},{128,136},{192,200},{256,264},{320,328},{384,392},{4... | collective-permute-start | bytes 1572872 | tf_op jit(solution)/shard_map/ppermute | solution.py:249
  69.3 7.4 %collective-permute-start.9 = (bf16[8,128]{1,0:T(8,128)(2,1)S(1)}, bf16[8,128]{1,0:T(8,128)(2,1)S(1)}, u32[]{:S(2)}, u32[]{:S(2)}) collective-permute-start(bf16[8,128]{1,0:T(8,128)(2,1)S(1)} %get-tuple-element.35), channel_id=1, source_target_pairs={{0,1},{1,2},{2,3},{3,4},{4,5},{5,6},{6,7},{7,0},{8,9},{9,10},{10,1... | collective-permute-start | bytes 6152 | tf_op jit(solution)/shard_map/ppermute | solution.py:249
  72.2 5.3 %collective-permute-start.10 = (bf16[8,128]{1,0:T(8,128)(2,1)S(1)}, bf16[8,128]{1,0:T(8,128)(2,1)S(1)}, u32[]{:S(2)}, u32[]{:S(2)}) collective-permute-start(bf16[8,128]{1,0:T(8,128)(2,1)S(1)} %get-tuple-element.36), channel_id=1, source_target_pairs={{1,0},{2,1},{3,2},{4,3},{5,4},{6,5},{7,6},{0,7},{9,8},{10,9},{11,1... | collective-permute-start | bytes 6152 | tf_op jit(solution)/shard_map/ppermute | solution.py:249
  78.5 20.1 %copy-start.4 = (bf16[512,128]{1,0:T(8,128)(2,1)S(1)}, bf16[512,128]{1,0:T(8,128)(2,1)}, u32[]{:S(2)}) copy-start(bf16[512,128]{1,0:T(8,128)(2,1)} %copy-done.3) | copy-start | bytes 393220
  78.5 20.1 %all-to-all-start.2 = ((bf16[16,16,512]{2,1,0:T(8,128)(2,1)}), bf16[16,16,512]{2,1,0:T(8,128)(2,1)S(1)}, u32[]{:S(2)}, u32[]{:S(2)}) async-start(bf16[16,16,512]{2,1,0:T(8,128)(2,1)} %get-tuple-element.37), calls=%async_computation.2 | async-start | bytes 524288 | tf_op jit(solution)/shard_map/all_to_all | solution.py:353
  86.9 4.5 %collective-permute-start.11 = (f32[2,2,512]{2,1,0:T(2,128)S(1)}, f32[2,2,512]{2,1,0:T(2,128)S(1)}, u32[]{:S(2)}, u32[]{:S(2)}) collective-permute-start(f32[2,2,512]{2,1,0:T(2,128)S(1)} %get-tuple-element.39), channel_id=1, source_target_pairs={{0,16},{8,24},{64,80},{72,88},{128,144},{136,152},{192,208},{200,2... | collective-permute-start | bytes 24584 | tf_op jit(solution)/shard_map/ppermute | solution.py:249
  88.7 2.6 %collective-permute-start.12 = (f32[2,2,512]{2,1,0:T(2,128)S(1)}, f32[2,2,512]{2,1,0:T(2,128)S(1)}, u32[]{:S(2)}, u32[]{:S(2)}) collective-permute-start(f32[2,2,512]{2,1,0:T(2,128)S(1)} %get-tuple-element.40), channel_id=1, source_target_pairs={{0,32},{8,40},{64,96},{72,104},{128,160},{136,168},{192,224},{200,... | collective-permute-start | bytes 24584 | tf_op jit(solution)/shard_map/ppermute | solution.py:249
  90.0 2.1 %collective-permute-start.13 = (f32[2,2,512]{2,1,0:T(2,128)S(1)}, f32[2,2,512]{2,1,0:T(2,128)S(1)}, u32[]{:S(2)}, u32[]{:S(2)}) collective-permute-start(f32[2,2,512]{2,1,0:T(2,128)S(1)} %get-tuple-element.41), channel_id=1, source_target_pairs={{0,48},{8,56},{64,112},{72,120},{128,176},{136,184},{192,240},{200... | collective-permute-start | bytes 24584 | tf_op jit(solution)/shard_map/ppermute | solution.py:249

commit v3 on v2

--- a/solution.py
+++ b/solution.py
@@ -13,7 +13,6 @@
 F32, BF16 = jnp.float32, jnp.bfloat16
 VMEM = pl.BlockSpec(memory_space=pltpu.VMEM)
 SMEM = pl.BlockSpec(memory_space=pltpu.SMEM)
-HBM = pl.BlockSpec(memory_space=pltpu.HBM)
 
 
 def call(kernel, out_shape, in_specs, flops, nbytes, mib=32, out_specs=None, **more):
@@ -76,88 +75,63 @@
     return dot(block, order).astype(BF16)
 
 
+def selections(faces, select_ref, order_ref):
+    select_ref[...] = one_hot_rows(faces[...], select_ref.shape[0])
+    order_ref[...] = permutation(order_ref.shape[0])
+
+
 def own_partials(
-    counts, exc, faces, ret, hist, inv,
-    d0_ref, d1_ref, up_ref, down_ref, r0_ref, h0_ref, h1_ref,
-    r1, inv_v, exc_v, faces_v, sems,
+    counts, exc, select, order, hist, ret, inv,
+    d0_ref, d1_ref, up_ref, down_ref, r0_ref,
+    r1, inv_v, sems,
 ):
-    moves = [(hist.at[0], h0_ref), (ret.at[0], r0_ref), (hist.at[1], h1_ref), (ret.at[1], r1), (exc, exc_v)]
-    moves += [(inv, inv_v), (faces, faces_v)]
+    moves = [(ret.at[0], r0_ref), (ret.at[1], r1), (inv, inv_v)]
     copies = [pltpu.make_async_copy(a, b, sems.at[k]) for k, (a, b) in enumerate(moves)]
     for copy in copies:
         copy.start()
     width = hist.shape[2]
-    half = faces.shape[1] // 2
+    half = select.shape[1] // 2
     col = column_of(lax.broadcasted_iota(jnp.int32, (width, 1), 0))
     first_col = position() * 2
     m0, m1 = live(counts, 0), live(counts, 1)
-    order = permutation(width)
 
     def placed(step):
-        e = exc_v[step]
+        e = exc[step]
         return jnp.where(col == first_col, e[0:1], jnp.where(col == first_col + 1, e[1:2], 0.0))
 
+    h0, h1 = permuted(hist[0], order[...]), permuted(hist[1], order[...])
     copies[0].wait()
-    h0 = permuted(h0_ref[...], order)
+    p0 = dot(r0_ref[...], h0) * m0
     copies[1].wait()
-    p0 = dot(r0_ref[...], h0) * m0
-    copies[2].wait()
-    h1 = permuted(h1_ref[...], order)
-    copies[3].wait()
     p0 += dot(r1[...], h1) * m1
-    copies[4].wait()
     d0 = (placed(0) - p0.T).astype(BF16)
     d0_ref[...] = d0
-    copies[5].wait()
+    copies[2].wait()
     first = dot_t(d0, inv_v[...]).astype(BF16)
-    copies[6].wait()
-    trace = dot(first, one_hot_rows(faces_v[...], inv.shape[0])).astype(BF16)
+    trace = dot(first, select[...]).astype(BF16)
     down_ref[...] = trace[:, :half]
     up_ref[...] = trace[:, half:]
     d1_ref[...] = placed(1) - (dot(r1[...], h0) * m1).T
 
 
-def pack_partials(
-    counts, d0, d1, up, down, r0, before, h0,
-    out, h0_out, done_ref,
-    d1_v, r0_v, before_v, p1_v, sems,
-):
+def pack_partials(counts, order, d0, d1, up, down, r0, before, out):
     n = d0.shape[1]
     half = up.shape[1]
-
-    def place(start, length):
-        return out.at[:, pl.ds(start, length)]
-
-    moves = [(before, before_v), (r0, r0_v), (d1, d1_v)]
-    moves += [(d0, place(0, n)), (up, place(n, half)), (down, place(n + half, half))]
-    copies = [pltpu.make_async_copy(a, b, sems.at[k]) for k, (a, b) in enumerate(moves)]
-    for copy in copies:
-        copy.start()
-    done_ref[...] = jnp.zeros_like(done_ref)
-    order = permutation(before.shape[1])
-    copies[0].wait()
-    packed = permuted(before_v[...], order)
-    copies[1].wait()
-    p1 = dot(r0_v[...], packed) * live(counts, 0)
-    copies[2].wait()
-    p1_v[...] = (d1_v[...] - p1.T).astype(BF16)
-    last = pltpu.make_async_copy(p1_v, place(n + 2 * half, n), sems.at[6])
-    last.start()
-    for copy in copies[3:]:
-        copy.wait()
-    last.wait()
-
-
-def sum_and_copy(x, after, out):
+    out[:, :n] = d0[...]
+    out[:, n : n + half] = up[...]
+    out[:, n + half : n + 2 * half] = down[...]
+    p1 = dot(r0[...], permuted(before[1], order[...])) * live(counts, 0)
+    out[:, n + 2 * half :] = (d1[...] - p1.T).astype(BF16)
+
+
+def sum_parts(x, out):
     total = x[0].astype(F32)
     for i in range(1, x.shape[0]):
         total += x[i].astype(F32)
-    total = total.astype(BF16)
-    for i in range(out.shape[0]):
-        out[i] = total
-
-
-def two_firsts(counts, x, inv, tra, faces, r0_even, r0_odd, cur_ref, first_ref, up_ref, down_ref, r0, sem):
+    out[...] = total
+
+
+def two_firsts(counts, x0, x1, x2, x3, inv, tra, select, r0_even, r0_odd, cur_ref, first_ref, up_ref, down_ref, r0, sem):
     odd = lax.axis_index("c") == 1
 
     @pl.when(odd)
@@ -169,11 +143,9 @@
         copied(r0_even, r0, sem)
 
     n = inv.shape[0]
-    faces_count = faces.shape[1]
+    faces_count = select.shape[1]
     half = faces_count // 2
-    total = x[0].astype(F32)
-    for i in range(1, x.shape[0]):
-        total += x[i].astype(F32)
+    total = (x0[...] + x1[...]) + (x2[...] + x3[...])
     rhs = total[:, :n].astype(BF16)
     neighbour = total[:, n : n + faces_count].astype(BF16)
     d1 = total[:, n + faces_count :]
@@ -184,7 +156,7 @@
     newest = dot_t(cur.astype(BF16), r0[...]) * alive
     first = dot_t((d1 - newest).astype(BF16), inv[...])
     first_ref[...] = first
-    trace = dot(first.astype(BF16), one_hot_rows(faces[...], n)).astype(BF16)
+    trace = dot(first.astype(BF16), select[...]).astype(BF16)
     down_ref[...] = trace[:, :half]
     up_ref[...] = trace[:, half:]
 
@@ -202,7 +174,7 @@
         share[1] = cur1[2 * i : 2 * i + 2]
 
 
-def finish(gathered, s0, s1, s2, s3, before0, before1, cur_ref, hist_ref):
+def finish(gathered, s0, s1, s2, s3, before, cur_ref, hist_ref):
     zh = lax.axis_index("zh")
     cur_ref[...] = jnp.where(zh < 2, jnp.where(zh == 0, s0[...], s1[...]), jnp.where(zh == 2, s2[...], s3[...]))
     leading = position() == 0
@@ -217,8 +189,7 @@
 
     @pl.when(jnp.logical_not(leading))
     def _():
-        hist_ref[0] = before0[...]
-        hist_ref[1] = before1[...]
+        hist_ref[...] = before[...]
 
 
 def relay(held_at, first_at, held, first, second, after, out, sem):
@@ -279,7 +250,15 @@
     chain = [(i, i + 1) for i in range(devices - 1)]
 
     macs = n * n * width
-    d0, d1, up, down, r0, h0, h1 = call(
+    before = permute(history, DELAY, chain)
+    select, order = call(
+        selections,
+        (shape((n, 2 * half), BF16), shape((width, width), BF16)),
+        [VMEM],
+        64 * 1024 * 1024,
+        8 * 1024 * 1024,
+    )(faces)
+    d0, d1, up, down, r0 = call(
         own_partials,
         (
             shape((width, n), BF16),
@@ -287,62 +266,38 @@
             shape((width, half), BF16),
             shape((width, half), BF16),
             shape((n, n), BF16),
-            shape((n, width), BF16),
-            shape((n, width), BF16),
         ),
-        [SMEM] + [HBM] * 5,
+        [SMEM] + [VMEM] * 4 + [any_spec] * 2,
         2 * macs * 4,
         2 * 1024 * 1024,
-        mib=60,
-        scratch_shapes=[
-            pltpu.VMEM((n, n), BF16),
-            pltpu.VMEM((n, n), BF16),
-            pltpu.VMEM((steps, 2, n), F32),
-            pltpu.VMEM(faces.shape, jnp.int32),
-            pltpu.SemaphoreType.DMA((7,)),
-        ],
-    )(counts, exc, faces, retarded, history, inverse)
+        mib=52,
+        scratch_shapes=[pltpu.VMEM((n, n), BF16), pltpu.VMEM((n, n), BF16), pltpu.SemaphoreType.DMA((3,))],
+    )(counts, exc, select, order, history, retarded, inverse)
     up = permute(up, "dom", ring)
     down = permute(down, "dom", back)
-    before = permute(h1, DELAY, chain)
     s1a, s1b = spread(r0, (0, 3)), spread(r0, (0, 5))
     lanes = 2 * n + 2 * half
-    packed, h0, done = call(
-        pack_partials,
-        (shape((width, lanes), BF16), shape((n, width), BF16), shape((8, 128), F32)),
-        [SMEM] + [any_spec] * 7,
-        2 * macs,
-        1024 * 1024,
-        mib=60,
-        out_specs=(any_spec, any_spec, VMEM),
-        input_output_aliases={7: 1},
-        scratch_shapes=[
-            pltpu.VMEM((width, n), F32),
-            pltpu.VMEM((n, n), BF16),
-            pltpu.VMEM((n, width), BF16),
-            pltpu.VMEM((width, n), BF16),
-            pltpu.SemaphoreType.DMA((7,)),
-        ],
-    )(counts, d0, d1, up, down, r0, before, h0)
+    packed = call(pack_partials, shape((width, lanes), BF16), [SMEM] + [VMEM] * 7, 2 * macs, 1024 * 1024)(
+        counts, order, d0, d1, up, down, r0, before
+    )
     x = lax.all_to_all(packed.reshape(OWNERS, cols, lanes), ("y", "c"), 0, 0, tiled=True)
-    before0 = permute(h0, DELAY, chain)
-    r0 = relayed((0,), (3,), r0, s1a, s1b, done)
+    r0 = relayed((0,), (3,), r0, s1a, s1b, packed)
     s2a, s2b = spread(r0, (0, 1), (3, 2), (5, 6)), spread(r0, (0, 7), (3, 4))
-    x = call(sum_and_copy, shape((ZH, cols, lanes), BF16), [VMEM, any_spec], 0, 512 * 1024)(x, before0)
+    x = call(sum_parts, shape((cols, lanes), F32), [VMEM], 0, 512 * 1024)(x)
+    xs = [x] + [permute(x, "zh", [(z, 0)]) for z in range(1, ZH)]
     r0 = relayed((0, 3, 5), (1, 2, 6), r0, s2a, s2b, x)
-    x = lax.all_to_all(x, "zh", 0, 0, tiled=True)
     s3 = permute(r0, DELAY, [(at(i, 0, 0), at(i, 0, 1)) for i in range(Y)])
 
     cur0, first, up, down = call(
         two_firsts,
         (shape((cols, n), F32), shape((cols, n), F32), shape((cols, half), BF16), shape((cols, half), BF16)),
-        [SMEM] + [VMEM] * 4 + [any_spec] * 2,
+        [SMEM] + [VMEM] * 7 + [any_spec] * 2,
         2 * 8 * n * n * 6,
         2 * 1024 * 1024,
         scratch_shapes=[pltpu.VMEM((n, n), BF16), pltpu.SemaphoreType.DMA],
-    )(counts, x, inverse, transfer, faces, r0, s3)
-    up = permute(up, "dom", ring)
-    down = permute(down, "dom", back)
+    )(counts, *xs, inverse, transfer, select, r0, s3)
+    up = permute(up, ("zh", "dom"), ring)
+    down = permute(down, ("zh", "dom"), back)
     gather, *share = call(
         second_current,
         [shape((OWNERS, 2 * cols, n), BF16)] + [shape((steps, 2, n), F32)] * ZH,
@@ -356,10 +311,10 @@
     currents, new_history = call(
         finish,
         (shape((steps, 2, n), F32), shape(history.shape, BF16)),
-        [VMEM] * 7,
+        [VMEM] * 6,
         0,
         1024 * 1024,
-    )(gather, *share, before0, before)
+    )(gather, *share, before)
     return jnp.transpose(currents, (0, 2, 1)), new_history
 
 

time: 100 us -> 92.7 us (0.927)
  blocking collectives: 14.6 us -> 0 us
  waiting for transfers between devices: 14.5 us -> 27.2 us
  Pallas kernels: 14.6 us -> 6.95 us
  starting transfers between devices: 53.4 us -> 54.6 us
    all_to_all x1 -> x0, blocking collectives: 14.6 us -> none  [body(): x = lax.all_to_all(x, 'zh', 0, 0, tiled=True)]
    all_to_all x1, waiting for transfers between devices: 3.3 us -> 11.6 us  [body(): lax.all_to_all(packed.reshape(OWNERS, cols, lanes), ('y', 'c'), 0, 0, til...]
    pallas_call x2 -> x3, Pallas kernels: 7.76 us -> 1.37 us  [the longest x1 1.25 us: body(): call(pack_partials, shape((width, lanes), BF16), [SMEM] + [VMEM] * 7, 2 *...]
    ppermute x14 -> x16, waiting for transfers between devices: 4.71 us -> 8.57 us  [permute(): return lax.ppermute(value, axes, pairs)]
    ppermute x14 -> x16, starting transfers between devices: 37.6 us -> 34.8 us  [permute(): return lax.ppermute(value, axes, pairs)]
    all_to_all x1, starting transfers between devices: 8.34 us -> 10.5 us  [body(): gather = lax.all_to_all(gather, ('y', 'c'), 0, 0, tiled=True)]
    all_to_all x1, starting transfers between devices: 7.37 us -> 9.39 us  [body(): lax.all_to_all(packed.reshape(OWNERS, cols, lanes), ('y', 'c'), 0, 0, til...]
    pallas_call x1, Pallas kernels: 3.84 us -> 2.61 us  [body(): call(own_partials, (shape((width, n), BF16), shape((width, n), F32), shap...]
  transfers between devices with their start and end apart: 16 -> 18, of which waited for: 6 -> 7; matrix products, arithmetic and copies ran while one was open for 0% -> 0% of each run, Pallas kernels for 8% -> 1%
where the time goes in v3:
time: 92.7 us; the launch traced here: 92 us
  starting transfers between devices  54.6 us (59%)
  waiting for transfers between devices  27.2 us (29%)
  Pallas kernels  6.95 us (7%)
  local copies, waits for them, and re-layouts  1.63 us (2%)
  between operations  1.56 us (2%)
    ppermute x16, starting transfers between devices, permute(): return lax.ppermute(value, axes, pairs)  34.8 us
    all_to_all x1, waiting for transfers between devices, body(): lax.all_to_all(packed.reshape(OWNERS, cols, lanes), ('y', 'c'), 0, 0, til...  11.6 us
    all_to_all x1, starting transfers between devices, body(): gather = lax.all_to_all(gather, ('y', 'c'), 0, 0, tiled=True)  10.5 us
    all_to_all x1, starting transfers between devices, body(): lax.all_to_all(packed.reshape(OWNERS, cols, lanes), ('y', 'c'), 0, 0, til...  9.39 us
    ppermute x16, waiting for transfers between devices, permute(): return lax.ppermute(value, axes, pairs)  8.57 us
    all_to_all x1, waiting for transfers between devices, body(): gather = lax.all_to_all(gather, ('y', 'c'), 0, 0, tiled=True)  7.05 us
    pallas_call x1, Pallas kernels, body(): call(own_partials, (shape((width, n), BF16), shape((width, n), F32), shap...  2.61 us
  transfers between devices with their start and end apart: 18, of which 7 were waited for; matrix products, arithmetic and copies ran while one was open for 0% of the time, Pallas kernels for 1%

profile of v3, /device:TPU:1, one launch (start us, length us, event | category | flops | bytes accessed | tf_op | source)
XLA Modules:
  0.0 92.0 jit_solution(246102706440034232)
XLA Ops:
  0.6 0.7 copy-done.4
  2.1 0.9 %copy-done.2 = bf16[2,512,128]{2,1,0:T(8,128)(2,1)S(1)} copy-done((bf16[2,512,128]{2,1,0:T(8,128)(2,1)S(1)}, bf16[2,512,128]{2,1,0:T(8,128)(2,1)}, u32[]{:S(2)}) %copy-start.2) | copy-done | bytes 262168
  3.0 2.6 %shard_map.87 = (bf16[128,512]{1,0:T(8,128)(2,1)S(1)}, f32[128,512]{1,0:T(8,128)S(1)}, bf16[128,128]{1,0:T(8,128)(2,1)S(1)}, bf16[128,128]{1,0:T(8,128)(2,1)S(1)}, bf16[512,512]{1,0:T(8,128)(2,1)S(1)}) custom-call(s32[1]{0:T(128)S(6)} %copy.9.counts, f32[2,2,512]{2,1,0:T(2,128)S(1)} %bitcast.3, bf16[512,256]{1,0:T(8,128)(2,1)S(1)} %get-tuple-element.21.select, ...), custom_call_target="tpu_custom_call" | custom-call | flops 268435456 | bytes 2097152 | tf_op jit(solution)/shard_map/pallas_call | solution.py:261
  5.6 0.7 collective-permute-start.6
  6.3 0.7 collective-permute-start.7
  7.0 7.2 %collective-permute-start.2 = (bf16[2,512,128]{2,1,0:T(8,128)(2,1)S(1)}, bf16[2,512,128]{2,1,0:T(8,128)(2,1)S(1)}, u32[]{:S(2)}, u32[]{:S(2)}) collective-permute-start(bf16[2,512,128]{2,1,0:T(8,128)(2,1)S(1)} %copy-done.2), channel_id=1, source_target_pairs={{0,8},{8,16},{16,24},{24,32},{32,40},{40,48},{48,56},{56,64},{64,7... | collective-permute-start | bytes 786440 | tf_op jit(solution)/shard_map/ppermute | solution.py:220
  14.2 4.0 %collective-permute-start = (bf16[128,128]{1,0:T(8,128)(2,1)S(1)}, bf16[128,128]{1,0:T(8,128)(2,1)S(1)}, u32[]{:S(2)}, u32[]{:S(2)}) collective-permute-start(bf16[128,128]{1,0:T(8,128)(2,1)S(1)} %get-tuple-element.24), channel_id=1, source_target_pairs={{0,1},{1,2},{2,3},{3,4},{4,5},{5,6},{6,7},{7,0},{8,9},{9,10},{10,1... | collective-permute-start | bytes 98312 | tf_op jit(solution)/shard_map/ppermute | solution.py:220
  18.2 4.1 %collective-permute-start.1 = (bf16[128,128]{1,0:T(8,128)(2,1)S(1)}, bf16[128,128]{1,0:T(8,128)(2,1)S(1)}, u32[]{:S(2)}, u32[]{:S(2)}) collective-permute-start(bf16[128,128]{1,0:T(8,128)(2,1)S(1)} %get-tuple-element.25), channel_id=1, source_target_pairs={{1,0},{2,1},{3,2},{4,3},{5,4},{6,5},{7,6},{0,7},{9,8},{10,9},{11,1... | collective-permute-start | bytes 98312 | tf_op jit(solution)/shard_map/ppermute | solution.py:220
  22.4 1.0 %collective-permute-done.1.down = bf16[128,128]{1,0:T(8,128)(2,1)S(1)} collective-permute-done((bf16[128,128]{1,0:T(8,128)(2,1)S(1)}, bf16[128,128]{1,0:T(8,128)(2,1)S(1)}, u32[]{:S(2)}, u32[]{:S(2)}) %collective-permute-start.1) | collective-permute-done | bytes 32800 | tf_op jit(solution)/shard_map/ppermute | solution.py:220
  23.4 1.2 %shard_map.88.after = bf16[128,1280]{1,0:T(8,128)(2,1)} custom-call(s32[1]{0:T(128)S(6)} %copy.9.counts, bf16[128,128]{1,0:T(8,128)(2,1)S(1)} %get-tuple-element.20.order, bf16[128,512]{1,0:T(8,128)(2,1)S(1)} %get-tuple-element.22.d0, f32[128,512]{1,0:T(8,128)S(1)} %get-tuple-element.23.d1, bf16[128,128]{1,0:T(8,128)(2,1)S(1)} %collective-permute-done.up, ...), custom_call_target="tpu_custom_call" | custom-call | flops 67108864 | bytes 1048576 | tf_op jit(solution)/shard_map/pallas_call | solution.py:280
  24.6 9.4 %all-to-all-start = ((bf16[16,8,1280]{2,1,0:T(8,128)(2,1)}), bf16[16,8,1280]{2,1,0:T(8,128)(2,1)S(1)}, u32[]{:S(2)}, u32[]{:S(2)}) async-start(bf16[16,8,1280]{2,1,0:T(8,128)(2,1)} %bitcast.1), calls=%async_computation | async-start | bytes 655360 | tf_op jit(solution)/shard_map/all_to_all | solution.py:283
  34.1 0.7 collective-permute-start.8
  34.8 0.7 collective-permute-start.9
  35.5 11.6 %all-to-all-done.x = bf16[16,8,1280]{2,1,0:T(8,128)(2,1)S(1)} async-done(((bf16[16,8,1280]{2,1,0:T(8,128)(2,1)}), bf16[16,8,1280]{2,1,0:T(8,128)(2,1)S(1)}, u32[]{:S(2)}, u32[]{:S(2)}) %all-to-all-start) | async-done | bytes 327712 | tf_op jit(solution)/shard_map/all_to_all | solution.py:283
  47.3 1.4 %collective-permute-start.10 = (bf16[512,512]{1,0:T(8,128)(2,1)S(1)}, bf16[512,512]{1,0:T(8,128)(2,1)S(1)}, u32[]{:S(2)}, u32[]{:S(2)}) collective-permute-start(bf16[512,512]{1,0:T(8,128)(2,1)S(1)} %shard_map.91.r0_even), channel_id=1, source_target_pairs={{0,8},{64,72},{128,136},{192,200},{256,264},{320,328},{384,392},{4... | collective-permute-start | bytes 1572872 | tf_op jit(solution)/shard_map/ppermute | solution.py:220
  48.7 1.3 %collective-permute-start.3 = (f32[8,1280]{1,0:T(8,128)S(1)}, f32[8,1280]{1,0:T(8,128)S(1)}, u32[]{:S(2)}, u32[]{:S(2)}) collective-permute-start(f32[8,1280]{1,0:T(8,128)S(1)} %shard_map.89.after.x0), channel_id=1, source_target_pairs={{16,0},{17,1},{18,2},{19,3},{20,4},{21,5},{22,6},{23,7},{24,8},{25... | collective-permute-start | bytes 122888 | tf_op jit(solution)/shard_map/ppermute | solution.py:220
  50.0 1.3 %collective-permute-start.4 = (f32[8,1280]{1,0:T(8,128)S(1)}, f32[8,1280]{1,0:T(8,128)S(1)}, u32[]{:S(2)}, u32[]{:S(2)}) collective-permute-start(f32[8,1280]{1,0:T(8,128)S(1)} %shard_map.89.after.x0), channel_id=1, source_target_pairs={{32,0},{33,1},{34,2},{35,3},{36,4},{37,5},{38,6},{39,7},{40,8},{41... | collective-permute-start | bytes 122888 | tf_op jit(solution)/shard_map/ppermute | solution.py:220
  51.3 1.3 %collective-permute-start.5 = (f32[8,1280]{1,0:T(8,128)S(1)}, f32[8,1280]{1,0:T(8,128)S(1)}, u32[]{:S(2)}, u32[]{:S(2)}) collective-permute-start(f32[8,1280]{1,0:T(8,128)S(1)} %shard_map.89.after.x0), channel_id=1, source_target_pairs={{48,0},{49,1},{50,2},{51,3},{52,4},{53,5},{54,6},{55,7},{56,8},{57... | collective-permute-start | bytes 122888 | tf_op jit(solution)/shard_map/ppermute | solution.py:220
  52.6 1.7 %collective-permute-done.3.x1 = f32[8,1280]{1,0:T(8,128)S(1)} collective-permute-done((f32[8,1280]{1,0:T(8,128)S(1)}, f32[8,1280]{1,0:T(8,128)S(1)}, u32[]{:S(2)}, u32[]{:S(2)}) %collective-permute-start.3) | collective-permute-done | bytes 40992 | tf_op jit(solution)/shard_map/ppermute | solution.py:220
  54.3 4.3 %collective-permute-done.4.x2 = f32[8,1280]{1,0:T(8,128)S(1)} collective-permute-done((f32[8,1280]{1,0:T(8,128)S(1)}, f32[8,1280]{1,0:T(8,128)S(1)}, u32[]{:S(2)}, u32[]{:S(2)}) %collective-permute-start.4) | collective-permute-done | bytes 40992 | tf_op jit(solution)/shard_map/ppermute | solution.py:220
  58.7 1.0 %shard_map.92 = (f32[8,512]{1,0:T(8,128)S(1)}, f32[8,512]{1,0:T(8,128)S(1)}, bf16[8,128]{1,0:T(8,128)(2,1)S(1)}, bf16[8,128]{1,0:T(8,128)(2,1)S(1)}) custom-call(s32[1]{0:T(128)S(6)} %copy.9.counts, f32[8,1280]{1,0:T(8,128)S(1)} %shard_map.89.after.x0, f32[8,1280]{1,0:T(8,128)S(1)} %collective-permute-done.3.x1, f32[8,1280]{1,0:T(8,128)S(1)} %collective-permute-done.4.x2, ...), custom_call_target="tpu_custom_call" | custom-call | flops 25165824 | bytes 2097152 | tf_op jit(solution)/shard_map/pallas_call | solution.py:291
  59.7 3.4 %collective-permute-start.11 = (bf16[8,128]{1,0:T(8,128)(2,1)S(1)}, bf16[8,128]{1,0:T(8,128)(2,1)S(1)}, u32[]{:S(2)}, u32[]{:S(2)}) collective-permute-start(bf16[8,128]{1,0:T(8,128)(2,1)S(1)} %get-tuple-element.29), channel_id=1, source_target_pairs={{0,1},{1,2},{2,3},{3,4},{4,5},{5,6},{6,7},{7,0},{8,9},{9,10},{10,1... | collective-permute-start | bytes 6152 | tf_op jit(solution)/shard_map/ppermute | solution.py:220
  63.2 4.1 %collective-permute-start.12 = (bf16[8,128]{1,0:T(8,128)(2,1)S(1)}, bf16[8,128]{1,0:T(8,128)(2,1)S(1)}, u32[]{:S(2)}, u32[]{:S(2)}) collective-permute-start(bf16[8,128]{1,0:T(8,128)(2,1)S(1)} %get-tuple-element.30), channel_id=1, source_target_pairs={{1,0},{2,1},{3,2},{4,3},{5,4},{6,5},{7,6},{0,7},{9,8},{10,9},{11,1... | collective-permute-start | bytes 6152 | tf_op jit(solution)/shard_map/ppermute | solution.py:220
  67.3 0.7 collective-permute-done.12.down
  68.0 1.1 %shard_map.93 = (bf16[16,16,512]{2,1,0:T(8,128)(2,1)}, f32[2,2,512]{2,1,0:T(2,128)S(1)}, f32[2,2,512]{2,1,0:T(2,128)S(1)}, f32[2,2,512]{2,1,0:T(2,128)S(1)}, f32[2,2,512]{2,1,0:T(2,128)S(1)}) custom-call(f32[8,512]{1,0:T(8,128)S(1)} %get-tuple-element.27.cur0, f32[8,512]{1,0:T(8,128)S(1)} %get-tuple-element.28.first, ...), custom_call_target="tpu_custom_call" | custom-call | flops 8388608 | bytes 1048576 | tf_op jit(solution)/shard_map/pallas_call | solution.py:301
  69.1 10.5 %all-to-all-start.1 = ((bf16[16,16,512]{2,1,0:T(8,128)(2,1)}), bf16[16,16,512]{2,1,0:T(8,128)(2,1)S(1)}, u32[]{:S(2)}, u32[]{:S(2)}) async-start(bf16[16,16,512]{2,1,0:T(8,128)(2,1)} %get-tuple-element.31), calls=%async_computation.1 | async-start | bytes 524288 | tf_op jit(solution)/shard_map/all_to_all | solution.py:308
  79.5 1.3 %collective-permute-start.13 = (f32[2,2,512]{2,1,0:T(2,128)S(1)}, f32[2,2,512]{2,1,0:T(2,128)S(1)}, u32[]{:S(2)}, u32[]{:S(2)}) collective-permute-start(f32[2,2,512]{2,1,0:T(2,128)S(1)} %get-tuple-element.33), channel_id=1, source_target_pairs={{0,16},{8,24},{64,80},{72,88},{128,144},{136,152},{192,208},{200,2... | collective-permute-start | bytes 24584 | tf_op jit(solution)/shard_map/ppermute | solution.py:220
  80.8 1.3 %collective-permute-start.14 = (f32[2,2,512]{2,1,0:T(2,128)S(1)}, f32[2,2,512]{2,1,0:T(2,128)S(1)}, u32[]{:S(2)}, u32[]{:S(2)}) collective-permute-start(f32[2,2,512]{2,1,0:T(2,128)S(1)} %get-tuple-element.34), channel_id=1, source_target_pairs={{0,32},{8,40},{64,96},{72,104},{128,160},{136,168},{192,224},{200,... | collective-permute-start | bytes 24584 | tf_op jit(solution)/shard_map/ppermute | solution.py:220
  82.1 1.3 %collective-permute-start.15 = (f32[2,2,512]{2,1,0:T(2,128)S(1)}, f32[2,2,512]{2,1,0:T(2,128)S(1)}, u32[]{:S(2)}, u32[]{:S(2)}) collective-permute-start(f32[2,2,512]{2,1,0:T(2,128)S(1)} %get-tuple-element.35), channel_id=1, source_target_pairs={{0,48},{8,56},{64,112},{72,120},{128,176},{136,184},{192,240},{200... | collective-permute-start | bytes 24584 | tf_op jit(solution)/shard_map/ppermute | solution.py:220
  83.5 0.8 collective-permute-done.15.s3
  84.2 7.1 %all-to-all-done.1.gathered = bf16[16,16,512]{2,1,0:T(8,128)(2,1)S(1)} async-done(((bf16[16,16,512]{2,1,0:T(8,128)(2,1)}), bf16[16,16,512]{2,1,0:T(8,128)(2,1)S(1)}, u32[]{:S(2)}, u32[]{:S(2)}) %all-to-all-start.1) | async-done | bytes 262176 | tf_op jit(solution)/shard_map/all_to_all | solution.py:308
  91.3 0.7 shard_map.94
  (23 shorter events, 0.3 us)
Async XLA Ops:
  0.6 0.7 copy-start.4
  1.3 0.7 copy-start.3
  2.0 1.0 %copy-start.2 = (bf16[2,512,128]{2,1,0:T(8,128)(2,1)S(1)}, bf16[2,512,128]{2,1,0:T(8,128)(2,1)}, u32[]{:S(2)}) copy-start(bf16[2,512,128]{2,1,0:T(8,128)(2,1)} %hist.1) | copy-start | bytes 786436
  5.6 28.4 %collective-permute-start.6 = (bf16[512,512]{1,0:T(8,128)(2,1)S(1)}, bf16[512,512]{1,0:T(8,128)(2,1)S(1)}, u32[]{:S(2)}, u32[]{:S(2)}) collective-permute-start(bf16[512,512]{1,0:T(8,128)(2,1)S(1)} %get-tuple-element.26.r0.held), channel_id=1, source_target_pairs={{0,192},{1,193},{2,194},{3,195},{4,196},{5,197},{6,198},{7,199}} | collective-permute-start | bytes 1572872 | tf_op jit(solution)/shard_map/ppermute | solution.py:220
  6.3 27.7 %collective-permute-start.7 = (bf16[512,512]{1,0:T(8,128)(2,1)S(1)}, bf16[512,512]{1,0:T(8,128)(2,1)S(1)}, u32[]{:S(2)}, u32[]{:S(2)}) collective-permute-start(bf16[512,512]{1,0:T(8,128)(2,1)S(1)} %get-tuple-element.26.r0.held), channel_id=1, source_target_pairs={{0,320},{1,321},{2,322},{3,323},{4,324},{5,325},{6,326},{7,327}} | collective-permute-start | bytes 1572872 | tf_op jit(solution)/shard_map/ppermute | solution.py:220
  7.0 16.3 %collective-permute-start.2 = (bf16[2,512,128]{2,1,0:T(8,128)(2,1)S(1)}, bf16[2,512,128]{2,1,0:T(8,128)(2,1)S(1)}, u32[]{:S(2)}, u32[]{:S(2)}) collective-permute-start(bf16[2,512,128]{2,1,0:T(8,128)(2,1)S(1)} %copy-done.2), channel_id=1, source_target_pairs={{0,8},{8,16},{16,24},{24,32},{32,40},{40,48},{48,56},{56,64},{64,7... | collective-permute-start | bytes 786440 | tf_op jit(solution)/shard_map/ppermute | solution.py:220
  14.2 8.1 %collective-permute-start = (bf16[128,128]{1,0:T(8,128)(2,1)S(1)}, bf16[128,128]{1,0:T(8,128)(2,1)S(1)}, u32[]{:S(2)}, u32[]{:S(2)}) collective-permute-start(bf16[128,128]{1,0:T(8,128)(2,1)S(1)} %get-tuple-element.24), channel_id=1, source_target_pairs={{0,1},{1,2},{2,3},{3,4},{4,5},{5,6},{6,7},{7,0},{8,9},{9,10},{10,1... | collective-permute-start | bytes 98312 | tf_op jit(solution)/shard_map/ppermute | solution.py:220
  18.2 5.1 %collective-permute-start.1 = (bf16[128,128]{1,0:T(8,128)(2,1)S(1)}, bf16[128,128]{1,0:T(8,128)(2,1)S(1)}, u32[]{:S(2)}, u32[]{:S(2)}) collective-permute-start(bf16[128,128]{1,0:T(8,128)(2,1)S(1)} %get-tuple-element.25), channel_id=1, source_target_pairs={{1,0},{2,1},{3,2},{4,3},{5,4},{6,5},{7,6},{0,7},{9,8},{10,9},{11,1... | collective-permute-start | bytes 98312 | tf_op jit(solution)/shard_map/ppermute | solution.py:220
  24.6 22.5 %all-to-all-start = ((bf16[16,8,1280]{2,1,0:T(8,128)(2,1)}), bf16[16,8,1280]{2,1,0:T(8,128)(2,1)S(1)}, u32[]{:S(2)}, u32[]{:S(2)}) async-start(bf16[16,8,1280]{2,1,0:T(8,128)(2,1)} %bitcast.1), calls=%async_computation | async-start | bytes 655360 | tf_op jit(solution)/shard_map/all_to_all | solution.py:283
  34.1 13.1 %collective-permute-start.8 = (bf16[512,512]{1,0:T(8,128)(2,1)S(1)}, bf16[512,512]{1,0:T(8,128)(2,1)S(1)}, u32[]{:S(2)}, u32[]{:S(2)}) collective-permute-start(bf16[512,512]{1,0:T(8,128)(2,1)S(1)} %shard_map.90.held), channel_id=1, source_target_pairs={{0,64},{192,128},{320,384},{1,65},{193,129},{321,385},{2,66},{194,... | collective-permute-start | bytes 1572872 | tf_op jit(solution)/shard_map/ppermute | solution.py:220
  34.8 12.4 %collective-permute-start.9 = (bf16[512,512]{1,0:T(8,128)(2,1)S(1)}, bf16[512,512]{1,0:T(8,128)(2,1)S(1)}, u32[]{:S(2)}, u32[]{:S(2)}) collective-permute-start(bf16[512,512]{1,0:T(8,128)(2,1)S(1)} %shard_map.90.held), channel_id=1, source_target_pairs={{0,448},{192,256},{1,449},{193,257},{2,450},{194,258},{3,451},{195... | collective-permute-start | bytes 1572872 | tf_op jit(solution)/shard_map/ppermute | solution.py:220
  47.1 11.6 %copy-start = (bf16[512,512]{1,0:T(8,128)(2,1)S(1)}, bf16[512,512]{1,0:T(8,128)(2,1)}, u32[]{:S(2)}) copy-start(bf16[512,512]{1,0:T(8,128)(2,1)} %inv.5) | copy-start | bytes 1572868
  47.1 11.6 %copy-start.1 = (bf16[512,256]{1,0:T(8,128)(2,1)S(1)}, bf16[512,256]{1,0:T(8,128)(2,1)}, u32[]{:S(2)}) copy-start(bf16[512,256]{1,0:T(8,128)(2,1)} %tra.3) | copy-start | bytes 786436
  47.3 11.4 %collective-permute-start.10 = (bf16[512,512]{1,0:T(8,128)(2,1)S(1)}, bf16[512,512]{1,0:T(8,128)(2,1)S(1)}, u32[]{:S(2)}, u32[]{:S(2)}) collective-permute-start(bf16[512,512]{1,0:T(8,128)(2,1)S(1)} %shard_map.91.r0_even), channel_id=1, source_target_pairs={{0,8},{64,72},{128,136},{192,200},{256,264},{320,328},{384,392},{4... | collective-permute-start | bytes 1572872 | tf_op jit(solution)/shard_map/ppermute | solution.py:220
  48.7 5.6 %collective-permute-start.3 = (f32[8,1280]{1,0:T(8,128)S(1)}, f32[8,1280]{1,0:T(8,128)S(1)}, u32[]{:S(2)}, u32[]{:S(2)}) collective-permute-start(f32[8,1280]{1,0:T(8,128)S(1)} %shard_map.89.after.x0), channel_id=1, source_target_pairs={{16,0},{17,1},{18,2},{19,3},{20,4},{21,5},{22,6},{23,7},{24,8},{25... | collective-permute-start | bytes 122888 | tf_op jit(solution)/shard_map/ppermute | solution.py:220
  50.0 8.7 %collective-permute-start.4 = (f32[8,1280]{1,0:T(8,128)S(1)}, f32[8,1280]{1,0:T(8,128)S(1)}, u32[]{:S(2)}, u32[]{:S(2)}) collective-permute-start(f32[8,1280]{1,0:T(8,128)S(1)} %shard_map.89.after.x0), channel_id=1, source_target_pairs={{32,0},{33,1},{34,2},{35,3},{36,4},{37,5},{38,6},{39,7},{40,8},{41... | collective-permute-start | bytes 122888 | tf_op jit(solution)/shard_map/ppermute | solution.py:220
  51.3 7.4 %collective-permute-start.5 = (f32[8,1280]{1,0:T(8,128)S(1)}, f32[8,1280]{1,0:T(8,128)S(1)}, u32[]{:S(2)}, u32[]{:S(2)}) collective-permute-start(f32[8,1280]{1,0:T(8,128)S(1)} %shard_map.89.after.x0), channel_id=1, source_target_pairs={{48,0},{49,1},{50,2},{51,3},{52,4},{53,5},{54,6},{55,7},{56,8},{57... | collective-permute-start | bytes 122888 | tf_op jit(solution)/shard_map/ppermute | solution.py:220
  59.7 7.6 %collective-permute-start.11 = (bf16[8,128]{1,0:T(8,128)(2,1)S(1)}, bf16[8,128]{1,0:T(8,128)(2,1)S(1)}, u32[]{:S(2)}, u32[]{:S(2)}) collective-permute-start(bf16[8,128]{1,0:T(8,128)(2,1)S(1)} %get-tuple-element.29), channel_id=1, source_target_pairs={{0,1},{1,2},{2,3},{3,4},{4,5},{5,6},{6,7},{7,0},{8,9},{9,10},{10,1... | collective-permute-start | bytes 6152 | tf_op jit(solution)/shard_map/ppermute | solution.py:220
  63.2 4.8 %collective-permute-start.12 = (bf16[8,128]{1,0:T(8,128)(2,1)S(1)}, bf16[8,128]{1,0:T(8,128)(2,1)S(1)}, u32[]{:S(2)}, u32[]{:S(2)}) collective-permute-start(bf16[8,128]{1,0:T(8,128)(2,1)S(1)} %get-tuple-element.30), channel_id=1, source_target_pairs={{1,0},{2,1},{3,2},{4,3},{5,4},{6,5},{7,6},{0,7},{9,8},{10,9},{11,1... | collective-permute-start | bytes 6152 | tf_op jit(solution)/shard_map/ppermute | solution.py:220
  69.1 22.2 %all-to-all-start.1 = ((bf16[16,16,512]{2,1,0:T(8,128)(2,1)}), bf16[16,16,512]{2,1,0:T(8,128)(2,1)S(1)}, u32[]{:S(2)}, u32[]{:S(2)}) async-start(bf16[16,16,512]{2,1,0:T(8,128)(2,1)} %get-tuple-element.31), calls=%async_computation.1 | async-start | bytes 524288 | tf_op jit(solution)/shard_map/all_to_all | solution.py:308
  79.5 3.9 %collective-permute-start.13 = (f32[2,2,512]{2,1,0:T(2,128)S(1)}, f32[2,2,512]{2,1,0:T(2,128)S(1)}, u32[]{:S(2)}, u32[]{:S(2)}) collective-permute-start(f32[2,2,512]{2,1,0:T(2,128)S(1)} %get-tuple-element.33), channel_id=1, source_target_pairs={{0,16},{8,24},{64,80},{72,88},{128,144},{136,152},{192,208},{200,2... | collective-permute-start | bytes 24584 | tf_op jit(solution)/shard_map/ppermute | solution.py:220
  80.8 2.6 %collective-permute-start.14 = (f32[2,2,512]{2,1,0:T(2,128)S(1)}, f32[2,2,512]{2,1,0:T(2,128)S(1)}, u32[]{:S(2)}, u32[]{:S(2)}) collective-permute-start(f32[2,2,512]{2,1,0:T(2,128)S(1)} %get-tuple-element.34), channel_id=1, source_target_pairs={{0,32},{8,40},{64,96},{72,104},{128,160},{136,168},{192,224},{200,... | collective-permute-start | bytes 24584 | tf_op jit(solution)/shard_map/ppermute | solution.py:220
  82.1 2.1 %collective-permute-start.15 = (f32[2,2,512]{2,1,0:T(2,128)S(1)}, f32[2,2,512]{2,1,0:T(2,128)S(1)}, u32[]{:S(2)}, u32[]{:S(2)}) collective-permute-start(f32[2,2,512]{2,1,0:T(2,128)S(1)} %get-tuple-element.35), channel_id=1, source_target_pairs={{0,48},{8,56},{64,112},{72,120},{128,176},{136,184},{192,240},{200... | collective-permute-start | bytes 24584 | tf_op jit(solution)/shard_map/ppermute | solution.py:220

commit v4 on v3

--- a/solution.py
+++ b/solution.py
@@ -75,22 +75,18 @@
     return dot(block, order).astype(BF16)
 
 
-def selections(faces, select_ref, order_ref):
+def selections(faces, ret, select_ref, order_ref, r0_ref, sem):
+    copy = pltpu.make_async_copy(ret.at[0], r0_ref, sem)
+    copy.start()
     select_ref[...] = one_hot_rows(faces[...], select_ref.shape[0])
     order_ref[...] = permutation(order_ref.shape[0])
-
-
-def own_partials(
-    counts, exc, select, order, hist, ret, inv,
-    d0_ref, d1_ref, up_ref, down_ref, r0_ref,
-    r1, inv_v, sems,
-):
-    moves = [(ret.at[0], r0_ref), (ret.at[1], r1), (inv, inv_v)]
-    copies = [pltpu.make_async_copy(a, b, sems.at[k]) for k, (a, b) in enumerate(moves)]
-    for copy in copies:
-        copy.start()
+    copy.wait()
+
+
+def own_partials(counts, exc, order, hist, r0, ret, d0_ref, d1_ref, r1, sem):
+    copy = pltpu.make_async_copy(ret.at[1], r1, sem)
+    copy.start()
     width = hist.shape[2]
-    half = select.shape[1] // 2
     col = column_of(lax.broadcasted_iota(jnp.int32, (width, 1), 0))
     first_col = position() * 2
     m0, m1 = live(counts, 0), live(counts, 1)
@@ -100,28 +96,18 @@
         return jnp.where(col == first_col, e[0:1], jnp.where(col == first_col + 1, e[1:2], 0.0))
 
     h0, h1 = permuted(hist[0], order[...]), permuted(hist[1], order[...])
-    copies[0].wait()
-    p0 = dot(r0_ref[...], h0) * m0
-    copies[1].wait()
+    p0 = dot(r0[...], h0) * m0
+    copy.wait()
     p0 += dot(r1[...], h1) * m1
-    d0 = (placed(0) - p0.T).astype(BF16)
-    d0_ref[...] = d0
-    copies[2].wait()
-    first = dot_t(d0, inv_v[...]).astype(BF16)
-    trace = dot(first, select[...]).astype(BF16)
-    down_ref[...] = trace[:, :half]
-    up_ref[...] = trace[:, half:]
+    d0_ref[...] = (placed(0) - p0.T).astype(BF16)
     d1_ref[...] = placed(1) - (dot(r1[...], h0) * m1).T
 
 
-def pack_partials(counts, order, d0, d1, up, down, r0, before, out):
+def pack_partials(counts, order, d0, d1, r0, before, out):
     n = d0.shape[1]
-    half = up.shape[1]
     out[:, :n] = d0[...]
-    out[:, n : n + half] = up[...]
-    out[:, n + half : n + 2 * half] = down[...]
     p1 = dot(r0[...], permuted(before[1], order[...])) * live(counts, 0)
-    out[:, n + 2 * half :] = (d1[...] - p1.T).astype(BF16)
+    out[:, n:] = (d1[...] - p1.T).astype(BF16)
 
 
 def sum_parts(x, out):
@@ -131,7 +117,33 @@
     out[...] = total
 
 
-def two_firsts(counts, x0, x1, x2, x3, inv, tra, select, r0_even, r0_odd, cur_ref, first_ref, up_ref, down_ref, r0, sem):
+def trace_of(first, select, up_ref, down_ref):
+    trace = dot(first.astype(BF16), select[...]).astype(BF16)
+    half = select.shape[1] // 2
+    down_ref[...] = trace[:, :half]
+    up_ref[...] = trace[:, half:]
+
+
+def coupled(up, down, inv, tra):
+    half = up.shape[1]
+    coupling = dot_t(up[...], tra[:, :half]) + dot_t(down[...], tra[:, half:])
+    return dot_t(coupling.astype(BF16), inv[...])
+
+
+def first_of_sum(x0, x1, x2, x3, inv, select, first_ref, rest_ref, up_ref, down_ref):
+    n = inv.shape[0]
+    total = (x0[...] + x1[...]) + (x2[...] + x3[...])
+    first = dot_t(total[:, :n].astype(BF16), inv[...])
+    first_ref[...] = first
+    rest_ref[...] = total[:, n:]
+    trace_of(first, select, up_ref, down_ref)
+
+
+def next_first(
+    counts, first, rest, up, down, inv, tra, select, r0_even, r0_odd,
+    cur_ref, first_ref, up_ref, down_ref,
+    r0, sem,
+):
     odd = lax.axis_index("c") == 1
 
     @pl.when(odd)
@@ -142,29 +154,17 @@
     def _():
         copied(r0_even, r0, sem)
 
-    n = inv.shape[0]
-    faces_count = select.shape[1]
-    half = faces_count // 2
-    total = (x0[...] + x1[...]) + (x2[...] + x3[...])
-    rhs = total[:, :n].astype(BF16)
-    neighbour = total[:, n : n + faces_count].astype(BF16)
-    d1 = total[:, n + faces_count :]
-    coupling = dot_t(neighbour, tra[...]).astype(BF16)
-    cur = dot_t(rhs, inv[...]) - dot_t(coupling, inv[...])
+    cur = first[...] - coupled(up, down, inv, tra)
     cur_ref[...] = cur
     alive = (counts[0] > 0).astype(F32)
     newest = dot_t(cur.astype(BF16), r0[...]) * alive
-    first = dot_t((d1 - newest).astype(BF16), inv[...])
-    first_ref[...] = first
-    trace = dot(first.astype(BF16), select[...]).astype(BF16)
-    down_ref[...] = trace[:, :half]
-    up_ref[...] = trace[:, half:]
+    following = dot_t((rest[...] - newest).astype(BF16), inv[...])
+    first_ref[...] = following
+    trace_of(following, select, up_ref, down_ref)
 
 
 def second_current(cur0, first, up, down, inv, tra, gather_ref, *share_refs):
-    half = up.shape[1]
-    coupling = dot_t(up[...], tra[:, :half]) + dot_t(down[...], tra[:, half:])
-    cur1 = first[...] - dot_t(coupling.astype(BF16), inv[...])
+    cur1 = first[...] - coupled(up, down, inv, tra)
     c0 = cur0[...]
     both = jnp.concatenate([cur1.astype(BF16), c0.astype(BF16)], axis=0)
     for i in range(gather_ref.shape[0]):
@@ -251,53 +251,58 @@
 
     macs = n * n * width
     before = permute(history, DELAY, chain)
-    select, order = call(
+    select, order, r0 = call(
         selections,
-        (shape((n, 2 * half), BF16), shape((width, width), BF16)),
-        [VMEM],
-        64 * 1024 * 1024,
-        8 * 1024 * 1024,
-    )(faces)
-    d0, d1, up, down, r0 = call(
+        (shape((n, 2 * half), BF16), shape((width, width), BF16), shape((n, n), BF16)),
+        [VMEM, any_spec],
+        0,
+        1024 * 1024,
+        mib=53,
+        scratch_shapes=[pltpu.SemaphoreType.DMA],
+    )(faces, retarded)
+    d0, d1 = call(
         own_partials,
-        (
-            shape((width, n), BF16),
-            shape((width, n), F32),
-            shape((width, half), BF16),
-            shape((width, half), BF16),
-            shape((n, n), BF16),
-        ),
-        [SMEM] + [VMEM] * 4 + [any_spec] * 2,
+        (shape((width, n), BF16), shape((width, n), F32)),
+        [SMEM] + [VMEM] * 4 + [any_spec],
         2 * macs * 4,
         2 * 1024 * 1024,
         mib=52,
-        scratch_shapes=[pltpu.VMEM((n, n), BF16), pltpu.VMEM((n, n), BF16), pltpu.SemaphoreType.DMA((3,))],
-    )(counts, exc, select, order, history, retarded, inverse)
-    up = permute(up, "dom", ring)
-    down = permute(down, "dom", back)
+        scratch_shapes=[pltpu.VMEM((n, n), BF16), pltpu.SemaphoreType.DMA],
+    )(counts, exc, order, history, r0, retarded)
     s1a, s1b = spread(r0, (0, 3)), spread(r0, (0, 5))
-    lanes = 2 * n + 2 * half
-    packed = call(pack_partials, shape((width, lanes), BF16), [SMEM] + [VMEM] * 7, 2 * macs, 1024 * 1024)(
-        counts, order, d0, d1, up, down, r0, before
+    lanes = 2 * n
+    packed = call(pack_partials, shape((width, lanes), BF16), [SMEM] + [VMEM] * 5, 2 * macs, 1024 * 1024)(
+        counts, order, d0, d1, r0, before
     )
     x = lax.all_to_all(packed.reshape(OWNERS, cols, lanes), ("y", "c"), 0, 0, tiled=True)
     r0 = relayed((0,), (3,), r0, s1a, s1b, packed)
     s2a, s2b = spread(r0, (0, 1), (3, 2), (5, 6)), spread(r0, (0, 7), (3, 4))
     x = call(sum_parts, shape((cols, lanes), F32), [VMEM], 0, 512 * 1024)(x)
     xs = [x] + [permute(x, "zh", [(z, 0)]) for z in range(1, ZH)]
-    r0 = relayed((0, 3, 5), (1, 2, 6), r0, s2a, s2b, x)
+    r0 = relayed((0, 3, 5), (1, 2, 6), r0, s2a, s2b, xs[1])
     s3 = permute(r0, DELAY, [(at(i, 0, 0), at(i, 0, 1)) for i in range(Y)])
 
+    def halo(up, down):
+        return permute(up, ("zh", "dom"), ring), permute(down, ("zh", "dom"), back)
+
+    trace_shape = (shape((cols, half), BF16),) * 2
+    first, rest, up, down = call(
+        first_of_sum,
+        (shape((cols, n), F32), shape((cols, n), F32)) + trace_shape,
+        [VMEM] * 6,
+        2 * 8 * n * n * 2,
+        1024 * 1024,
+    )(*xs, inverse, select)
+    up, down = halo(up, down)
     cur0, first, up, down = call(
-        two_firsts,
-        (shape((cols, n), F32), shape((cols, n), F32), shape((cols, half), BF16), shape((cols, half), BF16)),
+        next_first,
+        (shape((cols, n), F32), shape((cols, n), F32)) + trace_shape,
         [SMEM] + [VMEM] * 7 + [any_spec] * 2,
-        2 * 8 * n * n * 6,
+        2 * 8 * n * n * 5,
         2 * 1024 * 1024,
         scratch_shapes=[pltpu.VMEM((n, n), BF16), pltpu.SemaphoreType.DMA],
-    )(counts, *xs, inverse, transfer, select, r0, s3)
-    up = permute(up, ("zh", "dom"), ring)
-    down = permute(down, ("zh", "dom"), back)
+    )(counts, first, rest, up, down, inverse, transfer, select, r0, s3)
+    up, down = halo(up, down)
     gather, *share = call(
         second_current,
         [shape((OWNERS, 2 * cols, n), BF16)] + [shape((steps, 2, n), F32)] * ZH,

time: 92.7 us -> 98.9 us (1.067)
  waiting for transfers between devices: 27.2 us -> 31.2 us
  starting transfers between devices: 54.6 us -> 57.3 us
    all_to_all x1, starting transfers between devices: 9.39 us -> 15.2 us  [body(): lax.all_to_all(packed.reshape(OWNERS, cols, lanes), ('y', 'c'), 0, 0, til...]
    ppermute x16, waiting for transfers between devices: 8.57 us -> 13.7 us  [permute(): return lax.ppermute(value, axes, pairs)]
    all_to_all x1, starting transfers between devices: 10.5 us -> 7.9 us  [body(): gather = lax.all_to_all(gather, ('y', 'c'), 0, 0, tiled=True)]
    all_to_all x1, waiting for transfers between devices: 11.6 us -> 10.2 us  [body(): lax.all_to_all(packed.reshape(OWNERS, cols, lanes), ('y', 'c'), 0, 0, til...]
    pallas_call x3 -> x4, Pallas kernels: 4.87 us -> 4.43 us  [the longest x1 1.94 us: body(): call(own_partials, (shape((width, n), BF16), shape((width, n), F32)), [SM...]
  transfers between devices with their start and end apart: 18 -> 18, of which waited for: 7 -> 8; matrix products, arithmetic and copies ran while one was open for 0% -> 0% of each run, Pallas kernels for 1% -> 4%
where the time goes in v4:
time: 98.9 us; the launch traced here: 98.2 us
  starting transfers between devices  57.3 us (58%)
  waiting for transfers between devices  31.2 us (32%)
  Pallas kernels  7.48 us (8%)
  between operations  1.54 us (2%)
    ppermute x16, starting transfers between devices, permute(): return lax.ppermute(value, axes, pairs)  34.2 us
    all_to_all x1, starting transfers between devices, body(): lax.all_to_all(packed.reshape(OWNERS, cols, lanes), ('y', 'c'), 0, 0, til...  15.2 us
    ppermute x16, waiting for transfers between devices, permute(): return lax.ppermute(value, axes, pairs)  13.7 us
    all_to_all x1, waiting for transfers between devices, body(): lax.all_to_all(packed.reshape(OWNERS, cols, lanes), ('y', 'c'), 0, 0, til...  10.2 us
    all_to_all x1, starting transfers between devices, body(): gather = lax.all_to_all(gather, ('y', 'c'), 0, 0, tiled=True)  7.9 us
    all_to_all x1, waiting for transfers between devices, body(): gather = lax.all_to_all(gather, ('y', 'c'), 0, 0, tiled=True)  7.2 us
  transfers between devices with their start and end apart: 18, of which 8 were waited for; matrix products, arithmetic and copies ran while one was open for 0% of the time, Pallas kernels for 4%

profile of v4, /device:TPU:1, one launch (start us, length us, event | category | flops | bytes accessed | tf_op | source)
XLA Modules:
  0.0 98.2 jit_solution(7648126322005872321)
XLA Ops:
  0.6 0.7 copy-done.4
  1.4 1.1 %shard_map.86 = (bf16[512,256]{1,0:T(8,128)(2,1)S(1)}, bf16[128,128]{1,0:T(8,128)(2,1)S(1)}, bf16[512,512]{1,0:T(8,128)(2,1)S(1)}) custom-call(s32[1,256]{1,0:T(1,128)S(1)} %copy-done.4, bf16[2,512,512]{2,1,0:T(8,128)(2,1)} %ret.3), custom_call_target="tpu_custom_call" | custom-call | bytes 1048576 | tf_op jit(solution)/shard_map/pallas_call | solution.py:254
  2.4 0.7 collective-permute-start.6
  3.1 0.7 collective-permute-start.7
  3.8 7.2 %collective-permute-start = (bf16[2,512,128]{2,1,0:T(8,128)(2,1)S(1)}, bf16[2,512,128]{2,1,0:T(8,128)(2,1)S(1)}, u32[]{:S(2)}, u32[]{:S(2)}) collective-permute-start(bf16[2,512,128]{2,1,0:T(8,128)(2,1)S(1)} %copy-done.2), channel_id=1, source_target_pairs={{0,8},{8,16},{16,24},{24,32},{32,40},{40,48},{48,56},{56,64},{64,7... | collective-permute-start | bytes 786440 | tf_op jit(solution)/shard_map/ppermute | solution.py:220
  11.7 1.9 %shard_map.87 = (bf16[128,512]{1,0:T(8,128)(2,1)S(1)}, f32[128,512]{1,0:T(8,128)S(1)}) custom-call(s32[1]{0:T(128)S(6)} %copy.9.counts, f32[2,2,512]{2,1,0:T(2,128)S(1)} %bitcast.3, bf16[128,128]{1,0:T(8,128)(2,1)S(1)} %get-tuple-element.22.order, bf16[2,512,128]{2,1,0:T(8,128)(2,1)S(1)} %copy-done.2, bf16[512,512]{1,0:T(8,128)(2,1)S(1)} %get-tuple-element.23.r0.held, ...), custom_call_target="tpu_custom_call" | custom-call | flops 268435456 | bytes 2097152 | tf_op jit(solution)/shard_map/pallas_call | solution.py:263
  13.7 0.7 collective-permute-done.before
  14.4 1.2 %shard_map.88.after = bf16[128,1024]{1,0:T(8,128)(2,1)} custom-call(s32[1]{0:T(128)S(6)} %copy.9.counts, bf16[128,128]{1,0:T(8,128)(2,1)S(1)} %get-tuple-element.22.order, bf16[128,512]{1,0:T(8,128)(2,1)S(1)} %get-tuple-element.24.d0, f32[128,512]{1,0:T(8,128)S(1)} %get-tuple-element.25.d1, bf16[512,512]{1,0:T(8,128)(2,1)S(1)} %get-tuple-element.23.r0.held, ...), custom_call_target="tpu_custom_call" | custom-call | flops 67108864 | bytes 1048576 | tf_op jit(solution)/shard_map/pallas_call | solution.py:274
  15.6 15.2 %all-to-all-start = ((bf16[16,8,1024]{2,1,0:T(8,128)(2,1)}), bf16[16,8,1024]{2,1,0:T(8,128)(2,1)S(1)}, u32[]{:S(2)}, u32[]{:S(2)}) async-start(bf16[16,8,1024]{2,1,0:T(8,128)(2,1)} %bitcast.1), calls=%async_computation | async-start | bytes 524288 | tf_op jit(solution)/shard_map/all_to_all | solution.py:277
  30.9 0.7 collective-permute-start.8
  32.3 10.2 %all-to-all-done.x = bf16[16,8,1024]{2,1,0:T(8,128)(2,1)S(1)} async-done(((bf16[16,8,1024]{2,1,0:T(8,128)(2,1)}), bf16[16,8,1024]{2,1,0:T(8,128)(2,1)S(1)}, u32[]{:S(2)}, u32[]{:S(2)}) %all-to-all-start) | async-done | bytes 262176 | tf_op jit(solution)/shard_map/all_to_all | solution.py:277
  42.6 1.4 %collective-permute-start.1 = (f32[8,1024]{1,0:T(8,128)S(1)}, f32[8,1024]{1,0:T(8,128)S(1)}, u32[]{:S(2)}, u32[]{:S(2)}) collective-permute-start(f32[8,1024]{1,0:T(8,128)S(1)} %shard_map.89.x0), channel_id=1, source_target_pairs={{16,0},{17,1},{18,2},{19,3},{20,4},{21,5},{22,6},{23,7},{24,8},{25... | collective-permute-start | bytes 98312 | tf_op jit(solution)/shard_map/ppermute | solution.py:220
  44.0 4.9 %collective-permute-done.1.x1.after = f32[8,1024]{1,0:T(8,128)S(1)} collective-permute-done((f32[8,1024]{1,0:T(8,128)S(1)}, f32[8,1024]{1,0:T(8,128)S(1)}, u32[]{:S(2)}, u32[]{:S(2)}) %collective-permute-start.1) | collective-permute-done | bytes 32800 | tf_op jit(solution)/shard_map/ppermute | solution.py:220
  49.0 1.3 %collective-permute-start.10 = (bf16[512,512]{1,0:T(8,128)(2,1)S(1)}, bf16[512,512]{1,0:T(8,128)(2,1)S(1)}, u32[]{:S(2)}, u32[]{:S(2)}) collective-permute-start(bf16[512,512]{1,0:T(8,128)(2,1)S(1)} %shard_map.92.r0_even), channel_id=1, source_target_pairs={{0,8},{64,72},{128,136},{192,200},{256,264},{320,328},{384,392},{4... | collective-permute-start | bytes 1572872 | tf_op jit(solution)/shard_map/ppermute | solution.py:220
  50.3 1.3 %collective-permute-start.2 = (f32[8,1024]{1,0:T(8,128)S(1)}, f32[8,1024]{1,0:T(8,128)S(1)}, u32[]{:S(2)}, u32[]{:S(2)}) collective-permute-start(f32[8,1024]{1,0:T(8,128)S(1)} %shard_map.89.x0), channel_id=1, source_target_pairs={{32,0},{33,1},{34,2},{35,3},{36,4},{37,5},{38,6},{39,7},{40,8},{41... | collective-permute-start | bytes 98312 | tf_op jit(solution)/shard_map/ppermute | solution.py:220
  51.6 1.3 %collective-permute-start.3 = (f32[8,1024]{1,0:T(8,128)S(1)}, f32[8,1024]{1,0:T(8,128)S(1)}, u32[]{:S(2)}, u32[]{:S(2)}) collective-permute-start(f32[8,1024]{1,0:T(8,128)S(1)} %shard_map.89.x0), channel_id=1, source_target_pairs={{48,0},{49,1},{50,2},{51,3},{52,4},{53,5},{54,6},{55,7},{56,8},{57... | collective-permute-start | bytes 98312 | tf_op jit(solution)/shard_map/ppermute | solution.py:220
  52.9 6.0 %collective-permute-done.2.x2 = f32[8,1024]{1,0:T(8,128)S(1)} collective-permute-done((f32[8,1024]{1,0:T(8,128)S(1)}, f32[8,1024]{1,0:T(8,128)S(1)}, u32[]{:S(2)}, u32[]{:S(2)}) %collective-permute-start.2) | collective-permute-done | bytes 32800 | tf_op jit(solution)/shard_map/ppermute | solution.py:220
  59.2 3.3 %collective-permute-start.4 = (bf16[8,128]{1,0:T(8,128)(2,1)S(1)}, bf16[8,128]{1,0:T(8,128)(2,1)S(1)}, u32[]{:S(2)}, u32[]{:S(2)}) collective-permute-start(bf16[8,128]{1,0:T(8,128)(2,1)S(1)} %get-tuple-element.29), channel_id=1, source_target_pairs={{0,1},{1,2},{2,3},{3,4},{4,5},{5,6},{6,7},{7,0},{8,9},{9,10},{10,1... | collective-permute-start | bytes 6152 | tf_op jit(solution)/shard_map/ppermute | solution.py:220
  62.5 4.1 %collective-permute-start.5 = (bf16[8,128]{1,0:T(8,128)(2,1)S(1)}, bf16[8,128]{1,0:T(8,128)(2,1)S(1)}, u32[]{:S(2)}, u32[]{:S(2)}) collective-permute-start(bf16[8,128]{1,0:T(8,128)(2,1)S(1)} %get-tuple-element.30), channel_id=1, source_target_pairs={{1,0},{2,1},{3,2},{4,3},{5,4},{6,5},{7,6},{0,7},{9,8},{10,9},{11,1... | collective-permute-start | bytes 6152 | tf_op jit(solution)/shard_map/ppermute | solution.py:220
  66.7 0.7 collective-permute-done.5.down
  67.4 0.9 shard_map.93
  68.3 3.3 %collective-permute-start.11 = (bf16[8,128]{1,0:T(8,128)(2,1)S(1)}, bf16[8,128]{1,0:T(8,128)(2,1)S(1)}, u32[]{:S(2)}, u32[]{:S(2)}) collective-permute-start(bf16[8,128]{1,0:T(8,128)(2,1)S(1)} %get-tuple-element.33), channel_id=1, source_target_pairs={{0,1},{1,2},{2,3},{3,4},{4,5},{5,6},{6,7},{7,0},{8,9},{9,10},{10,1... | collective-permute-start | bytes 6152 | tf_op jit(solution)/shard_map/ppermute | solution.py:220
  71.6 4.3 %collective-permute-start.12 = (bf16[8,128]{1,0:T(8,128)(2,1)S(1)}, bf16[8,128]{1,0:T(8,128)(2,1)S(1)}, u32[]{:S(2)}, u32[]{:S(2)}) collective-permute-start(bf16[8,128]{1,0:T(8,128)(2,1)S(1)} %get-tuple-element.34), channel_id=1, source_target_pairs={{1,0},{2,1},{3,2},{4,3},{5,4},{6,5},{7,6},{0,7},{9,8},{10,9},{11,1... | collective-permute-start | bytes 6152 | tf_op jit(solution)/shard_map/ppermute | solution.py:220
  75.9 0.7 collective-permute-done.12.down
  76.6 1.1 %shard_map.94 = (bf16[16,16,512]{2,1,0:T(8,128)(2,1)}, f32[2,2,512]{2,1,0:T(2,128)S(1)}, f32[2,2,512]{2,1,0:T(2,128)S(1)}, f32[2,2,512]{2,1,0:T(2,128)S(1)}, f32[2,2,512]{2,1,0:T(2,128)S(1)}) custom-call(f32[8,512]{1,0:T(8,128)S(1)} %get-tuple-element.31.cur0, f32[8,512]{1,0:T(8,128)S(1)} %get-tuple-element.32.first, ...), custom_call_target="tpu_custom_call" | custom-call | flops 8388608 | bytes 1048576 | tf_op jit(solution)/shard_map/pallas_call | solution.py:306
  77.7 7.9 %all-to-all-start.1 = ((bf16[16,16,512]{2,1,0:T(8,128)(2,1)}), bf16[16,16,512]{2,1,0:T(8,128)(2,1)S(1)}, u32[]{:S(2)}, u32[]{:S(2)}) async-start(bf16[16,16,512]{2,1,0:T(8,128)(2,1)} %get-tuple-element.35), calls=%async_computation.1 | async-start | bytes 524288 | tf_op jit(solution)/shard_map/all_to_all | solution.py:313
  85.6 1.3 %collective-permute-start.13 = (f32[2,2,512]{2,1,0:T(2,128)S(1)}, f32[2,2,512]{2,1,0:T(2,128)S(1)}, u32[]{:S(2)}, u32[]{:S(2)}) collective-permute-start(f32[2,2,512]{2,1,0:T(2,128)S(1)} %get-tuple-element.37), channel_id=1, source_target_pairs={{0,16},{8,24},{64,80},{72,88},{128,144},{136,152},{192,208},{200,2... | collective-permute-start | bytes 24584 | tf_op jit(solution)/shard_map/ppermute | solution.py:220
  86.9 1.3 %collective-permute-start.14 = (f32[2,2,512]{2,1,0:T(2,128)S(1)}, f32[2,2,512]{2,1,0:T(2,128)S(1)}, u32[]{:S(2)}, u32[]{:S(2)}) collective-permute-start(f32[2,2,512]{2,1,0:T(2,128)S(1)} %get-tuple-element.38), channel_id=1, source_target_pairs={{0,32},{8,40},{64,96},{72,104},{128,160},{136,168},{192,224},{200,... | collective-permute-start | bytes 24584 | tf_op jit(solution)/shard_map/ppermute | solution.py:220
  88.2 1.3 %collective-permute-start.15 = (f32[2,2,512]{2,1,0:T(2,128)S(1)}, f32[2,2,512]{2,1,0:T(2,128)S(1)}, u32[]{:S(2)}, u32[]{:S(2)}) collective-permute-start(f32[2,2,512]{2,1,0:T(2,128)S(1)} %get-tuple-element.39), channel_id=1, source_target_pairs={{0,48},{8,56},{64,112},{72,120},{128,176},{136,184},{192,240},{200... | collective-permute-start | bytes 24584 | tf_op jit(solution)/shard_map/ppermute | solution.py:220
  89.5 0.8 collective-permute-done.15.s3
  90.3 7.2 %all-to-all-done.1.gathered = bf16[16,16,512]{2,1,0:T(8,128)(2,1)S(1)} async-done(((bf16[16,16,512]{2,1,0:T(8,128)(2,1)}), bf16[16,16,512]{2,1,0:T(8,128)(2,1)S(1)}, u32[]{:S(2)}, u32[]{:S(2)}) %all-to-all-start.1) | async-done | bytes 262176 | tf_op jit(solution)/shard_map/all_to_all | solution.py:313
  97.5 0.7 shard_map.95
  (24 shorter events, 1.3 us)
Async XLA Ops:
  0.6 3.2 %copy-start.2 = (bf16[2,512,128]{2,1,0:T(8,128)(2,1)S(1)}, bf16[2,512,128]{2,1,0:T(8,128)(2,1)}, u32[]{:S(2)}) copy-start(bf16[2,512,128]{2,1,0:T(8,128)(2,1)} %hist.1) | copy-start | bytes 786436
  0.6 0.7 copy-start.4
  1.4 10.3 %copy-start.3 = (f32[2,512,2]{1,2,0:T(2,128)S(1)}, f32[2,512,2]{1,2,0:T(2,128)}, u32[]{:S(2)}) copy-start(f32[2,512,2]{1,2,0:T(2,128)} %param.7) | copy-start | bytes 24580
  2.4 28.4 %collective-permute-start.6 = (bf16[512,512]{1,0:T(8,128)(2,1)S(1)}, bf16[512,512]{1,0:T(8,128)(2,1)S(1)}, u32[]{:S(2)}, u32[]{:S(2)}) collective-permute-start(bf16[512,512]{1,0:T(8,128)(2,1)S(1)} %get-tuple-element.23.r0.held), channel_id=1, source_target_pairs={{0,192},{1,193},{2,194},{3,195},{4,196},{5,197},{6,198},{7,199}} | collective-permute-start | bytes 1572872 | tf_op jit(solution)/shard_map/ppermute | solution.py:220
  3.1 27.7 %collective-permute-start.7 = (bf16[512,512]{1,0:T(8,128)(2,1)S(1)}, bf16[512,512]{1,0:T(8,128)(2,1)S(1)}, u32[]{:S(2)}, u32[]{:S(2)}) collective-permute-start(bf16[512,512]{1,0:T(8,128)(2,1)S(1)} %get-tuple-element.23.r0.held), channel_id=1, source_target_pairs={{0,320},{1,321},{2,322},{3,323},{4,324},{5,325},{6,326},{7,327}} | collective-permute-start | bytes 1572872 | tf_op jit(solution)/shard_map/ppermute | solution.py:220
  3.8 10.5 %collective-permute-start = (bf16[2,512,128]{2,1,0:T(8,128)(2,1)S(1)}, bf16[2,512,128]{2,1,0:T(8,128)(2,1)S(1)}, u32[]{:S(2)}, u32[]{:S(2)}) collective-permute-start(bf16[2,512,128]{2,1,0:T(8,128)(2,1)S(1)} %copy-done.2), channel_id=1, source_target_pairs={{0,8},{8,16},{16,24},{24,32},{32,40},{40,48},{48,56},{56,64},{64,7... | collective-permute-start | bytes 786440 | tf_op jit(solution)/shard_map/ppermute | solution.py:220
  15.6 26.9 %all-to-all-start = ((bf16[16,8,1024]{2,1,0:T(8,128)(2,1)}), bf16[16,8,1024]{2,1,0:T(8,128)(2,1)S(1)}, u32[]{:S(2)}, u32[]{:S(2)}) async-start(bf16[16,8,1024]{2,1,0:T(8,128)(2,1)} %bitcast.1), calls=%async_computation | async-start | bytes 524288 | tf_op jit(solution)/shard_map/all_to_all | solution.py:277
  30.9 18.0 %collective-permute-start.8 = (bf16[512,512]{1,0:T(8,128)(2,1)S(1)}, bf16[512,512]{1,0:T(8,128)(2,1)S(1)}, u32[]{:S(2)}, u32[]{:S(2)}) collective-permute-start(bf16[512,512]{1,0:T(8,128)(2,1)S(1)} %shard_map.91.held), channel_id=1, source_target_pairs={{0,64},{192,128},{320,384},{1,65},{193,129},{321,385},{2,66},{194,... | collective-permute-start | bytes 1572872 | tf_op jit(solution)/shard_map/ppermute | solution.py:220
  31.6 17.3 %collective-permute-start.9 = (bf16[512,512]{1,0:T(8,128)(2,1)S(1)}, bf16[512,512]{1,0:T(8,128)(2,1)S(1)}, u32[]{:S(2)}, u32[]{:S(2)}) collective-permute-start(bf16[512,512]{1,0:T(8,128)(2,1)S(1)} %shard_map.91.held), channel_id=1, source_target_pairs={{0,448},{192,256},{1,449},{193,257},{2,450},{194,258},{3,451},{195... | collective-permute-start | bytes 1572872 | tf_op jit(solution)/shard_map/ppermute | solution.py:220
  42.6 16.3 %copy-start = (bf16[512,512]{1,0:T(8,128)(2,1)S(1)}, bf16[512,512]{1,0:T(8,128)(2,1)}, u32[]{:S(2)}) copy-start(bf16[512,512]{1,0:T(8,128)(2,1)} %inv.5) | copy-start | bytes 1572868
  42.6 6.3 %collective-permute-start.1 = (f32[8,1024]{1,0:T(8,128)S(1)}, f32[8,1024]{1,0:T(8,128)S(1)}, u32[]{:S(2)}, u32[]{:S(2)}) collective-permute-start(f32[8,1024]{1,0:T(8,128)S(1)} %shard_map.89.x0), channel_id=1, source_target_pairs={{16,0},{17,1},{18,2},{19,3},{20,4},{21,5},{22,6},{23,7},{24,8},{25... | collective-permute-start | bytes 98312 | tf_op jit(solution)/shard_map/ppermute | solution.py:220
  49.0 18.4 %collective-permute-start.10 = (bf16[512,512]{1,0:T(8,128)(2,1)S(1)}, bf16[512,512]{1,0:T(8,128)(2,1)S(1)}, u32[]{:S(2)}, u32[]{:S(2)}) collective-permute-start(bf16[512,512]{1,0:T(8,128)(2,1)S(1)} %shard_map.92.r0_even), channel_id=1, source_target_pairs={{0,8},{64,72},{128,136},{192,200},{256,264},{320,328},{384,392},{4... | collective-permute-start | bytes 1572872 | tf_op jit(solution)/shard_map/ppermute | solution.py:220
  50.3 8.6 %collective-permute-start.2 = (f32[8,1024]{1,0:T(8,128)S(1)}, f32[8,1024]{1,0:T(8,128)S(1)}, u32[]{:S(2)}, u32[]{:S(2)}) collective-permute-start(f32[8,1024]{1,0:T(8,128)S(1)} %shard_map.89.x0), channel_id=1, source_target_pairs={{32,0},{33,1},{34,2},{35,3},{36,4},{37,5},{38,6},{39,7},{40,8},{41... | collective-permute-start | bytes 98312 | tf_op jit(solution)/shard_map/ppermute | solution.py:220
  51.6 7.3 %collective-permute-start.3 = (f32[8,1024]{1,0:T(8,128)S(1)}, f32[8,1024]{1,0:T(8,128)S(1)}, u32[]{:S(2)}, u32[]{:S(2)}) collective-permute-start(f32[8,1024]{1,0:T(8,128)S(1)} %shard_map.89.x0), channel_id=1, source_target_pairs={{48,0},{49,1},{50,2},{51,3},{52,4},{53,5},{54,6},{55,7},{56,8},{57... | collective-permute-start | bytes 98312 | tf_op jit(solution)/shard_map/ppermute | solution.py:220
  58.9 8.5 %copy-start.1 = (bf16[512,256]{1,0:T(8,128)(2,1)S(1)}, bf16[512,256]{1,0:T(8,128)(2,1)}, u32[]{:S(2)}) copy-start(bf16[512,256]{1,0:T(8,128)(2,1)} %tra.3) | copy-start | bytes 786436
  59.2 7.4 %collective-permute-start.4 = (bf16[8,128]{1,0:T(8,128)(2,1)S(1)}, bf16[8,128]{1,0:T(8,128)(2,1)S(1)}, u32[]{:S(2)}, u32[]{:S(2)}) collective-permute-start(bf16[8,128]{1,0:T(8,128)(2,1)S(1)} %get-tuple-element.29), channel_id=1, source_target_pairs={{0,1},{1,2},{2,3},{3,4},{4,5},{5,6},{6,7},{7,0},{8,9},{9,10},{10,1... | collective-permute-start | bytes 6152 | tf_op jit(solution)/shard_map/ppermute | solution.py:220
  62.5 4.8 %collective-permute-start.5 = (bf16[8,128]{1,0:T(8,128)(2,1)S(1)}, bf16[8,128]{1,0:T(8,128)(2,1)S(1)}, u32[]{:S(2)}, u32[]{:S(2)}) collective-permute-start(bf16[8,128]{1,0:T(8,128)(2,1)S(1)} %get-tuple-element.30), channel_id=1, source_target_pairs={{1,0},{2,1},{3,2},{4,3},{5,4},{6,5},{7,6},{0,7},{9,8},{10,9},{11,1... | collective-permute-start | bytes 6152 | tf_op jit(solution)/shard_map/ppermute | solution.py:220
  68.3 7.7 %collective-permute-start.11 = (bf16[8,128]{1,0:T(8,128)(2,1)S(1)}, bf16[8,128]{1,0:T(8,128)(2,1)S(1)}, u32[]{:S(2)}, u32[]{:S(2)}) collective-permute-start(bf16[8,128]{1,0:T(8,128)(2,1)S(1)} %get-tuple-element.33), channel_id=1, source_target_pairs={{0,1},{1,2},{2,3},{3,4},{4,5},{5,6},{6,7},{7,0},{8,9},{9,10},{10,1... | collective-permute-start | bytes 6152 | tf_op jit(solution)/shard_map/ppermute | solution.py:220
  71.6 5.0 %collective-permute-start.12 = (bf16[8,128]{1,0:T(8,128)(2,1)S(1)}, bf16[8,128]{1,0:T(8,128)(2,1)S(1)}, u32[]{:S(2)}, u32[]{:S(2)}) collective-permute-start(bf16[8,128]{1,0:T(8,128)(2,1)S(1)} %get-tuple-element.34), channel_id=1, source_target_pairs={{1,0},{2,1},{3,2},{4,3},{5,4},{6,5},{7,6},{0,7},{9,8},{10,9},{11,1... | collective-permute-start | bytes 6152 | tf_op jit(solution)/shard_map/ppermute | solution.py:220
  77.7 19.8 %all-to-all-start.1 = ((bf16[16,16,512]{2,1,0:T(8,128)(2,1)}), bf16[16,16,512]{2,1,0:T(8,128)(2,1)S(1)}, u32[]{:S(2)}, u32[]{:S(2)}) async-start(bf16[16,16,512]{2,1,0:T(8,128)(2,1)} %get-tuple-element.35), calls=%async_computation.1 | async-start | bytes 524288 | tf_op jit(solution)/shard_map/all_to_all | solution.py:313
  85.6 3.9 %collective-permute-start.13 = (f32[2,2,512]{2,1,0:T(2,128)S(1)}, f32[2,2,512]{2,1,0:T(2,128)S(1)}, u32[]{:S(2)}, u32[]{:S(2)}) collective-permute-start(f32[2,2,512]{2,1,0:T(2,128)S(1)} %get-tuple-element.37), channel_id=1, source_target_pairs={{0,16},{8,24},{64,80},{72,88},{128,144},{136,152},{192,208},{200,2... | collective-permute-start | bytes 24584 | tf_op jit(solution)/shard_map/ppermute | solution.py:220
  86.9 2.6 %collective-permute-start.14 = (f32[2,2,512]{2,1,0:T(2,128)S(1)}, f32[2,2,512]{2,1,0:T(2,128)S(1)}, u32[]{:S(2)}, u32[]{:S(2)}) collective-permute-start(f32[2,2,512]{2,1,0:T(2,128)S(1)} %get-tuple-element.38), channel_id=1, source_target_pairs={{0,32},{8,40},{64,96},{72,104},{128,160},{136,168},{192,224},{200,... | collective-permute-start | bytes 24584 | tf_op jit(solution)/shard_map/ppermute | solution.py:220
  88.2 2.1 %collective-permute-start.15 = (f32[2,2,512]{2,1,0:T(2,128)S(1)}, f32[2,2,512]{2,1,0:T(2,128)S(1)}, u32[]{:S(2)}, u32[]{:S(2)}) collective-permute-start(f32[2,2,512]{2,1,0:T(2,128)S(1)} %get-tuple-element.39), channel_id=1, source_target_pairs={{0,48},{8,56},{64,112},{72,120},{128,176},{136,184},{192,240},{200... | collective-permute-start | bytes 24584 | tf_op jit(solution)/shard_map/ppermute | solution.py:220

commit v5 on v3

--- a/solution.py
+++ b/solution.py
@@ -75,17 +75,23 @@
     return dot(block, order).astype(BF16)
 
 
-def selections(faces, select_ref, order_ref):
+def selections(faces, ret, hist, select_ref, order_ref, r0_ref, h1_ref, sems):
+    moves = [(hist.at[hist.shape[0] - 1], h1_ref), (ret.at[0], r0_ref)]
+    copies = [pltpu.make_async_copy(a, b, sems.at[k]) for k, (a, b) in enumerate(moves)]
+    for copy in copies:
+        copy.start()
     select_ref[...] = one_hot_rows(faces[...], select_ref.shape[0])
     order_ref[...] = permutation(order_ref.shape[0])
+    for copy in copies:
+        copy.wait()
 
 
 def own_partials(
-    counts, exc, select, order, hist, ret, inv,
-    d0_ref, d1_ref, up_ref, down_ref, r0_ref,
+    counts, exc, select, order, hist, r0, ret, inv,
+    d0_ref, d1_ref, up_ref, down_ref,
     r1, inv_v, sems,
 ):
-    moves = [(ret.at[0], r0_ref), (ret.at[1], r1), (inv, inv_v)]
+    moves = [(ret.at[1], r1), (inv, inv_v)]
     copies = [pltpu.make_async_copy(a, b, sems.at[k]) for k, (a, b) in enumerate(moves)]
     for copy in copies:
         copy.start()
@@ -100,13 +106,12 @@
         return jnp.where(col == first_col, e[0:1], jnp.where(col == first_col + 1, e[1:2], 0.0))
 
     h0, h1 = permuted(hist[0], order[...]), permuted(hist[1], order[...])
+    p0 = dot(r0[...], h0) * m0
     copies[0].wait()
-    p0 = dot(r0_ref[...], h0) * m0
-    copies[1].wait()
     p0 += dot(r1[...], h1) * m1
     d0 = (placed(0) - p0.T).astype(BF16)
     d0_ref[...] = d0
-    copies[2].wait()
+    copies[1].wait()
     first = dot_t(d0, inv_v[...]).astype(BF16)
     trace = dot(first, select[...]).astype(BF16)
     down_ref[...] = trace[:, :half]
@@ -114,13 +119,14 @@
     d1_ref[...] = placed(1) - (dot(r1[...], h0) * m1).T
 
 
-def pack_partials(counts, order, d0, d1, up, down, r0, before, out):
+def pack_partials(counts, order, d0, d1, up, down, r0, before, hist, out, h0_ref):
+    h0_ref[...] = hist[0]
     n = d0.shape[1]
     half = up.shape[1]
     out[:, :n] = d0[...]
     out[:, n : n + half] = up[...]
     out[:, n + half : n + 2 * half] = down[...]
-    p1 = dot(r0[...], permuted(before[1], order[...])) * live(counts, 0)
+    p1 = dot(r0[...], permuted(before[...], order[...])) * live(counts, 0)
     out[:, n + 2 * half :] = (d1[...] - p1.T).astype(BF16)
 
 
@@ -174,7 +180,7 @@
         share[1] = cur1[2 * i : 2 * i + 2]
 
 
-def finish(gathered, s0, s1, s2, s3, before, cur_ref, hist_ref):
+def finish(gathered, s0, s1, s2, s3, before0, before1, cur_ref, hist_ref):
     zh = lax.axis_index("zh")
     cur_ref[...] = jnp.where(zh < 2, jnp.where(zh == 0, s0[...], s1[...]), jnp.where(zh == 2, s2[...], s3[...]))
     leading = position() == 0
@@ -189,7 +195,8 @@
 
     @pl.when(jnp.logical_not(leading))
     def _():
-        hist_ref[...] = before[...]
+        hist_ref[0] = before0[...]
+        hist_ref[1] = before1[...]
 
 
 def relay(held_at, first_at, held, first, second, after, out, sem):
@@ -250,37 +257,38 @@
     chain = [(i, i + 1) for i in range(devices - 1)]
 
     macs = n * n * width
-    before = permute(history, DELAY, chain)
-    select, order = call(
+    select, order, r0, h1 = call(
         selections,
-        (shape((n, 2 * half), BF16), shape((width, width), BF16)),
-        [VMEM],
-        64 * 1024 * 1024,
-        8 * 1024 * 1024,
-    )(faces)
-    d0, d1, up, down, r0 = call(
+        (shape((n, 2 * half), BF16), shape((width, width), BF16), shape((n, n), BF16), shape((n, width), BF16)),
+        [VMEM] + [any_spec] * 2,
+        0,
+        1024 * 1024,
+        mib=52,
+        scratch_shapes=[pltpu.SemaphoreType.DMA((2,))],
+    )(faces, retarded, history)
+    before1 = permute(h1, DELAY, chain)
+    s1a, s1b = spread(r0, (0, 3)), spread(r0, (0, 5))
+    d0, d1, up, down = call(
         own_partials,
-        (
-            shape((width, n), BF16),
-            shape((width, n), F32),
-            shape((width, half), BF16),
-            shape((width, half), BF16),
-            shape((n, n), BF16),
-        ),
-        [SMEM] + [VMEM] * 4 + [any_spec] * 2,
+        (shape((width, n), BF16), shape((width, n), F32), shape((width, half), BF16), shape((width, half), BF16)),
+        [SMEM] + [VMEM] * 5 + [any_spec] * 2,
         2 * macs * 4,
         2 * 1024 * 1024,
         mib=52,
-        scratch_shapes=[pltpu.VMEM((n, n), BF16), pltpu.VMEM((n, n), BF16), pltpu.SemaphoreType.DMA((3,))],
-    )(counts, exc, select, order, history, retarded, inverse)
+        scratch_shapes=[pltpu.VMEM((n, n), BF16), pltpu.VMEM((n, n), BF16), pltpu.SemaphoreType.DMA((2,))],
+    )(counts, exc, select, order, history, r0, retarded, inverse)
     up = permute(up, "dom", ring)
     down = permute(down, "dom", back)
-    s1a, s1b = spread(r0, (0, 3)), spread(r0, (0, 5))
     lanes = 2 * n + 2 * half
-    packed = call(pack_partials, shape((width, lanes), BF16), [SMEM] + [VMEM] * 7, 2 * macs, 1024 * 1024)(
-        counts, order, d0, d1, up, down, r0, before
-    )
+    packed, h0 = call(
+        pack_partials,
+        (shape((width, lanes), BF16), shape((n, width), BF16)),
+        [SMEM] + [VMEM] * 8,
+        2 * macs,
+        1024 * 1024,
+    )(counts, order, d0, d1, up, down, r0, before1, history)
     x = lax.all_to_all(packed.reshape(OWNERS, cols, lanes), ("y", "c"), 0, 0, tiled=True)
+    before0 = permute(h0, DELAY, chain)
     r0 = relayed((0,), (3,), r0, s1a, s1b, packed)
     s2a, s2b = spread(r0, (0, 1), (3, 2), (5, 6)), spread(r0, (0, 7), (3, 4))
     x = call(sum_parts, shape((cols, lanes), F32), [VMEM], 0, 512 * 1024)(x)
@@ -311,10 +319,10 @@
     currents, new_history = call(
         finish,
         (shape((steps, 2, n), F32), shape(history.shape, BF16)),
-        [VMEM] * 6,
+        [VMEM] * 7,
         0,
         1024 * 1024,
-    )(gather, *share, before)
+    )(gather, *share, before0, before1)
     return jnp.transpose(currents, (0, 2, 1)), new_history
 
 

time: 92.7 us -> 91.7 us (0.989)
  waiting for transfers between devices: 27.2 us -> 21 us
  starting transfers between devices: 54.6 us -> 58.6 us
  Pallas kernels: 6.95 us -> 8.04 us
    ppermute x16 -> x17, starting transfers between devices: 34.8 us -> 41.1 us  [permute(): return lax.ppermute(value, axes, pairs)]
    all_to_all x1, waiting for transfers between devices: 7.05 us -> 0.85 us  [body(): gather = lax.all_to_all(gather, ('y', 'c'), 0, 0, tiled=True)]
    all_to_all x1, starting transfers between devices: 9.39 us -> 7.23 us  [body(): lax.all_to_all(packed.reshape(OWNERS, cols, lanes), ('y', 'c'), 0, 0, til...]
    pallas_call x1, Pallas kernels: 0.07 us -> 1.2 us  [body(): call(selections, (shape((n, 2 * half), BF16), shape((width, width), BF16)...]
    ppermute x16 -> x17, waiting for transfers between devices: 8.57 us -> 8.57 us  [permute(): return lax.ppermute(value, axes, pairs)]
  transfers between devices with their start and end apart: 18 -> 19, of which waited for: 7 -> 7; matrix products, arithmetic and copies ran while one was open for 0% -> 0% of each run, Pallas kernels for 1% -> 4%
where the time goes in v5:
time: 91.7 us; the launch traced here: 90.9 us
  starting transfers between devices  58.6 us (64%)
  waiting for transfers between devices  21 us (23%)
  Pallas kernels  8.04 us (9%)
  local copies, waits for them, and re-layouts  1.64 us (2%)
  between operations  1.59 us (2%)
    ppermute x17, starting transfers between devices, permute(): return lax.ppermute(value, axes, pairs)  41.1 us
    all_to_all x1, waiting for transfers between devices, body(): lax.all_to_all(packed.reshape(OWNERS, cols, lanes), ('y', 'c'), 0, 0, til...  11.6 us
    all_to_all x1, starting transfers between devices, body(): gather = lax.all_to_all(gather, ('y', 'c'), 0, 0, tiled=True)  10.3 us
    ppermute x17, waiting for transfers between devices, permute(): return lax.ppermute(value, axes, pairs)  8.57 us
    all_to_all x1, starting transfers between devices, body(): lax.all_to_all(packed.reshape(OWNERS, cols, lanes), ('y', 'c'), 0, 0, til...  7.23 us
    pallas_call x1, Pallas kernels, body(): call(own_partials, (shape((width, n), BF16), shape((width, n), F32), shap...  2.56 us
  transfers between devices with their start and end apart: 19, of which 7 were waited for; matrix products, arithmetic and copies ran while one was open for 0% of the time, Pallas kernels for 4%

profile of v5, /device:TPU:1, one launch (start us, length us, event | category | flops | bytes accessed | tf_op | source)
XLA Modules:
  0.0 90.9 jit_solution(4314226511806963536)
XLA Ops:
  0.6 0.9 %copy-done.1 = bf16[2,512,128]{2,1,0:T(8,128)(2,1)S(1)} copy-done((bf16[2,512,128]{2,1,0:T(8,128)(2,1)S(1)}, bf16[2,512,128]{2,1,0:T(8,128)(2,1)}, u32[]{:S(2)}) %copy-start.1) | copy-done | bytes 262168
  2.3 1.2 %shard_map.86 = (bf16[512,256]{1,0:T(8,128)(2,1)S(1)}, bf16[128,128]{1,0:T(8,128)(2,1)S(1)}, bf16[512,512]{1,0:T(8,128)(2,1)S(1)}, bf16[512,128]{1,0:T(8,128)(2,1)S(1)}) custom-call(s32[1,256]{1,0:T(1,128)S(1)} %copy-done.5, bf16[2,512,512]{2,1,0:T(8,128)(2,1)} %ret.3, bf16[2,512,128]{2,1,0:T(8,128)(2,1)S(1)} %copy-done.1), custom_call_target="tpu_custom_call" | custom-call | bytes 1048576 | tf_op jit(solution)/shard_map/pallas_call | solution.py:260
  3.5 0.7 collective-permute-start.6
  4.2 0.7 collective-permute-start.7
  4.9 7.2 %collective-permute-start.2 = (bf16[512,128]{1,0:T(8,128)(2,1)S(1)}, bf16[512,128]{1,0:T(8,128)(2,1)S(1)}, u32[]{:S(2)}, u32[]{:S(2)}) collective-permute-start(bf16[512,128]{1,0:T(8,128)(2,1)S(1)} %get-tuple-element.30), channel_id=1, source_target_pairs={{0,8},{8,16},{16,24},{24,32},{32,40},{40,48},{48,56},{56,64},{64,7... | collective-permute-start | bytes 393224 | tf_op jit(solution)/shard_map/ppermute | solution.py:227
  12.8 2.6 %shard_map.87 = (bf16[128,512]{1,0:T(8,128)(2,1)S(1)}, f32[128,512]{1,0:T(8,128)S(1)}, bf16[128,128]{1,0:T(8,128)(2,1)S(1)}, bf16[128,128]{1,0:T(8,128)(2,1)S(1)}) custom-call(s32[1]{0:T(128)S(6)} %copy.9.counts, f32[2,2,512]{2,1,0:T(2,128)S(1)} %bitcast.3, bf16[512,256]{1,0:T(8,128)(2,1)S(1)} %get-tuple-element.24.select, ...), custom_call_target="tpu_custom_call" | custom-call | flops 268435456 | bytes 2097152 | tf_op jit(solution)/shard_map/pallas_call | solution.py:271
  15.3 4.0 %collective-permute-start = (bf16[128,128]{1,0:T(8,128)(2,1)S(1)}, bf16[128,128]{1,0:T(8,128)(2,1)S(1)}, u32[]{:S(2)}, u32[]{:S(2)}) collective-permute-start(bf16[128,128]{1,0:T(8,128)(2,1)S(1)} %get-tuple-element.28), channel_id=1, source_target_pairs={{0,1},{1,2},{2,3},{3,4},{4,5},{5,6},{6,7},{7,0},{8,9},{9,10},{10,1... | collective-permute-start | bytes 98312 | tf_op jit(solution)/shard_map/ppermute | solution.py:227
  19.3 4.1 %collective-permute-start.1 = (bf16[128,128]{1,0:T(8,128)(2,1)S(1)}, bf16[128,128]{1,0:T(8,128)(2,1)S(1)}, u32[]{:S(2)}, u32[]{:S(2)}) collective-permute-start(bf16[128,128]{1,0:T(8,128)(2,1)S(1)} %get-tuple-element.29), channel_id=1, source_target_pairs={{1,0},{2,1},{3,2},{4,3},{5,4},{6,5},{7,6},{0,7},{9,8},{10,9},{11,1... | collective-permute-start | bytes 98312 | tf_op jit(solution)/shard_map/ppermute | solution.py:227
  23.5 1.0 %collective-permute-done.1.down = bf16[128,128]{1,0:T(8,128)(2,1)S(1)} collective-permute-done((bf16[128,128]{1,0:T(8,128)(2,1)S(1)}, bf16[128,128]{1,0:T(8,128)(2,1)S(1)}, u32[]{:S(2)}, u32[]{:S(2)}) %collective-permute-start.1) | collective-permute-done | bytes 32800 | tf_op jit(solution)/shard_map/ppermute | solution.py:227
  24.5 1.3 %shard_map.88 = (bf16[128,1280]{1,0:T(8,128)(2,1)}, bf16[512,128]{1,0:T(8,128)(2,1)S(1)}) custom-call(s32[1]{0:T(128)S(6)} %copy.9.counts, bf16[128,128]{1,0:T(8,128)(2,1)S(1)} %get-tuple-element.23.order, bf16[128,512]{1,0:T(8,128)(2,1)S(1)} %get-tuple-element.26.d0, f32[128,512]{1,0:T(8,128)S(1)} %get-tuple-element.27.d1, ...), custom_call_target="tpu_custom_call" | custom-call | flops 67108864 | bytes 1048576 | tf_op jit(solution)/shard_map/pallas_call | solution.py:283
  25.7 7.2 %all-to-all-start = ((bf16[16,8,1280]{2,1,0:T(8,128)(2,1)}), bf16[16,8,1280]{2,1,0:T(8,128)(2,1)S(1)}, u32[]{:S(2)}, u32[]{:S(2)}) async-start(bf16[16,8,1280]{2,1,0:T(8,128)(2,1)} %bitcast.1), calls=%async_computation | async-start | bytes 655360 | tf_op jit(solution)/shard_map/all_to_all | solution.py:290
  33.1 0.7 collective-permute-start.8
  34.5 11.6 %all-to-all-done.x = bf16[16,8,1280]{2,1,0:T(8,128)(2,1)S(1)} async-done(((bf16[16,8,1280]{2,1,0:T(8,128)(2,1)}), bf16[16,8,1280]{2,1,0:T(8,128)(2,1)S(1)}, u32[]{:S(2)}, u32[]{:S(2)}) %all-to-all-start) | async-done | bytes 327712 | tf_op jit(solution)/shard_map/all_to_all | solution.py:290
  46.2 1.4 %collective-permute-start.10 = (bf16[512,512]{1,0:T(8,128)(2,1)S(1)}, bf16[512,512]{1,0:T(8,128)(2,1)S(1)}, u32[]{:S(2)}, u32[]{:S(2)}) collective-permute-start(bf16[512,512]{1,0:T(8,128)(2,1)S(1)} %shard_map.91.r0_even), channel_id=1, source_target_pairs={{0,8},{64,72},{128,136},{192,200},{256,264},{320,328},{384,392},{4... | collective-permute-start | bytes 1572872 | tf_op jit(solution)/shard_map/ppermute | solution.py:227
  47.6 1.3 %collective-permute-start.3 = (f32[8,1280]{1,0:T(8,128)S(1)}, f32[8,1280]{1,0:T(8,128)S(1)}, u32[]{:S(2)}, u32[]{:S(2)}) collective-permute-start(f32[8,1280]{1,0:T(8,128)S(1)} %shard_map.89.after.x0), channel_id=1, source_target_pairs={{16,0},{17,1},{18,2},{19,3},{20,4},{21,5},{22,6},{23,7},{24,8},{25... | collective-permute-start | bytes 122888 | tf_op jit(solution)/shard_map/ppermute | solution.py:227
  48.9 1.3 %collective-permute-start.4 = (f32[8,1280]{1,0:T(8,128)S(1)}, f32[8,1280]{1,0:T(8,128)S(1)}, u32[]{:S(2)}, u32[]{:S(2)}) collective-permute-start(f32[8,1280]{1,0:T(8,128)S(1)} %shard_map.89.after.x0), channel_id=1, source_target_pairs={{32,0},{33,1},{34,2},{35,3},{36,4},{37,5},{38,6},{39,7},{40,8},{41... | collective-permute-start | bytes 122888 | tf_op jit(solution)/shard_map/ppermute | solution.py:227
  50.2 1.3 %collective-permute-start.5 = (f32[8,1280]{1,0:T(8,128)S(1)}, f32[8,1280]{1,0:T(8,128)S(1)}, u32[]{:S(2)}, u32[]{:S(2)}) collective-permute-start(f32[8,1280]{1,0:T(8,128)S(1)} %shard_map.89.after.x0), channel_id=1, source_target_pairs={{48,0},{49,1},{50,2},{51,3},{52,4},{53,5},{54,6},{55,7},{56,8},{57... | collective-permute-start | bytes 122888 | tf_op jit(solution)/shard_map/ppermute | solution.py:227
  51.5 2.5 %collective-permute-done.3.x1 = f32[8,1280]{1,0:T(8,128)S(1)} collective-permute-done((f32[8,1280]{1,0:T(8,128)S(1)}, f32[8,1280]{1,0:T(8,128)S(1)}, u32[]{:S(2)}, u32[]{:S(2)}) %collective-permute-start.3) | collective-permute-done | bytes 40992 | tf_op jit(solution)/shard_map/ppermute | solution.py:227
  54.1 3.5 %collective-permute-done.4.x2 = f32[8,1280]{1,0:T(8,128)S(1)} collective-permute-done((f32[8,1280]{1,0:T(8,128)S(1)}, f32[8,1280]{1,0:T(8,128)S(1)}, u32[]{:S(2)}, u32[]{:S(2)}) %collective-permute-start.4) | collective-permute-done | bytes 40992 | tf_op jit(solution)/shard_map/ppermute | solution.py:227
  57.7 1.0 %shard_map.92 = (f32[8,512]{1,0:T(8,128)S(1)}, f32[8,512]{1,0:T(8,128)S(1)}, bf16[8,128]{1,0:T(8,128)(2,1)S(1)}, bf16[8,128]{1,0:T(8,128)(2,1)S(1)}) custom-call(s32[1]{0:T(128)S(6)} %copy.9.counts, f32[8,1280]{1,0:T(8,128)S(1)} %shard_map.89.after.x0, f32[8,1280]{1,0:T(8,128)S(1)} %collective-permute-done.3.x1, f32[8,1280]{1,0:T(8,128)S(1)} %collective-permute-done.4.x2, ...), custom_call_target="tpu_custom_call" | custom-call | flops 25165824 | bytes 2097152 | tf_op jit(solution)/shard_map/pallas_call | solution.py:299
  58.7 3.2 %collective-permute-start.11 = (bf16[8,128]{1,0:T(8,128)(2,1)S(1)}, bf16[8,128]{1,0:T(8,128)(2,1)S(1)}, u32[]{:S(2)}, u32[]{:S(2)}) collective-permute-start(bf16[8,128]{1,0:T(8,128)(2,1)S(1)} %get-tuple-element.34), channel_id=1, source_target_pairs={{0,1},{1,2},{2,3},{3,4},{4,5},{5,6},{6,7},{7,0},{8,9},{9,10},{10,1... | collective-permute-start | bytes 6152 | tf_op jit(solution)/shard_map/ppermute | solution.py:227
  61.9 4.4 %collective-permute-start.12 = (bf16[8,128]{1,0:T(8,128)(2,1)S(1)}, bf16[8,128]{1,0:T(8,128)(2,1)S(1)}, u32[]{:S(2)}, u32[]{:S(2)}) collective-permute-start(bf16[8,128]{1,0:T(8,128)(2,1)S(1)} %get-tuple-element.35), channel_id=1, source_target_pairs={{1,0},{2,1},{3,2},{4,3},{5,4},{6,5},{7,6},{0,7},{9,8},{10,9},{11,1... | collective-permute-start | bytes 6152 | tf_op jit(solution)/shard_map/ppermute | solution.py:227
  66.3 0.7 collective-permute-done.12.down
  67.0 1.1 %shard_map.93 = (bf16[16,16,512]{2,1,0:T(8,128)(2,1)}, f32[2,2,512]{2,1,0:T(2,128)S(1)}, f32[2,2,512]{2,1,0:T(2,128)S(1)}, f32[2,2,512]{2,1,0:T(2,128)S(1)}, f32[2,2,512]{2,1,0:T(2,128)S(1)}) custom-call(f32[8,512]{1,0:T(8,128)S(1)} %get-tuple-element.32.cur0, f32[8,512]{1,0:T(8,128)S(1)} %get-tuple-element.33.first, ...), custom_call_target="tpu_custom_call" | custom-call | flops 8388608 | bytes 1048576 | tf_op jit(solution)/shard_map/pallas_call | solution.py:309
  68.1 10.3 %all-to-all-start.1 = ((bf16[16,16,512]{2,1,0:T(8,128)(2,1)}), bf16[16,16,512]{2,1,0:T(8,128)(2,1)S(1)}, u32[]{:S(2)}, u32[]{:S(2)}) async-start(bf16[16,16,512]{2,1,0:T(8,128)(2,1)} %get-tuple-element.36), calls=%async_computation.1 | async-start | bytes 524288 | tf_op jit(solution)/shard_map/all_to_all | solution.py:316
  78.5 1.9 %collective-permute-start.16 = (bf16[512,128]{1,0:T(8,128)(2,1)S(1)}, bf16[512,128]{1,0:T(8,128)(2,1)S(1)}, u32[]{:S(2)}, u32[]{:S(2)}) collective-permute-start(bf16[512,128]{1,0:T(8,128)(2,1)S(1)} %get-tuple-element.41), channel_id=1, source_target_pairs={{0,8},{8,16},{16,24},{24,32},{32,40},{40,48},{48,56},{56,64},{64,7... | collective-permute-start | bytes 393224 | tf_op jit(solution)/shard_map/ppermute | solution.py:227
  80.4 1.3 %collective-permute-start.13 = (f32[2,2,512]{2,1,0:T(2,128)S(1)}, f32[2,2,512]{2,1,0:T(2,128)S(1)}, u32[]{:S(2)}, u32[]{:S(2)}) collective-permute-start(f32[2,2,512]{2,1,0:T(2,128)S(1)} %get-tuple-element.38), channel_id=1, source_target_pairs={{0,16},{8,24},{64,80},{72,88},{128,144},{136,152},{192,208},{200,2... | collective-permute-start | bytes 24584 | tf_op jit(solution)/shard_map/ppermute | solution.py:227
  81.7 1.3 %collective-permute-start.14 = (f32[2,2,512]{2,1,0:T(2,128)S(1)}, f32[2,2,512]{2,1,0:T(2,128)S(1)}, u32[]{:S(2)}, u32[]{:S(2)}) collective-permute-start(f32[2,2,512]{2,1,0:T(2,128)S(1)} %get-tuple-element.39), channel_id=1, source_target_pairs={{0,32},{8,40},{64,96},{72,104},{128,160},{136,168},{192,224},{200,... | collective-permute-start | bytes 24584 | tf_op jit(solution)/shard_map/ppermute | solution.py:227
  83.0 5.6 %collective-permute-start.15 = (f32[2,2,512]{2,1,0:T(2,128)S(1)}, f32[2,2,512]{2,1,0:T(2,128)S(1)}, u32[]{:S(2)}, u32[]{:S(2)}) collective-permute-start(f32[2,2,512]{2,1,0:T(2,128)S(1)} %get-tuple-element.40), channel_id=1, source_target_pairs={{0,48},{8,56},{64,112},{72,120},{128,176},{136,184},{192,240},{200... | collective-permute-start | bytes 24584 | tf_op jit(solution)/shard_map/ppermute | solution.py:227
  88.6 0.7 collective-permute-done.15.s3
  89.3 0.9 all-to-all-done.1.gathered
  90.2 0.7 shard_map.94
  (27 shorter events, 1.6 us)
Async XLA Ops:
  0.6 1.0 %copy-start.1 = (bf16[2,512,128]{2,1,0:T(8,128)(2,1)S(1)}, bf16[2,512,128]{2,1,0:T(8,128)(2,1)}, u32[]{:S(2)}) copy-start(bf16[2,512,128]{2,1,0:T(8,128)(2,1)} %hist.5) | copy-start | bytes 786436
  1.6 0.7 copy-start.5
  2.3 10.5 %copy-start.2 = (bf16[2,512,128]{2,1,0:T(8,128)(2,1)S(1)}, bf16[2,512,128]{2,1,0:T(8,128)(2,1)}, u32[]{:S(2)}) copy-start(bf16[2,512,128]{2,1,0:T(8,128)(2,1)} %hist.5) | copy-start | bytes 786436
  3.5 9.3 %copy-start.4 = (f32[2,512,2]{1,2,0:T(2,128)S(1)}, f32[2,512,2]{1,2,0:T(2,128)}, u32[]{:S(2)}) copy-start(f32[2,512,2]{1,2,0:T(2,128)} %param.7) | copy-start | bytes 24580
  3.5 29.5 %collective-permute-start.6 = (bf16[512,512]{1,0:T(8,128)(2,1)S(1)}, bf16[512,512]{1,0:T(8,128)(2,1)S(1)}, u32[]{:S(2)}, u32[]{:S(2)}) collective-permute-start(bf16[512,512]{1,0:T(8,128)(2,1)S(1)} %get-tuple-element.25.r0.held), channel_id=1, source_target_pairs={{0,192},{1,193},{2,194},{3,195},{4,196},{5,197},{6,198},{7,199}} | collective-permute-start | bytes 1572872 | tf_op jit(solution)/shard_map/ppermute | solution.py:227
  4.2 28.8 %collective-permute-start.7 = (bf16[512,512]{1,0:T(8,128)(2,1)S(1)}, bf16[512,512]{1,0:T(8,128)(2,1)S(1)}, u32[]{:S(2)}, u32[]{:S(2)}) collective-permute-start(bf16[512,512]{1,0:T(8,128)(2,1)S(1)} %get-tuple-element.25.r0.held), channel_id=1, source_target_pairs={{0,320},{1,321},{2,322},{3,323},{4,324},{5,325},{6,326},{7,327}} | collective-permute-start | bytes 1572872 | tf_op jit(solution)/shard_map/ppermute | solution.py:227
  4.9 19.6 %collective-permute-start.2 = (bf16[512,128]{1,0:T(8,128)(2,1)S(1)}, bf16[512,128]{1,0:T(8,128)(2,1)S(1)}, u32[]{:S(2)}, u32[]{:S(2)}) collective-permute-start(bf16[512,128]{1,0:T(8,128)(2,1)S(1)} %get-tuple-element.30), channel_id=1, source_target_pairs={{0,8},{8,16},{16,24},{24,32},{32,40},{40,48},{48,56},{56,64},{64,7... | collective-permute-start | bytes 393224 | tf_op jit(solution)/shard_map/ppermute | solution.py:227
  15.3 8.1 %collective-permute-start = (bf16[128,128]{1,0:T(8,128)(2,1)S(1)}, bf16[128,128]{1,0:T(8,128)(2,1)S(1)}, u32[]{:S(2)}, u32[]{:S(2)}) collective-permute-start(bf16[128,128]{1,0:T(8,128)(2,1)S(1)} %get-tuple-element.28), channel_id=1, source_target_pairs={{0,1},{1,2},{2,3},{3,4},{4,5},{5,6},{6,7},{7,0},{8,9},{9,10},{10,1... | collective-permute-start | bytes 98312 | tf_op jit(solution)/shard_map/ppermute | solution.py:227
  19.3 5.1 %collective-permute-start.1 = (bf16[128,128]{1,0:T(8,128)(2,1)S(1)}, bf16[128,128]{1,0:T(8,128)(2,1)S(1)}, u32[]{:S(2)}, u32[]{:S(2)}) collective-permute-start(bf16[128,128]{1,0:T(8,128)(2,1)S(1)} %get-tuple-element.29), channel_id=1, source_target_pairs={{1,0},{2,1},{3,2},{4,3},{5,4},{6,5},{7,6},{0,7},{9,8},{10,9},{11,1... | collective-permute-start | bytes 98312 | tf_op jit(solution)/shard_map/ppermute | solution.py:227
  25.7 20.3 %all-to-all-start = ((bf16[16,8,1280]{2,1,0:T(8,128)(2,1)}), bf16[16,8,1280]{2,1,0:T(8,128)(2,1)S(1)}, u32[]{:S(2)}, u32[]{:S(2)}) async-start(bf16[16,8,1280]{2,1,0:T(8,128)(2,1)} %bitcast.1), calls=%async_computation | async-start | bytes 655360 | tf_op jit(solution)/shard_map/all_to_all | solution.py:290
  33.1 13.1 %collective-permute-start.8 = (bf16[512,512]{1,0:T(8,128)(2,1)S(1)}, bf16[512,512]{1,0:T(8,128)(2,1)S(1)}, u32[]{:S(2)}, u32[]{:S(2)}) collective-permute-start(bf16[512,512]{1,0:T(8,128)(2,1)S(1)} %shard_map.90.held), channel_id=1, source_target_pairs={{0,64},{192,128},{320,384},{1,65},{193,129},{321,385},{2,66},{194,... | collective-permute-start | bytes 1572872 | tf_op jit(solution)/shard_map/ppermute | solution.py:227
  33.8 12.4 %collective-permute-start.9 = (bf16[512,512]{1,0:T(8,128)(2,1)S(1)}, bf16[512,512]{1,0:T(8,128)(2,1)S(1)}, u32[]{:S(2)}, u32[]{:S(2)}) collective-permute-start(bf16[512,512]{1,0:T(8,128)(2,1)S(1)} %shard_map.90.held), channel_id=1, source_target_pairs={{0,448},{192,256},{1,449},{193,257},{2,450},{194,258},{3,451},{195... | collective-permute-start | bytes 1572872 | tf_op jit(solution)/shard_map/ppermute | solution.py:227
  46.1 11.6 %copy-start = (bf16[512,512]{1,0:T(8,128)(2,1)S(1)}, bf16[512,512]{1,0:T(8,128)(2,1)}, u32[]{:S(2)}) copy-start(bf16[512,512]{1,0:T(8,128)(2,1)} %inv.5) | copy-start | bytes 1572868
  46.1 11.6 %copy-start.3 = (bf16[512,256]{1,0:T(8,128)(2,1)S(1)}, bf16[512,256]{1,0:T(8,128)(2,1)}, u32[]{:S(2)}) copy-start(bf16[512,256]{1,0:T(8,128)(2,1)} %tra.3) | copy-start | bytes 786436
  46.2 11.4 %collective-permute-start.10 = (bf16[512,512]{1,0:T(8,128)(2,1)S(1)}, bf16[512,512]{1,0:T(8,128)(2,1)S(1)}, u32[]{:S(2)}, u32[]{:S(2)}) collective-permute-start(bf16[512,512]{1,0:T(8,128)(2,1)S(1)} %shard_map.91.r0_even), channel_id=1, source_target_pairs={{0,8},{64,72},{128,136},{192,200},{256,264},{320,328},{384,392},{4... | collective-permute-start | bytes 1572872 | tf_op jit(solution)/shard_map/ppermute | solution.py:227
  47.6 6.4 %collective-permute-start.3 = (f32[8,1280]{1,0:T(8,128)S(1)}, f32[8,1280]{1,0:T(8,128)S(1)}, u32[]{:S(2)}, u32[]{:S(2)}) collective-permute-start(f32[8,1280]{1,0:T(8,128)S(1)} %shard_map.89.after.x0), channel_id=1, source_target_pairs={{16,0},{17,1},{18,2},{19,3},{20,4},{21,5},{22,6},{23,7},{24,8},{25... | collective-permute-start | bytes 122888 | tf_op jit(solution)/shard_map/ppermute | solution.py:227
  48.9 8.7 %collective-permute-start.4 = (f32[8,1280]{1,0:T(8,128)S(1)}, f32[8,1280]{1,0:T(8,128)S(1)}, u32[]{:S(2)}, u32[]{:S(2)}) collective-permute-start(f32[8,1280]{1,0:T(8,128)S(1)} %shard_map.89.after.x0), channel_id=1, source_target_pairs={{32,0},{33,1},{34,2},{35,3},{36,4},{37,5},{38,6},{39,7},{40,8},{41... | collective-permute-start | bytes 122888 | tf_op jit(solution)/shard_map/ppermute | solution.py:227
  50.2 7.4 %collective-permute-start.5 = (f32[8,1280]{1,0:T(8,128)S(1)}, f32[8,1280]{1,0:T(8,128)S(1)}, u32[]{:S(2)}, u32[]{:S(2)}) collective-permute-start(f32[8,1280]{1,0:T(8,128)S(1)} %shard_map.89.after.x0), channel_id=1, source_target_pairs={{48,0},{49,1},{50,2},{51,3},{52,4},{53,5},{54,6},{55,7},{56,8},{57... | collective-permute-start | bytes 122888 | tf_op jit(solution)/shard_map/ppermute | solution.py:227
  58.7 7.7 %collective-permute-start.11 = (bf16[8,128]{1,0:T(8,128)(2,1)S(1)}, bf16[8,128]{1,0:T(8,128)(2,1)S(1)}, u32[]{:S(2)}, u32[]{:S(2)}) collective-permute-start(bf16[8,128]{1,0:T(8,128)(2,1)S(1)} %get-tuple-element.34), channel_id=1, source_target_pairs={{0,1},{1,2},{2,3},{3,4},{4,5},{5,6},{6,7},{7,0},{8,9},{9,10},{10,1... | collective-permute-start | bytes 6152 | tf_op jit(solution)/shard_map/ppermute | solution.py:227
  61.9 5.2 %collective-permute-start.12 = (bf16[8,128]{1,0:T(8,128)(2,1)S(1)}, bf16[8,128]{1,0:T(8,128)(2,1)S(1)}, u32[]{:S(2)}, u32[]{:S(2)}) collective-permute-start(bf16[8,128]{1,0:T(8,128)(2,1)S(1)} %get-tuple-element.35), channel_id=1, source_target_pairs={{1,0},{2,1},{3,2},{4,3},{5,4},{6,5},{7,6},{0,7},{9,8},{10,9},{11,1... | collective-permute-start | bytes 6152 | tf_op jit(solution)/shard_map/ppermute | solution.py:227
  68.1 22.0 %all-to-all-start.1 = ((bf16[16,16,512]{2,1,0:T(8,128)(2,1)}), bf16[16,16,512]{2,1,0:T(8,128)(2,1)S(1)}, u32[]{:S(2)}, u32[]{:S(2)}) async-start(bf16[16,16,512]{2,1,0:T(8,128)(2,1)} %get-tuple-element.36), calls=%async_computation.1 | async-start | bytes 524288 | tf_op jit(solution)/shard_map/all_to_all | solution.py:316
  78.5 10.1 %collective-permute-start.16 = (bf16[512,128]{1,0:T(8,128)(2,1)S(1)}, bf16[512,128]{1,0:T(8,128)(2,1)S(1)}, u32[]{:S(2)}, u32[]{:S(2)}) collective-permute-start(bf16[512,128]{1,0:T(8,128)(2,1)S(1)} %get-tuple-element.41), channel_id=1, source_target_pairs={{0,8},{8,16},{16,24},{24,32},{32,40},{40,48},{48,56},{56,64},{64,7... | collective-permute-start | bytes 393224 | tf_op jit(solution)/shard_map/ppermute | solution.py:227
  80.4 8.2 %collective-permute-start.13 = (f32[2,2,512]{2,1,0:T(2,128)S(1)}, f32[2,2,512]{2,1,0:T(2,128)S(1)}, u32[]{:S(2)}, u32[]{:S(2)}) collective-permute-start(f32[2,2,512]{2,1,0:T(2,128)S(1)} %get-tuple-element.38), channel_id=1, source_target_pairs={{0,16},{8,24},{64,80},{72,88},{128,144},{136,152},{192,208},{200,2... | collective-permute-start | bytes 24584 | tf_op jit(solution)/shard_map/ppermute | solution.py:227
  81.7 6.9 %collective-permute-start.14 = (f32[2,2,512]{2,1,0:T(2,128)S(1)}, f32[2,2,512]{2,1,0:T(2,128)S(1)}, u32[]{:S(2)}, u32[]{:S(2)}) collective-permute-start(f32[2,2,512]{2,1,0:T(2,128)S(1)} %get-tuple-element.39), channel_id=1, source_target_pairs={{0,32},{8,40},{64,96},{72,104},{128,160},{136,168},{192,224},{200,... | collective-permute-start | bytes 24584 | tf_op jit(solution)/shard_map/ppermute | solution.py:227
  83.0 6.3 %collective-permute-start.15 = (f32[2,2,512]{2,1,0:T(2,128)S(1)}, f32[2,2,512]{2,1,0:T(2,128)S(1)}, u32[]{:S(2)}, u32[]{:S(2)}) collective-permute-start(f32[2,2,512]{2,1,0:T(2,128)S(1)} %get-tuple-element.40), channel_id=1, source_target_pairs={{0,48},{8,56},{64,112},{72,120},{128,176},{136,184},{192,240},{200... | collective-permute-start | bytes 24584 | tf_op jit(solution)/shard_map/ppermute | solution.py:227

commit v6 on v4

--- a/solution.py
+++ b/solution.py
@@ -75,12 +75,15 @@
     return dot(block, order).astype(BF16)
 
 
-def selections(faces, ret, select_ref, order_ref, r0_ref, sem):
-    copy = pltpu.make_async_copy(ret.at[0], r0_ref, sem)
-    copy.start()
+def selections(faces, ret, hist, select_ref, order_ref, r0_ref, h1_ref, sems):
+    moves = [(hist.at[hist.shape[0] - 1], h1_ref), (ret.at[0], r0_ref)]
+    copies = [pltpu.make_async_copy(a, b, sems.at[k]) for k, (a, b) in enumerate(moves)]
+    for copy in copies:
+        copy.start()
     select_ref[...] = one_hot_rows(faces[...], select_ref.shape[0])
     order_ref[...] = permutation(order_ref.shape[0])
-    copy.wait()
+    for copy in copies:
+        copy.wait()
 
 
 def own_partials(counts, exc, order, hist, r0, ret, d0_ref, d1_ref, r1, sem):
@@ -103,10 +106,11 @@
     d1_ref[...] = placed(1) - (dot(r1[...], h0) * m1).T
 
 
-def pack_partials(counts, order, d0, d1, r0, before, out):
+def pack_partials(counts, order, d0, d1, r0, before, hist, out, h0_ref):
+    h0_ref[...] = hist[0]
     n = d0.shape[1]
     out[:, :n] = d0[...]
-    p1 = dot(r0[...], permuted(before[1], order[...])) * live(counts, 0)
+    p1 = dot(r0[...], permuted(before[...], order[...])) * live(counts, 0)
     out[:, n:] = (d1[...] - p1.T).astype(BF16)
 
 
@@ -174,7 +178,7 @@
         share[1] = cur1[2 * i : 2 * i + 2]
 
 
-def finish(gathered, s0, s1, s2, s3, before, cur_ref, hist_ref):
+def finish(gathered, s0, s1, s2, s3, before0, before1, cur_ref, hist_ref):
     zh = lax.axis_index("zh")
     cur_ref[...] = jnp.where(zh < 2, jnp.where(zh == 0, s0[...], s1[...]), jnp.where(zh == 2, s2[...], s3[...]))
     leading = position() == 0
@@ -189,7 +193,8 @@
 
     @pl.when(jnp.logical_not(leading))
     def _():
-        hist_ref[...] = before[...]
+        hist_ref[0] = before0[...]
+        hist_ref[1] = before1[...]
 
 
 def relay(held_at, first_at, held, first, second, after, out, sem):
@@ -250,16 +255,16 @@
     chain = [(i, i + 1) for i in range(devices - 1)]
 
     macs = n * n * width
-    before = permute(history, DELAY, chain)
-    select, order, r0 = call(
+    select, order, r0, h1 = call(
         selections,
-        (shape((n, 2 * half), BF16), shape((width, width), BF16), shape((n, n), BF16)),
-        [VMEM, any_spec],
+        (shape((n, 2 * half), BF16), shape((width, width), BF16), shape((n, n), BF16), shape((n, width), BF16)),
+        [VMEM] + [any_spec] * 2,
         0,
         1024 * 1024,
-        mib=53,
-        scratch_shapes=[pltpu.SemaphoreType.DMA],
-    )(faces, retarded)
+        mib=52,
+        scratch_shapes=[pltpu.SemaphoreType.DMA((2,))],
+    )(faces, retarded, history)
+    before1 = permute(h1, DELAY, chain)
     d0, d1 = call(
         own_partials,
         (shape((width, n), BF16), shape((width, n), F32)),
@@ -271,16 +276,19 @@
     )(counts, exc, order, history, r0, retarded)
     s1a, s1b = spread(r0, (0, 3)), spread(r0, (0, 5))
     lanes = 2 * n
-    packed = call(pack_partials, shape((width, lanes), BF16), [SMEM] + [VMEM] * 5, 2 * macs, 1024 * 1024)(
-        counts, order, d0, d1, r0, before
-    )
+    packed, h0 = call(
+        pack_partials,
+        (shape((width, lanes), BF16), shape((n, width), BF16)),
+        [SMEM] + [VMEM] * 6,
+        2 * macs,
+        1024 * 1024,
+    )(counts, order, d0, d1, r0, before1, history)
+    before0 = permute(h0, DELAY, chain)
     x = lax.all_to_all(packed.reshape(OWNERS, cols, lanes), ("y", "c"), 0, 0, tiled=True)
     r0 = relayed((0,), (3,), r0, s1a, s1b, packed)
     s2a, s2b = spread(r0, (0, 1), (3, 2), (5, 6)), spread(r0, (0, 7), (3, 4))
     x = call(sum_parts, shape((cols, lanes), F32), [VMEM], 0, 512 * 1024)(x)
     xs = [x] + [permute(x, "zh", [(z, 0)]) for z in range(1, ZH)]
-    r0 = relayed((0, 3, 5), (1, 2, 6), r0, s2a, s2b, xs[1])
-    s3 = permute(r0, DELAY, [(at(i, 0, 0), at(i, 0, 1)) for i in range(Y)])
 
     def halo(up, down):
         return permute(up, ("zh", "dom"), ring), permute(down, ("zh", "dom"), back)
@@ -293,6 +301,8 @@
         2 * 8 * n * n * 2,
         1024 * 1024,
     )(*xs, inverse, select)
+    r0 = relayed((0, 3, 5), (1, 2, 6), r0, s2a, s2b, rest)
+    s3 = permute(r0, DELAY, [(at(i, 0, 0), at(i, 0, 1)) for i in range(Y)])
     up, down = halo(up, down)
     cur0, first, up, down = call(
         next_first,
@@ -316,10 +326,10 @@
     currents, new_history = call(
         finish,
         (shape((steps, 2, n), F32), shape(history.shape, BF16)),
-        [VMEM] * 6,
+        [VMEM] * 7,
         0,
         1024 * 1024,
-    )(gather, *share, before)
+    )(gather, *share, before0, before1)
     return jnp.transpose(currents, (0, 2, 1)), new_history
 
 

time: 98.9 us -> 91.7 us (0.927)
  waiting for transfers between devices: 31.2 us -> 20.6 us
  starting transfers between devices: 57.3 us -> 59.5 us
    all_to_all x1, waiting for transfers between devices: 7.2 us -> 1 us  [body(): gather = lax.all_to_all(gather, ('y', 'c'), 0, 0, tiled=True)]
    ppermute x16 -> x17, starting transfers between devices: 34.2 us -> 40.4 us  [permute(): return lax.ppermute(value, axes, pairs)]
    ppermute x16 -> x17, waiting for transfers between devices: 13.7 us -> 9.48 us  [permute(): return lax.ppermute(value, axes, pairs)]
    all_to_all x1, starting transfers between devices: 15.2 us -> 12.4 us  [body(): lax.all_to_all(packed.reshape(OWNERS, cols, lanes), ('y', 'c'), 0, 0, til...]
    all_to_all x1, starting transfers between devices: 7.9 us -> 6.76 us  [body(): gather = lax.all_to_all(gather, ('y', 'c'), 0, 0, tiled=True)]
  transfers between devices with their start and end apart: 18 -> 19, of which waited for: 8 -> 8; matrix products, arithmetic and copies ran while one was open for 0% -> 0% of each run, Pallas kernels for 4% -> 4%
where the time goes in v6:
time: 91.7 us; the launch traced here: 90.9 us
  starting transfers between devices  59.5 us (65%)
  waiting for transfers between devices  20.6 us (22%)
  Pallas kernels  7.64 us (8%)
  local copies, waits for them, and re-layouts  1.64 us (2%)
  between operations  1.57 us (2%)
    ppermute x17, starting transfers between devices, permute(): return lax.ppermute(value, axes, pairs)  40.4 us
    all_to_all x1, starting transfers between devices, body(): lax.all_to_all(packed.reshape(OWNERS, cols, lanes), ('y', 'c'), 0, 0, til...  12.4 us
    all_to_all x1, waiting for transfers between devices, body(): lax.all_to_all(packed.reshape(OWNERS, cols, lanes), ('y', 'c'), 0, 0, til...  10.1 us
    ppermute x17, waiting for transfers between devices, permute(): return lax.ppermute(value, axes, pairs)  9.48 us
    all_to_all x1, starting transfers between devices, body(): gather = lax.all_to_all(gather, ('y', 'c'), 0, 0, tiled=True)  6.76 us
    pallas_call x1, Pallas kernels, body(): call(own_partials, (shape((width, n), BF16), shape((width, n), F32)), [SM...  1.94 us
  transfers between devices with their start and end apart: 19, of which 8 were waited for; matrix products, arithmetic and copies ran while one was open for 0% of the time, Pallas kernels for 4%

profile of v6, /device:TPU:1, one launch (start us, length us, event | category | flops | bytes accessed | tf_op | source)
XLA Modules:
  0.0 90.9 jit_solution(12453961773431433754)
XLA Ops:
  0.6 0.9 %copy-done.1 = bf16[2,512,128]{2,1,0:T(8,128)(2,1)S(1)} copy-done((bf16[2,512,128]{2,1,0:T(8,128)(2,1)S(1)}, bf16[2,512,128]{2,1,0:T(8,128)(2,1)}, u32[]{:S(2)}) %copy-start.1) | copy-done | bytes 262168
  2.3 1.2 %shard_map.86 = (bf16[512,256]{1,0:T(8,128)(2,1)S(1)}, bf16[128,128]{1,0:T(8,128)(2,1)S(1)}, bf16[512,512]{1,0:T(8,128)(2,1)S(1)}, bf16[512,128]{1,0:T(8,128)(2,1)S(1)}) custom-call(s32[1,256]{1,0:T(1,128)S(1)} %copy-done.5, bf16[2,512,512]{2,1,0:T(8,128)(2,1)} %ret.3, bf16[2,512,128]{2,1,0:T(8,128)(2,1)S(1)} %copy-done.1), custom_call_target="tpu_custom_call" | custom-call | bytes 1048576 | tf_op jit(solution)/shard_map/pallas_call | solution.py:258
  3.5 0.7 collective-permute-start.7
  4.9 7.2 %collective-permute-start = (bf16[512,128]{1,0:T(8,128)(2,1)S(1)}, bf16[512,128]{1,0:T(8,128)(2,1)S(1)}, u32[]{:S(2)}, u32[]{:S(2)}) collective-permute-start(bf16[512,128]{1,0:T(8,128)(2,1)S(1)} %get-tuple-element.29), channel_id=1, source_target_pairs={{0,8},{8,16},{16,24},{24,32},{32,40},{40,48},{48,56},{56,64},{64,7... | collective-permute-start | bytes 393224 | tf_op jit(solution)/shard_map/ppermute | solution.py:225
  12.8 1.9 %shard_map.87 = (bf16[128,512]{1,0:T(8,128)(2,1)S(1)}, f32[128,512]{1,0:T(8,128)S(1)}) custom-call(s32[1]{0:T(128)S(6)} %copy.9.counts, f32[2,2,512]{2,1,0:T(2,128)S(1)} %bitcast.3, bf16[128,128]{1,0:T(8,128)(2,1)S(1)} %get-tuple-element.25.order, bf16[2,512,128]{2,1,0:T(8,128)(2,1)S(1)} %copy-done.2, bf16[512,512]{1,0:T(8,128)(2,1)S(1)} %get-tuple-element.26.r0.held, ...), custom_call_target="tpu_custom_call" | custom-call | flops 268435456 | bytes 2097152 | tf_op jit(solution)/shard_map/pallas_call | solution.py:268
  14.7 0.7 collective-permute-done.before.before1
  15.4 1.2 %shard_map.88 = (bf16[128,1024]{1,0:T(8,128)(2,1)}, bf16[512,128]{1,0:T(8,128)(2,1)S(1)}) custom-call(s32[1]{0:T(128)S(6)} %copy.9.counts, bf16[128,128]{1,0:T(8,128)(2,1)S(1)} %get-tuple-element.25.order, bf16[128,512]{1,0:T(8,128)(2,1)S(1)} %get-tuple-element.27.d0, f32[128,512]{1,0:T(8,128)S(1)} %get-tuple-element.28.d1, ...), custom_call_target="tpu_custom_call" | custom-call | flops 67108864 | bytes 1048576 | tf_op jit(solution)/shard_map/pallas_call | solution.py:279
  16.7 12.4 %all-to-all-start = ((bf16[16,8,1024]{2,1,0:T(8,128)(2,1)}), bf16[16,8,1024]{2,1,0:T(8,128)(2,1)S(1)}, u32[]{:S(2)}, u32[]{:S(2)}) async-start(bf16[16,8,1024]{2,1,0:T(8,128)(2,1)} %bitcast.1), calls=%async_computation | async-start | bytes 524288 | tf_op jit(solution)/shard_map/all_to_all | solution.py:287
  29.2 0.8 collective-permute-start.9
  30.7 10.1 %all-to-all-done.x = bf16[16,8,1024]{2,1,0:T(8,128)(2,1)S(1)} async-done(((bf16[16,8,1024]{2,1,0:T(8,128)(2,1)}), bf16[16,8,1024]{2,1,0:T(8,128)(2,1)S(1)}, u32[]{:S(2)}, u32[]{:S(2)}) %all-to-all-start) | async-done | bytes 262176 | tf_op jit(solution)/shard_map/all_to_all | solution.py:287
  40.8 1.3 %collective-permute-start.3 = (f32[8,1024]{1,0:T(8,128)S(1)}, f32[8,1024]{1,0:T(8,128)S(1)}, u32[]{:S(2)}, u32[]{:S(2)}) collective-permute-start(f32[8,1024]{1,0:T(8,128)S(1)} %shard_map.89.x0), channel_id=1, source_target_pairs={{48,0},{49,1},{50,2},{51,3},{52,4},{53,5},{54,6},{55,7},{56,8},{57... | collective-permute-start | bytes 98312 | tf_op jit(solution)/shard_map/ppermute | solution.py:225
  42.1 1.3 %collective-permute-start.2 = (f32[8,1024]{1,0:T(8,128)S(1)}, f32[8,1024]{1,0:T(8,128)S(1)}, u32[]{:S(2)}, u32[]{:S(2)}) collective-permute-start(f32[8,1024]{1,0:T(8,128)S(1)} %shard_map.89.x0), channel_id=1, source_target_pairs={{32,0},{33,1},{34,2},{35,3},{36,4},{37,5},{38,6},{39,7},{40,8},{41... | collective-permute-start | bytes 98312 | tf_op jit(solution)/shard_map/ppermute | solution.py:225
  43.4 1.3 %collective-permute-start.1 = (f32[8,1024]{1,0:T(8,128)S(1)}, f32[8,1024]{1,0:T(8,128)S(1)}, u32[]{:S(2)}, u32[]{:S(2)}) collective-permute-start(f32[8,1024]{1,0:T(8,128)S(1)} %shard_map.89.x0), channel_id=1, source_target_pairs={{16,0},{17,1},{18,2},{19,3},{20,4},{21,5},{22,6},{23,7},{24,8},{25... | collective-permute-start | bytes 98312 | tf_op jit(solution)/shard_map/ppermute | solution.py:225
  44.7 3.5 %collective-permute-done.3.x3 = f32[8,1024]{1,0:T(8,128)S(1)} collective-permute-done((f32[8,1024]{1,0:T(8,128)S(1)}, f32[8,1024]{1,0:T(8,128)S(1)}, u32[]{:S(2)}, u32[]{:S(2)}) %collective-permute-start.3) | collective-permute-done | bytes 32800 | tf_op jit(solution)/shard_map/ppermute | solution.py:225
  48.2 3.1 %collective-permute-done.2.x2 = f32[8,1024]{1,0:T(8,128)S(1)} collective-permute-done((f32[8,1024]{1,0:T(8,128)S(1)}, f32[8,1024]{1,0:T(8,128)S(1)}, u32[]{:S(2)}, u32[]{:S(2)}) %collective-permute-start.2) | collective-permute-done | bytes 32800 | tf_op jit(solution)/shard_map/ppermute | solution.py:225
  51.8 1.3 %collective-permute-start.10 = (bf16[512,512]{1,0:T(8,128)(2,1)S(1)}, bf16[512,512]{1,0:T(8,128)(2,1)S(1)}, u32[]{:S(2)}, u32[]{:S(2)}) collective-permute-start(bf16[512,512]{1,0:T(8,128)(2,1)S(1)} %shard_map.92.r0_even), channel_id=1, source_target_pairs={{0,8},{64,72},{128,136},{192,200},{256,264},{320,328},{384,392},{4... | collective-permute-start | bytes 1572872 | tf_op jit(solution)/shard_map/ppermute | solution.py:225
  53.1 3.2 %collective-permute-start.4 = (bf16[8,128]{1,0:T(8,128)(2,1)S(1)}, bf16[8,128]{1,0:T(8,128)(2,1)S(1)}, u32[]{:S(2)}, u32[]{:S(2)}) collective-permute-start(bf16[8,128]{1,0:T(8,128)(2,1)S(1)} %get-tuple-element.34), channel_id=1, source_target_pairs={{0,1},{1,2},{2,3},{3,4},{4,5},{5,6},{6,7},{7,0},{8,9},{9,10},{10,1... | collective-permute-start | bytes 6152 | tf_op jit(solution)/shard_map/ppermute | solution.py:225
  56.3 4.2 %collective-permute-start.5 = (bf16[8,128]{1,0:T(8,128)(2,1)S(1)}, bf16[8,128]{1,0:T(8,128)(2,1)S(1)}, u32[]{:S(2)}, u32[]{:S(2)}) collective-permute-start(bf16[8,128]{1,0:T(8,128)(2,1)S(1)} %get-tuple-element.35), channel_id=1, source_target_pairs={{1,0},{2,1},{3,2},{4,3},{5,4},{6,5},{7,6},{0,7},{9,8},{10,9},{11,1... | collective-permute-start | bytes 6152 | tf_op jit(solution)/shard_map/ppermute | solution.py:225
  60.5 0.7 collective-permute-done.5.down
  61.2 0.9 shard_map.93
  62.1 3.3 %collective-permute-start.11 = (bf16[8,128]{1,0:T(8,128)(2,1)S(1)}, bf16[8,128]{1,0:T(8,128)(2,1)S(1)}, u32[]{:S(2)}, u32[]{:S(2)}) collective-permute-start(bf16[8,128]{1,0:T(8,128)(2,1)S(1)} %get-tuple-element.38), channel_id=1, source_target_pairs={{0,1},{1,2},{2,3},{3,4},{4,5},{5,6},{6,7},{7,0},{8,9},{9,10},{10,1... | collective-permute-start | bytes 6152 | tf_op jit(solution)/shard_map/ppermute | solution.py:225
  65.5 4.3 %collective-permute-start.12 = (bf16[8,128]{1,0:T(8,128)(2,1)S(1)}, bf16[8,128]{1,0:T(8,128)(2,1)S(1)}, u32[]{:S(2)}, u32[]{:S(2)}) collective-permute-start(bf16[8,128]{1,0:T(8,128)(2,1)S(1)} %get-tuple-element.39), channel_id=1, source_target_pairs={{1,0},{2,1},{3,2},{4,3},{5,4},{6,5},{7,6},{0,7},{9,8},{10,9},{11,1... | collective-permute-start | bytes 6152 | tf_op jit(solution)/shard_map/ppermute | solution.py:225
  69.8 0.7 collective-permute-done.12.down
  70.5 1.1 %shard_map.94 = (bf16[16,16,512]{2,1,0:T(8,128)(2,1)}, f32[2,2,512]{2,1,0:T(2,128)S(1)}, f32[2,2,512]{2,1,0:T(2,128)S(1)}, f32[2,2,512]{2,1,0:T(2,128)S(1)}, f32[2,2,512]{2,1,0:T(2,128)S(1)}) custom-call(f32[8,512]{1,0:T(8,128)S(1)} %get-tuple-element.36.cur0, f32[8,512]{1,0:T(8,128)S(1)} %get-tuple-element.37.first, ...), custom_call_target="tpu_custom_call" | custom-call | flops 8388608 | bytes 1048576 | tf_op jit(solution)/shard_map/pallas_call | solution.py:316
  71.6 6.8 %all-to-all-start.1 = ((bf16[16,16,512]{2,1,0:T(8,128)(2,1)}), bf16[16,16,512]{2,1,0:T(8,128)(2,1)S(1)}, u32[]{:S(2)}, u32[]{:S(2)}) async-start(bf16[16,16,512]{2,1,0:T(8,128)(2,1)} %get-tuple-element.40), calls=%async_computation.1 | async-start | bytes 524288 | tf_op jit(solution)/shard_map/all_to_all | solution.py:323
  78.3 1.9 %collective-permute-start.16 = (bf16[512,128]{1,0:T(8,128)(2,1)S(1)}, bf16[512,128]{1,0:T(8,128)(2,1)S(1)}, u32[]{:S(2)}, u32[]{:S(2)}) collective-permute-start(bf16[512,128]{1,0:T(8,128)(2,1)S(1)} %get-tuple-element.45), channel_id=1, source_target_pairs={{0,8},{8,16},{16,24},{24,32},{32,40},{40,48},{48,56},{56,64},{64,7... | collective-permute-start | bytes 393224 | tf_op jit(solution)/shard_map/ppermute | solution.py:225
  80.3 1.3 %collective-permute-start.13 = (f32[2,2,512]{2,1,0:T(2,128)S(1)}, f32[2,2,512]{2,1,0:T(2,128)S(1)}, u32[]{:S(2)}, u32[]{:S(2)}) collective-permute-start(f32[2,2,512]{2,1,0:T(2,128)S(1)} %get-tuple-element.42), channel_id=1, source_target_pairs={{0,16},{8,24},{64,80},{72,88},{128,144},{136,152},{192,208},{200,2... | collective-permute-start | bytes 24584 | tf_op jit(solution)/shard_map/ppermute | solution.py:225
  81.6 1.3 %collective-permute-start.14 = (f32[2,2,512]{2,1,0:T(2,128)S(1)}, f32[2,2,512]{2,1,0:T(2,128)S(1)}, u32[]{:S(2)}, u32[]{:S(2)}) collective-permute-start(f32[2,2,512]{2,1,0:T(2,128)S(1)} %get-tuple-element.43), channel_id=1, source_target_pairs={{0,32},{8,40},{64,96},{72,104},{128,160},{136,168},{192,224},{200,... | collective-permute-start | bytes 24584 | tf_op jit(solution)/shard_map/ppermute | solution.py:225
  82.9 5.6 %collective-permute-start.15 = (f32[2,2,512]{2,1,0:T(2,128)S(1)}, f32[2,2,512]{2,1,0:T(2,128)S(1)}, u32[]{:S(2)}, u32[]{:S(2)}) collective-permute-start(f32[2,2,512]{2,1,0:T(2,128)S(1)} %get-tuple-element.44), channel_id=1, source_target_pairs={{0,48},{8,56},{64,112},{72,120},{128,176},{136,184},{192,240},{200... | collective-permute-start | bytes 24584 | tf_op jit(solution)/shard_map/ppermute | solution.py:225
  88.5 0.7 collective-permute-done.15.s3
  89.2 1.0 %all-to-all-done.1.gathered = bf16[16,16,512]{2,1,0:T(8,128)(2,1)S(1)} async-done(((bf16[16,16,512]{2,1,0:T(8,128)(2,1)}), bf16[16,16,512]{2,1,0:T(8,128)(2,1)S(1)}, u32[]{:S(2)}, u32[]{:S(2)}) %all-to-all-start.1) | async-done | bytes 262176 | tf_op jit(solution)/shard_map/all_to_all | solution.py:323
  90.2 0.7 shard_map.95
  (28 shorter events, 2.7 us)
Async XLA Ops:
  0.6 1.0 %copy-start.1 = (bf16[2,512,128]{2,1,0:T(8,128)(2,1)S(1)}, bf16[2,512,128]{2,1,0:T(8,128)(2,1)}, u32[]{:S(2)}) copy-start(bf16[2,512,128]{2,1,0:T(8,128)(2,1)} %hist.5) | copy-start | bytes 786436
  1.6 0.7 copy-start.5
  2.3 10.5 %copy-start.2 = (bf16[2,512,128]{2,1,0:T(8,128)(2,1)S(1)}, bf16[2,512,128]{2,1,0:T(8,128)(2,1)}, u32[]{:S(2)}) copy-start(bf16[2,512,128]{2,1,0:T(8,128)(2,1)} %hist.5) | copy-start | bytes 786436
  3.5 9.3 %copy-start.4 = (f32[2,512,2]{1,2,0:T(2,128)S(1)}, f32[2,512,2]{1,2,0:T(2,128)}, u32[]{:S(2)}) copy-start(f32[2,512,2]{1,2,0:T(2,128)} %param.7) | copy-start | bytes 24580
  3.5 25.6 %collective-permute-start.7 = (bf16[512,512]{1,0:T(8,128)(2,1)S(1)}, bf16[512,512]{1,0:T(8,128)(2,1)S(1)}, u32[]{:S(2)}, u32[]{:S(2)}) collective-permute-start(bf16[512,512]{1,0:T(8,128)(2,1)S(1)} %get-tuple-element.26.r0.held), channel_id=1, source_target_pairs={{0,320},{1,321},{2,322},{3,323},{4,324},{5,325},{6,326},{7,327}} | collective-permute-start | bytes 1572872 | tf_op jit(solution)/shard_map/ppermute | solution.py:225
  4.2 24.9 %collective-permute-start.6 = (bf16[512,512]{1,0:T(8,128)(2,1)S(1)}, bf16[512,512]{1,0:T(8,128)(2,1)S(1)}, u32[]{:S(2)}, u32[]{:S(2)}) collective-permute-start(bf16[512,512]{1,0:T(8,128)(2,1)S(1)} %get-tuple-element.26.r0.held), channel_id=1, source_target_pairs={{0,192},{1,193},{2,194},{3,195},{4,196},{5,197},{6,198},{7,199}} | collective-permute-start | bytes 1572872 | tf_op jit(solution)/shard_map/ppermute | solution.py:225
  4.9 10.5 %collective-permute-start = (bf16[512,128]{1,0:T(8,128)(2,1)S(1)}, bf16[512,128]{1,0:T(8,128)(2,1)S(1)}, u32[]{:S(2)}, u32[]{:S(2)}) collective-permute-start(bf16[512,128]{1,0:T(8,128)(2,1)S(1)} %get-tuple-element.29), channel_id=1, source_target_pairs={{0,8},{8,16},{16,24},{24,32},{32,40},{40,48},{48,56},{56,64},{64,7... | collective-permute-start | bytes 393224 | tf_op jit(solution)/shard_map/ppermute | solution.py:225
  16.7 24.1 %all-to-all-start = ((bf16[16,8,1024]{2,1,0:T(8,128)(2,1)}), bf16[16,8,1024]{2,1,0:T(8,128)(2,1)S(1)}, u32[]{:S(2)}, u32[]{:S(2)}) async-start(bf16[16,8,1024]{2,1,0:T(8,128)(2,1)} %bitcast.1), calls=%async_computation | async-start | bytes 524288 | tf_op jit(solution)/shard_map/all_to_all | solution.py:287
  29.1 22.2 %copy-start = (bf16[512,512]{1,0:T(8,128)(2,1)S(1)}, bf16[512,512]{1,0:T(8,128)(2,1)}, u32[]{:S(2)}) copy-start(bf16[512,512]{1,0:T(8,128)(2,1)} %inv.5) | copy-start | bytes 1572868
  29.2 22.5 %collective-permute-start.9 = (bf16[512,512]{1,0:T(8,128)(2,1)S(1)}, bf16[512,512]{1,0:T(8,128)(2,1)S(1)}, u32[]{:S(2)}, u32[]{:S(2)}) collective-permute-start(bf16[512,512]{1,0:T(8,128)(2,1)S(1)} %shard_map.91.held), channel_id=1, source_target_pairs={{0,448},{192,256},{1,449},{193,257},{2,450},{194,258},{3,451},{195... | collective-permute-start | bytes 1572872 | tf_op jit(solution)/shard_map/ppermute | solution.py:225
  30.0 21.7 %collective-permute-start.8 = (bf16[512,512]{1,0:T(8,128)(2,1)S(1)}, bf16[512,512]{1,0:T(8,128)(2,1)S(1)}, u32[]{:S(2)}, u32[]{:S(2)}) collective-permute-start(bf16[512,512]{1,0:T(8,128)(2,1)S(1)} %shard_map.91.held), channel_id=1, source_target_pairs={{0,64},{192,128},{320,384},{1,65},{193,129},{321,385},{2,66},{194,... | collective-permute-start | bytes 1572872 | tf_op jit(solution)/shard_map/ppermute | solution.py:225
  40.8 7.4 %collective-permute-start.3 = (f32[8,1024]{1,0:T(8,128)S(1)}, f32[8,1024]{1,0:T(8,128)S(1)}, u32[]{:S(2)}, u32[]{:S(2)}) collective-permute-start(f32[8,1024]{1,0:T(8,128)S(1)} %shard_map.89.x0), channel_id=1, source_target_pairs={{48,0},{49,1},{50,2},{51,3},{52,4},{53,5},{54,6},{55,7},{56,8},{57... | collective-permute-start | bytes 98312 | tf_op jit(solution)/shard_map/ppermute | solution.py:225
  42.1 9.2 %collective-permute-start.2 = (f32[8,1024]{1,0:T(8,128)S(1)}, f32[8,1024]{1,0:T(8,128)S(1)}, u32[]{:S(2)}, u32[]{:S(2)}) collective-permute-start(f32[8,1024]{1,0:T(8,128)S(1)} %shard_map.89.x0), channel_id=1, source_target_pairs={{32,0},{33,1},{34,2},{35,3},{36,4},{37,5},{38,6},{39,7},{40,8},{41... | collective-permute-start | bytes 98312 | tf_op jit(solution)/shard_map/ppermute | solution.py:225
  43.4 7.9 %collective-permute-start.1 = (f32[8,1024]{1,0:T(8,128)S(1)}, f32[8,1024]{1,0:T(8,128)S(1)}, u32[]{:S(2)}, u32[]{:S(2)}) collective-permute-start(f32[8,1024]{1,0:T(8,128)S(1)} %shard_map.89.x0), channel_id=1, source_target_pairs={{16,0},{17,1},{18,2},{19,3},{20,4},{21,5},{22,6},{23,7},{24,8},{25... | collective-permute-start | bytes 98312 | tf_op jit(solution)/shard_map/ppermute | solution.py:225
  51.7 9.5 %copy-start.3 = (bf16[512,256]{1,0:T(8,128)(2,1)S(1)}, bf16[512,256]{1,0:T(8,128)(2,1)}, u32[]{:S(2)}) copy-start(bf16[512,256]{1,0:T(8,128)(2,1)} %tra.3) | copy-start | bytes 786436
  51.8 9.4 %collective-permute-start.10 = (bf16[512,512]{1,0:T(8,128)(2,1)S(1)}, bf16[512,512]{1,0:T(8,128)(2,1)S(1)}, u32[]{:S(2)}, u32[]{:S(2)}) collective-permute-start(bf16[512,512]{1,0:T(8,128)(2,1)S(1)} %shard_map.92.r0_even), channel_id=1, source_target_pairs={{0,8},{64,72},{128,136},{192,200},{256,264},{320,328},{384,392},{4... | collective-permute-start | bytes 1572872 | tf_op jit(solution)/shard_map/ppermute | solution.py:225
  53.1 7.4 %collective-permute-start.4 = (bf16[8,128]{1,0:T(8,128)(2,1)S(1)}, bf16[8,128]{1,0:T(8,128)(2,1)S(1)}, u32[]{:S(2)}, u32[]{:S(2)}) collective-permute-start(bf16[8,128]{1,0:T(8,128)(2,1)S(1)} %get-tuple-element.34), channel_id=1, source_target_pairs={{0,1},{1,2},{2,3},{3,4},{4,5},{5,6},{6,7},{7,0},{8,9},{9,10},{10,1... | collective-permute-start | bytes 6152 | tf_op jit(solution)/shard_map/ppermute | solution.py:225
  56.3 4.9 %collective-permute-start.5 = (bf16[8,128]{1,0:T(8,128)(2,1)S(1)}, bf16[8,128]{1,0:T(8,128)(2,1)S(1)}, u32[]{:S(2)}, u32[]{:S(2)}) collective-permute-start(bf16[8,128]{1,0:T(8,128)(2,1)S(1)} %get-tuple-element.35), channel_id=1, source_target_pairs={{1,0},{2,1},{3,2},{4,3},{5,4},{6,5},{7,6},{0,7},{9,8},{10,9},{11,1... | collective-permute-start | bytes 6152 | tf_op jit(solution)/shard_map/ppermute | solution.py:225
  62.1 7.7 %collective-permute-start.11 = (bf16[8,128]{1,0:T(8,128)(2,1)S(1)}, bf16[8,128]{1,0:T(8,128)(2,1)S(1)}, u32[]{:S(2)}, u32[]{:S(2)}) collective-permute-start(bf16[8,128]{1,0:T(8,128)(2,1)S(1)} %get-tuple-element.38), channel_id=1, source_target_pairs={{0,1},{1,2},{2,3},{3,4},{4,5},{5,6},{6,7},{7,0},{8,9},{9,10},{10,1... | collective-permute-start | bytes 6152 | tf_op jit(solution)/shard_map/ppermute | solution.py:225
  65.5 5.0 %collective-permute-start.12 = (bf16[8,128]{1,0:T(8,128)(2,1)S(1)}, bf16[8,128]{1,0:T(8,128)(2,1)S(1)}, u32[]{:S(2)}, u32[]{:S(2)}) collective-permute-start(bf16[8,128]{1,0:T(8,128)(2,1)S(1)} %get-tuple-element.39), channel_id=1, source_target_pairs={{1,0},{2,1},{3,2},{4,3},{5,4},{6,5},{7,6},{0,7},{9,8},{10,9},{11,1... | collective-permute-start | bytes 6152 | tf_op jit(solution)/shard_map/ppermute | solution.py:225
  71.6 18.6 %all-to-all-start.1 = ((bf16[16,16,512]{2,1,0:T(8,128)(2,1)}), bf16[16,16,512]{2,1,0:T(8,128)(2,1)S(1)}, u32[]{:S(2)}, u32[]{:S(2)}) async-start(bf16[16,16,512]{2,1,0:T(8,128)(2,1)} %get-tuple-element.40), calls=%async_computation.1 | async-start | bytes 524288 | tf_op jit(solution)/shard_map/all_to_all | solution.py:323
  78.3 10.1 %collective-permute-start.16 = (bf16[512,128]{1,0:T(8,128)(2,1)S(1)}, bf16[512,128]{1,0:T(8,128)(2,1)S(1)}, u32[]{:S(2)}, u32[]{:S(2)}) collective-permute-start(bf16[512,128]{1,0:T(8,128)(2,1)S(1)} %get-tuple-element.45), channel_id=1, source_target_pairs={{0,8},{8,16},{16,24},{24,32},{32,40},{40,48},{48,56},{56,64},{64,7... | collective-permute-start | bytes 393224 | tf_op jit(solution)/shard_map/ppermute | solution.py:225
  80.3 8.2 %collective-permute-start.13 = (f32[2,2,512]{2,1,0:T(2,128)S(1)}, f32[2,2,512]{2,1,0:T(2,128)S(1)}, u32[]{:S(2)}, u32[]{:S(2)}) collective-permute-start(f32[2,2,512]{2,1,0:T(2,128)S(1)} %get-tuple-element.42), channel_id=1, source_target_pairs={{0,16},{8,24},{64,80},{72,88},{128,144},{136,152},{192,208},{200,2... | collective-permute-start | bytes 24584 | tf_op jit(solution)/shard_map/ppermute | solution.py:225
  81.6 6.9 %collective-permute-start.14 = (f32[2,2,512]{2,1,0:T(2,128)S(1)}, f32[2,2,512]{2,1,0:T(2,128)S(1)}, u32[]{:S(2)}, u32[]{:S(2)}) collective-permute-start(f32[2,2,512]{2,1,0:T(2,128)S(1)} %get-tuple-element.43), channel_id=1, source_target_pairs={{0,32},{8,40},{64,96},{72,104},{128,160},{136,168},{192,224},{200,... | collective-permute-start | bytes 24584 | tf_op jit(solution)/shard_map/ppermute | solution.py:225
  82.9 6.3 %collective-permute-start.15 = (f32[2,2,512]{2,1,0:T(2,128)S(1)}, f32[2,2,512]{2,1,0:T(2,128)S(1)}, u32[]{:S(2)}, u32[]{:S(2)}) collective-permute-start(f32[2,2,512]{2,1,0:T(2,128)S(1)} %get-tuple-element.44), channel_id=1, source_target_pairs={{0,48},{8,56},{64,112},{72,120},{128,176},{136,184},{192,240},{200... | collective-permute-start | bytes 24584 | tf_op jit(solution)/shard_map/ppermute | solution.py:225

commit v7 on v6

--- a/solution.py
+++ b/solution.py
@@ -75,18 +75,16 @@
     return dot(block, order).astype(BF16)
 
 
-def selections(faces, ret, hist, select_ref, order_ref, r0_ref, h1_ref, sems):
+def first_blocks(ret, hist, r0_ref, h1_ref, sems):
     moves = [(hist.at[hist.shape[0] - 1], h1_ref), (ret.at[0], r0_ref)]
     copies = [pltpu.make_async_copy(a, b, sems.at[k]) for k, (a, b) in enumerate(moves)]
     for copy in copies:
         copy.start()
-    select_ref[...] = one_hot_rows(faces[...], select_ref.shape[0])
-    order_ref[...] = permutation(order_ref.shape[0])
     for copy in copies:
         copy.wait()
 
 
-def own_partials(counts, exc, order, hist, r0, ret, d0_ref, d1_ref, r1, sem):
+def own_partials(counts, exc, faces, hist, r0, ret, d0_ref, d1_ref, select_ref, order_ref, r1, sem):
     copy = pltpu.make_async_copy(ret.at[1], r1, sem)
     copy.start()
     width = hist.shape[2]
@@ -98,7 +96,10 @@
         e = exc[step]
         return jnp.where(col == first_col, e[0:1], jnp.where(col == first_col + 1, e[1:2], 0.0))
 
-    h0, h1 = permuted(hist[0], order[...]), permuted(hist[1], order[...])
+    order = permutation(width)
+    order_ref[...] = order
+    select_ref[...] = one_hot_rows(faces[...], select_ref.shape[0])
+    h0, h1 = permuted(hist[0], order), permuted(hist[1], order)
     p0 = dot(r0[...], h0) * m0
     copy.wait()
     p0 += dot(r1[...], h1) * m1
@@ -114,38 +115,43 @@
     out[:, n:] = (d1[...] - p1.T).astype(BF16)
 
 
-def sum_parts(x, out):
+def sum_parts(x, out, sent):
     total = x[0].astype(F32)
     for i in range(1, x.shape[0]):
         total += x[i].astype(F32)
     out[...] = total
-
-
-def trace_of(first, select, up_ref, down_ref):
+    sent[...] = total.astype(BF16)
+
+
+def send_traces(first, select, out):
     trace = dot(first.astype(BF16), select[...]).astype(BF16)
     half = select.shape[1] // 2
-    down_ref[...] = trace[:, :half]
-    up_ref[...] = trace[:, half:]
-
-
-def coupled(up, down, inv, tra):
-    half = up.shape[1]
-    coupling = dot_t(up[...], tra[:, :half]) + dot_t(down[...], tra[:, half:])
+    dom = lax.axis_index("dom")
+    out[...] = jnp.zeros_like(out)
+    out[(dom + 1) % DOM] = trace[:, half:]
+    out[(dom + DOM - 1) % DOM] = trace[:, :half]
+
+
+def coupled(traces, inv, tra):
+    half = traces.shape[2]
+    dom = lax.axis_index("dom")
+    up, down = traces[(dom + DOM - 1) % DOM], traces[(dom + 1) % DOM]
+    coupling = dot_t(up, tra[:, :half]) + dot_t(down, tra[:, half:])
     return dot_t(coupling.astype(BF16), inv[...])
 
 
-def first_of_sum(x0, x1, x2, x3, inv, select, first_ref, rest_ref, up_ref, down_ref):
+def first_of_sum(x0, x1, x2, x3, inv, select, first_ref, rest_ref, traces_ref):
     n = inv.shape[0]
-    total = (x0[...] + x1[...]) + (x2[...] + x3[...])
+    total = (x0[...] + x1[...].astype(F32)) + (x2[...].astype(F32) + x3[...].astype(F32))
     first = dot_t(total[:, :n].astype(BF16), inv[...])
     first_ref[...] = first
     rest_ref[...] = total[:, n:]
-    trace_of(first, select, up_ref, down_ref)
+    send_traces(first, select, traces_ref)
 
 
 def next_first(
-    counts, first, rest, up, down, inv, tra, select, r0_even, r0_odd,
-    cur_ref, first_ref, up_ref, down_ref,
+    counts, first, rest, traces, inv, tra, select, r0_even, r0_odd,
+    cur_ref, first_ref, traces_ref,
     r0, sem,
 ):
     odd = lax.axis_index("c") == 1
@@ -158,17 +164,17 @@
     def _():
         copied(r0_even, r0, sem)
 
-    cur = first[...] - coupled(up, down, inv, tra)
+    cur = first[...] - coupled(traces, inv, tra)
     cur_ref[...] = cur
     alive = (counts[0] > 0).astype(F32)
     newest = dot_t(cur.astype(BF16), r0[...]) * alive
     following = dot_t((rest[...] - newest).astype(BF16), inv[...])
     first_ref[...] = following
-    trace_of(following, select, up_ref, down_ref)
-
-
-def second_current(cur0, first, up, down, inv, tra, gather_ref, *share_refs):
-    cur1 = first[...] - coupled(up, down, inv, tra)
+    send_traces(following, select, traces_ref)
+
+
+def second_current(cur0, first, traces, inv, tra, gather_ref, *share_refs):
+    cur1 = first[...] - coupled(traces, inv, tra)
     c0 = cur0[...]
     both = jnp.concatenate([cur1.astype(BF16), c0.astype(BF16)], axis=0)
     for i in range(gather_ref.shape[0]):
@@ -250,30 +256,28 @@
             scratch_shapes=[pltpu.SemaphoreType.DMA],
         )(*operands)
 
-    ring = [(i, (i + 1) % DOM) for i in range(DOM)]
-    back = [(j, i) for i, j in ring]
     chain = [(i, i + 1) for i in range(devices - 1)]
 
     macs = n * n * width
-    select, order, r0, h1 = call(
-        selections,
-        (shape((n, 2 * half), BF16), shape((width, width), BF16), shape((n, n), BF16), shape((n, width), BF16)),
-        [VMEM] + [any_spec] * 2,
+    r0, h1 = call(
+        first_blocks,
+        (shape((n, n), BF16), shape((n, width), BF16)),
+        [any_spec] * 2,
         0,
         1024 * 1024,
-        mib=52,
+        mib=53,
         scratch_shapes=[pltpu.SemaphoreType.DMA((2,))],
-    )(faces, retarded, history)
+    )(retarded, history)
     before1 = permute(h1, DELAY, chain)
-    d0, d1 = call(
+    d0, d1, select, order = call(
         own_partials,
-        (shape((width, n), BF16), shape((width, n), F32)),
+        (shape((width, n), BF16), shape((width, n), F32), shape((n, 2 * half), BF16), shape((width, width), BF16)),
         [SMEM] + [VMEM] * 4 + [any_spec],
         2 * macs * 4,
         2 * 1024 * 1024,
         mib=52,
         scratch_shapes=[pltpu.VMEM((n, n), BF16), pltpu.SemaphoreType.DMA],
-    )(counts, exc, order, history, r0, retarded)
+    )(counts, exc, faces, history, r0, retarded)
     s1a, s1b = spread(r0, (0, 3)), spread(r0, (0, 5))
     lanes = 2 * n
     packed, h0 = call(
@@ -287,39 +291,42 @@
     x = lax.all_to_all(packed.reshape(OWNERS, cols, lanes), ("y", "c"), 0, 0, tiled=True)
     r0 = relayed((0,), (3,), r0, s1a, s1b, packed)
     s2a, s2b = spread(r0, (0, 1), (3, 2), (5, 6)), spread(r0, (0, 7), (3, 4))
-    x = call(sum_parts, shape((cols, lanes), F32), [VMEM], 0, 512 * 1024)(x)
-    xs = [x] + [permute(x, "zh", [(z, 0)]) for z in range(1, ZH)]
-
-    def halo(up, down):
-        return permute(up, ("zh", "dom"), ring), permute(down, ("zh", "dom"), back)
-
-    trace_shape = (shape((cols, half), BF16),) * 2
-    first, rest, up, down = call(
+    x, sent = call(
+        sum_parts, (shape((cols, lanes), F32), shape((cols, lanes), BF16)), [VMEM], 0, 512 * 1024
+    )(x)
+    xs = [x] + [permute(sent, "zh", [(z, 0)]) for z in range(1, ZH)]
+
+    def halo(traces):
+        return lax.all_to_all(traces, "dom", 0, 0, tiled=True)
+
+    owned = shape((cols, n), F32)
+    traces_shape = shape((DOM, cols, half), BF16)
+    first, rest, traces = call(
         first_of_sum,
-        (shape((cols, n), F32), shape((cols, n), F32)) + trace_shape,
+        (owned, owned, traces_shape),
         [VMEM] * 6,
         2 * 8 * n * n * 2,
         1024 * 1024,
     )(*xs, inverse, select)
     r0 = relayed((0, 3, 5), (1, 2, 6), r0, s2a, s2b, rest)
     s3 = permute(r0, DELAY, [(at(i, 0, 0), at(i, 0, 1)) for i in range(Y)])
-    up, down = halo(up, down)
-    cur0, first, up, down = call(
+    traces = halo(traces)
+    cur0, first, traces = call(
         next_first,
-        (shape((cols, n), F32), shape((cols, n), F32)) + trace_shape,
-        [SMEM] + [VMEM] * 7 + [any_spec] * 2,
+        (owned, owned, traces_shape),
+        [SMEM] + [VMEM] * 6 + [any_spec] * 2,
         2 * 8 * n * n * 5,
         2 * 1024 * 1024,
         scratch_shapes=[pltpu.VMEM((n, n), BF16), pltpu.SemaphoreType.DMA],
-    )(counts, first, rest, up, down, inverse, transfer, select, r0, s3)
-    up, down = halo(up, down)
+    )(counts, first, rest, traces, inverse, transfer, select, r0, s3)
+    traces = halo(traces)
     gather, *share = call(
         second_current,
         [shape((OWNERS, 2 * cols, n), BF16)] + [shape((steps, 2, n), F32)] * ZH,
-        [VMEM] * 6,
+        [VMEM] * 5,
         2 * 8 * n * n * 2,
         1024 * 1024,
-    )(cur0, first, up, down, inverse, transfer)
+    )(cur0, first, traces, inverse, transfer)
     gather = lax.all_to_all(gather, ("y", "c"), 0, 0, tiled=True)
     for z in range(1, ZH):
         share[z] = permute(share[z], DELAY, [(at(i, 0, c), at(i, z, c)) for i in range(Y) for c in range(CORE)])

time: 91.7 us -> 94.9 us (1.035)
  blocking collectives: 0 us -> 43.5 us
  starting transfers between devices: 59.5 us -> 33.1 us
  waiting for transfers between devices: 20.6 us -> 7.42 us
    all_to_all x0 -> x3, blocking collectives: none -> 43.5 us  [the longest x1 26.4 us: body(): lax.all_to_all(packed.reshape(OWNERS, cols, lanes), ('y', 'c'), 0, 0, til...]
    ppermute x17 -> x13, starting transfers between devices: 40.4 us -> 25.3 us  [permute(): return lax.ppermute(value, axes, pairs)]
    all_to_all x1 -> x0, starting transfers between devices: 12.4 us -> none  [body(): lax.all_to_all(packed.reshape(OWNERS, cols, lanes), ('y', 'c'), 0, 0, til...]
    all_to_all x1 -> x0, waiting for transfers between devices: 10.1 us -> none  [body(): lax.all_to_all(packed.reshape(OWNERS, cols, lanes), ('y', 'c'), 0, 0, til...]
    ppermute x17 -> x13, waiting for transfers between devices: 9.48 us -> 6.56 us  [permute(): return lax.ppermute(value, axes, pairs)]
    all_to_all x1, starting transfers between devices: 6.76 us -> 7.73 us  [body(): gather = lax.all_to_all(gather, ('y', 'c'), 0, 0, tiled=True)]
  transfers between devices with their start and end apart: 19 -> 14, of which waited for: 8 -> 4; matrix products, arithmetic and copies ran while one was open for 0% -> 0% of each run, Pallas kernels for 4% -> 3%
where the time goes in v7:
time: 94.9 us; the launch traced here: 94.2 us
  blocking collectives  43.5 us (46%)
  starting transfers between devices  33.1 us (35%)
  waiting for transfers between devices  7.42 us (8%)
  Pallas kernels  7.06 us (7%)
  local copies, waits for them, and re-layouts  1.62 us (2%)
  between operations  1.54 us (2%)
    all_to_all x1, blocking collectives, body(): lax.all_to_all(packed.reshape(OWNERS, cols, lanes), ('y', 'c'), 0, 0, til...  26.4 us
    ppermute x13, starting transfers between devices, permute(): return lax.ppermute(value, axes, pairs)  25.3 us
    all_to_all x2, blocking collectives, halo(): return lax.all_to_all(traces, 'dom', 0, 0, tiled=True)  17.1 us
    all_to_all x1, starting transfers between devices, body(): gather = lax.all_to_all(gather, ('y', 'c'), 0, 0, tiled=True)  7.73 us
    ppermute x13, waiting for transfers between devices, permute(): return lax.ppermute(value, axes, pairs)  6.56 us
    pallas_call x1, Pallas kernels, body(): call(own_partials, (shape((width, n), BF16), shape((width, n), F32), shap...  2.05 us
  transfers between devices with their start and end apart: 14, of which 4 were waited for; matrix products, arithmetic and copies ran while one was open for 0% of the time, Pallas kernels for 3%

profile of v7, /device:TPU:1, one launch (start us, length us, event | category | flops | bytes accessed | tf_op | source)
XLA Modules:
  0.0 94.2 jit_solution(2691614569744426274)
XLA Ops:
  0.6 0.9 copy-done.1
  1.6 1.2 %shard_map.86 = (bf16[512,512]{1,0:T(8,128)(2,1)S(1)}, bf16[512,128]{1,0:T(8,128)(2,1)S(1)}) custom-call(bf16[2,512,512]{2,1,0:T(8,128)(2,1)} %ret.3, bf16[2,512,128]{2,1,0:T(8,128)(2,1)S(1)} %copy-done.1), custom_call_target="tpu_custom_call" | custom-call | bytes 1048576 | tf_op jit(solution)/shard_map/pallas_call | solution.py:262
  2.8 0.7 collective-permute-start.5
  3.5 0.7 collective-permute-start.4
  4.2 7.2 %collective-permute-start = (bf16[512,128]{1,0:T(8,128)(2,1)S(1)}, bf16[512,128]{1,0:T(8,128)(2,1)S(1)}, u32[]{:S(2)}, u32[]{:S(2)}) collective-permute-start(bf16[512,128]{1,0:T(8,128)(2,1)S(1)} %get-tuple-element.29), channel_id=1, source_target_pairs={{0,8},{8,16},{16,24},{24,32},{32,40},{40,48},{48,56},{56,64},{64,7... | collective-permute-start | bytes 393224 | tf_op jit(solution)/shard_map/ppermute | solution.py:231
  12.1 0.7 copy-done.5
  12.7 2.0 %shard_map.87 = (bf16[128,512]{1,0:T(8,128)(2,1)S(1)}, f32[128,512]{1,0:T(8,128)S(1)}, bf16[512,256]{1,0:T(8,128)(2,1)S(1)}, bf16[128,128]{1,0:T(8,128)(2,1)S(1)}) custom-call(s32[1]{0:T(128)S(6)} %copy.9.counts, f32[2,2,512]{2,1,0:T(2,128)S(1)} %bitcast.4, s32[1,256]{1,0:T(1,128)S(1)} %copy-done.5, bf16[2,512,128]{2,1,0:T(8,128)(2,1)S(1)} %copy-done.2, ...), custom_call_target="tpu_custom_call" | custom-call | flops 268435456 | bytes 2097152 | tf_op jit(solution)/shard_map/pallas_call | solution.py:272
  14.8 0.5 shard_map.88
  15.4 0.1 shard_map.91.held
  15.5 0.8 collective-permute-start.7
  16.3 0.7 collective-permute-start.6
  17.0 26.4 %all_to_all.20.x = bf16[16,8,1024]{2,1,0:T(8,128)(2,1)S(1)} all-to-all(bf16[16,8,1024]{2,1,0:T(8,128)(2,1)S(1)} %bitcast.3), channel_id=1, replica_groups=mesh['y'=8,'zh'=4,'c'=2,'dom'=8] {'y','c'}, dimensions={0} | all-to-all | bytes 524288 | tf_op jit(solution)/shard_map/all_to_all | solution.py:291
  43.5 1.3 %collective-permute-start.3 = (bf16[8,1024]{1,0:T(8,128)(2,1)S(1)}, bf16[8,1024]{1,0:T(8,128)(2,1)S(1)}, u32[]{:S(2)}, u32[]{:S(2)}) collective-permute-start(bf16[8,1024]{1,0:T(8,128)(2,1)S(1)} %get-tuple-element.32), channel_id=1, source_target_pairs={{48,0},{49,1},{50,2},{51,3},{52,4},{53,5},{54,6},{55,7},{56,8},{57... | collective-permute-start | bytes 49160 | tf_op jit(solution)/shard_map/ppermute | solution.py:231
  44.8 1.3 %collective-permute-start.2 = (bf16[8,1024]{1,0:T(8,128)(2,1)S(1)}, bf16[8,1024]{1,0:T(8,128)(2,1)S(1)}, u32[]{:S(2)}, u32[]{:S(2)}) collective-permute-start(bf16[8,1024]{1,0:T(8,128)(2,1)S(1)} %get-tuple-element.32), channel_id=1, source_target_pairs={{32,0},{33,1},{34,2},{35,3},{36,4},{37,5},{38,6},{39,7},{40,8},{41... | collective-permute-start | bytes 49160 | tf_op jit(solution)/shard_map/ppermute | solution.py:231
  46.1 1.3 %collective-permute-start.1 = (bf16[8,1024]{1,0:T(8,128)(2,1)S(1)}, bf16[8,1024]{1,0:T(8,128)(2,1)S(1)}, u32[]{:S(2)}, u32[]{:S(2)}) collective-permute-start(bf16[8,1024]{1,0:T(8,128)(2,1)S(1)} %get-tuple-element.32), channel_id=1, source_target_pairs={{16,0},{17,1},{18,2},{19,3},{20,4},{21,5},{22,6},{23,7},{24,8},{25... | collective-permute-start | bytes 49160 | tf_op jit(solution)/shard_map/ppermute | solution.py:231
  47.4 2.7 %collective-permute-done.3.x3 = bf16[8,1024]{1,0:T(8,128)(2,1)S(1)} collective-permute-done((bf16[8,1024]{1,0:T(8,128)(2,1)S(1)}, bf16[8,1024]{1,0:T(8,128)(2,1)S(1)}, u32[]{:S(2)}, u32[]{:S(2)}) %collective-permute-start.3) | collective-permute-done | bytes 16416 | tf_op jit(solution)/shard_map/ppermute | solution.py:231
  50.1 3.0 %collective-permute-done.2.x2 = bf16[8,1024]{1,0:T(8,128)(2,1)S(1)} collective-permute-done((bf16[8,1024]{1,0:T(8,128)(2,1)S(1)}, bf16[8,1024]{1,0:T(8,128)(2,1)S(1)}, u32[]{:S(2)}, u32[]{:S(2)}) %collective-permute-start.2) | collective-permute-done | bytes 16416 | tf_op jit(solution)/shard_map/ppermute | solution.py:231
  53.2 0.4 shard_map.90
  53.6 0.1 shard_map.92.r0_even
  53.7 1.3 %collective-permute-start.8 = (bf16[512,512]{1,0:T(8,128)(2,1)S(1)}, bf16[512,512]{1,0:T(8,128)(2,1)S(1)}, u32[]{:S(2)}, u32[]{:S(2)}) collective-permute-start(bf16[512,512]{1,0:T(8,128)(2,1)S(1)} %shard_map.92.r0_even), channel_id=1, source_target_pairs={{0,8},{64,72},{128,136},{192,200},{256,264},{320,328},{384,392},{4... | collective-permute-start | bytes 1572872 | tf_op jit(solution)/shard_map/ppermute | solution.py:231
  55.0 9.7 %all_to_all.21.traces = bf16[8,8,128]{2,1,0:T(8,128)(2,1)S(1)} all-to-all(bf16[8,8,128]{2,1,0:T(8,128)(2,1)S(1)} %get-tuple-element.36), channel_id=1, replica_groups=mesh['y'=8,'zh'=4,'c'=2,'dom'=8] {'dom'}, dimensions={0} | all-to-all | bytes 32768 | tf_op jit(solution)/shard_map/all_to_all | solution.py:300
  64.6 0.9 shard_map.93
  65.5 7.4 %all_to_all.22.traces = bf16[8,8,128]{2,1,0:T(8,128)(2,1)S(1)} all-to-all(bf16[8,8,128]{2,1,0:T(8,128)(2,1)S(1)} %get-tuple-element.39), channel_id=1, replica_groups=mesh['y'=8,'zh'=4,'c'=2,'dom'=8] {'dom'}, dimensions={0} | all-to-all | bytes 32768 | tf_op jit(solution)/shard_map/all_to_all | solution.py:300
  72.9 1.1 %shard_map.94 = (bf16[16,16,512]{2,1,0:T(8,128)(2,1)}, f32[2,2,512]{2,1,0:T(2,128)S(1)}, f32[2,2,512]{2,1,0:T(2,128)S(1)}, f32[2,2,512]{2,1,0:T(2,128)S(1)}, f32[2,2,512]{2,1,0:T(2,128)S(1)}) custom-call(f32[8,512]{1,0:T(8,128)S(1)} %get-tuple-element.37.cur0, f32[8,512]{1,0:T(8,128)S(1)} %get-tuple-element.38.first, ...), custom_call_target="tpu_custom_call" | custom-call | flops 8388608 | bytes 1048576 | tf_op jit(solution)/shard_map/pallas_call | solution.py:323
  74.0 7.7 %all-to-all-start.3 = ((bf16[16,16,512]{2,1,0:T(8,128)(2,1)}), bf16[16,16,512]{2,1,0:T(8,128)(2,1)S(1)}, u32[]{:S(2)}, u32[]{:S(2)}) async-start(bf16[16,16,512]{2,1,0:T(8,128)(2,1)} %get-tuple-element.40), calls=%async_computation.3 | async-start | bytes 524288 | tf_op jit(solution)/shard_map/all_to_all | solution.py:330
  81.8 1.9 %collective-permute-start.12 = (bf16[512,128]{1,0:T(8,128)(2,1)S(1)}, bf16[512,128]{1,0:T(8,128)(2,1)S(1)}, u32[]{:S(2)}, u32[]{:S(2)}) collective-permute-start(bf16[512,128]{1,0:T(8,128)(2,1)S(1)} %get-tuple-element.45), channel_id=1, source_target_pairs={{0,8},{8,16},{16,24},{24,32},{32,40},{40,48},{48,56},{56,64},{64,7... | collective-permute-start | bytes 393224 | tf_op jit(solution)/shard_map/ppermute | solution.py:231
  83.7 1.3 %collective-permute-start.9 = (f32[2,2,512]{2,1,0:T(2,128)S(1)}, f32[2,2,512]{2,1,0:T(2,128)S(1)}, u32[]{:S(2)}, u32[]{:S(2)}) collective-permute-start(f32[2,2,512]{2,1,0:T(2,128)S(1)} %get-tuple-element.42), channel_id=1, source_target_pairs={{0,16},{8,24},{64,80},{72,88},{128,144},{136,152},{192,208},{200,2... | collective-permute-start | bytes 24584 | tf_op jit(solution)/shard_map/ppermute | solution.py:231
  85.0 1.3 %collective-permute-start.10 = (f32[2,2,512]{2,1,0:T(2,128)S(1)}, f32[2,2,512]{2,1,0:T(2,128)S(1)}, u32[]{:S(2)}, u32[]{:S(2)}) collective-permute-start(f32[2,2,512]{2,1,0:T(2,128)S(1)} %get-tuple-element.43), channel_id=1, source_target_pairs={{0,32},{8,40},{64,96},{72,104},{128,160},{136,168},{192,224},{200,... | collective-permute-start | bytes 24584 | tf_op jit(solution)/shard_map/ppermute | solution.py:231
  86.3 5.6 %collective-permute-start.11 = (f32[2,2,512]{2,1,0:T(2,128)S(1)}, f32[2,2,512]{2,1,0:T(2,128)S(1)}, u32[]{:S(2)}, u32[]{:S(2)}) collective-permute-start(f32[2,2,512]{2,1,0:T(2,128)S(1)} %get-tuple-element.44), channel_id=1, source_target_pairs={{0,48},{8,56},{64,112},{72,120},{128,176},{136,184},{192,240},{200... | collective-permute-start | bytes 24584 | tf_op jit(solution)/shard_map/ppermute | solution.py:231
  91.9 0.7 collective-permute-done.11.s3
  92.6 0.9 all-to-all-done.3.gathered
  93.5 0.7 shard_map.95
  (21 shorter events, 0.1 us)
Async XLA Ops:
  0.6 1.0 %copy-start.1 = (bf16[2,512,128]{2,1,0:T(8,128)(2,1)S(1)}, bf16[2,512,128]{2,1,0:T(8,128)(2,1)}, u32[]{:S(2)}) copy-start(bf16[2,512,128]{2,1,0:T(8,128)(2,1)} %hist.5) | copy-start | bytes 786436
  1.6 10.5 %copy-start.2 = (bf16[2,512,128]{2,1,0:T(8,128)(2,1)S(1)}, bf16[2,512,128]{2,1,0:T(8,128)(2,1)}, u32[]{:S(2)}) copy-start(bf16[2,512,128]{2,1,0:T(8,128)(2,1)} %hist.5) | copy-start | bytes 786436
  1.6 10.5 %copy-start.4 = (f32[2,512,2]{1,2,0:T(2,128)S(1)}, f32[2,512,2]{1,2,0:T(2,128)}, u32[]{:S(2)}) copy-start(f32[2,512,2]{1,2,0:T(2,128)} %param.7) | copy-start | bytes 24580
  2.8 12.5 %collective-permute-start.5 = (bf16[512,512]{1,0:T(8,128)(2,1)S(1)}, bf16[512,512]{1,0:T(8,128)(2,1)S(1)}, u32[]{:S(2)}, u32[]{:S(2)}) collective-permute-start(bf16[512,512]{1,0:T(8,128)(2,1)S(1)} %get-tuple-element.25.r0.held), channel_id=1, source_target_pairs={{0,320},{1,321},{2,322},{3,323},{4,324},{5,325},{6,326},{7,327}} | collective-permute-start | bytes 1572872 | tf_op jit(solution)/shard_map/ppermute | solution.py:231
  3.5 11.9 %collective-permute-start.4 = (bf16[512,512]{1,0:T(8,128)(2,1)S(1)}, bf16[512,512]{1,0:T(8,128)(2,1)S(1)}, u32[]{:S(2)}, u32[]{:S(2)}) collective-permute-start(bf16[512,512]{1,0:T(8,128)(2,1)S(1)} %get-tuple-element.25.r0.held), channel_id=1, source_target_pairs={{0,192},{1,193},{2,194},{3,195},{4,196},{5,197},{6,198},{7,199}} | collective-permute-start | bytes 1572872 | tf_op jit(solution)/shard_map/ppermute | solution.py:231
  4.2 10.6 %collective-permute-start = (bf16[512,128]{1,0:T(8,128)(2,1)S(1)}, bf16[512,128]{1,0:T(8,128)(2,1)S(1)}, u32[]{:S(2)}, u32[]{:S(2)}) collective-permute-start(bf16[512,128]{1,0:T(8,128)(2,1)S(1)} %get-tuple-element.29), channel_id=1, source_target_pairs={{0,8},{8,16},{16,24},{24,32},{32,40},{40,48},{48,56},{56,64},{64,7... | collective-permute-start | bytes 393224 | tf_op jit(solution)/shard_map/ppermute | solution.py:231
  12.1 0.7 copy-start.5
  15.4 37.7 %copy-start = (bf16[512,512]{1,0:T(8,128)(2,1)S(1)}, bf16[512,512]{1,0:T(8,128)(2,1)}, u32[]{:S(2)}) copy-start(bf16[512,512]{1,0:T(8,128)(2,1)} %inv.5) | copy-start | bytes 1572868
  15.5 38.1 %collective-permute-start.7 = (bf16[512,512]{1,0:T(8,128)(2,1)S(1)}, bf16[512,512]{1,0:T(8,128)(2,1)S(1)}, u32[]{:S(2)}, u32[]{:S(2)}) collective-permute-start(bf16[512,512]{1,0:T(8,128)(2,1)S(1)} %shard_map.91.held), channel_id=1, source_target_pairs={{0,448},{192,256},{1,449},{193,257},{2,450},{194,258},{3,451},{195... | collective-permute-start | bytes 1572872 | tf_op jit(solution)/shard_map/ppermute | solution.py:231
  16.3 37.3 %collective-permute-start.6 = (bf16[512,512]{1,0:T(8,128)(2,1)S(1)}, bf16[512,512]{1,0:T(8,128)(2,1)S(1)}, u32[]{:S(2)}, u32[]{:S(2)}) collective-permute-start(bf16[512,512]{1,0:T(8,128)(2,1)S(1)} %shard_map.91.held), channel_id=1, source_target_pairs={{0,64},{192,128},{320,384},{1,65},{193,129},{321,385},{2,66},{194,... | collective-permute-start | bytes 1572872 | tf_op jit(solution)/shard_map/ppermute | solution.py:231
  43.5 6.6 %collective-permute-start.3 = (bf16[8,1024]{1,0:T(8,128)(2,1)S(1)}, bf16[8,1024]{1,0:T(8,128)(2,1)S(1)}, u32[]{:S(2)}, u32[]{:S(2)}) collective-permute-start(bf16[8,1024]{1,0:T(8,128)(2,1)S(1)} %get-tuple-element.32), channel_id=1, source_target_pairs={{48,0},{49,1},{50,2},{51,3},{52,4},{53,5},{54,6},{55,7},{56,8},{57... | collective-permute-start | bytes 49160 | tf_op jit(solution)/shard_map/ppermute | solution.py:231
  44.8 8.4 %collective-permute-start.2 = (bf16[8,1024]{1,0:T(8,128)(2,1)S(1)}, bf16[8,1024]{1,0:T(8,128)(2,1)S(1)}, u32[]{:S(2)}, u32[]{:S(2)}) collective-permute-start(bf16[8,1024]{1,0:T(8,128)(2,1)S(1)} %get-tuple-element.32), channel_id=1, source_target_pairs={{32,0},{33,1},{34,2},{35,3},{36,4},{37,5},{38,6},{39,7},{40,8},{41... | collective-permute-start | bytes 49160 | tf_op jit(solution)/shard_map/ppermute | solution.py:231
  46.1 7.1 %collective-permute-start.1 = (bf16[8,1024]{1,0:T(8,128)(2,1)S(1)}, bf16[8,1024]{1,0:T(8,128)(2,1)S(1)}, u32[]{:S(2)}, u32[]{:S(2)}) collective-permute-start(bf16[8,1024]{1,0:T(8,128)(2,1)S(1)} %get-tuple-element.32), channel_id=1, source_target_pairs={{16,0},{17,1},{18,2},{19,3},{20,4},{21,5},{22,6},{23,7},{24,8},{25... | collective-permute-start | bytes 49160 | tf_op jit(solution)/shard_map/ppermute | solution.py:231
  53.6 11.1 %copy-start.3 = (bf16[512,256]{1,0:T(8,128)(2,1)S(1)}, bf16[512,256]{1,0:T(8,128)(2,1)}, u32[]{:S(2)}) copy-start(bf16[512,256]{1,0:T(8,128)(2,1)} %tra.3) | copy-start | bytes 786436
  53.7 11.0 %collective-permute-start.8 = (bf16[512,512]{1,0:T(8,128)(2,1)S(1)}, bf16[512,512]{1,0:T(8,128)(2,1)S(1)}, u32[]{:S(2)}, u32[]{:S(2)}) collective-permute-start(bf16[512,512]{1,0:T(8,128)(2,1)S(1)} %shard_map.92.r0_even), channel_id=1, source_target_pairs={{0,8},{64,72},{128,136},{192,200},{256,264},{320,328},{384,392},{4... | collective-permute-start | bytes 1572872 | tf_op jit(solution)/shard_map/ppermute | solution.py:231
  74.0 19.4 %all-to-all-start.3 = ((bf16[16,16,512]{2,1,0:T(8,128)(2,1)}), bf16[16,16,512]{2,1,0:T(8,128)(2,1)S(1)}, u32[]{:S(2)}, u32[]{:S(2)}) async-start(bf16[16,16,512]{2,1,0:T(8,128)(2,1)} %get-tuple-element.40), calls=%async_computation.3 | async-start | bytes 524288 | tf_op jit(solution)/shard_map/all_to_all | solution.py:330
  81.8 10.1 %collective-permute-start.12 = (bf16[512,128]{1,0:T(8,128)(2,1)S(1)}, bf16[512,128]{1,0:T(8,128)(2,1)S(1)}, u32[]{:S(2)}, u32[]{:S(2)}) collective-permute-start(bf16[512,128]{1,0:T(8,128)(2,1)S(1)} %get-tuple-element.45), channel_id=1, source_target_pairs={{0,8},{8,16},{16,24},{24,32},{32,40},{40,48},{48,56},{56,64},{64,7... | collective-permute-start | bytes 393224 | tf_op jit(solution)/shard_map/ppermute | solution.py:231
  83.7 8.2 %collective-permute-start.9 = (f32[2,2,512]{2,1,0:T(2,128)S(1)}, f32[2,2,512]{2,1,0:T(2,128)S(1)}, u32[]{:S(2)}, u32[]{:S(2)}) collective-permute-start(f32[2,2,512]{2,1,0:T(2,128)S(1)} %get-tuple-element.42), channel_id=1, source_target_pairs={{0,16},{8,24},{64,80},{72,88},{128,144},{136,152},{192,208},{200,2... | collective-permute-start | bytes 24584 | tf_op jit(solution)/shard_map/ppermute | solution.py:231
  85.0 6.9 %collective-permute-start.10 = (f32[2,2,512]{2,1,0:T(2,128)S(1)}, f32[2,2,512]{2,1,0:T(2,128)S(1)}, u32[]{:S(2)}, u32[]{:S(2)}) collective-permute-start(f32[2,2,512]{2,1,0:T(2,128)S(1)} %get-tuple-element.43), channel_id=1, source_target_pairs={{0,32},{8,40},{64,96},{72,104},{128,160},{136,168},{192,224},{200,... | collective-permute-start | bytes 24584 | tf_op jit(solution)/shard_map/ppermute | solution.py:231
  86.3 6.3 %collective-permute-start.11 = (f32[2,2,512]{2,1,0:T(2,128)S(1)}, f32[2,2,512]{2,1,0:T(2,128)S(1)}, u32[]{:S(2)}, u32[]{:S(2)}) collective-permute-start(f32[2,2,512]{2,1,0:T(2,128)S(1)} %get-tuple-element.44), channel_id=1, source_target_pairs={{0,48},{8,56},{64,112},{72,120},{128,176},{136,184},{192,240},{200... | collective-permute-start | bytes 24584 | tf_op jit(solution)/shard_map/ppermute | solution.py:231

commit v8 on v6

--- a/solution.py
+++ b/solution.py
@@ -75,18 +75,11 @@
     return dot(block, order).astype(BF16)
 
 
-def selections(faces, ret, hist, select_ref, order_ref, r0_ref, h1_ref, sems):
-    moves = [(hist.at[hist.shape[0] - 1], h1_ref), (ret.at[0], r0_ref)]
-    copies = [pltpu.make_async_copy(a, b, sems.at[k]) for k, (a, b) in enumerate(moves)]
-    for copy in copies:
-        copy.start()
-    select_ref[...] = one_hot_rows(faces[...], select_ref.shape[0])
-    order_ref[...] = permutation(order_ref.shape[0])
-    for copy in copies:
-        copy.wait()
-
-
-def own_partials(counts, exc, order, hist, r0, ret, d0_ref, d1_ref, r1, sem):
+def first_block(ret, after, r0_ref, sem):
+    copied(ret.at[0], r0_ref, sem)
+
+
+def own_partials(counts, exc, faces, hist, r0, ret, d0_ref, d1_ref, select_ref, order_ref, r1, sem):
     copy = pltpu.make_async_copy(ret.at[1], r1, sem)
     copy.start()
     width = hist.shape[2]
@@ -98,7 +91,10 @@
         e = exc[step]
         return jnp.where(col == first_col, e[0:1], jnp.where(col == first_col + 1, e[1:2], 0.0))
 
-    h0, h1 = permuted(hist[0], order[...]), permuted(hist[1], order[...])
+    order = permutation(width)
+    order_ref[...] = order
+    select_ref[...] = one_hot_rows(faces[...], select_ref.shape[0])
+    h0, h1 = permuted(hist[0], order), permuted(hist[1], order)
     p0 = dot(r0[...], h0) * m0
     copy.wait()
     p0 += dot(r1[...], h1) * m1
@@ -255,25 +251,26 @@
     chain = [(i, i + 1) for i in range(devices - 1)]
 
     macs = n * n * width
-    select, order, r0, h1 = call(
-        selections,
-        (shape((n, 2 * half), BF16), shape((width, width), BF16), shape((n, n), BF16), shape((n, width), BF16)),
-        [VMEM] + [any_spec] * 2,
+    last = history[slots - 1]
+    before1 = permute(last, DELAY, chain)
+    r0 = call(
+        first_block,
+        shape((n, n), BF16),
+        [any_spec] * 2,
         0,
         1024 * 1024,
-        mib=52,
-        scratch_shapes=[pltpu.SemaphoreType.DMA((2,))],
-    )(faces, retarded, history)
-    before1 = permute(h1, DELAY, chain)
-    d0, d1 = call(
+        mib=53,
+        scratch_shapes=[pltpu.SemaphoreType.DMA],
+    )(retarded, last)
+    d0, d1, select, order = call(
         own_partials,
-        (shape((width, n), BF16), shape((width, n), F32)),
+        (shape((width, n), BF16), shape((width, n), F32), shape((n, 2 * half), BF16), shape((width, width), BF16)),
         [SMEM] + [VMEM] * 4 + [any_spec],
         2 * macs * 4,
         2 * 1024 * 1024,
         mib=52,
         scratch_shapes=[pltpu.VMEM((n, n), BF16), pltpu.SemaphoreType.DMA],
-    )(counts, exc, order, history, r0, retarded)
+    )(counts, exc, faces, history, r0, retarded)
     s1a, s1b = spread(r0, (0, 3)), spread(r0, (0, 5))
     lanes = 2 * n
     packed, h0 = call(
@@ -288,7 +285,7 @@
     r0 = relayed((0,), (3,), r0, s1a, s1b, packed)
     s2a, s2b = spread(r0, (0, 1), (3, 2), (5, 6)), spread(r0, (0, 7), (3, 4))
     x = call(sum_parts, shape((cols, lanes), F32), [VMEM], 0, 512 * 1024)(x)
-    xs = [x] + [permute(x, "zh", [(z, 0)]) for z in range(1, ZH)]
+    xs = [x] + [permute(x, "zh", [(z, 0)]) for z in (1, 3, 2)]
 
     def halo(up, down):
         return permute(up, ("zh", "dom"), ring), permute(down, ("zh", "dom"), back)

time: 91.7 us -> 90 us (0.981)
  waiting for transfers between devices: 20.6 us -> 18.8 us
    ppermute x17, waiting for transfers between devices: 9.48 us -> 7.67 us  [permute(): return lax.ppermute(value, axes, pairs)]
    unnamed x12 -> x10, local copies, waits for them, and re-layouts: 1.64 us -> 0.68 us
  transfers between devices with their start and end apart: 19 -> 19, of which waited for: 8 -> 7; matrix products, arithmetic and copies ran while one was open for 0% -> 0% of each run, Pallas kernels for 4% -> 4%
where the time goes in v8:
time: 90 us; the launch traced here: 89.3 us
  starting transfers between devices  59.7 us (66%)
  waiting for transfers between devices  18.8 us (21%)
  Pallas kernels  7.64 us (8%)
  local copies, waits for them, and re-layouts  1.6 us (2%)
  between operations  1.59 us (2%)
    ppermute x17, starting transfers between devices, permute(): return lax.ppermute(value, axes, pairs)  40.9 us
    all_to_all x1, starting transfers between devices, body(): lax.all_to_all(packed.reshape(OWNERS, cols, lanes), ('y', 'c'), 0, 0, til...  12.3 us
    all_to_all x1, waiting for transfers between devices, body(): lax.all_to_all(packed.reshape(OWNERS, cols, lanes), ('y', 'c'), 0, 0, til...  10.1 us
    ppermute x17, waiting for transfers between devices, permute(): return lax.ppermute(value, axes, pairs)  7.67 us
    all_to_all x1, starting transfers between devices, body(): gather = lax.all_to_all(gather, ('y', 'c'), 0, 0, tiled=True)  6.48 us
    pallas_call x1, Pallas kernels, body(): call(own_partials, (shape((width, n), BF16), shape((width, n), F32), shap...  2.05 us
  transfers between devices with their start and end apart: 19, of which 7 were waited for; matrix products, arithmetic and copies ran while one was open for 0% of the time, Pallas kernels for 4%

profile of v8, /device:TPU:1, one launch (start us, length us, event | category | flops | bytes accessed | tf_op | source)
XLA Modules:
  0.0 89.3 jit_solution(3628891891107648401)
XLA Ops:
  0.6 0.9 %slice_bitcast_fusion.after = bf16[512,128]{1,0:T(8,128)(2,1)S(1)} fusion(bf16[2,512,128]{2,1,0:T(8,128)(2,1)} %hist.3), kind=kLoop, calls=%fused_computation | loop fusion | bytes 262144 | tf_op jit(solution)/shard_map/squeeze | solution.py:254
  1.6 1.1 %shard_map.86.r0.held = bf16[512,512]{1,0:T(8,128)(2,1)S(1)} custom-call(bf16[2,512,512]{2,1,0:T(8,128)(2,1)} %ret.3, bf16[512,128]{1,0:T(8,128)(2,1)S(1)} %slice_bitcast_fusion.after), custom_call_target="tpu_custom_call" | custom-call | bytes 1048576 | tf_op jit(solution)/shard_map/pallas_call | solution.py:256
  2.7 0.7 collective-permute-start.7
  3.4 0.7 collective-permute-start.6
  4.1 7.2 %collective-permute-start = (bf16[512,128]{1,0:T(8,128)(2,1)S(1)}, bf16[512,128]{1,0:T(8,128)(2,1)S(1)}, u32[]{:S(2)}, u32[]{:S(2)}) collective-permute-start(bf16[512,128]{1,0:T(8,128)(2,1)S(1)} %slice_bitcast_fusion.after), channel_id=1, source_target_pairs={{0,8},{8,16},{16,24},{24,32},{32,40},{40,48},{48,56},{56,64},{64,7... | collective-permute-start | bytes 393224 | tf_op jit(solution)/shard_map/ppermute | solution.py:221
  12.6 2.0 %shard_map.87 = (bf16[128,512]{1,0:T(8,128)(2,1)S(1)}, f32[128,512]{1,0:T(8,128)S(1)}, bf16[512,256]{1,0:T(8,128)(2,1)S(1)}, bf16[128,128]{1,0:T(8,128)(2,1)S(1)}) custom-call(s32[1]{0:T(128)S(6)} %copy.9.counts, f32[2,2,512]{2,1,0:T(2,128)S(1)} %bitcast.5, s32[1,256]{1,0:T(1,128)S(1)} %copy-done.4, bf16[2,512,128]{2,1,0:T(8,128)(2,1)S(1)} %copy-done.1, ...), custom_call_target="tpu_custom_call" | custom-call | flops 268435456 | bytes 2097152 | tf_op jit(solution)/shard_map/pallas_call | solution.py:265
  14.7 1.2 %shard_map.88 = (bf16[128,1024]{1,0:T(8,128)(2,1)}, bf16[512,128]{1,0:T(8,128)(2,1)S(1)}) custom-call(s32[1]{0:T(128)S(6)} %copy.9.counts, bf16[128,128]{1,0:T(8,128)(2,1)S(1)} %get-tuple-element.23.order, bf16[128,512]{1,0:T(8,128)(2,1)S(1)} %get-tuple-element.24.d0, f32[128,512]{1,0:T(8,128)S(1)} %get-tuple-element.25.d1, ...), custom_call_target="tpu_custom_call" | custom-call | flops 67108864 | bytes 1048576 | tf_op jit(solution)/shard_map/pallas_call | solution.py:276
  15.9 12.3 %all-to-all-start = ((bf16[16,8,1024]{2,1,0:T(8,128)(2,1)}), bf16[16,8,1024]{2,1,0:T(8,128)(2,1)S(1)}, u32[]{:S(2)}, u32[]{:S(2)}) async-start(bf16[16,8,1024]{2,1,0:T(8,128)(2,1)} %bitcast.2), calls=%async_computation | async-start | bytes 524288 | tf_op jit(solution)/shard_map/all_to_all | solution.py:284
  28.4 0.8 collective-permute-start.9
  29.2 0.7 collective-permute-start.8
  29.9 10.1 %all-to-all-done.x = bf16[16,8,1024]{2,1,0:T(8,128)(2,1)S(1)} async-done(((bf16[16,8,1024]{2,1,0:T(8,128)(2,1)}), bf16[16,8,1024]{2,1,0:T(8,128)(2,1)S(1)}, u32[]{:S(2)}, u32[]{:S(2)}) %all-to-all-start) | async-done | bytes 262176 | tf_op jit(solution)/shard_map/all_to_all | solution.py:284
  40.0 1.3 %collective-permute-start.3 = (f32[8,1024]{1,0:T(8,128)S(1)}, f32[8,1024]{1,0:T(8,128)S(1)}, u32[]{:S(2)}, u32[]{:S(2)}) collective-permute-start(f32[8,1024]{1,0:T(8,128)S(1)} %shard_map.89.x0), channel_id=1, source_target_pairs={{32,0},{33,1},{34,2},{35,3},{36,4},{37,5},{38,6},{39,7},{40,8},{41... | collective-permute-start | bytes 98312 | tf_op jit(solution)/shard_map/ppermute | solution.py:221
  41.3 1.3 %collective-permute-start.2 = (f32[8,1024]{1,0:T(8,128)S(1)}, f32[8,1024]{1,0:T(8,128)S(1)}, u32[]{:S(2)}, u32[]{:S(2)}) collective-permute-start(f32[8,1024]{1,0:T(8,128)S(1)} %shard_map.89.x0), channel_id=1, source_target_pairs={{48,0},{49,1},{50,2},{51,3},{52,4},{53,5},{54,6},{55,7},{56,8},{57... | collective-permute-start | bytes 98312 | tf_op jit(solution)/shard_map/ppermute | solution.py:221
  42.6 1.3 %collective-permute-start.1 = (f32[8,1024]{1,0:T(8,128)S(1)}, f32[8,1024]{1,0:T(8,128)S(1)}, u32[]{:S(2)}, u32[]{:S(2)}) collective-permute-start(f32[8,1024]{1,0:T(8,128)S(1)} %shard_map.89.x0), channel_id=1, source_target_pairs={{16,0},{17,1},{18,2},{19,3},{20,4},{21,5},{22,6},{23,7},{24,8},{25... | collective-permute-start | bytes 98312 | tf_op jit(solution)/shard_map/ppermute | solution.py:221
  43.9 5.3 %collective-permute-done.3.x3 = f32[8,1024]{1,0:T(8,128)S(1)} collective-permute-done((f32[8,1024]{1,0:T(8,128)S(1)}, f32[8,1024]{1,0:T(8,128)S(1)}, u32[]{:S(2)}, u32[]{:S(2)}) %collective-permute-start.3) | collective-permute-done | bytes 32800 | tf_op jit(solution)/shard_map/ppermute | solution.py:221
  49.9 1.3 %collective-permute-start.10 = (bf16[512,512]{1,0:T(8,128)(2,1)S(1)}, bf16[512,512]{1,0:T(8,128)(2,1)S(1)}, u32[]{:S(2)}, u32[]{:S(2)}) collective-permute-start(bf16[512,512]{1,0:T(8,128)(2,1)S(1)} %shard_map.92.r0_even), channel_id=1, source_target_pairs={{0,8},{64,72},{128,136},{192,200},{256,264},{320,328},{384,392},{4... | collective-permute-start | bytes 1572872 | tf_op jit(solution)/shard_map/ppermute | solution.py:221
  51.2 3.8 %collective-permute-start.4 = (bf16[8,128]{1,0:T(8,128)(2,1)S(1)}, bf16[8,128]{1,0:T(8,128)(2,1)S(1)}, u32[]{:S(2)}, u32[]{:S(2)}) collective-permute-start(bf16[8,128]{1,0:T(8,128)(2,1)S(1)} %get-tuple-element.30), channel_id=1, source_target_pairs={{0,1},{1,2},{2,3},{3,4},{4,5},{5,6},{6,7},{7,0},{8,9},{9,10},{10,1... | collective-permute-start | bytes 6152 | tf_op jit(solution)/shard_map/ppermute | solution.py:221
  55.0 4.1 %collective-permute-start.5 = (bf16[8,128]{1,0:T(8,128)(2,1)S(1)}, bf16[8,128]{1,0:T(8,128)(2,1)S(1)}, u32[]{:S(2)}, u32[]{:S(2)}) collective-permute-start(bf16[8,128]{1,0:T(8,128)(2,1)S(1)} %get-tuple-element.31), channel_id=1, source_target_pairs={{1,0},{2,1},{3,2},{4,3},{5,4},{6,5},{7,6},{0,7},{9,8},{10,9},{11,1... | collective-permute-start | bytes 6152 | tf_op jit(solution)/shard_map/ppermute | solution.py:221
  59.2 0.7 collective-permute-done.5.down
  59.9 0.9 %shard_map.93 = (f32[8,512]{1,0:T(8,128)S(1)}, f32[8,512]{1,0:T(8,128)S(1)}, bf16[8,128]{1,0:T(8,128)(2,1)S(1)}, bf16[8,128]{1,0:T(8,128)(2,1)S(1)}) custom-call(s32[1]{0:T(128)S(6)} %copy.9.counts, f32[8,512]{1,0:T(8,128)S(1)} %get-tuple-element.28.first, f32[8,512]{1,0:T(8,128)S(1)} %get-tuple-element.29.after.rest, ...), custom_call_target="tpu_custom_call" | custom-call | flops 20971520 | bytes 2097152 | tf_op jit(solution)/shard_map/pallas_call | solution.py:304
  60.8 2.8 %collective-permute-start.11 = (bf16[8,128]{1,0:T(8,128)(2,1)S(1)}, bf16[8,128]{1,0:T(8,128)(2,1)S(1)}, u32[]{:S(2)}, u32[]{:S(2)}) collective-permute-start(bf16[8,128]{1,0:T(8,128)(2,1)S(1)} %get-tuple-element.34), channel_id=1, source_target_pairs={{0,1},{1,2},{2,3},{3,4},{4,5},{5,6},{6,7},{7,0},{8,9},{9,10},{10,1... | collective-permute-start | bytes 6152 | tf_op jit(solution)/shard_map/ppermute | solution.py:221
  63.6 4.9 %collective-permute-start.12 = (bf16[8,128]{1,0:T(8,128)(2,1)S(1)}, bf16[8,128]{1,0:T(8,128)(2,1)S(1)}, u32[]{:S(2)}, u32[]{:S(2)}) collective-permute-start(bf16[8,128]{1,0:T(8,128)(2,1)S(1)} %get-tuple-element.35), channel_id=1, source_target_pairs={{1,0},{2,1},{3,2},{4,3},{5,4},{6,5},{7,6},{0,7},{9,8},{10,9},{11,1... | collective-permute-start | bytes 6152 | tf_op jit(solution)/shard_map/ppermute | solution.py:221
  68.4 0.7 collective-permute-done.12.down
  69.1 1.1 %shard_map.94 = (bf16[16,16,512]{2,1,0:T(8,128)(2,1)}, f32[2,2,512]{2,1,0:T(2,128)S(1)}, f32[2,2,512]{2,1,0:T(2,128)S(1)}, f32[2,2,512]{2,1,0:T(2,128)S(1)}, f32[2,2,512]{2,1,0:T(2,128)S(1)}) custom-call(f32[8,512]{1,0:T(8,128)S(1)} %get-tuple-element.32.cur0, f32[8,512]{1,0:T(8,128)S(1)} %get-tuple-element.33.first, ...), custom_call_target="tpu_custom_call" | custom-call | flops 8388608 | bytes 1048576 | tf_op jit(solution)/shard_map/pallas_call | solution.py:313
  70.2 6.5 %all-to-all-start.1 = ((bf16[16,16,512]{2,1,0:T(8,128)(2,1)}), bf16[16,16,512]{2,1,0:T(8,128)(2,1)S(1)}, u32[]{:S(2)}, u32[]{:S(2)}) async-start(bf16[16,16,512]{2,1,0:T(8,128)(2,1)} %get-tuple-element.36), calls=%async_computation.1 | async-start | bytes 524288 | tf_op jit(solution)/shard_map/all_to_all | solution.py:320
  76.7 1.9 %collective-permute-start.16 = (bf16[512,128]{1,0:T(8,128)(2,1)S(1)}, bf16[512,128]{1,0:T(8,128)(2,1)S(1)}, u32[]{:S(2)}, u32[]{:S(2)}) collective-permute-start(bf16[512,128]{1,0:T(8,128)(2,1)S(1)} %get-tuple-element.41), channel_id=1, source_target_pairs={{0,8},{8,16},{16,24},{24,32},{32,40},{40,48},{48,56},{56,64},{64,7... | collective-permute-start | bytes 393224 | tf_op jit(solution)/shard_map/ppermute | solution.py:221
  78.6 1.3 %collective-permute-start.13 = (f32[2,2,512]{2,1,0:T(2,128)S(1)}, f32[2,2,512]{2,1,0:T(2,128)S(1)}, u32[]{:S(2)}, u32[]{:S(2)}) collective-permute-start(f32[2,2,512]{2,1,0:T(2,128)S(1)} %get-tuple-element.38), channel_id=1, source_target_pairs={{0,16},{8,24},{64,80},{72,88},{128,144},{136,152},{192,208},{200,2... | collective-permute-start | bytes 24584 | tf_op jit(solution)/shard_map/ppermute | solution.py:221
  79.9 1.3 %collective-permute-start.14 = (f32[2,2,512]{2,1,0:T(2,128)S(1)}, f32[2,2,512]{2,1,0:T(2,128)S(1)}, u32[]{:S(2)}, u32[]{:S(2)}) collective-permute-start(f32[2,2,512]{2,1,0:T(2,128)S(1)} %get-tuple-element.39), channel_id=1, source_target_pairs={{0,32},{8,40},{64,96},{72,104},{128,160},{136,168},{192,224},{200,... | collective-permute-start | bytes 24584 | tf_op jit(solution)/shard_map/ppermute | solution.py:221
  81.2 5.6 %collective-permute-start.15 = (f32[2,2,512]{2,1,0:T(2,128)S(1)}, f32[2,2,512]{2,1,0:T(2,128)S(1)}, u32[]{:S(2)}, u32[]{:S(2)}) collective-permute-start(f32[2,2,512]{2,1,0:T(2,128)S(1)} %get-tuple-element.40), channel_id=1, source_target_pairs={{0,48},{8,56},{64,112},{72,120},{128,176},{136,184},{192,240},{200... | collective-permute-start | bytes 24584 | tf_op jit(solution)/shard_map/ppermute | solution.py:221
  86.8 0.7 collective-permute-done.15.s3
  87.6 1.0 %all-to-all-done.1.gathered = bf16[16,16,512]{2,1,0:T(8,128)(2,1)S(1)} async-done(((bf16[16,16,512]{2,1,0:T(8,128)(2,1)}), bf16[16,16,512]{2,1,0:T(8,128)(2,1)S(1)}, u32[]{:S(2)}, u32[]{:S(2)}) %all-to-all-start.1) | async-done | bytes 262176 | tf_op jit(solution)/shard_map/all_to_all | solution.py:320
  88.6 0.7 shard_map.95
  (27 shorter events, 1.5 us)
Async XLA Ops:
  1.5 10.4 %copy-start.1 = (bf16[2,512,128]{2,1,0:T(8,128)(2,1)S(1)}, bf16[2,512,128]{2,1,0:T(8,128)(2,1)}, u32[]{:S(2)}) copy-start(bf16[2,512,128]{2,1,0:T(8,128)(2,1)} %hist.3) | copy-start | bytes 786436
  1.6 10.4 %copy-start.3 = (f32[2,512,2]{1,2,0:T(2,128)S(1)}, f32[2,512,2]{1,2,0:T(2,128)}, u32[]{:S(2)}) copy-start(f32[2,512,2]{1,2,0:T(2,128)} %param.7) | copy-start | bytes 24580
  2.7 25.6 %collective-permute-start.7 = (bf16[512,512]{1,0:T(8,128)(2,1)S(1)}, bf16[512,512]{1,0:T(8,128)(2,1)S(1)}, u32[]{:S(2)}, u32[]{:S(2)}) collective-permute-start(bf16[512,512]{1,0:T(8,128)(2,1)S(1)} %shard_map.86.r0.held), channel_id=1, source_target_pairs={{0,320},{1,321},{2,322},{3,323},{4,324},{5,325},{6,326},{7,327}} | collective-permute-start | bytes 1572872 | tf_op jit(solution)/shard_map/ppermute | solution.py:221
  3.4 24.9 %collective-permute-start.6 = (bf16[512,512]{1,0:T(8,128)(2,1)S(1)}, bf16[512,512]{1,0:T(8,128)(2,1)S(1)}, u32[]{:S(2)}, u32[]{:S(2)}) collective-permute-start(bf16[512,512]{1,0:T(8,128)(2,1)S(1)} %shard_map.86.r0.held), channel_id=1, source_target_pairs={{0,192},{1,193},{2,194},{3,195},{4,196},{5,197},{6,198},{7,199}} | collective-permute-start | bytes 1572872 | tf_op jit(solution)/shard_map/ppermute | solution.py:221
  4.1 10.6 %collective-permute-start = (bf16[512,128]{1,0:T(8,128)(2,1)S(1)}, bf16[512,128]{1,0:T(8,128)(2,1)S(1)}, u32[]{:S(2)}, u32[]{:S(2)}) collective-permute-start(bf16[512,128]{1,0:T(8,128)(2,1)S(1)} %slice_bitcast_fusion.after), channel_id=1, source_target_pairs={{0,8},{8,16},{16,24},{24,32},{32,40},{40,48},{48,56},{56,64},{64,7... | collective-permute-start | bytes 393224 | tf_op jit(solution)/shard_map/ppermute | solution.py:221
  11.9 0.7 copy-start.4
  15.9 24.1 %all-to-all-start = ((bf16[16,8,1024]{2,1,0:T(8,128)(2,1)}), bf16[16,8,1024]{2,1,0:T(8,128)(2,1)S(1)}, u32[]{:S(2)}, u32[]{:S(2)}) async-start(bf16[16,8,1024]{2,1,0:T(8,128)(2,1)} %bitcast.2), calls=%async_computation | async-start | bytes 524288 | tf_op jit(solution)/shard_map/all_to_all | solution.py:284
  28.3 21.1 %copy-start = (bf16[512,512]{1,0:T(8,128)(2,1)S(1)}, bf16[512,512]{1,0:T(8,128)(2,1)}, u32[]{:S(2)}) copy-start(bf16[512,512]{1,0:T(8,128)(2,1)} %inv.5) | copy-start | bytes 1572868
  28.4 21.4 %collective-permute-start.9 = (bf16[512,512]{1,0:T(8,128)(2,1)S(1)}, bf16[512,512]{1,0:T(8,128)(2,1)S(1)}, u32[]{:S(2)}, u32[]{:S(2)}) collective-permute-start(bf16[512,512]{1,0:T(8,128)(2,1)S(1)} %shard_map.91.held), channel_id=1, source_target_pairs={{0,448},{192,256},{1,449},{193,257},{2,450},{194,258},{3,451},{195... | collective-permute-start | bytes 1572872 | tf_op jit(solution)/shard_map/ppermute | solution.py:221
  29.2 20.6 %collective-permute-start.8 = (bf16[512,512]{1,0:T(8,128)(2,1)S(1)}, bf16[512,512]{1,0:T(8,128)(2,1)S(1)}, u32[]{:S(2)}, u32[]{:S(2)}) collective-permute-start(bf16[512,512]{1,0:T(8,128)(2,1)S(1)} %shard_map.91.held), channel_id=1, source_target_pairs={{0,64},{192,128},{320,384},{1,65},{193,129},{321,385},{2,66},{194,... | collective-permute-start | bytes 1572872 | tf_op jit(solution)/shard_map/ppermute | solution.py:221
  40.0 9.2 %collective-permute-start.3 = (f32[8,1024]{1,0:T(8,128)S(1)}, f32[8,1024]{1,0:T(8,128)S(1)}, u32[]{:S(2)}, u32[]{:S(2)}) collective-permute-start(f32[8,1024]{1,0:T(8,128)S(1)} %shard_map.89.x0), channel_id=1, source_target_pairs={{32,0},{33,1},{34,2},{35,3},{36,4},{37,5},{38,6},{39,7},{40,8},{41... | collective-permute-start | bytes 98312 | tf_op jit(solution)/shard_map/ppermute | solution.py:221
  41.3 8.1 %collective-permute-start.2 = (f32[8,1024]{1,0:T(8,128)S(1)}, f32[8,1024]{1,0:T(8,128)S(1)}, u32[]{:S(2)}, u32[]{:S(2)}) collective-permute-start(f32[8,1024]{1,0:T(8,128)S(1)} %shard_map.89.x0), channel_id=1, source_target_pairs={{48,0},{49,1},{50,2},{51,3},{52,4},{53,5},{54,6},{55,7},{56,8},{57... | collective-permute-start | bytes 98312 | tf_op jit(solution)/shard_map/ppermute | solution.py:221
  42.6 6.8 %collective-permute-start.1 = (f32[8,1024]{1,0:T(8,128)S(1)}, f32[8,1024]{1,0:T(8,128)S(1)}, u32[]{:S(2)}, u32[]{:S(2)}) collective-permute-start(f32[8,1024]{1,0:T(8,128)S(1)} %shard_map.89.x0), channel_id=1, source_target_pairs={{16,0},{17,1},{18,2},{19,3},{20,4},{21,5},{22,6},{23,7},{24,8},{25... | collective-permute-start | bytes 98312 | tf_op jit(solution)/shard_map/ppermute | solution.py:221
  49.8 10.1 %copy-start.2 = (bf16[512,256]{1,0:T(8,128)(2,1)S(1)}, bf16[512,256]{1,0:T(8,128)(2,1)}, u32[]{:S(2)}) copy-start(bf16[512,256]{1,0:T(8,128)(2,1)} %tra.3) | copy-start | bytes 786436
  49.9 10.0 %collective-permute-start.10 = (bf16[512,512]{1,0:T(8,128)(2,1)S(1)}, bf16[512,512]{1,0:T(8,128)(2,1)S(1)}, u32[]{:S(2)}, u32[]{:S(2)}) collective-permute-start(bf16[512,512]{1,0:T(8,128)(2,1)S(1)} %shard_map.92.r0_even), channel_id=1, source_target_pairs={{0,8},{64,72},{128,136},{192,200},{256,264},{320,328},{384,392},{4... | collective-permute-start | bytes 1572872 | tf_op jit(solution)/shard_map/ppermute | solution.py:221
  51.2 8.0 %collective-permute-start.4 = (bf16[8,128]{1,0:T(8,128)(2,1)S(1)}, bf16[8,128]{1,0:T(8,128)(2,1)S(1)}, u32[]{:S(2)}, u32[]{:S(2)}) collective-permute-start(bf16[8,128]{1,0:T(8,128)(2,1)S(1)} %get-tuple-element.30), channel_id=1, source_target_pairs={{0,1},{1,2},{2,3},{3,4},{4,5},{5,6},{6,7},{7,0},{8,9},{9,10},{10,1... | collective-permute-start | bytes 6152 | tf_op jit(solution)/shard_map/ppermute | solution.py:221
  55.0 4.8 %collective-permute-start.5 = (bf16[8,128]{1,0:T(8,128)(2,1)S(1)}, bf16[8,128]{1,0:T(8,128)(2,1)S(1)}, u32[]{:S(2)}, u32[]{:S(2)}) collective-permute-start(bf16[8,128]{1,0:T(8,128)(2,1)S(1)} %get-tuple-element.31), channel_id=1, source_target_pairs={{1,0},{2,1},{3,2},{4,3},{5,4},{6,5},{7,6},{0,7},{9,8},{10,9},{11,1... | collective-permute-start | bytes 6152 | tf_op jit(solution)/shard_map/ppermute | solution.py:221
  60.8 7.7 %collective-permute-start.11 = (bf16[8,128]{1,0:T(8,128)(2,1)S(1)}, bf16[8,128]{1,0:T(8,128)(2,1)S(1)}, u32[]{:S(2)}, u32[]{:S(2)}) collective-permute-start(bf16[8,128]{1,0:T(8,128)(2,1)S(1)} %get-tuple-element.34), channel_id=1, source_target_pairs={{0,1},{1,2},{2,3},{3,4},{4,5},{5,6},{6,7},{7,0},{8,9},{9,10},{10,1... | collective-permute-start | bytes 6152 | tf_op jit(solution)/shard_map/ppermute | solution.py:221
  63.6 5.6 %collective-permute-start.12 = (bf16[8,128]{1,0:T(8,128)(2,1)S(1)}, bf16[8,128]{1,0:T(8,128)(2,1)S(1)}, u32[]{:S(2)}, u32[]{:S(2)}) collective-permute-start(bf16[8,128]{1,0:T(8,128)(2,1)S(1)} %get-tuple-element.35), channel_id=1, source_target_pairs={{1,0},{2,1},{3,2},{4,3},{5,4},{6,5},{7,6},{0,7},{9,8},{10,9},{11,1... | collective-permute-start | bytes 6152 | tf_op jit(solution)/shard_map/ppermute | solution.py:221
  70.2 18.3 %all-to-all-start.1 = ((bf16[16,16,512]{2,1,0:T(8,128)(2,1)}), bf16[16,16,512]{2,1,0:T(8,128)(2,1)S(1)}, u32[]{:S(2)}, u32[]{:S(2)}) async-start(bf16[16,16,512]{2,1,0:T(8,128)(2,1)} %get-tuple-element.36), calls=%async_computation.1 | async-start | bytes 524288 | tf_op jit(solution)/shard_map/all_to_all | solution.py:320
  76.7 10.1 %collective-permute-start.16 = (bf16[512,128]{1,0:T(8,128)(2,1)S(1)}, bf16[512,128]{1,0:T(8,128)(2,1)S(1)}, u32[]{:S(2)}, u32[]{:S(2)}) collective-permute-start(bf16[512,128]{1,0:T(8,128)(2,1)S(1)} %get-tuple-element.41), channel_id=1, source_target_pairs={{0,8},{8,16},{16,24},{24,32},{32,40},{40,48},{48,56},{56,64},{64,7... | collective-permute-start | bytes 393224 | tf_op jit(solution)/shard_map/ppermute | solution.py:221
  78.6 8.2 %collective-permute-start.13 = (f32[2,2,512]{2,1,0:T(2,128)S(1)}, f32[2,2,512]{2,1,0:T(2,128)S(1)}, u32[]{:S(2)}, u32[]{:S(2)}) collective-permute-start(f32[2,2,512]{2,1,0:T(2,128)S(1)} %get-tuple-element.38), channel_id=1, source_target_pairs={{0,16},{8,24},{64,80},{72,88},{128,144},{136,152},{192,208},{200,2... | collective-permute-start | bytes 24584 | tf_op jit(solution)/shard_map/ppermute | solution.py:221
  79.9 6.9 %collective-permute-start.14 = (f32[2,2,512]{2,1,0:T(2,128)S(1)}, f32[2,2,512]{2,1,0:T(2,128)S(1)}, u32[]{:S(2)}, u32[]{:S(2)}) collective-permute-start(f32[2,2,512]{2,1,0:T(2,128)S(1)} %get-tuple-element.39), channel_id=1, source_target_pairs={{0,32},{8,40},{64,96},{72,104},{128,160},{136,168},{192,224},{200,... | collective-permute-start | bytes 24584 | tf_op jit(solution)/shard_map/ppermute | solution.py:221
  81.2 6.3 %collective-permute-start.15 = (f32[2,2,512]{2,1,0:T(2,128)S(1)}, f32[2,2,512]{2,1,0:T(2,128)S(1)}, u32[]{:S(2)}, u32[]{:S(2)}) collective-permute-start(f32[2,2,512]{2,1,0:T(2,128)S(1)} %get-tuple-element.40), channel_id=1, source_target_pairs={{0,48},{8,56},{64,112},{72,120},{128,176},{136,184},{192,240},{200... | collective-permute-start | bytes 24584 | tf_op jit(solution)/shard_map/ppermute | solution.py:221

commit v9 on v8

--- a/solution.py
+++ b/solution.py
@@ -148,30 +148,32 @@
 
     @pl.when(odd)
     def _():
-        copied(r0_odd, r0, sem)
+        pltpu.make_async_copy(r0_odd, r0, sem).start()
 
     @pl.when(jnp.logical_not(odd))
     def _():
-        copied(r0_even, r0, sem)
+        pltpu.make_async_copy(r0_even, r0, sem).start()
 
     cur = first[...] - coupled(up, down, inv, tra)
     cur_ref[...] = cur
     alive = (counts[0] > 0).astype(F32)
+    pltpu.make_async_copy(r0_even, r0, sem).wait()
     newest = dot_t(cur.astype(BF16), r0[...]) * alive
     following = dot_t((rest[...] - newest).astype(BF16), inv[...])
     first_ref[...] = following
     trace_of(following, select, up_ref, down_ref)
 
 
-def second_current(cur0, first, up, down, inv, tra, gather_ref, *share_refs):
+def second_current(cur0, first, up, down, inv, tra, gather_ref, s0, s1, s2, s3, both, sem):
     cur1 = first[...] - coupled(up, down, inv, tra)
     c0 = cur0[...]
-    both = jnp.concatenate([cur1.astype(BF16), c0.astype(BF16)], axis=0)
-    for i in range(gather_ref.shape[0]):
-        gather_ref[i] = both
-    for i, share in enumerate(share_refs):
+    both[...] = jnp.concatenate([cur1.astype(BF16), c0.astype(BF16)], axis=0)
+    copy = pltpu.make_async_copy(both, gather_ref.at[0], sem)
+    copy.start()
+    for i, share in enumerate((s0, s1, s2, s3)):
         share[0] = c0[2 * i : 2 * i + 2]
         share[1] = cur1[2 * i : 2 * i + 2]
+    copy.wait()
 
 
 def finish(gathered, s0, s1, s2, s3, before0, before1, cur_ref, hist_ref):
@@ -185,7 +187,8 @@
         order = permutation(owners * cols)
         for slot in range(2):
             both = gathered[:, slot * cols : (slot + 1) * cols, :].reshape(owners * cols, -1)
-            hist_ref[slot] = dot_t(both.astype(F32).T.astype(BF16), order).astype(BF16)
+            turned = lax.dot_general(both, order, (((0,), (1,)), ((), ())), preferred_element_type=F32)
+            hist_ref[slot] = turned.astype(BF16)
 
     @pl.when(jnp.logical_not(leading))
     def _():
@@ -316,6 +319,8 @@
         [VMEM] * 6,
         2 * 8 * n * n * 2,
         1024 * 1024,
+        out_specs=[any_spec] + [VMEM] * ZH,
+        scratch_shapes=[pltpu.VMEM((2 * cols, n), BF16), pltpu.SemaphoreType.DMA],
     )(cur0, first, up, down, inverse, transfer)
     gather = lax.all_to_all(gather, ("y", "c"), 0, 0, tiled=True)
     for z in range(1, ZH):

time: 90 us -> 90 us (level)
  no operation moved by 1% of the time
where the time goes in v9:
time: 90 us; the launch traced here: 89.3 us
  starting transfers between devices  59.7 us (66%)
  waiting for transfers between devices  18.8 us (21%)
  Pallas kernels  7.63 us (8%)
  local copies, waits for them, and re-layouts  1.6 us (2%)
  between operations  1.59 us (2%)
    ppermute x17, starting transfers between devices, permute(): return lax.ppermute(value, axes, pairs)  40.9 us
    all_to_all x1, starting transfers between devices, body(): lax.all_to_all(packed.reshape(OWNERS, cols, lanes), ('y', 'c'), 0, 0, til...  12.3 us
    all_to_all x1, waiting for transfers between devices, body(): lax.all_to_all(packed.reshape(OWNERS, cols, lanes), ('y', 'c'), 0, 0, til...  10.1 us
    ppermute x17, waiting for transfers between devices, permute(): return lax.ppermute(value, axes, pairs)  7.67 us
    all_to_all x1, starting transfers between devices, body(): gather = lax.all_to_all(gather, ('y', 'c'), 0, 0, tiled=True)  6.49 us
    pallas_call x1, Pallas kernels, body(): call(own_partials, (shape((width, n), BF16), shape((width, n), F32), shap...  2.05 us
  transfers between devices with their start and end apart: 19, of which 7 were waited for; matrix products, arithmetic and copies ran while one was open for 0% of the time, Pallas kernels for 4%

profile of v9, /device:TPU:1, one launch (start us, length us, event | category | flops | bytes accessed | tf_op | source)
XLA Modules:
  0.0 89.3 jit_solution(1708544837750905603)
XLA Ops:
  0.6 0.9 %slice_bitcast_fusion.after = bf16[512,128]{1,0:T(8,128)(2,1)S(1)} fusion(bf16[2,512,128]{2,1,0:T(8,128)(2,1)} %hist.3), kind=kLoop, calls=%fused_computation | loop fusion | bytes 262144 | tf_op jit(solution)/shard_map/squeeze | solution.py:257
  1.6 1.1 %shard_map.86.r0.held = bf16[512,512]{1,0:T(8,128)(2,1)S(1)} custom-call(bf16[2,512,512]{2,1,0:T(8,128)(2,1)} %ret.3, bf16[512,128]{1,0:T(8,128)(2,1)S(1)} %slice_bitcast_fusion.after), custom_call_target="tpu_custom_call" | custom-call | bytes 1048576 | tf_op jit(solution)/shard_map/pallas_call | solution.py:259
  2.7 0.7 collective-permute-start.7
  3.4 0.7 collective-permute-start.6
  4.1 7.2 %collective-permute-start = (bf16[512,128]{1,0:T(8,128)(2,1)S(1)}, bf16[512,128]{1,0:T(8,128)(2,1)S(1)}, u32[]{:S(2)}, u32[]{:S(2)}) collective-permute-start(bf16[512,128]{1,0:T(8,128)(2,1)S(1)} %slice_bitcast_fusion.after), channel_id=1, source_target_pairs={{0,8},{8,16},{16,24},{24,32},{32,40},{40,48},{48,56},{56,64},{64,7... | collective-permute-start | bytes 393224 | tf_op jit(solution)/shard_map/ppermute | solution.py:224
  12.6 2.0 %shard_map.87 = (bf16[128,512]{1,0:T(8,128)(2,1)S(1)}, f32[128,512]{1,0:T(8,128)S(1)}, bf16[512,256]{1,0:T(8,128)(2,1)S(1)}, bf16[128,128]{1,0:T(8,128)(2,1)S(1)}) custom-call(s32[1]{0:T(128)S(6)} %copy.9.counts, f32[2,2,512]{2,1,0:T(2,128)S(1)} %bitcast.5, s32[1,256]{1,0:T(1,128)S(1)} %copy-done.4, bf16[2,512,128]{2,1,0:T(8,128)(2,1)S(1)} %copy-done.1, ...), custom_call_target="tpu_custom_call" | custom-call | flops 268435456 | bytes 2097152 | tf_op jit(solution)/shard_map/pallas_call | solution.py:268
  14.7 1.2 %shard_map.88 = (bf16[128,1024]{1,0:T(8,128)(2,1)}, bf16[512,128]{1,0:T(8,128)(2,1)S(1)}) custom-call(s32[1]{0:T(128)S(6)} %copy.9.counts, bf16[128,128]{1,0:T(8,128)(2,1)S(1)} %get-tuple-element.23.order, bf16[128,512]{1,0:T(8,128)(2,1)S(1)} %get-tuple-element.24.d0, f32[128,512]{1,0:T(8,128)S(1)} %get-tuple-element.25.d1, ...), custom_call_target="tpu_custom_call" | custom-call | flops 67108864 | bytes 1048576 | tf_op jit(solution)/shard_map/pallas_call | solution.py:279
  15.9 12.3 %all-to-all-start = ((bf16[16,8,1024]{2,1,0:T(8,128)(2,1)}), bf16[16,8,1024]{2,1,0:T(8,128)(2,1)S(1)}, u32[]{:S(2)}, u32[]{:S(2)}) async-start(bf16[16,8,1024]{2,1,0:T(8,128)(2,1)} %bitcast.2), calls=%async_computation | async-start | bytes 524288 | tf_op jit(solution)/shard_map/all_to_all | solution.py:287
  28.4 0.8 collective-permute-start.9
  29.2 0.7 collective-permute-start.8
  29.9 10.1 %all-to-all-done.x = bf16[16,8,1024]{2,1,0:T(8,128)(2,1)S(1)} async-done(((bf16[16,8,1024]{2,1,0:T(8,128)(2,1)}), bf16[16,8,1024]{2,1,0:T(8,128)(2,1)S(1)}, u32[]{:S(2)}, u32[]{:S(2)}) %all-to-all-start) | async-done | bytes 262176 | tf_op jit(solution)/shard_map/all_to_all | solution.py:287
  40.0 1.3 %collective-permute-start.3 = (f32[8,1024]{1,0:T(8,128)S(1)}, f32[8,1024]{1,0:T(8,128)S(1)}, u32[]{:S(2)}, u32[]{:S(2)}) collective-permute-start(f32[8,1024]{1,0:T(8,128)S(1)} %shard_map.89.x0), channel_id=1, source_target_pairs={{32,0},{33,1},{34,2},{35,3},{36,4},{37,5},{38,6},{39,7},{40,8},{41... | collective-permute-start | bytes 98312 | tf_op jit(solution)/shard_map/ppermute | solution.py:224
  41.3 1.3 %collective-permute-start.2 = (f32[8,1024]{1,0:T(8,128)S(1)}, f32[8,1024]{1,0:T(8,128)S(1)}, u32[]{:S(2)}, u32[]{:S(2)}) collective-permute-start(f32[8,1024]{1,0:T(8,128)S(1)} %shard_map.89.x0), channel_id=1, source_target_pairs={{48,0},{49,1},{50,2},{51,3},{52,4},{53,5},{54,6},{55,7},{56,8},{57... | collective-permute-start | bytes 98312 | tf_op jit(solution)/shard_map/ppermute | solution.py:224
  42.6 1.3 %collective-permute-start.1 = (f32[8,1024]{1,0:T(8,128)S(1)}, f32[8,1024]{1,0:T(8,128)S(1)}, u32[]{:S(2)}, u32[]{:S(2)}) collective-permute-start(f32[8,1024]{1,0:T(8,128)S(1)} %shard_map.89.x0), channel_id=1, source_target_pairs={{16,0},{17,1},{18,2},{19,3},{20,4},{21,5},{22,6},{23,7},{24,8},{25... | collective-permute-start | bytes 98312 | tf_op jit(solution)/shard_map/ppermute | solution.py:224
  43.9 5.3 %collective-permute-done.3.x3 = f32[8,1024]{1,0:T(8,128)S(1)} collective-permute-done((f32[8,1024]{1,0:T(8,128)S(1)}, f32[8,1024]{1,0:T(8,128)S(1)}, u32[]{:S(2)}, u32[]{:S(2)}) %collective-permute-start.3) | collective-permute-done | bytes 32800 | tf_op jit(solution)/shard_map/ppermute | solution.py:224
  49.9 1.3 %collective-permute-start.10 = (bf16[512,512]{1,0:T(8,128)(2,1)S(1)}, bf16[512,512]{1,0:T(8,128)(2,1)S(1)}, u32[]{:S(2)}, u32[]{:S(2)}) collective-permute-start(bf16[512,512]{1,0:T(8,128)(2,1)S(1)} %shard_map.92.r0_even), channel_id=1, source_target_pairs={{0,8},{64,72},{128,136},{192,200},{256,264},{320,328},{384,392},{4... | collective-permute-start | bytes 1572872 | tf_op jit(solution)/shard_map/ppermute | solution.py:224
  51.2 3.8 %collective-permute-start.4 = (bf16[8,128]{1,0:T(8,128)(2,1)S(1)}, bf16[8,128]{1,0:T(8,128)(2,1)S(1)}, u32[]{:S(2)}, u32[]{:S(2)}) collective-permute-start(bf16[8,128]{1,0:T(8,128)(2,1)S(1)} %get-tuple-element.30), channel_id=1, source_target_pairs={{0,1},{1,2},{2,3},{3,4},{4,5},{5,6},{6,7},{7,0},{8,9},{9,10},{10,1... | collective-permute-start | bytes 6152 | tf_op jit(solution)/shard_map/ppermute | solution.py:224
  55.0 4.1 %collective-permute-start.5 = (bf16[8,128]{1,0:T(8,128)(2,1)S(1)}, bf16[8,128]{1,0:T(8,128)(2,1)S(1)}, u32[]{:S(2)}, u32[]{:S(2)}) collective-permute-start(bf16[8,128]{1,0:T(8,128)(2,1)S(1)} %get-tuple-element.31), channel_id=1, source_target_pairs={{1,0},{2,1},{3,2},{4,3},{5,4},{6,5},{7,6},{0,7},{9,8},{10,9},{11,1... | collective-permute-start | bytes 6152 | tf_op jit(solution)/shard_map/ppermute | solution.py:224
  59.2 0.7 collective-permute-done.5.down
  59.9 1.0 %shard_map.93 = (f32[8,512]{1,0:T(8,128)S(1)}, f32[8,512]{1,0:T(8,128)S(1)}, bf16[8,128]{1,0:T(8,128)(2,1)S(1)}, bf16[8,128]{1,0:T(8,128)(2,1)S(1)}) custom-call(s32[1]{0:T(128)S(6)} %copy.9.counts, f32[8,512]{1,0:T(8,128)S(1)} %get-tuple-element.28.first, f32[8,512]{1,0:T(8,128)S(1)} %get-tuple-element.29.after.rest, ...), custom_call_target="tpu_custom_call" | custom-call | flops 20971520 | bytes 2097152 | tf_op jit(solution)/shard_map/pallas_call | solution.py:307
  60.9 2.8 %collective-permute-start.11 = (bf16[8,128]{1,0:T(8,128)(2,1)S(1)}, bf16[8,128]{1,0:T(8,128)(2,1)S(1)}, u32[]{:S(2)}, u32[]{:S(2)}) collective-permute-start(bf16[8,128]{1,0:T(8,128)(2,1)S(1)} %get-tuple-element.34), channel_id=1, source_target_pairs={{0,1},{1,2},{2,3},{3,4},{4,5},{5,6},{6,7},{7,0},{8,9},{9,10},{10,1... | collective-permute-start | bytes 6152 | tf_op jit(solution)/shard_map/ppermute | solution.py:224
  63.6 4.9 %collective-permute-start.12 = (bf16[8,128]{1,0:T(8,128)(2,1)S(1)}, bf16[8,128]{1,0:T(8,128)(2,1)S(1)}, u32[]{:S(2)}, u32[]{:S(2)}) collective-permute-start(bf16[8,128]{1,0:T(8,128)(2,1)S(1)} %get-tuple-element.35), channel_id=1, source_target_pairs={{1,0},{2,1},{3,2},{4,3},{5,4},{6,5},{7,6},{0,7},{9,8},{10,9},{11,1... | collective-permute-start | bytes 6152 | tf_op jit(solution)/shard_map/ppermute | solution.py:224
  68.5 0.7 collective-permute-done.12.down
  69.2 1.0 %shard_map.94 = (bf16[16,16,512]{2,1,0:T(8,128)(2,1)}, f32[2,2,512]{2,1,0:T(2,128)S(1)}, f32[2,2,512]{2,1,0:T(2,128)S(1)}, f32[2,2,512]{2,1,0:T(2,128)S(1)}, f32[2,2,512]{2,1,0:T(2,128)S(1)}) custom-call(f32[8,512]{1,0:T(8,128)S(1)} %get-tuple-element.32.cur0, f32[8,512]{1,0:T(8,128)S(1)} %get-tuple-element.33.first, ...), custom_call_target="tpu_custom_call" | custom-call | flops 8388608 | bytes 1048576 | tf_op jit(solution)/shard_map/pallas_call | solution.py:316
  70.2 6.5 %all-to-all-start.1 = ((bf16[16,16,512]{2,1,0:T(8,128)(2,1)}), bf16[16,16,512]{2,1,0:T(8,128)(2,1)S(1)}, u32[]{:S(2)}, u32[]{:S(2)}) async-start(bf16[16,16,512]{2,1,0:T(8,128)(2,1)} %get-tuple-element.36), calls=%async_computation.1 | async-start | bytes 524288 | tf_op jit(solution)/shard_map/all_to_all | solution.py:325
  76.7 1.9 %collective-permute-start.16 = (bf16[512,128]{1,0:T(8,128)(2,1)S(1)}, bf16[512,128]{1,0:T(8,128)(2,1)S(1)}, u32[]{:S(2)}, u32[]{:S(2)}) collective-permute-start(bf16[512,128]{1,0:T(8,128)(2,1)S(1)} %get-tuple-element.41), channel_id=1, source_target_pairs={{0,8},{8,16},{16,24},{24,32},{32,40},{40,48},{48,56},{56,64},{64,7... | collective-permute-start | bytes 393224 | tf_op jit(solution)/shard_map/ppermute | solution.py:224
  78.6 1.3 %collective-permute-start.13 = (f32[2,2,512]{2,1,0:T(2,128)S(1)}, f32[2,2,512]{2,1,0:T(2,128)S(1)}, u32[]{:S(2)}, u32[]{:S(2)}) collective-permute-start(f32[2,2,512]{2,1,0:T(2,128)S(1)} %get-tuple-element.38), channel_id=1, source_target_pairs={{0,16},{8,24},{64,80},{72,88},{128,144},{136,152},{192,208},{200,2... | collective-permute-start | bytes 24584 | tf_op jit(solution)/shard_map/ppermute | solution.py:224
  79.9 1.3 %collective-permute-start.14 = (f32[2,2,512]{2,1,0:T(2,128)S(1)}, f32[2,2,512]{2,1,0:T(2,128)S(1)}, u32[]{:S(2)}, u32[]{:S(2)}) collective-permute-start(f32[2,2,512]{2,1,0:T(2,128)S(1)} %get-tuple-element.39), channel_id=1, source_target_pairs={{0,32},{8,40},{64,96},{72,104},{128,160},{136,168},{192,224},{200,... | collective-permute-start | bytes 24584 | tf_op jit(solution)/shard_map/ppermute | solution.py:224
  81.2 5.6 %collective-permute-start.15 = (f32[2,2,512]{2,1,0:T(2,128)S(1)}, f32[2,2,512]{2,1,0:T(2,128)S(1)}, u32[]{:S(2)}, u32[]{:S(2)}) collective-permute-start(f32[2,2,512]{2,1,0:T(2,128)S(1)} %get-tuple-element.40), channel_id=1, source_target_pairs={{0,48},{8,56},{64,112},{72,120},{128,176},{136,184},{192,240},{200... | collective-permute-start | bytes 24584 | tf_op jit(solution)/shard_map/ppermute | solution.py:224
  86.8 0.7 collective-permute-done.15.s3
  87.6 1.0 %all-to-all-done.1.gathered = bf16[16,16,512]{2,1,0:T(8,128)(2,1)S(1)} async-done(((bf16[16,16,512]{2,1,0:T(8,128)(2,1)}), bf16[16,16,512]{2,1,0:T(8,128)(2,1)S(1)}, u32[]{:S(2)}, u32[]{:S(2)}) %all-to-all-start.1) | async-done | bytes 262176 | tf_op jit(solution)/shard_map/all_to_all | solution.py:325
  88.6 0.7 shard_map.95
  (27 shorter events, 1.5 us)
Async XLA Ops:
  1.5 10.4 %copy-start.1 = (bf16[2,512,128]{2,1,0:T(8,128)(2,1)S(1)}, bf16[2,512,128]{2,1,0:T(8,128)(2,1)}, u32[]{:S(2)}) copy-start(bf16[2,512,128]{2,1,0:T(8,128)(2,1)} %hist.3) | copy-start | bytes 786436
  1.6 10.4 %copy-start.3 = (f32[2,512,2]{1,2,0:T(2,128)S(1)}, f32[2,512,2]{1,2,0:T(2,128)}, u32[]{:S(2)}) copy-start(f32[2,512,2]{1,2,0:T(2,128)} %param.7) | copy-start | bytes 24580
  2.7 25.6 %collective-permute-start.7 = (bf16[512,512]{1,0:T(8,128)(2,1)S(1)}, bf16[512,512]{1,0:T(8,128)(2,1)S(1)}, u32[]{:S(2)}, u32[]{:S(2)}) collective-permute-start(bf16[512,512]{1,0:T(8,128)(2,1)S(1)} %shard_map.86.r0.held), channel_id=1, source_target_pairs={{0,320},{1,321},{2,322},{3,323},{4,324},{5,325},{6,326},{7,327}} | collective-permute-start | bytes 1572872 | tf_op jit(solution)/shard_map/ppermute | solution.py:224
  3.4 24.9 %collective-permute-start.6 = (bf16[512,512]{1,0:T(8,128)(2,1)S(1)}, bf16[512,512]{1,0:T(8,128)(2,1)S(1)}, u32[]{:S(2)}, u32[]{:S(2)}) collective-permute-start(bf16[512,512]{1,0:T(8,128)(2,1)S(1)} %shard_map.86.r0.held), channel_id=1, source_target_pairs={{0,192},{1,193},{2,194},{3,195},{4,196},{5,197},{6,198},{7,199}} | collective-permute-start | bytes 1572872 | tf_op jit(solution)/shard_map/ppermute | solution.py:224
  4.1 10.6 %collective-permute-start = (bf16[512,128]{1,0:T(8,128)(2,1)S(1)}, bf16[512,128]{1,0:T(8,128)(2,1)S(1)}, u32[]{:S(2)}, u32[]{:S(2)}) collective-permute-start(bf16[512,128]{1,0:T(8,128)(2,1)S(1)} %slice_bitcast_fusion.after), channel_id=1, source_target_pairs={{0,8},{8,16},{16,24},{24,32},{32,40},{40,48},{48,56},{56,64},{64,7... | collective-permute-start | bytes 393224 | tf_op jit(solution)/shard_map/ppermute | solution.py:224
  11.9 0.7 copy-start.4
  15.9 24.1 %all-to-all-start = ((bf16[16,8,1024]{2,1,0:T(8,128)(2,1)}), bf16[16,8,1024]{2,1,0:T(8,128)(2,1)S(1)}, u32[]{:S(2)}, u32[]{:S(2)}) async-start(bf16[16,8,1024]{2,1,0:T(8,128)(2,1)} %bitcast.2), calls=%async_computation | async-start | bytes 524288 | tf_op jit(solution)/shard_map/all_to_all | solution.py:287
  28.3 21.1 %copy-start = (bf16[512,512]{1,0:T(8,128)(2,1)S(1)}, bf16[512,512]{1,0:T(8,128)(2,1)}, u32[]{:S(2)}) copy-start(bf16[512,512]{1,0:T(8,128)(2,1)} %inv.5) | copy-start | bytes 1572868
  28.4 21.4 %collective-permute-start.9 = (bf16[512,512]{1,0:T(8,128)(2,1)S(1)}, bf16[512,512]{1,0:T(8,128)(2,1)S(1)}, u32[]{:S(2)}, u32[]{:S(2)}) collective-permute-start(bf16[512,512]{1,0:T(8,128)(2,1)S(1)} %shard_map.91.held), channel_id=1, source_target_pairs={{0,448},{192,256},{1,449},{193,257},{2,450},{194,258},{3,451},{195... | collective-permute-start | bytes 1572872 | tf_op jit(solution)/shard_map/ppermute | solution.py:224
  29.2 20.6 %collective-permute-start.8 = (bf16[512,512]{1,0:T(8,128)(2,1)S(1)}, bf16[512,512]{1,0:T(8,128)(2,1)S(1)}, u32[]{:S(2)}, u32[]{:S(2)}) collective-permute-start(bf16[512,512]{1,0:T(8,128)(2,1)S(1)} %shard_map.91.held), channel_id=1, source_target_pairs={{0,64},{192,128},{320,384},{1,65},{193,129},{321,385},{2,66},{194,... | collective-permute-start | bytes 1572872 | tf_op jit(solution)/shard_map/ppermute | solution.py:224
  40.0 9.2 %collective-permute-start.3 = (f32[8,1024]{1,0:T(8,128)S(1)}, f32[8,1024]{1,0:T(8,128)S(1)}, u32[]{:S(2)}, u32[]{:S(2)}) collective-permute-start(f32[8,1024]{1,0:T(8,128)S(1)} %shard_map.89.x0), channel_id=1, source_target_pairs={{32,0},{33,1},{34,2},{35,3},{36,4},{37,5},{38,6},{39,7},{40,8},{41... | collective-permute-start | bytes 98312 | tf_op jit(solution)/shard_map/ppermute | solution.py:224
  41.3 8.1 %collective-permute-start.2 = (f32[8,1024]{1,0:T(8,128)S(1)}, f32[8,1024]{1,0:T(8,128)S(1)}, u32[]{:S(2)}, u32[]{:S(2)}) collective-permute-start(f32[8,1024]{1,0:T(8,128)S(1)} %shard_map.89.x0), channel_id=1, source_target_pairs={{48,0},{49,1},{50,2},{51,3},{52,4},{53,5},{54,6},{55,7},{56,8},{57... | collective-permute-start | bytes 98312 | tf_op jit(solution)/shard_map/ppermute | solution.py:224
  42.6 6.8 %collective-permute-start.1 = (f32[8,1024]{1,0:T(8,128)S(1)}, f32[8,1024]{1,0:T(8,128)S(1)}, u32[]{:S(2)}, u32[]{:S(2)}) collective-permute-start(f32[8,1024]{1,0:T(8,128)S(1)} %shard_map.89.x0), channel_id=1, source_target_pairs={{16,0},{17,1},{18,2},{19,3},{20,4},{21,5},{22,6},{23,7},{24,8},{25... | collective-permute-start | bytes 98312 | tf_op jit(solution)/shard_map/ppermute | solution.py:224
  49.8 10.1 %copy-start.2 = (bf16[512,256]{1,0:T(8,128)(2,1)S(1)}, bf16[512,256]{1,0:T(8,128)(2,1)}, u32[]{:S(2)}) copy-start(bf16[512,256]{1,0:T(8,128)(2,1)} %tra.3) | copy-start | bytes 786436
  49.9 10.0 %collective-permute-start.10 = (bf16[512,512]{1,0:T(8,128)(2,1)S(1)}, bf16[512,512]{1,0:T(8,128)(2,1)S(1)}, u32[]{:S(2)}, u32[]{:S(2)}) collective-permute-start(bf16[512,512]{1,0:T(8,128)(2,1)S(1)} %shard_map.92.r0_even), channel_id=1, source_target_pairs={{0,8},{64,72},{128,136},{192,200},{256,264},{320,328},{384,392},{4... | collective-permute-start | bytes 1572872 | tf_op jit(solution)/shard_map/ppermute | solution.py:224
  51.2 8.0 %collective-permute-start.4 = (bf16[8,128]{1,0:T(8,128)(2,1)S(1)}, bf16[8,128]{1,0:T(8,128)(2,1)S(1)}, u32[]{:S(2)}, u32[]{:S(2)}) collective-permute-start(bf16[8,128]{1,0:T(8,128)(2,1)S(1)} %get-tuple-element.30), channel_id=1, source_target_pairs={{0,1},{1,2},{2,3},{3,4},{4,5},{5,6},{6,7},{7,0},{8,9},{9,10},{10,1... | collective-permute-start | bytes 6152 | tf_op jit(solution)/shard_map/ppermute | solution.py:224
  55.0 4.8 %collective-permute-start.5 = (bf16[8,128]{1,0:T(8,128)(2,1)S(1)}, bf16[8,128]{1,0:T(8,128)(2,1)S(1)}, u32[]{:S(2)}, u32[]{:S(2)}) collective-permute-start(bf16[8,128]{1,0:T(8,128)(2,1)S(1)} %get-tuple-element.31), channel_id=1, source_target_pairs={{1,0},{2,1},{3,2},{4,3},{5,4},{6,5},{7,6},{0,7},{9,8},{10,9},{11,1... | collective-permute-start | bytes 6152 | tf_op jit(solution)/shard_map/ppermute | solution.py:224
  60.9 7.7 %collective-permute-start.11 = (bf16[8,128]{1,0:T(8,128)(2,1)S(1)}, bf16[8,128]{1,0:T(8,128)(2,1)S(1)}, u32[]{:S(2)}, u32[]{:S(2)}) collective-permute-start(bf16[8,128]{1,0:T(8,128)(2,1)S(1)} %get-tuple-element.34), channel_id=1, source_target_pairs={{0,1},{1,2},{2,3},{3,4},{4,5},{5,6},{6,7},{7,0},{8,9},{9,10},{10,1... | collective-permute-start | bytes 6152 | tf_op jit(solution)/shard_map/ppermute | solution.py:224
  63.6 5.6 %collective-permute-start.12 = (bf16[8,128]{1,0:T(8,128)(2,1)S(1)}, bf16[8,128]{1,0:T(8,128)(2,1)S(1)}, u32[]{:S(2)}, u32[]{:S(2)}) collective-permute-start(bf16[8,128]{1,0:T(8,128)(2,1)S(1)} %get-tuple-element.35), channel_id=1, source_target_pairs={{1,0},{2,1},{3,2},{4,3},{5,4},{6,5},{7,6},{0,7},{9,8},{10,9},{11,1... | collective-permute-start | bytes 6152 | tf_op jit(solution)/shard_map/ppermute | solution.py:224
  70.2 18.3 %all-to-all-start.1 = ((bf16[16,16,512]{2,1,0:T(8,128)(2,1)}), bf16[16,16,512]{2,1,0:T(8,128)(2,1)S(1)}, u32[]{:S(2)}, u32[]{:S(2)}) async-start(bf16[16,16,512]{2,1,0:T(8,128)(2,1)} %get-tuple-element.36), calls=%async_computation.1 | async-start | bytes 524288 | tf_op jit(solution)/shard_map/all_to_all | solution.py:325
  76.7 10.1 %collective-permute-start.16 = (bf16[512,128]{1,0:T(8,128)(2,1)S(1)}, bf16[512,128]{1,0:T(8,128)(2,1)S(1)}, u32[]{:S(2)}, u32[]{:S(2)}) collective-permute-start(bf16[512,128]{1,0:T(8,128)(2,1)S(1)} %get-tuple-element.41), channel_id=1, source_target_pairs={{0,8},{8,16},{16,24},{24,32},{32,40},{40,48},{48,56},{56,64},{64,7... | collective-permute-start | bytes 393224 | tf_op jit(solution)/shard_map/ppermute | solution.py:224
  78.6 8.2 %collective-permute-start.13 = (f32[2,2,512]{2,1,0:T(2,128)S(1)}, f32[2,2,512]{2,1,0:T(2,128)S(1)}, u32[]{:S(2)}, u32[]{:S(2)}) collective-permute-start(f32[2,2,512]{2,1,0:T(2,128)S(1)} %get-tuple-element.38), channel_id=1, source_target_pairs={{0,16},{8,24},{64,80},{72,88},{128,144},{136,152},{192,208},{200,2... | collective-permute-start | bytes 24584 | tf_op jit(solution)/shard_map/ppermute | solution.py:224
  79.9 6.9 %collective-permute-start.14 = (f32[2,2,512]{2,1,0:T(2,128)S(1)}, f32[2,2,512]{2,1,0:T(2,128)S(1)}, u32[]{:S(2)}, u32[]{:S(2)}) collective-permute-start(f32[2,2,512]{2,1,0:T(2,128)S(1)} %get-tuple-element.39), channel_id=1, source_target_pairs={{0,32},{8,40},{64,96},{72,104},{128,160},{136,168},{192,224},{200,... | collective-permute-start | bytes 24584 | tf_op jit(solution)/shard_map/ppermute | solution.py:224
  81.2 6.3 %collective-permute-start.15 = (f32[2,2,512]{2,1,0:T(2,128)S(1)}, f32[2,2,512]{2,1,0:T(2,128)S(1)}, u32[]{:S(2)}, u32[]{:S(2)}) collective-permute-start(f32[2,2,512]{2,1,0:T(2,128)S(1)} %get-tuple-element.40), channel_id=1, source_target_pairs={{0,48},{8,56},{64,112},{72,120},{128,176},{136,184},{192,240},{200... | collective-permute-start | bytes 24584 | tf_op jit(solution)/shard_map/ppermute | solution.py:224

commit v10 on v9

--- a/solution.py
+++ b/solution.py
@@ -141,7 +141,7 @@
 
 def next_first(
     counts, first, rest, up, down, inv, tra, select, r0_even, r0_odd,
-    cur_ref, first_ref, up_ref, down_ref,
+    cur_ref, first_ref, traces_ref,
     r0, sem,
 ):
     odd = lax.axis_index("c") == 1
@@ -161,10 +161,17 @@
     newest = dot_t(cur.astype(BF16), r0[...]) * alive
     following = dot_t((rest[...] - newest).astype(BF16), inv[...])
     first_ref[...] = following
-    trace_of(following, select, up_ref, down_ref)
-
-
-def second_current(cur0, first, up, down, inv, tra, gather_ref, s0, s1, s2, s3, both, sem):
+    half = select.shape[1] // 2
+    trace = dot(following.astype(BF16), select[...]).astype(BF16)
+    dom = lax.axis_index("dom")
+    traces_ref[...] = jnp.zeros_like(traces_ref)
+    traces_ref[(dom + 1) % DOM] = trace[:, half:]
+    traces_ref[(dom + DOM - 1) % DOM] = trace[:, :half]
+
+
+def second_current(cur0, first, traces, inv, tra, gather_ref, s0, s1, s2, s3, both, sem):
+    dom = lax.axis_index("dom")
+    up, down = traces[(dom + DOM - 1) % DOM], traces[(dom + 1) % DOM]
     cur1 = first[...] - coupled(up, down, inv, tra)
     c0 = cur0[...]
     both[...] = jnp.concatenate([cur1.astype(BF16), c0.astype(BF16)], axis=0)
@@ -304,24 +311,24 @@
     r0 = relayed((0, 3, 5), (1, 2, 6), r0, s2a, s2b, rest)
     s3 = permute(r0, DELAY, [(at(i, 0, 0), at(i, 0, 1)) for i in range(Y)])
     up, down = halo(up, down)
-    cur0, first, up, down = call(
+    cur0, first, traces = call(
         next_first,
-        (shape((cols, n), F32), shape((cols, n), F32)) + trace_shape,
+        (shape((cols, n), F32), shape((cols, n), F32), shape((DOM, cols, half), BF16)),
         [SMEM] + [VMEM] * 7 + [any_spec] * 2,
         2 * 8 * n * n * 5,
         2 * 1024 * 1024,
         scratch_shapes=[pltpu.VMEM((n, n), BF16), pltpu.SemaphoreType.DMA],
     )(counts, first, rest, up, down, inverse, transfer, select, r0, s3)
-    up, down = halo(up, down)
+    traces = lax.all_to_all(traces, "dom", 0, 0, tiled=True)
     gather, *share = call(
         second_current,
         [shape((OWNERS, 2 * cols, n), BF16)] + [shape((steps, 2, n), F32)] * ZH,
-        [VMEM] * 6,
+        [VMEM] * 5,
         2 * 8 * n * n * 2,
         1024 * 1024,
         out_specs=[any_spec] + [VMEM] * ZH,
         scratch_shapes=[pltpu.VMEM((2 * cols, n), BF16), pltpu.SemaphoreType.DMA],
-    )(cur0, first, up, down, inverse, transfer)
+    )(cur0, first, traces, inverse, transfer)
     gather = lax.all_to_all(gather, ("y", "c"), 0, 0, tiled=True)
     for z in range(1, ZH):
         share[z] = permute(share[z], DELAY, [(at(i, 0, c), at(i, z, c)) for i in range(Y) for c in range(CORE)])

time: 90 us -> 92.2 us (1.024)
  blocking collectives: 0 us -> 9.95 us
  starting transfers between devices: 59.7 us -> 52.7 us
    all_to_all x0 -> x1, blocking collectives: none -> 9.95 us  [body(): traces = lax.all_to_all(traces, 'dom', 0, 0, tiled=True)]
    ppermute x17 -> x15, starting transfers between devices: 40.9 us -> 33.3 us  [permute(): return lax.ppermute(value, axes, pairs)]
    ppermute x17 -> x15, waiting for transfers between devices: 7.67 us -> 6.97 us  [permute(): return lax.ppermute(value, axes, pairs)]
  transfers between devices with their start and end apart: 19 -> 17, of which waited for: 7 -> 6; matrix products, arithmetic and copies ran while one was open for 0% -> 0% of each run, Pallas kernels for 4% -> 4%
where the time goes in v10:
time: 92.2 us; the launch traced here: 91.5 us
  starting transfers between devices  52.7 us (57%)
  waiting for transfers between devices  18 us (20%)
  blocking collectives  9.95 us (11%)
  Pallas kernels  7.63 us (8%)
  local copies, waits for them, and re-layouts  1.6 us (2%)
  between operations  1.57 us (2%)
    ppermute x15, starting transfers between devices, permute(): return lax.ppermute(value, axes, pairs)  33.3 us
    all_to_all x1, starting transfers between devices, body(): lax.all_to_all(packed.reshape(OWNERS, cols, lanes), ('y', 'c'), 0, 0, til...  12.3 us
    all_to_all x1, waiting for transfers between devices, body(): lax.all_to_all(packed.reshape(OWNERS, cols, lanes), ('y', 'c'), 0, 0, til...  10.1 us
    all_to_all x1, blocking collectives, body(): traces = lax.all_to_all(traces, 'dom', 0, 0, tiled=True)  9.95 us
    all_to_all x1, starting transfers between devices, body(): gather = lax.all_to_all(gather, ('y', 'c'), 0, 0, tiled=True)  7.07 us
    ppermute x15, waiting for transfers between devices, permute(): return lax.ppermute(value, axes, pairs)  6.97 us
    pallas_call x1, Pallas kernels, body(): call(own_partials, (shape((width, n), BF16), shape((width, n), F32), shap...  2.05 us
  transfers between devices with their start and end apart: 17, of which 6 were waited for; matrix products, arithmetic and copies ran while one was open for 0% of the time, Pallas kernels for 4%

profile of v10, /device:TPU:1, one launch (start us, length us, event | category | flops | bytes accessed | tf_op | source)
XLA Modules:
  0.0 91.5 jit_solution(521386752608219240)
XLA Ops:
  0.6 0.9 %slice_bitcast_fusion.after = bf16[512,128]{1,0:T(8,128)(2,1)S(1)} fusion(bf16[2,512,128]{2,1,0:T(8,128)(2,1)} %hist.3), kind=kLoop, calls=%fused_computation | loop fusion | bytes 262144 | tf_op jit(solution)/shard_map/squeeze | solution.py:264
  1.6 1.1 %shard_map.86.r0.held = bf16[512,512]{1,0:T(8,128)(2,1)S(1)} custom-call(bf16[2,512,512]{2,1,0:T(8,128)(2,1)} %ret.3, bf16[512,128]{1,0:T(8,128)(2,1)S(1)} %slice_bitcast_fusion.after), custom_call_target="tpu_custom_call" | custom-call | bytes 1048576 | tf_op jit(solution)/shard_map/pallas_call | solution.py:266
  2.7 0.7 collective-permute-start.7
  3.4 0.7 collective-permute-start.6
  4.1 7.2 %collective-permute-start = (bf16[512,128]{1,0:T(8,128)(2,1)S(1)}, bf16[512,128]{1,0:T(8,128)(2,1)S(1)}, u32[]{:S(2)}, u32[]{:S(2)}) collective-permute-start(bf16[512,128]{1,0:T(8,128)(2,1)S(1)} %slice_bitcast_fusion.after), channel_id=1, source_target_pairs={{0,8},{8,16},{16,24},{24,32},{32,40},{40,48},{48,56},{56,64},{64,7... | collective-permute-start | bytes 393224 | tf_op jit(solution)/shard_map/ppermute | solution.py:231
  12.0 0.7 copy-done.4
  12.6 2.0 %shard_map.87 = (bf16[128,512]{1,0:T(8,128)(2,1)S(1)}, f32[128,512]{1,0:T(8,128)S(1)}, bf16[512,256]{1,0:T(8,128)(2,1)S(1)}, bf16[128,128]{1,0:T(8,128)(2,1)S(1)}) custom-call(s32[1]{0:T(128)S(6)} %copy.9.counts, f32[2,2,512]{2,1,0:T(2,128)S(1)} %bitcast.5, s32[1,256]{1,0:T(1,128)S(1)} %copy-done.4, bf16[2,512,128]{2,1,0:T(8,128)(2,1)S(1)} %copy-done.1, ...), custom_call_target="tpu_custom_call" | custom-call | flops 268435456 | bytes 2097152 | tf_op jit(solution)/shard_map/pallas_call | solution.py:275
  14.7 1.2 %shard_map.88 = (bf16[128,1024]{1,0:T(8,128)(2,1)}, bf16[512,128]{1,0:T(8,128)(2,1)S(1)}) custom-call(s32[1]{0:T(128)S(6)} %copy.9.counts, bf16[128,128]{1,0:T(8,128)(2,1)S(1)} %get-tuple-element.22.order, bf16[128,512]{1,0:T(8,128)(2,1)S(1)} %get-tuple-element.23.d0, f32[128,512]{1,0:T(8,128)S(1)} %get-tuple-element.24.d1, ...), custom_call_target="tpu_custom_call" | custom-call | flops 67108864 | bytes 1048576 | tf_op jit(solution)/shard_map/pallas_call | solution.py:286
  15.9 12.3 %all-to-all-start = ((bf16[16,8,1024]{2,1,0:T(8,128)(2,1)}), bf16[16,8,1024]{2,1,0:T(8,128)(2,1)S(1)}, u32[]{:S(2)}, u32[]{:S(2)}) async-start(bf16[16,8,1024]{2,1,0:T(8,128)(2,1)} %bitcast.2), calls=%async_computation | async-start | bytes 524288 | tf_op jit(solution)/shard_map/all_to_all | solution.py:294
  28.4 0.8 collective-permute-start.9
  29.2 0.7 collective-permute-start.8
  29.9 10.1 %all-to-all-done.x = bf16[16,8,1024]{2,1,0:T(8,128)(2,1)S(1)} async-done(((bf16[16,8,1024]{2,1,0:T(8,128)(2,1)}), bf16[16,8,1024]{2,1,0:T(8,128)(2,1)S(1)}, u32[]{:S(2)}, u32[]{:S(2)}) %all-to-all-start) | async-done | bytes 262176 | tf_op jit(solution)/shard_map/all_to_all | solution.py:294
  40.0 1.3 %collective-permute-start.3 = (f32[8,1024]{1,0:T(8,128)S(1)}, f32[8,1024]{1,0:T(8,128)S(1)}, u32[]{:S(2)}, u32[]{:S(2)}) collective-permute-start(f32[8,1024]{1,0:T(8,128)S(1)} %shard_map.89.x0), channel_id=1, source_target_pairs={{32,0},{33,1},{34,2},{35,3},{36,4},{37,5},{38,6},{39,7},{40,8},{41... | collective-permute-start | bytes 98312 | tf_op jit(solution)/shard_map/ppermute | solution.py:231
  41.3 1.3 %collective-permute-start.2 = (f32[8,1024]{1,0:T(8,128)S(1)}, f32[8,1024]{1,0:T(8,128)S(1)}, u32[]{:S(2)}, u32[]{:S(2)}) collective-permute-start(f32[8,1024]{1,0:T(8,128)S(1)} %shard_map.89.x0), channel_id=1, source_target_pairs={{48,0},{49,1},{50,2},{51,3},{52,4},{53,5},{54,6},{55,7},{56,8},{57... | collective-permute-start | bytes 98312 | tf_op jit(solution)/shard_map/ppermute | solution.py:231
  42.6 1.3 %collective-permute-start.1 = (f32[8,1024]{1,0:T(8,128)S(1)}, f32[8,1024]{1,0:T(8,128)S(1)}, u32[]{:S(2)}, u32[]{:S(2)}) collective-permute-start(f32[8,1024]{1,0:T(8,128)S(1)} %shard_map.89.x0), channel_id=1, source_target_pairs={{16,0},{17,1},{18,2},{19,3},{20,4},{21,5},{22,6},{23,7},{24,8},{25... | collective-permute-start | bytes 98312 | tf_op jit(solution)/shard_map/ppermute | solution.py:231
  43.9 5.3 %collective-permute-done.3.x3 = f32[8,1024]{1,0:T(8,128)S(1)} collective-permute-done((f32[8,1024]{1,0:T(8,128)S(1)}, f32[8,1024]{1,0:T(8,128)S(1)}, u32[]{:S(2)}, u32[]{:S(2)}) %collective-permute-start.3) | collective-permute-done | bytes 32800 | tf_op jit(solution)/shard_map/ppermute | solution.py:231
  49.4 0.4 shard_map.90
  49.9 1.3 %collective-permute-start.10 = (bf16[512,512]{1,0:T(8,128)(2,1)S(1)}, bf16[512,512]{1,0:T(8,128)(2,1)S(1)}, u32[]{:S(2)}, u32[]{:S(2)}) collective-permute-start(bf16[512,512]{1,0:T(8,128)(2,1)S(1)} %shard_map.92.r0_even), channel_id=1, source_target_pairs={{0,8},{64,72},{128,136},{192,200},{256,264},{320,328},{384,392},{4... | collective-permute-start | bytes 1572872 | tf_op jit(solution)/shard_map/ppermute | solution.py:231
  51.2 3.8 %collective-permute-start.4 = (bf16[8,128]{1,0:T(8,128)(2,1)S(1)}, bf16[8,128]{1,0:T(8,128)(2,1)S(1)}, u32[]{:S(2)}, u32[]{:S(2)}) collective-permute-start(bf16[8,128]{1,0:T(8,128)(2,1)S(1)} %get-tuple-element.29), channel_id=1, source_target_pairs={{0,1},{1,2},{2,3},{3,4},{4,5},{5,6},{6,7},{7,0},{8,9},{9,10},{10,1... | collective-permute-start | bytes 6152 | tf_op jit(solution)/shard_map/ppermute | solution.py:231
  55.0 4.1 %collective-permute-start.5 = (bf16[8,128]{1,0:T(8,128)(2,1)S(1)}, bf16[8,128]{1,0:T(8,128)(2,1)S(1)}, u32[]{:S(2)}, u32[]{:S(2)}) collective-permute-start(bf16[8,128]{1,0:T(8,128)(2,1)S(1)} %get-tuple-element.30), channel_id=1, source_target_pairs={{1,0},{2,1},{3,2},{4,3},{5,4},{6,5},{7,6},{0,7},{9,8},{10,9},{11,1... | collective-permute-start | bytes 6152 | tf_op jit(solution)/shard_map/ppermute | solution.py:231
  59.2 0.7 collective-permute-done.5.down
  59.9 1.0 %shard_map.93 = (f32[8,512]{1,0:T(8,128)S(1)}, f32[8,512]{1,0:T(8,128)S(1)}, bf16[8,8,128]{2,1,0:T(8,128)(2,1)S(1)}) custom-call(s32[1]{0:T(128)S(6)} %copy.9.counts, f32[8,512]{1,0:T(8,128)S(1)} %get-tuple-element.27.first, f32[8,512]{1,0:T(8,128)S(1)} %get-tuple-element.28.after.rest, bf16[8,128]{1,0:T(8,128)(2,1)S(1)} %collective-permute-done.4.up, ...), custom_call_target="tpu_custom_call" | custom-call | flops 20971520 | bytes 2097152 | tf_op jit(solution)/shard_map/pallas_call | solution.py:314
  60.9 9.9 %all_to_all.15.traces = bf16[8,8,128]{2,1,0:T(8,128)(2,1)S(1)} all-to-all(bf16[8,8,128]{2,1,0:T(8,128)(2,1)S(1)} %get-tuple-element.33), channel_id=1, replica_groups=mesh['y'=8,'zh'=4,'c'=2,'dom'=8] {'dom'}, dimensions={0} | all-to-all | bytes 32768 | tf_op jit(solution)/shard_map/all_to_all | solution.py:322
  70.8 1.0 %shard_map.94 = (bf16[16,16,512]{2,1,0:T(8,128)(2,1)}, f32[2,2,512]{2,1,0:T(2,128)S(1)}, f32[2,2,512]{2,1,0:T(2,128)S(1)}, f32[2,2,512]{2,1,0:T(2,128)S(1)}, f32[2,2,512]{2,1,0:T(2,128)S(1)}) custom-call(f32[8,512]{1,0:T(8,128)S(1)} %get-tuple-element.31.cur0, f32[8,512]{1,0:T(8,128)S(1)} %get-tuple-element.32.first, ...), custom_call_target="tpu_custom_call" | custom-call | flops 8388608 | bytes 1048576 | tf_op jit(solution)/shard_map/pallas_call | solution.py:323
  71.8 7.1 %all-to-all-start.2 = ((bf16[16,16,512]{2,1,0:T(8,128)(2,1)}), bf16[16,16,512]{2,1,0:T(8,128)(2,1)S(1)}, u32[]{:S(2)}, u32[]{:S(2)}) async-start(bf16[16,16,512]{2,1,0:T(8,128)(2,1)} %get-tuple-element.34), calls=%async_computation.2 | async-start | bytes 524288 | tf_op jit(solution)/shard_map/all_to_all | solution.py:332
  78.9 1.9 %collective-permute-start.14 = (bf16[512,128]{1,0:T(8,128)(2,1)S(1)}, bf16[512,128]{1,0:T(8,128)(2,1)S(1)}, u32[]{:S(2)}, u32[]{:S(2)}) collective-permute-start(bf16[512,128]{1,0:T(8,128)(2,1)S(1)} %get-tuple-element.39), channel_id=1, source_target_pairs={{0,8},{8,16},{16,24},{24,32},{32,40},{40,48},{48,56},{56,64},{64,7... | collective-permute-start | bytes 393224 | tf_op jit(solution)/shard_map/ppermute | solution.py:231
  80.8 1.3 %collective-permute-start.11 = (f32[2,2,512]{2,1,0:T(2,128)S(1)}, f32[2,2,512]{2,1,0:T(2,128)S(1)}, u32[]{:S(2)}, u32[]{:S(2)}) collective-permute-start(f32[2,2,512]{2,1,0:T(2,128)S(1)} %get-tuple-element.36), channel_id=1, source_target_pairs={{0,16},{8,24},{64,80},{72,88},{128,144},{136,152},{192,208},{200,2... | collective-permute-start | bytes 24584 | tf_op jit(solution)/shard_map/ppermute | solution.py:231
  82.1 1.3 %collective-permute-start.12 = (f32[2,2,512]{2,1,0:T(2,128)S(1)}, f32[2,2,512]{2,1,0:T(2,128)S(1)}, u32[]{:S(2)}, u32[]{:S(2)}) collective-permute-start(f32[2,2,512]{2,1,0:T(2,128)S(1)} %get-tuple-element.37), channel_id=1, source_target_pairs={{0,32},{8,40},{64,96},{72,104},{128,160},{136,168},{192,224},{200,... | collective-permute-start | bytes 24584 | tf_op jit(solution)/shard_map/ppermute | solution.py:231
  83.4 5.6 %collective-permute-start.13 = (f32[2,2,512]{2,1,0:T(2,128)S(1)}, f32[2,2,512]{2,1,0:T(2,128)S(1)}, u32[]{:S(2)}, u32[]{:S(2)}) collective-permute-start(f32[2,2,512]{2,1,0:T(2,128)S(1)} %get-tuple-element.38), channel_id=1, source_target_pairs={{0,48},{8,56},{64,112},{72,120},{128,176},{136,184},{192,240},{200... | collective-permute-start | bytes 24584 | tf_op jit(solution)/shard_map/ppermute | solution.py:231
  89.0 0.7 collective-permute-done.13.s3
  89.7 1.0 %all-to-all-done.2.gathered = bf16[16,16,512]{2,1,0:T(8,128)(2,1)S(1)} async-done(((bf16[16,16,512]{2,1,0:T(8,128)(2,1)}), bf16[16,16,512]{2,1,0:T(8,128)(2,1)S(1)}, u32[]{:S(2)}, u32[]{:S(2)}) %all-to-all-start.2) | async-done | bytes 262176 | tf_op jit(solution)/shard_map/all_to_all | solution.py:332
  90.7 0.7 shard_map.95
  (24 shorter events, 0.5 us)
Async XLA Ops:
  1.5 10.4 %copy-start.1 = (bf16[2,512,128]{2,1,0:T(8,128)(2,1)S(1)}, bf16[2,512,128]{2,1,0:T(8,128)(2,1)}, u32[]{:S(2)}) copy-start(bf16[2,512,128]{2,1,0:T(8,128)(2,1)} %hist.3) | copy-start | bytes 786436
  1.6 10.4 %copy-start.3 = (f32[2,512,2]{1,2,0:T(2,128)S(1)}, f32[2,512,2]{1,2,0:T(2,128)}, u32[]{:S(2)}) copy-start(f32[2,512,2]{1,2,0:T(2,128)} %param.7) | copy-start | bytes 24580
  2.7 25.6 %collective-permute-start.7 = (bf16[512,512]{1,0:T(8,128)(2,1)S(1)}, bf16[512,512]{1,0:T(8,128)(2,1)S(1)}, u32[]{:S(2)}, u32[]{:S(2)}) collective-permute-start(bf16[512,512]{1,0:T(8,128)(2,1)S(1)} %shard_map.86.r0.held), channel_id=1, source_target_pairs={{0,320},{1,321},{2,322},{3,323},{4,324},{5,325},{6,326},{7,327}} | collective-permute-start | bytes 1572872 | tf_op jit(solution)/shard_map/ppermute | solution.py:231
  3.4 24.9 %collective-permute-start.6 = (bf16[512,512]{1,0:T(8,128)(2,1)S(1)}, bf16[512,512]{1,0:T(8,128)(2,1)S(1)}, u32[]{:S(2)}, u32[]{:S(2)}) collective-permute-start(bf16[512,512]{1,0:T(8,128)(2,1)S(1)} %shard_map.86.r0.held), channel_id=1, source_target_pairs={{0,192},{1,193},{2,194},{3,195},{4,196},{5,197},{6,198},{7,199}} | collective-permute-start | bytes 1572872 | tf_op jit(solution)/shard_map/ppermute | solution.py:231
  4.1 10.6 %collective-permute-start = (bf16[512,128]{1,0:T(8,128)(2,1)S(1)}, bf16[512,128]{1,0:T(8,128)(2,1)S(1)}, u32[]{:S(2)}, u32[]{:S(2)}) collective-permute-start(bf16[512,128]{1,0:T(8,128)(2,1)S(1)} %slice_bitcast_fusion.after), channel_id=1, source_target_pairs={{0,8},{8,16},{16,24},{24,32},{32,40},{40,48},{48,56},{56,64},{64,7... | collective-permute-start | bytes 393224 | tf_op jit(solution)/shard_map/ppermute | solution.py:231
  11.9 0.7 copy-start.4
  15.9 24.1 %all-to-all-start = ((bf16[16,8,1024]{2,1,0:T(8,128)(2,1)}), bf16[16,8,1024]{2,1,0:T(8,128)(2,1)S(1)}, u32[]{:S(2)}, u32[]{:S(2)}) async-start(bf16[16,8,1024]{2,1,0:T(8,128)(2,1)} %bitcast.2), calls=%async_computation | async-start | bytes 524288 | tf_op jit(solution)/shard_map/all_to_all | solution.py:294
  28.3 21.1 %copy-start = (bf16[512,512]{1,0:T(8,128)(2,1)S(1)}, bf16[512,512]{1,0:T(8,128)(2,1)}, u32[]{:S(2)}) copy-start(bf16[512,512]{1,0:T(8,128)(2,1)} %inv.5) | copy-start | bytes 1572868
  28.4 21.4 %collective-permute-start.9 = (bf16[512,512]{1,0:T(8,128)(2,1)S(1)}, bf16[512,512]{1,0:T(8,128)(2,1)S(1)}, u32[]{:S(2)}, u32[]{:S(2)}) collective-permute-start(bf16[512,512]{1,0:T(8,128)(2,1)S(1)} %shard_map.91.held), channel_id=1, source_target_pairs={{0,448},{192,256},{1,449},{193,257},{2,450},{194,258},{3,451},{195... | collective-permute-start | bytes 1572872 | tf_op jit(solution)/shard_map/ppermute | solution.py:231
  29.2 20.6 %collective-permute-start.8 = (bf16[512,512]{1,0:T(8,128)(2,1)S(1)}, bf16[512,512]{1,0:T(8,128)(2,1)S(1)}, u32[]{:S(2)}, u32[]{:S(2)}) collective-permute-start(bf16[512,512]{1,0:T(8,128)(2,1)S(1)} %shard_map.91.held), channel_id=1, source_target_pairs={{0,64},{192,128},{320,384},{1,65},{193,129},{321,385},{2,66},{194,... | collective-permute-start | bytes 1572872 | tf_op jit(solution)/shard_map/ppermute | solution.py:231
  40.0 9.2 %collective-permute-start.3 = (f32[8,1024]{1,0:T(8,128)S(1)}, f32[8,1024]{1,0:T(8,128)S(1)}, u32[]{:S(2)}, u32[]{:S(2)}) collective-permute-start(f32[8,1024]{1,0:T(8,128)S(1)} %shard_map.89.x0), channel_id=1, source_target_pairs={{32,0},{33,1},{34,2},{35,3},{36,4},{37,5},{38,6},{39,7},{40,8},{41... | collective-permute-start | bytes 98312 | tf_op jit(solution)/shard_map/ppermute | solution.py:231
  41.3 8.1 %collective-permute-start.2 = (f32[8,1024]{1,0:T(8,128)S(1)}, f32[8,1024]{1,0:T(8,128)S(1)}, u32[]{:S(2)}, u32[]{:S(2)}) collective-permute-start(f32[8,1024]{1,0:T(8,128)S(1)} %shard_map.89.x0), channel_id=1, source_target_pairs={{48,0},{49,1},{50,2},{51,3},{52,4},{53,5},{54,6},{55,7},{56,8},{57... | collective-permute-start | bytes 98312 | tf_op jit(solution)/shard_map/ppermute | solution.py:231
  42.6 6.8 %collective-permute-start.1 = (f32[8,1024]{1,0:T(8,128)S(1)}, f32[8,1024]{1,0:T(8,128)S(1)}, u32[]{:S(2)}, u32[]{:S(2)}) collective-permute-start(f32[8,1024]{1,0:T(8,128)S(1)} %shard_map.89.x0), channel_id=1, source_target_pairs={{16,0},{17,1},{18,2},{19,3},{20,4},{21,5},{22,6},{23,7},{24,8},{25... | collective-permute-start | bytes 98312 | tf_op jit(solution)/shard_map/ppermute | solution.py:231
  49.8 10.1 %copy-start.2 = (bf16[512,256]{1,0:T(8,128)(2,1)S(1)}, bf16[512,256]{1,0:T(8,128)(2,1)}, u32[]{:S(2)}) copy-start(bf16[512,256]{1,0:T(8,128)(2,1)} %tra.3) | copy-start | bytes 786436
  49.9 10.0 %collective-permute-start.10 = (bf16[512,512]{1,0:T(8,128)(2,1)S(1)}, bf16[512,512]{1,0:T(8,128)(2,1)S(1)}, u32[]{:S(2)}, u32[]{:S(2)}) collective-permute-start(bf16[512,512]{1,0:T(8,128)(2,1)S(1)} %shard_map.92.r0_even), channel_id=1, source_target_pairs={{0,8},{64,72},{128,136},{192,200},{256,264},{320,328},{384,392},{4... | collective-permute-start | bytes 1572872 | tf_op jit(solution)/shard_map/ppermute | solution.py:231
  51.2 8.0 %collective-permute-start.4 = (bf16[8,128]{1,0:T(8,128)(2,1)S(1)}, bf16[8,128]{1,0:T(8,128)(2,1)S(1)}, u32[]{:S(2)}, u32[]{:S(2)}) collective-permute-start(bf16[8,128]{1,0:T(8,128)(2,1)S(1)} %get-tuple-element.29), channel_id=1, source_target_pairs={{0,1},{1,2},{2,3},{3,4},{4,5},{5,6},{6,7},{7,0},{8,9},{9,10},{10,1... | collective-permute-start | bytes 6152 | tf_op jit(solution)/shard_map/ppermute | solution.py:231
  55.0 4.8 %collective-permute-start.5 = (bf16[8,128]{1,0:T(8,128)(2,1)S(1)}, bf16[8,128]{1,0:T(8,128)(2,1)S(1)}, u32[]{:S(2)}, u32[]{:S(2)}) collective-permute-start(bf16[8,128]{1,0:T(8,128)(2,1)S(1)} %get-tuple-element.30), channel_id=1, source_target_pairs={{1,0},{2,1},{3,2},{4,3},{5,4},{6,5},{7,6},{0,7},{9,8},{10,9},{11,1... | collective-permute-start | bytes 6152 | tf_op jit(solution)/shard_map/ppermute | solution.py:231
  71.8 18.9 %all-to-all-start.2 = ((bf16[16,16,512]{2,1,0:T(8,128)(2,1)}), bf16[16,16,512]{2,1,0:T(8,128)(2,1)S(1)}, u32[]{:S(2)}, u32[]{:S(2)}) async-start(bf16[16,16,512]{2,1,0:T(8,128)(2,1)} %get-tuple-element.34), calls=%async_computation.2 | async-start | bytes 524288 | tf_op jit(solution)/shard_map/all_to_all | solution.py:332
  78.9 10.1 %collective-permute-start.14 = (bf16[512,128]{1,0:T(8,128)(2,1)S(1)}, bf16[512,128]{1,0:T(8,128)(2,1)S(1)}, u32[]{:S(2)}, u32[]{:S(2)}) collective-permute-start(bf16[512,128]{1,0:T(8,128)(2,1)S(1)} %get-tuple-element.39), channel_id=1, source_target_pairs={{0,8},{8,16},{16,24},{24,32},{32,40},{40,48},{48,56},{56,64},{64,7... | collective-permute-start | bytes 393224 | tf_op jit(solution)/shard_map/ppermute | solution.py:231
  80.8 8.2 %collective-permute-start.11 = (f32[2,2,512]{2,1,0:T(2,128)S(1)}, f32[2,2,512]{2,1,0:T(2,128)S(1)}, u32[]{:S(2)}, u32[]{:S(2)}) collective-permute-start(f32[2,2,512]{2,1,0:T(2,128)S(1)} %get-tuple-element.36), channel_id=1, source_target_pairs={{0,16},{8,24},{64,80},{72,88},{128,144},{136,152},{192,208},{200,2... | collective-permute-start | bytes 24584 | tf_op jit(solution)/shard_map/ppermute | solution.py:231
  82.1 6.9 %collective-permute-start.12 = (f32[2,2,512]{2,1,0:T(2,128)S(1)}, f32[2,2,512]{2,1,0:T(2,128)S(1)}, u32[]{:S(2)}, u32[]{:S(2)}) collective-permute-start(f32[2,2,512]{2,1,0:T(2,128)S(1)} %get-tuple-element.37), channel_id=1, source_target_pairs={{0,32},{8,40},{64,96},{72,104},{128,160},{136,168},{192,224},{200,... | collective-permute-start | bytes 24584 | tf_op jit(solution)/shard_map/ppermute | solution.py:231
  83.4 6.3 %collective-permute-start.13 = (f32[2,2,512]{2,1,0:T(2,128)S(1)}, f32[2,2,512]{2,1,0:T(2,128)S(1)}, u32[]{:S(2)}, u32[]{:S(2)}) collective-permute-start(f32[2,2,512]{2,1,0:T(2,128)S(1)} %get-tuple-element.38), channel_id=1, source_target_pairs={{0,48},{8,56},{64,112},{72,120},{128,176},{136,184},{192,240},{200... | collective-permute-start | bytes 24584 | tf_op jit(solution)/shard_map/ppermute | solution.py:231

commit v11 on v9

--- a/solution.py
+++ b/solution.py
@@ -196,21 +196,13 @@
         hist_ref[1] = before1[...]
 
 
-def relay(held_at, first_at, held, first, second, after, out, sem):
+def relay(members, *refs):
+    *sources, after, out, sem = refs
     y = lax.axis_index("y")
-    holds, from_first = one_of(y, held_at), one_of(y, first_at)
-
-    @pl.when(holds)
-    def _():
-        copied(held, out, sem)
-
-    @pl.when(jnp.logical_and(jnp.logical_not(holds), from_first))
-    def _():
-        copied(first, out, sem)
-
-    @pl.when(jnp.logical_not(jnp.logical_or(holds, from_first)))
-    def _():
-        copied(second, out, sem)
+    for held_at, source in zip(members, sources):
+        @pl.when(one_of(y, held_at))
+        def _(source=source):
+            copied(source, out, sem)
 
 
 def one_of(value, members):
@@ -239,11 +231,11 @@
     def spread(value, *hops):
         return permute(value, DELAY, [(at(i, 0, 0), at(j, 0, 0)) for i, j in hops])
 
-    def relayed(held_at, first_at, *operands):
+    def relayed(members, *operands):
         return call(
-            functools.partial(relay, held_at, first_at),
+            functools.partial(relay, members),
             shape((n, n), BF16),
-            [any_spec] * 4,
+            [any_spec] * len(operands),
             0,
             1024 * 1024,
             scratch_shapes=[pltpu.SemaphoreType.DMA],
@@ -274,7 +266,7 @@
         mib=52,
         scratch_shapes=[pltpu.VMEM((n, n), BF16), pltpu.SemaphoreType.DMA],
     )(counts, exc, faces, history, r0, retarded)
-    s1a, s1b = spread(r0, (0, 3)), spread(r0, (0, 5))
+    s1 = spread(r0, (0, 4))
     lanes = 2 * n
     packed, h0 = call(
         pack_partials,
@@ -285,8 +277,8 @@
     )(counts, order, d0, d1, r0, before1, history)
     before0 = permute(h0, DELAY, chain)
     x = lax.all_to_all(packed.reshape(OWNERS, cols, lanes), ("y", "c"), 0, 0, tiled=True)
-    r0 = relayed((0,), (3,), r0, s1a, s1b, packed)
-    s2a, s2b = spread(r0, (0, 1), (3, 2), (5, 6)), spread(r0, (0, 7), (3, 4))
+    r0 = relayed(((0, 1, 2, 3), (4, 5, 6, 7)), r0, s1, packed)
+    s2 = [spread(r0, (0, k), (4, (4 + k) % Y)) for k in (1, 7, 2)]
     x = call(sum_parts, shape((cols, lanes), F32), [VMEM], 0, 512 * 1024)(x)
     xs = [x] + [permute(x, "zh", [(z, 0)]) for z in (1, 3, 2)]
 
@@ -301,7 +293,7 @@
         2 * 8 * n * n * 2,
         1024 * 1024,
     )(*xs, inverse, select)
-    r0 = relayed((0, 3, 5), (1, 2, 6), r0, s2a, s2b, rest)
+    r0 = relayed(((0, 4), (1, 5), (7, 3), (2, 6)), r0, *s2, rest)
     s3 = permute(r0, DELAY, [(at(i, 0, 0), at(i, 0, 1)) for i in range(Y)])
     up, down = halo(up, down)
     cur0, first, up, down = call(

time: 90 us -> 95.3 us (1.059)
  waiting for transfers between devices: 18.8 us -> 23.5 us
    ppermute x17, waiting for transfers between devices: 7.67 us -> 13.1 us  [permute(): return lax.ppermute(value, axes, pairs)]
    all_to_all x1, starting transfers between devices: 6.49 us -> 7.69 us  [body(): gather = lax.all_to_all(gather, ('y', 'c'), 0, 0, tiled=True)]
  transfers between devices with their start and end apart: 19 -> 19, of which waited for: 7 -> 8; matrix products, arithmetic and copies ran while one was open for 0% -> 0% of each run, Pallas kernels for 4% -> 4%
where the time goes in v11:
time: 95.3 us; the launch traced here: 94.6 us
  starting transfers between devices  60.3 us (63%)
  waiting for transfers between devices  23.5 us (25%)
  Pallas kernels  7.63 us (8%)
  local copies, waits for them, and re-layouts  1.6 us (2%)
  between operations  1.59 us (2%)
    ppermute x17, starting transfers between devices, permute(): return lax.ppermute(value, axes, pairs)  40.3 us
    ppermute x17, waiting for transfers between devices, permute(): return lax.ppermute(value, axes, pairs)  13.1 us
    all_to_all x1, starting transfers between devices, body(): lax.all_to_all(packed.reshape(OWNERS, cols, lanes), ('y', 'c'), 0, 0, til...  12.2 us
    all_to_all x1, waiting for transfers between devices, body(): lax.all_to_all(packed.reshape(OWNERS, cols, lanes), ('y', 'c'), 0, 0, til...  9.38 us
    all_to_all x1, starting transfers between devices, body(): gather = lax.all_to_all(gather, ('y', 'c'), 0, 0, tiled=True)  7.69 us
    pallas_call x1, Pallas kernels, body(): call(own_partials, (shape((width, n), BF16), shape((width, n), F32), shap...  2.05 us
  transfers between devices with their start and end apart: 19, of which 8 were waited for; matrix products, arithmetic and copies ran while one was open for 0% of the time, Pallas kernels for 4%

profile of v11, /device:TPU:1, one launch (start us, length us, event | category | flops | bytes accessed | tf_op | source)
XLA Modules:
  0.0 94.6 jit_solution(17282838742302456663)
XLA Ops:
  0.6 0.9 slice_bitcast_fusion.after
  1.6 1.1 %shard_map.86.r0.refs_0_ = bf16[512,512]{1,0:T(8,128)(2,1)S(1)} custom-call(bf16[2,512,512]{2,1,0:T(8,128)(2,1)} %ret.3, bf16[512,128]{1,0:T(8,128)(2,1)S(1)} %slice_bitcast_fusion.after), custom_call_target="tpu_custom_call" | custom-call | bytes 1048576 | tf_op jit(solution)/shard_map/pallas_call | solution.py:251
  2.7 0.7 collective-permute-start.6
  3.4 7.2 %collective-permute-start = (bf16[512,128]{1,0:T(8,128)(2,1)S(1)}, bf16[512,128]{1,0:T(8,128)(2,1)S(1)}, u32[]{:S(2)}, u32[]{:S(2)}) collective-permute-start(bf16[512,128]{1,0:T(8,128)(2,1)S(1)} %slice_bitcast_fusion.after), channel_id=1, source_target_pairs={{0,8},{8,16},{16,24},{24,32},{32,40},{40,48},{48,56},{56,64},{64,7... | collective-permute-start | bytes 393224 | tf_op jit(solution)/shard_map/ppermute | solution.py:216
  11.9 2.1 %shard_map.87 = (bf16[128,512]{1,0:T(8,128)(2,1)S(1)}, f32[128,512]{1,0:T(8,128)S(1)}, bf16[512,256]{1,0:T(8,128)(2,1)S(1)}, bf16[128,128]{1,0:T(8,128)(2,1)S(1)}) custom-call(s32[1]{0:T(128)S(6)} %copy.9.counts, f32[2,2,512]{2,1,0:T(2,128)S(1)} %bitcast.5, s32[1,256]{1,0:T(1,128)S(1)} %copy-done.4, bf16[2,512,128]{2,1,0:T(8,128)(2,1)S(1)} %copy-done.1, ...), custom_call_target="tpu_custom_call" | custom-call | flops 268435456 | bytes 2097152 | tf_op jit(solution)/shard_map/pallas_call | solution.py:260
  14.1 1.2 %shard_map.88 = (bf16[128,1024]{1,0:T(8,128)(2,1)}, bf16[512,128]{1,0:T(8,128)(2,1)S(1)}) custom-call(s32[1]{0:T(128)S(6)} %copy.9.counts, bf16[128,128]{1,0:T(8,128)(2,1)S(1)} %get-tuple-element.23.order, bf16[128,512]{1,0:T(8,128)(2,1)S(1)} %get-tuple-element.24.d0, f32[128,512]{1,0:T(8,128)S(1)} %get-tuple-element.25.d1, ...), custom_call_target="tpu_custom_call" | custom-call | flops 67108864 | bytes 1048576 | tf_op jit(solution)/shard_map/pallas_call | solution.py:271
  15.3 12.2 %all-to-all-start = ((bf16[16,8,1024]{2,1,0:T(8,128)(2,1)}), bf16[16,8,1024]{2,1,0:T(8,128)(2,1)S(1)}, u32[]{:S(2)}, u32[]{:S(2)}) async-start(bf16[16,8,1024]{2,1,0:T(8,128)(2,1)} %bitcast.2), calls=%async_computation | async-start | bytes 524288 | tf_op jit(solution)/shard_map/all_to_all | solution.py:279
  27.6 0.8 collective-permute-start.9
  28.5 0.7 collective-permute-start.8
  29.9 9.4 %all-to-all-done.x = bf16[16,8,1024]{2,1,0:T(8,128)(2,1)S(1)} async-done(((bf16[16,8,1024]{2,1,0:T(8,128)(2,1)}), bf16[16,8,1024]{2,1,0:T(8,128)(2,1)S(1)}, u32[]{:S(2)}, u32[]{:S(2)}) %all-to-all-start) | async-done | bytes 262176 | tf_op jit(solution)/shard_map/all_to_all | solution.py:279
  39.3 1.3 %collective-permute-start.3 = (f32[8,1024]{1,0:T(8,128)S(1)}, f32[8,1024]{1,0:T(8,128)S(1)}, u32[]{:S(2)}, u32[]{:S(2)}) collective-permute-start(f32[8,1024]{1,0:T(8,128)S(1)} %shard_map.89.x0), channel_id=1, source_target_pairs={{32,0},{33,1},{34,2},{35,3},{36,4},{37,5},{38,6},{39,7},{40,8},{41... | collective-permute-start | bytes 98312 | tf_op jit(solution)/shard_map/ppermute | solution.py:216
  40.6 1.3 %collective-permute-start.2 = (f32[8,1024]{1,0:T(8,128)S(1)}, f32[8,1024]{1,0:T(8,128)S(1)}, u32[]{:S(2)}, u32[]{:S(2)}) collective-permute-start(f32[8,1024]{1,0:T(8,128)S(1)} %shard_map.89.x0), channel_id=1, source_target_pairs={{48,0},{49,1},{50,2},{51,3},{52,4},{53,5},{54,6},{55,7},{56,8},{57... | collective-permute-start | bytes 98312 | tf_op jit(solution)/shard_map/ppermute | solution.py:216
  41.9 6.6 %collective-permute-done.3.x3 = f32[8,1024]{1,0:T(8,128)S(1)} collective-permute-done((f32[8,1024]{1,0:T(8,128)S(1)}, f32[8,1024]{1,0:T(8,128)S(1)}, u32[]{:S(2)}, u32[]{:S(2)}) %collective-permute-start.3) | collective-permute-done | bytes 32800 | tf_op jit(solution)/shard_map/ppermute | solution.py:216
  48.5 1.3 %collective-permute-start.1 = (f32[8,1024]{1,0:T(8,128)S(1)}, f32[8,1024]{1,0:T(8,128)S(1)}, u32[]{:S(2)}, u32[]{:S(2)}) collective-permute-start(f32[8,1024]{1,0:T(8,128)S(1)} %shard_map.89.x0), channel_id=1, source_target_pairs={{16,0},{17,1},{18,2},{19,3},{20,4},{21,5},{22,6},{23,7},{24,8},{25... | collective-permute-start | bytes 98312 | tf_op jit(solution)/shard_map/ppermute | solution.py:216
  49.8 4.2 %collective-permute-done.1.x1 = f32[8,1024]{1,0:T(8,128)S(1)} collective-permute-done((f32[8,1024]{1,0:T(8,128)S(1)}, f32[8,1024]{1,0:T(8,128)S(1)}, u32[]{:S(2)}, u32[]{:S(2)}) %collective-permute-start.1) | collective-permute-done | bytes 32800 | tf_op jit(solution)/shard_map/ppermute | solution.py:216
  54.5 1.3 %collective-permute-start.10 = (bf16[512,512]{1,0:T(8,128)(2,1)S(1)}, bf16[512,512]{1,0:T(8,128)(2,1)S(1)}, u32[]{:S(2)}, u32[]{:S(2)}) collective-permute-start(bf16[512,512]{1,0:T(8,128)(2,1)S(1)} %shard_map.92.r0_even), channel_id=1, source_target_pairs={{0,8},{64,72},{128,136},{192,200},{256,264},{320,328},{384,392},{4... | collective-permute-start | bytes 1572872 | tf_op jit(solution)/shard_map/ppermute | solution.py:216
  55.8 3.2 %collective-permute-start.4 = (bf16[8,128]{1,0:T(8,128)(2,1)S(1)}, bf16[8,128]{1,0:T(8,128)(2,1)S(1)}, u32[]{:S(2)}, u32[]{:S(2)}) collective-permute-start(bf16[8,128]{1,0:T(8,128)(2,1)S(1)} %get-tuple-element.30), channel_id=1, source_target_pairs={{0,1},{1,2},{2,3},{3,4},{4,5},{5,6},{6,7},{7,0},{8,9},{9,10},{10,1... | collective-permute-start | bytes 6152 | tf_op jit(solution)/shard_map/ppermute | solution.py:216
  59.1 4.2 %collective-permute-start.5 = (bf16[8,128]{1,0:T(8,128)(2,1)S(1)}, bf16[8,128]{1,0:T(8,128)(2,1)S(1)}, u32[]{:S(2)}, u32[]{:S(2)}) collective-permute-start(bf16[8,128]{1,0:T(8,128)(2,1)S(1)} %get-tuple-element.31), channel_id=1, source_target_pairs={{1,0},{2,1},{3,2},{4,3},{5,4},{6,5},{7,6},{0,7},{9,8},{10,9},{11,1... | collective-permute-start | bytes 6152 | tf_op jit(solution)/shard_map/ppermute | solution.py:216
  63.2 0.7 collective-permute-done.5.down
  63.9 1.0 %shard_map.93 = (f32[8,512]{1,0:T(8,128)S(1)}, f32[8,512]{1,0:T(8,128)S(1)}, bf16[8,128]{1,0:T(8,128)(2,1)S(1)}, bf16[8,128]{1,0:T(8,128)(2,1)S(1)}) custom-call(s32[1]{0:T(128)S(6)} %copy.9.counts, f32[8,512]{1,0:T(8,128)S(1)} %get-tuple-element.28.first, f32[8,512]{1,0:T(8,128)S(1)} %get-tuple-element.29.refs_4_.rest, ...), custom_call_target="tpu_custom_call" | custom-call | flops 20971520 | bytes 2097152 | tf_op jit(solution)/shard_map/pallas_call | solution.py:299
  64.9 3.3 %collective-permute-start.11 = (bf16[8,128]{1,0:T(8,128)(2,1)S(1)}, bf16[8,128]{1,0:T(8,128)(2,1)S(1)}, u32[]{:S(2)}, u32[]{:S(2)}) collective-permute-start(bf16[8,128]{1,0:T(8,128)(2,1)S(1)} %get-tuple-element.34), channel_id=1, source_target_pairs={{0,1},{1,2},{2,3},{3,4},{4,5},{5,6},{6,7},{7,0},{8,9},{9,10},{10,1... | collective-permute-start | bytes 6152 | tf_op jit(solution)/shard_map/ppermute | solution.py:216
  68.3 4.3 %collective-permute-start.12 = (bf16[8,128]{1,0:T(8,128)(2,1)S(1)}, bf16[8,128]{1,0:T(8,128)(2,1)S(1)}, u32[]{:S(2)}, u32[]{:S(2)}) collective-permute-start(bf16[8,128]{1,0:T(8,128)(2,1)S(1)} %get-tuple-element.35), channel_id=1, source_target_pairs={{1,0},{2,1},{3,2},{4,3},{5,4},{6,5},{7,6},{0,7},{9,8},{10,9},{11,1... | collective-permute-start | bytes 6152 | tf_op jit(solution)/shard_map/ppermute | solution.py:216
  72.6 0.7 collective-permute-done.12.down
  73.3 1.0 %shard_map.94 = (bf16[16,16,512]{2,1,0:T(8,128)(2,1)}, f32[2,2,512]{2,1,0:T(2,128)S(1)}, f32[2,2,512]{2,1,0:T(2,128)S(1)}, f32[2,2,512]{2,1,0:T(2,128)S(1)}, f32[2,2,512]{2,1,0:T(2,128)S(1)}) custom-call(f32[8,512]{1,0:T(8,128)S(1)} %get-tuple-element.32.cur0, f32[8,512]{1,0:T(8,128)S(1)} %get-tuple-element.33.first, ...), custom_call_target="tpu_custom_call" | custom-call | flops 8388608 | bytes 1048576 | tf_op jit(solution)/shard_map/pallas_call | solution.py:308
  74.3 7.7 %all-to-all-start.1 = ((bf16[16,16,512]{2,1,0:T(8,128)(2,1)}), bf16[16,16,512]{2,1,0:T(8,128)(2,1)S(1)}, u32[]{:S(2)}, u32[]{:S(2)}) async-start(bf16[16,16,512]{2,1,0:T(8,128)(2,1)} %get-tuple-element.36), calls=%async_computation.1 | async-start | bytes 524288 | tf_op jit(solution)/shard_map/all_to_all | solution.py:317
  82.0 1.9 %collective-permute-start.16 = (bf16[512,128]{1,0:T(8,128)(2,1)S(1)}, bf16[512,128]{1,0:T(8,128)(2,1)S(1)}, u32[]{:S(2)}, u32[]{:S(2)}) collective-permute-start(bf16[512,128]{1,0:T(8,128)(2,1)S(1)} %get-tuple-element.41), channel_id=1, source_target_pairs={{0,8},{8,16},{16,24},{24,32},{32,40},{40,48},{48,56},{56,64},{64,7... | collective-permute-start | bytes 393224 | tf_op jit(solution)/shard_map/ppermute | solution.py:216
  83.9 1.3 %collective-permute-start.13 = (f32[2,2,512]{2,1,0:T(2,128)S(1)}, f32[2,2,512]{2,1,0:T(2,128)S(1)}, u32[]{:S(2)}, u32[]{:S(2)}) collective-permute-start(f32[2,2,512]{2,1,0:T(2,128)S(1)} %get-tuple-element.38), channel_id=1, source_target_pairs={{0,16},{8,24},{64,80},{72,88},{128,144},{136,152},{192,208},{200,2... | collective-permute-start | bytes 24584 | tf_op jit(solution)/shard_map/ppermute | solution.py:216
  85.2 1.3 %collective-permute-start.14 = (f32[2,2,512]{2,1,0:T(2,128)S(1)}, f32[2,2,512]{2,1,0:T(2,128)S(1)}, u32[]{:S(2)}, u32[]{:S(2)}) collective-permute-start(f32[2,2,512]{2,1,0:T(2,128)S(1)} %get-tuple-element.39), channel_id=1, source_target_pairs={{0,32},{8,40},{64,96},{72,104},{128,160},{136,168},{192,224},{200,... | collective-permute-start | bytes 24584 | tf_op jit(solution)/shard_map/ppermute | solution.py:216
  86.5 5.6 %collective-permute-start.15 = (f32[2,2,512]{2,1,0:T(2,128)S(1)}, f32[2,2,512]{2,1,0:T(2,128)S(1)}, u32[]{:S(2)}, u32[]{:S(2)}) collective-permute-start(f32[2,2,512]{2,1,0:T(2,128)S(1)} %get-tuple-element.40), channel_id=1, source_target_pairs={{0,48},{8,56},{64,112},{72,120},{128,176},{136,184},{192,240},{200... | collective-permute-start | bytes 24584 | tf_op jit(solution)/shard_map/ppermute | solution.py:216
  92.1 0.7 collective-permute-done.15.s3
  92.9 1.0 %all-to-all-done.1.gathered = bf16[16,16,512]{2,1,0:T(8,128)(2,1)S(1)} async-done(((bf16[16,16,512]{2,1,0:T(8,128)(2,1)}), bf16[16,16,512]{2,1,0:T(8,128)(2,1)S(1)}, u32[]{:S(2)}, u32[]{:S(2)}) %all-to-all-start.1) | async-done | bytes 262176 | tf_op jit(solution)/shard_map/all_to_all | solution.py:317
  93.9 0.7 shard_map.95
  (27 shorter events, 2.0 us)
Async XLA Ops:
  1.5 9.7 %copy-start.1 = (bf16[2,512,128]{2,1,0:T(8,128)(2,1)S(1)}, bf16[2,512,128]{2,1,0:T(8,128)(2,1)}, u32[]{:S(2)}) copy-start(bf16[2,512,128]{2,1,0:T(8,128)(2,1)} %hist.3) | copy-start | bytes 786436
  1.6 9.7 %copy-start.3 = (f32[2,512,2]{1,2,0:T(2,128)S(1)}, f32[2,512,2]{1,2,0:T(2,128)}, u32[]{:S(2)}) copy-start(f32[2,512,2]{1,2,0:T(2,128)} %param.7) | copy-start | bytes 24580
  2.7 24.9 %collective-permute-start.6 = (bf16[512,512]{1,0:T(8,128)(2,1)S(1)}, bf16[512,512]{1,0:T(8,128)(2,1)S(1)}, u32[]{:S(2)}, u32[]{:S(2)}) collective-permute-start(bf16[512,512]{1,0:T(8,128)(2,1)S(1)} %shard_map.86.r0.refs_0_), channel_id=1, source_target_pairs={{0,256},{1,257},{2,258},{3,259},{4,260},{5,261},{6,262},{7,263}} | collective-permute-start | bytes 1572872 | tf_op jit(solution)/shard_map/ppermute | solution.py:216
  3.4 10.7 %collective-permute-start = (bf16[512,128]{1,0:T(8,128)(2,1)S(1)}, bf16[512,128]{1,0:T(8,128)(2,1)S(1)}, u32[]{:S(2)}, u32[]{:S(2)}) collective-permute-start(bf16[512,128]{1,0:T(8,128)(2,1)S(1)} %slice_bitcast_fusion.after), channel_id=1, source_target_pairs={{0,8},{8,16},{16,24},{24,32},{32,40},{40,48},{48,56},{56,64},{64,7... | collective-permute-start | bytes 393224 | tf_op jit(solution)/shard_map/ppermute | solution.py:216
  11.2 0.7 copy-start.4
  15.3 23.9 %all-to-all-start = ((bf16[16,8,1024]{2,1,0:T(8,128)(2,1)}), bf16[16,8,1024]{2,1,0:T(8,128)(2,1)S(1)}, u32[]{:S(2)}, u32[]{:S(2)}) async-start(bf16[16,8,1024]{2,1,0:T(8,128)(2,1)} %bitcast.2), calls=%async_computation | async-start | bytes 524288 | tf_op jit(solution)/shard_map/all_to_all | solution.py:279
  27.6 26.5 %copy-start = (bf16[512,512]{1,0:T(8,128)(2,1)S(1)}, bf16[512,512]{1,0:T(8,128)(2,1)}, u32[]{:S(2)}) copy-start(bf16[512,512]{1,0:T(8,128)(2,1)} %inv.5) | copy-start | bytes 1572868
  27.6 26.8 %collective-permute-start.9 = (bf16[512,512]{1,0:T(8,128)(2,1)S(1)}, bf16[512,512]{1,0:T(8,128)(2,1)S(1)}, u32[]{:S(2)}, u32[]{:S(2)}) collective-permute-start(bf16[512,512]{1,0:T(8,128)(2,1)S(1)} %shard_map.91.refs_0_), channel_id=1, source_target_pairs={{0,128},{256,384},{1,129},{257,385},{2,130},{258,386},{3,131},{259... | collective-permute-start | bytes 1572872 | tf_op jit(solution)/shard_map/ppermute | solution.py:216
  28.5 25.9 %collective-permute-start.8 = (bf16[512,512]{1,0:T(8,128)(2,1)S(1)}, bf16[512,512]{1,0:T(8,128)(2,1)S(1)}, u32[]{:S(2)}, u32[]{:S(2)}) collective-permute-start(bf16[512,512]{1,0:T(8,128)(2,1)S(1)} %shard_map.91.refs_0_), channel_id=1, source_target_pairs={{0,448},{256,192},{1,449},{257,193},{2,450},{258,194},{3,451},{259... | collective-permute-start | bytes 1572872 | tf_op jit(solution)/shard_map/ppermute | solution.py:216
  29.2 25.2 %collective-permute-start.7 = (bf16[512,512]{1,0:T(8,128)(2,1)S(1)}, bf16[512,512]{1,0:T(8,128)(2,1)S(1)}, u32[]{:S(2)}, u32[]{:S(2)}) collective-permute-start(bf16[512,512]{1,0:T(8,128)(2,1)S(1)} %shard_map.91.refs_0_), channel_id=1, source_target_pairs={{0,64},{256,320},{1,65},{257,321},{2,66},{258,322},{3,67},{259,323... | collective-permute-start | bytes 1572872 | tf_op jit(solution)/shard_map/ppermute | solution.py:216
  39.3 9.2 %collective-permute-start.3 = (f32[8,1024]{1,0:T(8,128)S(1)}, f32[8,1024]{1,0:T(8,128)S(1)}, u32[]{:S(2)}, u32[]{:S(2)}) collective-permute-start(f32[8,1024]{1,0:T(8,128)S(1)} %shard_map.89.x0), channel_id=1, source_target_pairs={{32,0},{33,1},{34,2},{35,3},{36,4},{37,5},{38,6},{39,7},{40,8},{41... | collective-permute-start | bytes 98312 | tf_op jit(solution)/shard_map/ppermute | solution.py:216
  40.6 9.2 %collective-permute-start.2 = (f32[8,1024]{1,0:T(8,128)S(1)}, f32[8,1024]{1,0:T(8,128)S(1)}, u32[]{:S(2)}, u32[]{:S(2)}) collective-permute-start(f32[8,1024]{1,0:T(8,128)S(1)} %shard_map.89.x0), channel_id=1, source_target_pairs={{48,0},{49,1},{50,2},{51,3},{52,4},{53,5},{54,6},{55,7},{56,8},{57... | collective-permute-start | bytes 98312 | tf_op jit(solution)/shard_map/ppermute | solution.py:216
  48.5 5.5 %collective-permute-start.1 = (f32[8,1024]{1,0:T(8,128)S(1)}, f32[8,1024]{1,0:T(8,128)S(1)}, u32[]{:S(2)}, u32[]{:S(2)}) collective-permute-start(f32[8,1024]{1,0:T(8,128)S(1)} %shard_map.89.x0), channel_id=1, source_target_pairs={{16,0},{17,1},{18,2},{19,3},{20,4},{21,5},{22,6},{23,7},{24,8},{25... | collective-permute-start | bytes 98312 | tf_op jit(solution)/shard_map/ppermute | solution.py:216
  54.4 9.5 %copy-start.2 = (bf16[512,256]{1,0:T(8,128)(2,1)S(1)}, bf16[512,256]{1,0:T(8,128)(2,1)}, u32[]{:S(2)}) copy-start(bf16[512,256]{1,0:T(8,128)(2,1)} %tra.3) | copy-start | bytes 786436
  54.5 9.4 %collective-permute-start.10 = (bf16[512,512]{1,0:T(8,128)(2,1)S(1)}, bf16[512,512]{1,0:T(8,128)(2,1)S(1)}, u32[]{:S(2)}, u32[]{:S(2)}) collective-permute-start(bf16[512,512]{1,0:T(8,128)(2,1)S(1)} %shard_map.92.r0_even), channel_id=1, source_target_pairs={{0,8},{64,72},{128,136},{192,200},{256,264},{320,328},{384,392},{4... | collective-permute-start | bytes 1572872 | tf_op jit(solution)/shard_map/ppermute | solution.py:216
  55.8 7.4 %collective-permute-start.4 = (bf16[8,128]{1,0:T(8,128)(2,1)S(1)}, bf16[8,128]{1,0:T(8,128)(2,1)S(1)}, u32[]{:S(2)}, u32[]{:S(2)}) collective-permute-start(bf16[8,128]{1,0:T(8,128)(2,1)S(1)} %get-tuple-element.30), channel_id=1, source_target_pairs={{0,1},{1,2},{2,3},{3,4},{4,5},{5,6},{6,7},{7,0},{8,9},{9,10},{10,1... | collective-permute-start | bytes 6152 | tf_op jit(solution)/shard_map/ppermute | solution.py:216
  59.1 4.9 %collective-permute-start.5 = (bf16[8,128]{1,0:T(8,128)(2,1)S(1)}, bf16[8,128]{1,0:T(8,128)(2,1)S(1)}, u32[]{:S(2)}, u32[]{:S(2)}) collective-permute-start(bf16[8,128]{1,0:T(8,128)(2,1)S(1)} %get-tuple-element.31), channel_id=1, source_target_pairs={{1,0},{2,1},{3,2},{4,3},{5,4},{6,5},{7,6},{0,7},{9,8},{10,9},{11,1... | collective-permute-start | bytes 6152 | tf_op jit(solution)/shard_map/ppermute | solution.py:216
  64.9 7.7 %collective-permute-start.11 = (bf16[8,128]{1,0:T(8,128)(2,1)S(1)}, bf16[8,128]{1,0:T(8,128)(2,1)S(1)}, u32[]{:S(2)}, u32[]{:S(2)}) collective-permute-start(bf16[8,128]{1,0:T(8,128)(2,1)S(1)} %get-tuple-element.34), channel_id=1, source_target_pairs={{0,1},{1,2},{2,3},{3,4},{4,5},{5,6},{6,7},{7,0},{8,9},{9,10},{10,1... | collective-permute-start | bytes 6152 | tf_op jit(solution)/shard_map/ppermute | solution.py:216
  68.3 5.0 %collective-permute-start.12 = (bf16[8,128]{1,0:T(8,128)(2,1)S(1)}, bf16[8,128]{1,0:T(8,128)(2,1)S(1)}, u32[]{:S(2)}, u32[]{:S(2)}) collective-permute-start(bf16[8,128]{1,0:T(8,128)(2,1)S(1)} %get-tuple-element.35), channel_id=1, source_target_pairs={{1,0},{2,1},{3,2},{4,3},{5,4},{6,5},{7,6},{0,7},{9,8},{10,9},{11,1... | collective-permute-start | bytes 6152 | tf_op jit(solution)/shard_map/ppermute | solution.py:216
  74.3 19.6 %all-to-all-start.1 = ((bf16[16,16,512]{2,1,0:T(8,128)(2,1)}), bf16[16,16,512]{2,1,0:T(8,128)(2,1)S(1)}, u32[]{:S(2)}, u32[]{:S(2)}) async-start(bf16[16,16,512]{2,1,0:T(8,128)(2,1)} %get-tuple-element.36), calls=%async_computation.1 | async-start | bytes 524288 | tf_op jit(solution)/shard_map/all_to_all | solution.py:317
  82.0 10.1 %collective-permute-start.16 = (bf16[512,128]{1,0:T(8,128)(2,1)S(1)}, bf16[512,128]{1,0:T(8,128)(2,1)S(1)}, u32[]{:S(2)}, u32[]{:S(2)}) collective-permute-start(bf16[512,128]{1,0:T(8,128)(2,1)S(1)} %get-tuple-element.41), channel_id=1, source_target_pairs={{0,8},{8,16},{16,24},{24,32},{32,40},{40,48},{48,56},{56,64},{64,7... | collective-permute-start | bytes 393224 | tf_op jit(solution)/shard_map/ppermute | solution.py:216
  83.9 8.2 %collective-permute-start.13 = (f32[2,2,512]{2,1,0:T(2,128)S(1)}, f32[2,2,512]{2,1,0:T(2,128)S(1)}, u32[]{:S(2)}, u32[]{:S(2)}) collective-permute-start(f32[2,2,512]{2,1,0:T(2,128)S(1)} %get-tuple-element.38), channel_id=1, source_target_pairs={{0,16},{8,24},{64,80},{72,88},{128,144},{136,152},{192,208},{200,2... | collective-permute-start | bytes 24584 | tf_op jit(solution)/shard_map/ppermute | solution.py:216
  85.2 6.9 %collective-permute-start.14 = (f32[2,2,512]{2,1,0:T(2,128)S(1)}, f32[2,2,512]{2,1,0:T(2,128)S(1)}, u32[]{:S(2)}, u32[]{:S(2)}) collective-permute-start(f32[2,2,512]{2,1,0:T(2,128)S(1)} %get-tuple-element.39), channel_id=1, source_target_pairs={{0,32},{8,40},{64,96},{72,104},{128,160},{136,168},{192,224},{200,... | collective-permute-start | bytes 24584 | tf_op jit(solution)/shard_map/ppermute | solution.py:216
  86.5 6.3 %collective-permute-start.15 = (f32[2,2,512]{2,1,0:T(2,128)S(1)}, f32[2,2,512]{2,1,0:T(2,128)S(1)}, u32[]{:S(2)}, u32[]{:S(2)}) collective-permute-start(f32[2,2,512]{2,1,0:T(2,128)S(1)} %get-tuple-element.40), channel_id=1, source_target_pairs={{0,48},{8,56},{64,112},{72,120},{128,176},{136,184},{192,240},{200... | collective-permute-start | bytes 24584 | tf_op jit(solution)/shard_map/ppermute | solution.py:216
